TPU v7x, 32 devices: a whole 2x2x4 slice. The times are simulated.
32 devices in a mesh: dp: 4 (over z), fsdp: 8 (over y, x, core).
Axes of the slice: x: 2, y: 2, z: 4, core: 2. Of those that a mesh axis runs over, the one named last changes fastest.
Arguments:
- images: bfloat16 [512, 16, 16, 256], P(('dp', 'fsdp')), may hold values from -6 to 6
- timesteps: int32 [512], P(('dp', 'fsdp')), may hold values from 0 to 999
- counts: int32 [32], P(('dp', 'fsdp')), may hold values from 1 to 16
- cotangent: bfloat16 [512, 16, 16, 256], P(('dp', 'fsdp')), may hold values from -6 to 6
- conv_master: float32 [1, 2, 9, 256, 256], P(None, None, None, 'dp', 'fsdp'), may hold values from -0.125 to 0.125
- conv_moment: float32 [1, 2, 9, 256, 256], P(None, None, None, 'dp', 'fsdp'), may hold values from -1 to 1
- conv_square: float32 [1, 2, 9, 256, 256], P(None, None, None, 'dp', 'fsdp'), may hold values from 0 to 1
- embed_master: float32 [1, 512, 256], P(None, 'dp', 'fsdp'), may hold values from -0.5 to 0.5
- embed_moment: float32 [1, 512, 256], P(None, 'dp', 'fsdp'), may hold values from -1 to 1
- embed_square: float32 [1, 512, 256], P(None, 'dp', 'fsdp'), may hold values from 0 to 1
- attend_master: float32 [1, 256, 768], P(None, 'dp', 'fsdp'), may hold values from -0.375 to 0.375
- attend_moment: float32 [1, 256, 768], P(None, 'dp', 'fsdp'), may hold values from -1 to 1
- attend_square: float32 [1, 256, 768], P(None, 'dp', 'fsdp'), may hold values from 0 to 1
- output_master: float32 [1, 256, 256], P(None, 'dp', 'fsdp'), may hold values from -1 to 1
- output_moment: float32 [1, 256, 256], P(None, 'dp', 'fsdp'), may hold values from -1 to 1
- output_square: float32 [1, 256, 256], P(None, 'dp', 'fsdp'), may hold values from 0 to 1
- vector_master: float32 [1, 3072], P(None, ('dp', 'fsdp')), may hold values from -3 to 3
- vector_moment: float32 [1, 3072], P(None, ('dp', 'fsdp')), may hold values from -1 to 1
- vector_square: float32 [1, 3072], P(None, ('dp', 'fsdp')), may hold values from 0 to 1
Outputs:
- block_output: float32 [512, 16, 16, 256], P(('dp', 'fsdp'))
- input_grad: float32 [512, 16, 16, 256], P(('dp', 'fsdp'))
- conv_first: float32 [1, 2, 9, 256, 256], P(None, None, None, 'dp', 'fsdp')
- conv_second: float32 [1, 2, 9, 256, 256], P(None, None, None, 'dp', 'fsdp')
- conv_updated: float32 [1, 2, 9, 256, 256], P(None, None, None, 'dp', 'fsdp')
- embed_first: float32 [1, 512, 256], P(None, 'dp', 'fsdp')
- embed_second: float32 [1, 512, 256], P(None, 'dp', 'fsdp')
- embed_updated: float32 [1, 512, 256], P(None, 'dp', 'fsdp')
- attend_first: float32 [1, 256, 768], P(None, 'dp', 'fsdp')
- attend_second: float32 [1, 256, 768], P(None, 'dp', 'fsdp')
- attend_updated: float32 [1, 256, 768], P(None, 'dp', 'fsdp')
- output_first: float32 [1, 256, 256], P(None, 'dp', 'fsdp')
- output_second: float32 [1, 256, 256], P(None, 'dp', 'fsdp')
- output_updated: float32 [1, 256, 256], P(None, 'dp', 'fsdp')
- vector_first: float32 [1, 3072], P(None, ('dp', 'fsdp'))
- vector_second: float32 [1, 3072], P(None, ('dp', 'fsdp'))
- vector_updated: float32 [1, 3072], P(None, ('dp', 'fsdp'))
- grad_norm: float32 [], replicated
Inputs may be any that keep to these rules, and one draw needn't show every extreme that they name: `counts`: a device's live images are its first slots in order.
All inputs are finite; a program needn't handle non-finite values.
Results may differ from a plain program's by a relative error of at most 0.018.
The roundings to bfloat16 on the way count: a program that leaves them out, or rounds other values in their place, can miss the bound.
Values may be sent and summed in bfloat16 or wider, within the bound.
No kernel may reach another device: no remote copies, remote signals or barrier semaphores. Data moves between devices by JAX's collectives and lax.ppermute only.
A program may use at most 192 MiB of HBM per device.

v0:
```python
import math

import jax
import jax.numpy as jnp
from jax import lax
from jax.experimental import pallas as pl
from jax.experimental.pallas import tpu as pltpu
from jax.sharding import PartitionSpec as P

BF = jnp.bfloat16
F32 = jnp.float32
EPS = 1e-6
E = 512
STEP = 10
clip_norm = 1.0
beta_first = 0.9
beta_second = 0.999
adam_eps = 1e-08
rates_kind = (0.01, 0.03, 0.02, 0.05, 0.3)
decays_kind = (0.1, 0.1, 0.1, 0.1, 0.0)
AXES = ("dp", "fsdp")
VMEM = pltpu.CompilerParams(vmem_limit_bytes=60 * 2**20)
NB = 4
HB = 2
CH = 32
R = range(0, 256, CH)
RA = 160
RB = 240
GB = 256
GA = 144

sd = jax.ShapeDtypeStruct


def dot(a, b):
    return lax.dot_general(a, b, (((1,), (0,)), ((), ())), preferred_element_type=F32)


def dot_nt(a, b):
    return lax.dot_general(a, b, (((1,), (1,)), ((), ())), preferred_element_type=F32)


def dot_tn(a, b):
    return lax.dot_general(a, b, (((0,), (0,)), ((), ())), preferred_element_type=F32)


def gsum(s):
    n = s.shape[0]
    c = jnp.concatenate([s[:, :128], s[:, 128:]], axis=0)
    lane = lax.broadcasted_iota(jnp.int32, c.shape, 1)
    for k in (1, 2, 4):
        up = pltpu.roll(c, 128 - k, 1)
        down = pltpu.roll(c, k, 1)
        c = c + jnp.where((lane & k) == 0, up, down)
    return jnp.concatenate([c[:n], c[n:]], axis=1)


def csum(v):
    return jnp.sum(v.reshape(-1, 8, v.shape[-1]), axis=0)


def fsum(v):
    return jnp.sum(v, axis=0, keepdims=True)


def row_sums(load, base):
    s1 = s2 = None
    for r in R:
        v = load(r) - base
        a = csum(v)
        b = csum(v * v)
        s1 = a if s1 is None else s1 + a
        s2 = b if s2 is None else s2 + b
    return fsum(s1), fsum(s2)


def stats(loads, extras=None):
    firsts = [load(0)[0:1] for load in loads]
    p = jnp.concatenate(firsts, axis=0)
    if extras is not None:
        p = p + jnp.concatenate(extras, axis=0)
    q = gsum(p) * 0.125
    sums = [row_sums(load, first) for load, first in zip(loads, firsts)]
    s1 = jnp.concatenate([t[0] for t in sums], axis=0)
    s2 = jnp.concatenate([t[1] for t in sums], axis=0)
    d = p - q
    g = gsum(jnp.concatenate([s1 + 256.0 * d, s2 + d * (2.0 * s1 + 256.0 * d)], axis=0)) * (1.0 / 2048.0)
    n = len(loads)
    dm = g[:n]
    return q + dm, lax.rsqrt(g[n:] - dm * dm + EPS)


def back_coefs(sum_dy, sum_dyn, gain, rs, m):
    n = sum_dy.shape[0]
    g = gsum(jnp.concatenate([sum_dy * gain, sum_dyn * gain], axis=0)) * (1.0 / 2048.0)
    be = -rs * rs * g[n:]
    return rs * gain, be, -rs * g[:n] - m * be


def put3(pref, n, r, a, rev=False):
    rows = a.shape[0]
    col = lax.broadcasted_iota(jnp.int32, a.shape, 0) & 15
    prev = jnp.where(col == 0, 0.0, pltpu.roll(a, 1, 0))
    post = jnp.where(col == 15, 0.0, pltpu.roll(a, rows - 1, 0))
    lo, hi = (post, prev) if rev else (prev, post)
    pref[n, 16 + r : 16 + r + rows, 0:256] = lo.astype(BF)
    pref[n, 16 + r : 16 + r + rows, 256:512] = a.astype(BF)
    pref[n, 16 + r : 16 + r + rows, 512:768] = hi.astype(BF)


def zero_pads(pref):
    z = jnp.zeros((16, 768), BF)
    for n in range(NB):
        pref[n, 0:16, :] = z
        pref[n, 272:288, :] = z


def conv_forward(pref, wt_ref, N):
    acc = None
    for i in range(3):
        for j in range(3):
            rows = pref[N.start : N.stop, 16 * i : 16 * i + 256, 256 * j : 256 * j + 256]
            k = 3 * i + j
            d = dot_nt(rows.reshape(len(N) * 256, 256), wt_ref[256 * k : 256 * k + 256, :])
            acc = d if acc is None else acc + d
    return acc


def conv_turned(pref, wt_ref, N):
    acc = None
    for i in range(3):
        o = 16 * (2 - i)
        rows = pref[N.start : N.stop, o : o + 256, :].reshape(len(N) * 256, 768)
        d = dot(rows, wt_ref[768 * i : 768 * i + 768, :])
        acc = d if acc is None else acc + d
    return acc


def add_taps(acc_ref, gt, pref, N):
    for i in range(3):
        rows = pref[N.start : N.stop, 16 * i : 16 * i + 256, :].reshape(len(N) * 256, 768)
        acc_ref[256 * i : 256 * i + 256, :] += dot(gt, rows)


def interleave(gens):
    gens = list(gens)
    done = [False] * len(gens)
    at = 0
    while not all(done):
        for j, g in enumerate(gens):
            if not done[j] and at >= j:
                try:
                    next(g)
                except StopIteration:
                    done[j] = True
        at += 1


def parts():
    return [range(j, j + HB) for j in range(0, NB, HB)]


def row(ref, j):
    return ref[j : j + 1, :]


def whole(shape):
    return pl.BlockSpec(shape, lambda i, c: (0,) * len(shape))


def clamped(i, c):
    return jnp.minimum(i, (c[0] - 1) // NB)


def blocks(*tail):
    return pl.BlockSpec((NB,) + tail, lambda i, c: (clamped(i, c),) + (0,) * len(tail))


def out_blocks(*tail):
    return pl.BlockSpec((NB,) + tail, lambda i, c: (i,) + (0,) * len(tail))


def image_call(body, name, n_img, cost, in_specs, out_specs, out_shape, scratch, args):
    products, passes = cost
    return pl.pallas_call(
        body,
        grid_spec=pltpu.PrefetchScalarGridSpec(
            num_scalar_prefetch=1,
            grid=(n_img // NB,),
            in_specs=in_specs,
            out_specs=out_specs,
            scratch_shapes=scratch,
        ),
        out_shape=out_shape,
        cost_estimate=pl.CostEstimate(
            flops=n_img * products * 2 * 256**3,
            transcendentals=n_img * passes * 256**2,
            bytes_accessed=n_img * passes * 4 * 256**2,
        ),
        compiler_params=VMEM,
        name=name,
    )(*args)


def figures_body(cnt_ref, x_ref, cf_ref):
    @pl.when(pl.program_id(0) * NB < cnt_ref[0])
    def _():
        m, rs = stats([lambda r, n=n: x_ref[n, r : r + CH, :].astype(F32) for n in range(NB)])
        for n in range(NB):
            cf_ref[n] = jnp.concatenate([m[n : n + 1], rs[n : n + 1], jnp.zeros((6, 256), F32)], axis=0)


def figures(cnt, x):
    n = x.shape[0]
    return image_call(
        figures_body, "figures", n, (1, 2), [blocks(256, 256)], out_blocks(8, 256), sd((n, 8, 256), F32), [], (cnt, x)
    )


def conv_one_body(cnt_ref, x_ref, cf_ref, vec_ref, wat_ref, h0_ref, pa_ref):
    zero_pads(pa_ref)

    @pl.when(pl.program_id(0) * NB < cnt_ref[0])
    def _():
        def part(N):
            for n in N:
                sc = 0.5 * cf_ref[n, 1:2, :] * row(vec_ref, 0)
                sh = 0.5 * row(vec_ref, 1) - cf_ref[n, 0:1, :] * sc
                for r in R:
                    h = x_ref[n, r : r + CH, :].astype(F32) * sc + sh
                    put3(pa_ref, n, r, h + h * jnp.tanh(h))
            yield
            h0_ref[N.start : N.stop] = conv_forward(pa_ref, wat_ref, N).reshape(len(N), 256, 256)
            yield

        interleave([part(N) for N in parts()])


def conv_one(cnt, x, cf, vec, wat):
    n = x.shape[0]
    return image_call(
        conv_one_body,
        "conv_one",
        n,
        (18, 10),
        [blocks(256, 256), blocks(8, 256), whole((16, 256)), whole((2304, 256))],
        [out_blocks(256, 256), out_blocks(288, 768)],
        [sd((n, 256, 256), F32), sd((n, 288, 768), BF)],
        [],
        (cnt, x, cf, vec, wat),
    )


def middle_body(finish, n_out, *refs):
    (cnt_ref, x_ref, h0_ref, cot_ref, emb_ref, vec_ref, me_ref, wet_ref, wbt_ref, wqt_ref, wot_ref) = refs[:11]
    out_ref, ga_ref, dm_ref = refs[11:14]
    ends = refs[14 : 14 + n_out]
    (pa, pg, gt, mid, a3, mx, dmx, dz, she, dsr, dwb, dwq, dwo, dvec, turn) = refs[14 + n_out :]
    i = pl.program_id(0)
    cnt = cnt_ref[0]

    @pl.when(i == 0)
    def _():
        zero_pads(pa)
        zero_pads(pg)
        for ref in (dwb, dwq, dwo, dvec, dsr):
            ref[...] = jnp.zeros_like(ref)
        she[...] = dot_nt(emb_ref[...], wet_ref[...]) + (row(vec_ref, 2) + row(vec_ref, 3))

    live = i * NB < cnt

    @pl.when(jnp.logical_not(live))
    def _():
        for ref in (out_ref, ga_ref, dm_ref):
            ref[...] = jnp.zeros_like(ref)

    @pl.when(live)
    def _():
        g2, b2, c2, g3, b3, qb, vb, ob = (row(vec_ref, j) for j in range(4, 12))
        tot = {}

        def add(key, v):
            tot[key] = v if key not in tot else tot[key] + v

        def part(N):
            lo = N.start * 256
            hi = N.stop * 256
            W = range(len(N))
            L = lambda j: slice(j * 256, j * 256 + 256)
            masks = [(i * NB + n < cnt).astype(F32) for n in N]
            shifts = [she[pl.ds(i * NB + n, 1), :] for n in N]
            br = jnp.concatenate(shifts, axis=0)
            hload = [lambda r, n=n: h0_ref[n, r : r + CH, :] for n in N]
            m2, rs2 = stats(hload, shifts)
            sc2 = 0.5 * rs2 * g2
            sh2 = 0.5 * b2 + (br - m2) * sc2
            hm2 = br - m2
            for j, n in enumerate(N):
                for r in R:
                    h = hload[j](r) * sc2[j : j + 1] + sh2[j : j + 1]
                    put3(pa, n, r, h + h * jnp.tanh(h))
            yield
            o = conv_forward(pa, wbt_ref, N)
            yield
            for j, n in enumerate(N):
                for r in R:
                    mid[n, r : r + CH, :] = o[j * 256 + r : j * 256 + r + CH] + (x_ref[n, r : r + CH, :].astype(F32) + c2)
            mload = [lambda r, n=n: mid[n, r : r + CH, :] for n in N]
            m3, rs3 = stats(mload)
            sc3 = rs3 * g3
            sh3 = b3 - m3 * sc3
            for j, n in enumerate(N):
                for r in R:
                    a3[n * 256 + r : n * 256 + r + CH, :] = (mload[j](r) * sc3[j : j + 1] + sh3[j : j + 1]).astype(BF)
            gob = []
            for j, n in enumerate(N):
                go = cot_ref[n].astype(F32) * masks[j]
                add("ob", csum(go))
                gob.append(go.astype(BF))
            gall = jnp.concatenate(gob, axis=0)
            yield
            bc = jnp.concatenate([qb, jnp.zeros_like(qb), vb], axis=1)
            mx[lo:hi] = (dot_nt(a3[lo:hi], wqt_ref[...]) + bc).astype(BF)
            M = lambda j, p: mx[lo + j * 256 : lo + j * 256 + 256, 256 * p : 256 * p + 256]
            datt = dot(gall, wot_ref[...]).astype(BF)
            yield
            st = [dot_nt(M(j, 1), M(j, 0)) for j in W]
            dpt = [dot_nt(M(j, 2), datt[L(j)]) for j in W]
            yield
            pts = []
            ptb = []
            for j in W:
                s = st[j] * 0.0625
                e = jnp.exp(s - jnp.max(s, axis=0, keepdims=True))
                p = e * (1.0 / jnp.sum(e, axis=0, keepdims=True))
                pts.append(p)
                ptb.append(p.astype(BF))
            yield
            att = [dot_tn(ptb[j], M(j, 2)).astype(BF) for j in W]
            dv = [dot(ptb[j], datt[L(j)]).astype(BF) for j in W]
            yield
            dst = []
            for j in W:
                t = dpt[j] * pts[j]
                dst.append((t - pts[j] * jnp.sum(t, axis=0, keepdims=True)).astype(BF))
            yield
            attall = jnp.concatenate(att, axis=0)
            proj = dot_nt(attall, wot_ref[...])
            dwo[...] += dot_tn(gall, attall)
            dq = [(dot_tn(dst[j], M(j, 1)) * 0.0625).astype(BF) for j in W]
            dk = [(dot(dst[j], M(j, 0)) * 0.0625).astype(BF) for j in W]
            yield
            for j, n in enumerate(N):
                out_ref[n] = (mid[n] + (proj[L(j)] + ob)) * masks[j]
                s = slice(n * 256, n * 256 + 256)
                dmx[s, 0:256] = dq[j]
                dmx[s, 256:512] = dk[j]
                dmx[s, 512:768] = dv[j]
                add("qb", csum(dq[j].astype(F32)))
                add("vb", csum(dv[j].astype(F32)))
            yield
            d3 = dot(dmx[lo:hi], wqt_ref[...])
            dwq[...] += dot_tn(a3[lo:hi], dmx[lo:hi])
            yield
            As = []
            Bs = []
            for j, n in enumerate(N):
                A = B = jnp.zeros((8, 256), F32)
                for r in R:
                    dy = d3[j * 256 + r : j * 256 + r + CH]
                    A = A + csum(dy)
                    B = B + csum(dy * (mid[n, r : r + CH, :] - m3[j : j + 1]))
                As.append(fsum(A))
                Bs.append(fsum(B))
            A3 = jnp.concatenate(As, axis=0)
            B3 = jnp.concatenate(Bs, axis=0) * rs3
            add("b3", fsum(A3))
            add("g3", fsum(B3))
            al, be, ga = back_coefs(A3, B3, g3, rs3, m3)
            for j, n in enumerate(N):
                for r in R:
                    dm = cot_ref[n, r : r + CH, :].astype(F32) * masks[j] + (
                        d3[j * 256 + r : j * 256 + r + CH] * al[j : j + 1]
                        + (mid[n, r : r + CH, :] * be[j : j + 1] + ga[j : j + 1])
                    )
                    dm_ref[n, r : r + CH, :] = dm
                    add("c2", csum(dm))
                    put3(pg, n, r, dm, True)
                gt[:, n * 256 : n * 256 + 256] = pg[n, 16:272, 256:512].T
            yield
            o = conv_turned(pg, wbt_ref, N)
            add_taps(dwb, gt[:, lo:hi], pa, N)
            yield
            As = []
            Bs = []
            for j, n in enumerate(N):
                A = B = jnp.zeros((8, 256), F32)
                for r in R:
                    h0 = hload[j](r)
                    h = h0 * sc2[j : j + 1] + sh2[j : j + 1]
                    t = jnp.tanh(h)
                    dzz = o[j * 256 + r : j * 256 + r + CH] * ((1.0 + t) * (1.0 + (h - h * t)))
                    dz[n * 256 + r : n * 256 + r + CH, :] = dzz
                    A = A + csum(dzz)
                    B = B + csum(dzz * (h0 + hm2[j : j + 1]))
                As.append(fsum(A))
                Bs.append(fsum(B))
            A2 = jnp.concatenate(As, axis=0) * 0.5
            B2 = jnp.concatenate(Bs, axis=0) * (rs2 * 0.5)
            add("b2", fsum(A2))
            add("g2", fsum(B2))
            al, be, ga = back_coefs(A2, B2, g2, rs2, -hm2)
            al = al * 0.5
            for j, n in enumerate(N):
                ds = jnp.zeros((8, 256), F32)
                for r in R:
                    dh = dz[n * 256 + r : n * 256 + r + CH, :] * al[j : j + 1] + (
                        hload[j](r) * be[j : j + 1] + ga[j : j + 1]
                    )
                    ga_ref[n, r : r + CH, :] = dh.astype(BF)
                    ds = ds + csum(dh)
                dsr[pl.ds(i * NB + n, 1), :] = fsum(ds)
            yield

        interleave([part(N) for N in parts()])
        z = jnp.zeros((4, 256), F32)
        rows = [tot["g2"], tot["b2"], fsum(tot["c2"]), tot["g3"], tot["b3"]]
        rows += [fsum(tot[k]) for k in ("qb", "vb", "ob")]
        dvec[...] += jnp.concatenate([z] + rows + [z], axis=0)

    @pl.when(i == pl.num_programs(0) - 1)
    def _():
        ds = dsr[...]
        total = fsum(ds)
        rows = jnp.concatenate([jnp.zeros((2, 256), F32), total, total, dvec[4:16, :]], axis=0)
        finish(ends, me_ref, dwb, dwq, dwo, dot_tn(ds.astype(BF), emb_ref[...]), rows, turn)


def middle(cnt, x, h0, cot, emb, vec, me, wet, wbt, wqt, wot, finish, ends):
    n = x.shape[0]
    V = pltpu.VMEM
    return image_call(
        lambda *refs: middle_body(finish, len(ends), *refs),
        "middle",
        n,
        (90, 40),
        [blocks(256, 256)] * 3
        + [whole(emb.shape), whole((16, 256)), pl.BlockSpec(memory_space=pltpu.SMEM)]
        + [whole(w.shape) for w in (wet, wbt, wqt, wot)],
        [out_blocks(256, 256)] * 3 + [whole(e.shape) for e in ends],
        [sd((n, 256, 256), F32), sd((n, 256, 256), BF), sd((n, 256, 256), F32)] + list(ends),
        [
            V((NB, 288, 768), BF),
            V((NB, 288, 768), BF),
            V((256, NB * 256), BF),
            V((NB, 256, 256), F32),
            V((NB * 256, 256), BF),
            V((NB * 256, 768), BF),
            V((NB * 256, 768), BF),
            V((NB * 256, 256), F32),
            V((n, 256), F32),
            V((n, 256), F32),
            V((768, 768), F32),
            V((256, 768), F32),
            V((256, 256), F32),
            V((16, 256), F32),
            V((1280, 512), F32),
        ],
        (cnt, x, h0, cot, emb, vec, me, wet, wbt, wqt, wot),
    )


def conv_one_grad_body(finish, n_out, *refs):
    cnt_ref, ga_ref, pa_ref, me_ref = refs[:4]
    ends = refs[4 : 4 + n_out]
    gt, dwa = refs[4 + n_out :]
    i = pl.program_id(0)

    @pl.when(i == 0)
    def _():
        dwa[...] = jnp.zeros_like(dwa)

    @pl.when(i * NB < cnt_ref[0])
    def _():
        for n in range(NB):
            gt[:, n * 256 : n * 256 + 256] = ga_ref[n].T
        add_taps(dwa, gt[...], pa_ref, range(NB))

    @pl.when(i == pl.num_programs(0) - 1)
    def _():
        finish(ends, me_ref, dwa)


def conv_one_grad(cnt, ga, pa, me, finish, ends):
    n = ga.shape[0]
    return image_call(
        lambda *refs: conv_one_grad_body(finish, len(ends), *refs),
        "conv_one_grad",
        n,
        (18, 10),
        [blocks(256, 256), blocks(288, 768), pl.BlockSpec(memory_space=pltpu.SMEM)],
        [whole(e.shape) for e in ends],
        list(ends),
        [pltpu.VMEM((256, NB * 256), BF), pltpu.VMEM((768, 768), F32)],
        (cnt, ga, pa, me),
    )


def input_grad_body(finish, n_out, *refs):
    cnt_ref, x_ref, ga_ref, dm_ref, cf_ref, vec_ref, me_ref, wat_ref = refs[:8]
    ig_ref = refs[8]
    ends = refs[9 : 9 + n_out]
    pg, dz, dvec = refs[9 + n_out :]
    i = pl.program_id(0)

    @pl.when(i == 0)
    def _():
        zero_pads(pg)
        dvec[...] = jnp.zeros_like(dvec)

    live = i * NB < cnt_ref[0]

    @pl.when(jnp.logical_not(live))
    def _():
        ig_ref[...] = jnp.zeros_like(ig_ref)

    @pl.when(live)
    def _():
        g1 = row(vec_ref, 0)
        tot = {}

        def add(key, v):
            tot[key] = v if key not in tot else tot[key] + v

        def part(N):
            for n in N:
                for r in R:
                    put3(pg, n, r, ga_ref[n, r : r + CH, :].astype(F32), True)
            yield
            o = conv_turned(pg, wat_ref, N)
            yield
            As = []
            Bs = []
            ms = jnp.concatenate([cf_ref[n, 0:1, :] for n in N], axis=0)
            rss = jnp.concatenate([cf_ref[n, 1:2, :] for n in N], axis=0)
            for j, n in enumerate(N):
                m = cf_ref[n, 0:1, :]
                sc = 0.5 * cf_ref[n, 1:2, :] * g1
                sh = 0.5 * row(vec_ref, 1) - m * sc
                A = B = jnp.zeros((8, 256), F32)
                for r in R:
                    x = x_ref[n, r : r + CH, :].astype(F32)
                    h = x * sc + sh
                    t = jnp.tanh(h)
                    dzz = o[j * 256 + r : j * 256 + r + CH] * ((1.0 + t) * (1.0 + (h - h * t)))
                    dz[n * 256 + r : n * 256 + r + CH, :] = dzz
                    A = A + csum(dzz)
                    B = B + csum(dzz * (x - m))
                As.append(fsum(A))
                Bs.append(fsum(B))
            A1 = jnp.concatenate(As, axis=0) * 0.5
            B1 = jnp.concatenate(Bs, axis=0) * (rss * 0.5)
            add("b1", fsum(A1))
            add("g1", fsum(B1))
            al, be, ga = back_coefs(A1, B1, g1, rss, ms)
            al = al * 0.5
            for j, n in enumerate(N):
                for r in R:
                    ig_ref[n, r : r + CH, :] = dm_ref[n, r : r + CH, :] + (
                        dz[n * 256 + r : n * 256 + r + CH, :] * al[j : j + 1]
                        + (x_ref[n, r : r + CH, :].astype(F32) * be[j : j + 1] + ga[j : j + 1])
                    )
            yield

        interleave([part(N) for N in parts()])
        dvec[...] += jnp.concatenate([tot["g1"], tot["b1"], jnp.zeros((14, 256), F32)], axis=0)

    @pl.when(i == pl.num_programs(0) - 1)
    def _():
        finish(ends, me_ref, dvec[...])


def input_grad(cnt, x, ga, dm, cf, vec, me, wat, finish, ends):
    n = x.shape[0]
    return image_call(
        lambda *refs: input_grad_body(finish, len(ends), *refs),
        "input_grad",
        n,
        (24, 14),
        [blocks(256, 256)] * 3
        + [blocks(8, 256), whole((16, 256)), pl.BlockSpec(memory_space=pltpu.SMEM), whole(wat.shape)],
        [out_blocks(256, 256)] + [whole(e.shape) for e in ends],
        [sd((n, 256, 256), F32)] + list(ends),
        [pltpu.VMEM((NB, 288, 768), BF), pltpu.VMEM((NB * 256, 256), F32), pltpu.VMEM((16, 256), F32)],
        (cnt, x, ga, dm, cf, vec, me, wat),
    )


def sinus_embed(steps_in):
    half_width = E // 2
    frequency = jnp.exp(
        -math.log(10000.0) * jnp.arange(half_width, dtype=jnp.float32) / (half_width - 1)
    )
    angles = steps_in.astype(jnp.float32)[:, None] * frequency[None, :]
    return jnp.concatenate([jnp.sin(angles), jnp.cos(angles)], axis=1)


def halves(s0, s1):
    first = jnp.concatenate([s0[:, :64], s1[:, :64]], axis=1)
    second = jnp.concatenate([s0[:, 64:], s1[:, 64:]], axis=1)
    return first, second


def pack_body(conv, embed, attend, output, vec, a_ref, b_ref):
    for side, ref, base in ((0, a_ref, 0), (1, b_ref, 32)):
        for k in range(9):
            w = conv[9 * side + k]
            ref[base + 16 * k : base + 16 * k + 16, :] = jnp.concatenate([w[:16], w[16:]], axis=1).astype(BF)
    line = jnp.concatenate([vec[...], jnp.zeros((1, 32), F32)], axis=1)
    a_ref[144:160, :] = jnp.broadcast_to(line, (16, 128)).astype(BF)
    b_ref[0:32, :] = embed[...].astype(BF)
    at = jnp.concatenate([attend[...], jnp.zeros((64, 32), F32)], axis=1).T
    b_ref[176:224, :] = jnp.concatenate([at[:48], at[48:96]], axis=1).astype(BF)
    o = output[...]
    b_ref[224:240, :] = jnp.concatenate([o[:16], o[16:]], axis=1).astype(BF)


def pack(masters):
    return pl.pallas_call(
        pack_body, out_shape=[sd((RA, 128), BF), sd((RB, 128), BF)], compiler_params=VMEM, name="pack_shards"
    )(*masters)


def swap(x, bits):
    return lax.ppermute(x, AXES, [(i, i ^ bits) for i in range(32)])


def pairs(g, z, lo, rows, h):
    s0 = g[z ^ (2 * h), lo : lo + rows, :]
    s1 = g[z ^ (2 * h + 1), lo : lo + rows, :]
    return halves(s0, s1)


def unpack_a_body(me, *refs):
    gs = refs[:8]
    wat_ref, vec_ref, vrows = refs[8:]
    z = me[0]
    f = me[1]
    for rf in range(8):
        d0 = (f ^ rf) * 32
        for h in range(2):
            for k in range(9):
                j0, j1 = pairs(gs[rf], z, 16 * k, 16, h)
                at = pl.multiple_of(256 * k + d0, 32)
                wat_ref[pl.ds(at, 16), 128 * h : 128 * h + 128] = j0
                wat_ref[pl.ds(at + 16, 16), 128 * h : 128 * h + 128] = j1
        for rz in range(4):
            vrows[pl.ds((z ^ rz) * 8 + (f ^ rf), 1), :] = gs[rf][rz, 144:160, :].astype(F32)[0:1]
    v = vrows[...]
    v3 = jnp.concatenate([v, pltpu.roll(v, 96, 1), pltpu.roll(v, 64, 1)], axis=0).astype(BF)
    col = lax.broadcasted_iota(jnp.int32, (16, 96), 1)
    line = lax.broadcasted_iota(jnp.int32, (16, 96), 0)
    unit = 3 * (col & 31) + (col >> 5)
    lane = lax.broadcasted_iota(jnp.int32, (16, 128), 1)
    for half in range(2):
        acc = jnp.zeros((16, 128), F32)
        for t in range(4):
            sel = jnp.where(unit == 8 * line + 4 * half + t, 1.0, 0.0).astype(BF)
            piece = dot(sel, v3)
            if t:
                piece = pltpu.roll(piece, 32 * t, 1)
            acc = jnp.where((lane >> 5) == t, piece, acc)
        vec_ref[:, 128 * half : 128 * half + 128] = acc


def unpack_b_body(me, *refs):
    gs = refs[:8]
    wet_ref, wbt_ref, wqt_ref, wot_ref = refs[8:]
    z = me[0]
    f = me[1]
    for rf in range(8):
        own = f ^ rf
        d0 = own * 32
        g = gs[rf]
        for d in range(4):
            wet_ref[pl.ds(pl.multiple_of(d0, 32), 32), 128 * d : 128 * d + 128] = g[z ^ d, 0:32, :]
        for h in range(2):
            lanes = slice(128 * h, 128 * h + 128)
            for k in range(9):
                j0, j1 = pairs(g, z, 32 + 16 * k, 16, h)
                at = pl.multiple_of(256 * k + d0, 32)
                wbt_ref[pl.ds(at, 16), lanes] = j0
                wbt_ref[pl.ds(at + 16, 16), lanes] = j1
            j0, j1 = pairs(g, z, 176, 48, h)
            at = pl.multiple_of(own * 96, 32)
            wqt_ref[pl.ds(at, 48), lanes] = j0
            wqt_ref[pl.ds(at + 48, 48), lanes] = j1
            j0, j1 = pairs(g, z, 224, 16, h)
            at = pl.multiple_of(d0, 32)
            wot_ref[pl.ds(at, 16), lanes] = j0
            wot_ref[pl.ds(at + 16, 16), lanes] = j1


def unpack(body, name, me, gs, outs, scratch):
    return pl.pallas_call(
        body,
        in_specs=[pl.BlockSpec(memory_space=pltpu.SMEM)] + [pl.BlockSpec(g.shape) for g in gs],
        out_shape=outs,
        scratch_shapes=scratch,
        compiler_params=VMEM,
        name=name,
    )(me, *gs)


def place(outs, me, src, base, lanes, lo, rows, step):
    z = me[0]
    f = me[1]
    for rf in range(8):
        at = pl.multiple_of(base + (f ^ rf) * step, 16)
        ref = outs[rf & 1]
        for h in range(2):
            cut = slice(lanes + 128 * h, lanes + 128 * h + 128)
            e0, e1 = halves(src[pl.ds(at, rows), cut], src[pl.ds(at + rows, rows), cut])
            ref[rf >> 1, z ^ (2 * h), lo : lo + rows, :] = e0.astype(BF)
            ref[rf >> 1, z ^ (2 * h + 1), lo : lo + rows, :] = e1.astype(BF)


def spread_rows(rows, me):
    a8 = []
    for s in range(8):
        piece = rows[:, 128 * (s // 4) : 128 * (s // 4) + 128]
        a8.append(pltpu.roll(piece, 128 - 32 * (s % 4), 1) if s % 4 else piece)
    a8 = jnp.concatenate(a8, axis=0)
    top = a8.astype(BF)
    rest = (a8 - top.astype(F32)).astype(BF)
    col = lax.broadcasted_iota(jnp.int32, (32, 128), 1)
    line = lax.broadcasted_iota(jnp.int32, (32, 128), 0)
    owner = ((line & 3) ^ me[0]) * 8 + ((line >> 2) ^ me[1])
    acc = jnp.zeros((32, 128), F32)
    unit = 8 * (col & 15) + (col >> 4)
    for u in range(3):
        sel = jnp.where(unit == 3 * owner + u, 1.0, 0.0).astype(BF)
        piece = dot(sel, top) + dot(sel, rest)
        if u:
            piece = pltpu.roll(piece, 32 * u, 1)
        acc = jnp.where((col >> 5) == u, piece, acc)
    return acc


def finish_b(outs, me, dwb, dwq, dwo, de, rows, turn):
    for k in range(9):
        place(outs, me, dwb, 256 * (k // 3), 256 * (k % 3), 16 * k, 16, 32)
    for k in range(3):
        turn[256 * k : 256 * k + 256, 0:256] = dwq[:, 256 * k : 256 * k + 256].T
    place(outs, me, turn, 0, 0, 144, 48, 96)
    place(outs, me, dwo, 0, 0, 192, 16, 32)
    turn[1024:1280, :] = de
    for d in range(4):
        for rf in range(8):
            at = pl.multiple_of(1024 + (me[1] ^ rf) * 32, 32)
            block = turn[pl.ds(at, 32), 128 * d : 128 * d + 128]
            outs[rf & 1][rf >> 1, me[0] ^ d, 208:240, :] = block.astype(BF)
    acc = spread_rows(rows, me)
    for rf in range(8):
        for rz in range(4):
            r = 4 * rf + rz
            outs[rf & 1][rf >> 1, rz, 240:256, :] = jnp.broadcast_to(acc[r : r + 1], (16, 128)).astype(BF)


def finish_a(outs, me, dwa):
    for k in range(9):
        place(outs, me, dwa, 256 * (k // 3), 256 * (k % 3), 16 * k, 16, 32)


def finish_v(outs, me, rows):
    acc = spread_rows(rows, me)
    for rf in range(8):
        outs[rf & 1][rf >> 1] = acc[4 * rf : 4 * rf + 4]


def core_sum_body(keep, got, *outs):
    for j in range(4):
        outs[j][...] = (keep[j].astype(F32) + got[j].astype(F32)).astype(outs[j].dtype)


def over_core(keep, send):
    got = swap(send, 1)
    tail = keep.shape[2:]
    return pl.pallas_call(
        core_sum_body,
        grid=(4,),
        in_specs=[pl.BlockSpec((4, 1) + tail, lambda i: (0, i, 0, 0))] * 2,
        out_specs=[pl.BlockSpec((1,) + tail, lambda i: (i, 0, 0))] * 4,
        out_shape=[pltpu.HBM((4,) + tail, keep.dtype)] * 4,
        compiler_params=VMEM,
        name="core_sum",
    )(keep, got)


def over_core_small(keep, send):
    s = keep + swap(send, 1)
    return [s[j] for j in range(4)]


def to_plane(parts):
    return [swap(parts[1], 2), swap(parts[2], 4), swap(parts[3], 6)]


def plane_sum(own, got):
    line = [sum((g[rz].astype(F32) for g in got), own[rz].astype(F32)) for rz in range(4)]
    return line[0], [v.astype(own.dtype) for v in line[1:]]


def over_line(others):
    return [swap(v, 8 * (rz + 1)) for rz, v in enumerate(others)]


def shares_body(*refs):
    sb, sa, sv = (refs[4 * k][...] + sum(r[...].astype(F32) for r in refs[4 * k + 1 : 4 * k + 4]) for k in range(3))
    gb, ga, out = refs[12:]
    gb[0:240, :] = sb[0:240]
    vec = sb[240:241] + sv[0:1]
    gb[240:256, :] = jnp.broadcast_to(vec, (16, 128))
    ga[...] = sa
    fold = lambda v: jnp.sum((v * v).reshape(-1, 8, 128), axis=0)
    t = fsum(fold(sb[0:240]) + fold(sa)) + vec * vec
    out[...] = jnp.broadcast_to(jnp.sum(t, axis=1, keepdims=True), (8, 128))


def shares(b, a, v):
    args = []
    for own, got in (b, a, v):
        args += [own, *got]
    return pl.pallas_call(
        shares_body,
        out_shape=[sd((GB, 128), F32), sd((GA, 128), F32), sd((8, 128), F32)],
        compiler_params=VMEM,
        name="shares",
    )(*args)


def total_over(s):
    s = s + swap(s, 1)
    s = (s + swap(s, 2)) + (swap(s, 4) + swap(s, 6))
    return s, swap(s, 8), swap(s, 16), swap(s, 24)


def adam_body(*refs):
    t0, t1, t2, t3, gb, ga = refs[:6]
    state = refs[6:21]
    outs = refs[21:]
    norm = jnp.sqrt((t0[...] + t1[...]) + (t2[...] + t3[...]))[0:1]
    factor = clip_norm / jnp.maximum(norm, clip_norm)

    def put(kind, at, grad):
        clipped = grad * factor[:, : grad.shape[1]]
        mas, mom, squ = (r[at] for r in state[3 * kind : 3 * kind + 3])
        first_new = beta_first * mom + (1.0 - beta_first) * clipped
        second_new = beta_second * squ + (1.0 - beta_second) * clipped * clipped
        first_hat = first_new / (1.0 - beta_first**STEP)
        second_hat = second_new / (1.0 - beta_second**STEP)
        update = mas - rates_kind[kind] * (
            first_hat / (jnp.sqrt(second_hat) + adam_eps) + decays_kind[kind] * mas
        )
        outs[3 * kind][at] = first_new
        outs[3 * kind + 1][at] = second_new
        outs[3 * kind + 2][at] = update

    for side, ref in ((0, ga), (1, gb)):
        for k in range(9):
            g = ref[16 * k : 16 * k + 16, :]
            put(0, (9 * side + k,), jnp.concatenate([g[:, :64], g[:, 64:]], axis=0))
    put(1, (Ellipsis,), gb[208:240, :])
    g = gb[144:192, :]
    g = jnp.concatenate([jnp.concatenate([g[:, :64], g[:, 64:]], axis=0), jnp.zeros((96, 64), F32)], axis=1)
    g = jnp.concatenate([g, jnp.zeros((32, 128), F32)], axis=0).T
    put(2, (Ellipsis,), g[:64, :96])
    g = gb[192:208, :]
    put(3, (Ellipsis,), jnp.concatenate([g[:, :64], g[:, 64:]], axis=0))
    put(4, (Ellipsis,), gb[240:241, :96])
    outs[15][0] = norm[0, 0]


def adam(totals, gb, ga, state):
    return pl.pallas_call(
        adam_body,
        out_specs=[pl.BlockSpec(s.shape) for s in state] + [pl.BlockSpec(memory_space=pltpu.SMEM)],
        out_shape=[sd(s.shape, F32) for s in state] + [sd((1,), F32)],
        compiler_params=VMEM,
        name="clipped_adamw",
    )(*totals, gb, ga, *state)


def turned_state(state):
    out = []
    for kind in range(5):
        for a in state[3 * kind : 3 * kind + 3]:
            if kind == 0:
                a = jnp.swapaxes(a, 3, 4).reshape(18, 32, 64)
            elif kind == 2:
                a = a[0]
            elif kind < 4:
                a = jnp.swapaxes(a, 1, 2)[0]
            out.append(a)
    return out


def turned_back(results):
    out = []
    for kind in range(5):
        for a in results[3 * kind : 3 * kind + 3]:
            if kind == 0:
                a = jnp.swapaxes(a.reshape(1, 2, 9, 32, 64), 3, 4)
            elif kind == 2:
                a = a[None]
            elif kind < 4:
                a = jnp.swapaxes(a[None], 1, 2)
            out.append(a)
    return out


def per_device_here(images, timesteps, counts, cotangent, *state):
    n_img = images.shape[0]
    state = turned_state(state)
    me = jnp.stack([lax.axis_index("dp"), lax.axis_index("fsdp")]).astype(jnp.int32)
    sa, sb = pack(state[0::3])
    x = images.reshape(n_img, 256, 256)
    cot = cotangent.reshape(n_img, 256, 256)
    cf = figures(counts, x)
    emb = jax.nn.silu(sinus_embed(timesteps)).astype(BF)

    line_a = jnp.stack([sa] + [swap(sa, 8 * rz) for rz in range(1, 4)])
    rows_b = [sb] + [swap(sb, 8 * rz) for rz in range(1, 4)]
    plane_a = [line_a] + [swap(line_a, bits) for bits in (2, 4, 6)]
    rows_b, plane_a, cf = lax.optimization_barrier((rows_b, plane_a, cf))
    all_a = [p for line in plane_a for p in (line, swap(line, 1))]
    line_b = jnp.stack(rows_b)
    plane_b = [line_b] + [swap(line_b, bits) for bits in (2, 4, 6)]
    wat, vec = unpack(
        unpack_a_body, "unpack_first", me, all_a, [sd((2304, 256), BF), sd((16, 256), F32)], [pltpu.VMEM((32, 128), F32)]
    )
    wat, line_b = lax.optimization_barrier((wat, line_b))
    h0, pa1 = conv_one(counts, x, cf, vec, wat)
    h0, plane_b = lax.optimization_barrier((h0, plane_b))
    all_b = [p for line in plane_b for p in (line, swap(line, 1))]
    wet, wbt, wqt, wot = unpack(
        unpack_b_body,
        "unpack_second",
        me,
        all_b,
        [sd((256, 512), BF), sd((2304, 256), BF), sd((768, 256), BF), sd((256, 256), BF)],
        [],
    )
    out, ga, dm, keep, send = middle(
        counts, x, h0, cot, emb, vec, me, wet, wbt, wqt, wot, finish_b, [sd((4, 4, GB, 128), BF)] * 2
    )
    parts_b = over_core(keep, send)
    ga, parts_b = lax.optimization_barrier((ga, parts_b))
    plane_b = to_plane(parts_b)
    keep, send = conv_one_grad(counts, ga, pa1, me, finish_a, [sd((4, 4, GA, 128), BF)] * 2)
    keep, send, plane_b = lax.optimization_barrier((keep, send, plane_b))
    parts_a = over_core(keep, send)
    own_b, others = plane_sum(parts_b[0], plane_b)
    dm, parts_a, others = lax.optimization_barrier((dm, parts_a, others))
    plane_a = to_plane(parts_a)
    got_b = over_line(others)
    ig, keep, send = input_grad(counts, x, ga, dm, cf, vec, me, wat, finish_v, [sd((4, 4, 128), F32)] * 2)
    keep, send, plane_a, got_b = lax.optimization_barrier((keep, send, plane_a, got_b))
    own_a, others = plane_sum(parts_a[0], plane_a)
    got_a = over_line(others)
    parts_v = over_core_small(keep, send)
    own_v, others = plane_sum(parts_v[0], to_plane(parts_v))
    got_v = over_line(others)
    wide = lambda v: v[None]
    gb, ga, squares = shares(
        (own_b, got_b), (own_a, got_a), (wide(own_v), [wide(g) for g in got_v])
    )
    results = adam(total_over(squares), gb, ga, state)
    return (out.reshape(images.shape), ig.reshape(images.shape), *turned_back(results[:15]), results[15].reshape(()))


def gather_flat(masters, dp, fs):
    sizes = [m.size for m in masters]
    total = sum(sizes)
    full = -(-total // 2048) * 2048
    flat = jnp.concatenate([m.reshape(-1).astype(BF) for m in masters] + [jnp.zeros((full - total,), BF)])
    flat = flat.reshape(-1, 128)
    g = lax.all_gather(lax.all_gather(flat, "dp"), "fsdp").reshape(fs, dp, full)
    out = []
    at = 0
    for n in sizes:
        out.append(g[:, :, at : at + n])
        at += n
    conv = out[0].reshape((fs, dp) + masters[0].shape[1:]).transpose(2, 3, 0, 5, 1, 4)
    conv = conv.reshape(2, 2304, 256)
    mats = []
    for p, m in zip(out[1:4], masters[1:4]):
        r, c = m.shape[1:]
        mats.append(p.reshape(fs, dp, r, c).transpose(0, 3, 1, 2).reshape(fs * c, dp * r))
    vec = out[4].transpose(1, 0, 2).reshape(12, 256).astype(F32)
    return conv, mats, vec


def reduce_flat(grads, dp, fs):
    conv, mats, vec = grads
    pieces = [conv.reshape(18, fs, 256 // fs, dp, 256 // dp).transpose(1, 3, 0, 4, 2).reshape(fs, dp, -1)]
    for g in mats:
        c, r = g.shape
        pieces.append(g.reshape(fs, c // fs, dp, r // dp).transpose(0, 2, 3, 1).reshape(fs, dp, -1))
    pieces.append(vec.reshape(dp, fs, -1).transpose(1, 0, 2))
    sizes = [p.shape[2] for p in pieces]
    total = sum(sizes)
    full = -(-total // 2048) * 2048
    pieces.append(jnp.zeros((fs, dp, full - total), F32))
    flat = jnp.concatenate(pieces, axis=2).reshape(fs, dp, -1, 128)
    part = lax.psum_scatter(flat, "fsdp", scatter_dimension=0, tiled=False)
    part = lax.psum_scatter(part, "dp", scatter_dimension=0, tiled=False).reshape(-1)
    out = []
    at = 0
    for n in sizes:
        out.append(part[at : at + n])
        at += n
    return out


def finish_whole(outs, me, dwb, dwq, dwo, de, rows, turn):
    for out, got in zip(outs, (dwb[...], dwq[...], dwo[...], de, rows)):
        out[...] = got


def finish_one(outs, me, got):
    outs[0][...] = got[...]


def per_device_any(images, timesteps, counts, cotangent, *state):
    masters = state[0::3]
    moments = state[1::3]
    squares = state[2::3]
    dp = lax.axis_size("dp")
    fs = lax.axis_size("fsdp")
    n_img = images.shape[0]
    me = jnp.zeros((2,), jnp.int32)
    emb = jax.nn.silu(sinus_embed(timesteps)).astype(BF)
    x = images.reshape(n_img, 256, 256)
    cot = cotangent.reshape(n_img, 256, 256)
    conv, (wet, wqt, wot), vec = gather_flat(masters, dp, fs)
    vec = jnp.pad(vec, ((0, 4), (0, 0)))
    cf = figures(counts, x)
    h0, pa1 = conv_one(counts, x, cf, vec, conv[0])
    ends = [sd(s, F32) for s in ((768, 768), (256, 768), (256, 256), (256, 512), (16, 256))]
    out, ga, dm, dwb, dwq, dwo, de, rows = middle(
        counts, x, h0, cot, emb, vec, me, wet, conv[1], wqt, wot, finish_whole, ends
    )
    (dwa,) = conv_one_grad(counts, ga, pa1, me, finish_one, [sd((768, 768), F32)])
    ig, first = input_grad(counts, x, ga, dm, cf, vec, me, conv[0], finish_one, [sd((16, 256), F32)])
    apart = lambda w: w.reshape(3, 256, 3, 256).transpose(0, 2, 1, 3).reshape(9, 256, 256)
    shares_here = reduce_flat(
        (jnp.stack([apart(dwa), apart(dwb)]), (de, dwq.T, dwo), (rows + first)[:12]), dp, fs
    )
    local = sum(jnp.sum(s * s) for s in shares_here)
    norm = jnp.sqrt(lax.psum(lax.psum(local, "fsdp"), "dp"))
    factor = clip_norm / jnp.maximum(norm, clip_norm)
    results = []
    for kind in range(5):
        clipped = shares_here[kind].reshape(masters[kind].shape) * factor
        first_new = beta_first * moments[kind] + (1.0 - beta_first) * clipped
        second_new = beta_second * squares[kind] + (1.0 - beta_second) * clipped * clipped
        first_hat = first_new / (1.0 - beta_first**STEP)
        second_hat = second_new / (1.0 - beta_second**STEP)
        update_new = masters[kind] - rates_kind[kind] * (
            first_hat / (jnp.sqrt(second_hat) + adam_eps) + decays_kind[kind] * masters[kind]
        )
        results += [first_new, second_new, update_new]
    return (out.reshape(images.shape), ig.reshape(images.shape), *results, norm)


def solution(mesh):
    both = P(("dp", "fsdp"), None, None, None)
    one = P(("dp", "fsdp"))
    conv = P(None, None, None, "dp", "fsdp")
    mat = P(None, "dp", "fsdp")
    vec = P(None, ("dp", "fsdp"))
    trios = (conv,) * 3 + (mat,) * 9 + (vec,) * 3
    here = mesh.shape["dp"] == 4 and mesh.shape["fsdp"] == 8
    return jax.shard_map(
        per_device_here if here else per_device_any,
        mesh=mesh,
        in_specs=(both, one, one, both) + trios,
        out_specs=(both, both) + trios + (P(),),
        check_vma=False,
    )
```

profile of v0, /device:TPU:0, one launch (start us, length us, event | category | flops | bytes accessed | tf_op | source)
XLA Modules:
  0.0 181.0 jit_solution(11540199488934181000)
XLA Ops:
  0.7 1.8 %pack_shards.1 = (bf16[160,128]{1,0:T(8,128)(2,1)}, bf16[240,128]{1,0:T(8,128)(2,1)}) custom-call(f32[18,32,64]{2,1,0:T(8,128)} %bitcast.150, f32[32,128]{1,0:T(8,128)} %bitcast.156, f32[64,96]{1,0:T(8,128)} %bitcast.154, f32[32,64]{1,0:T(8,128)} %bitcast.158, f32[1,96]{1,0:T(1,128)} %refs_18_.1), custom_call_target="tpu_custom_call" | custom-call | tf_op jit(solution)/shard_map/pack_shards/pallas_call | solution.py:629
  2.5 5.0 %collective-permute-start.5 = (bf16[160,128]{1,0:T(8,128)(2,1)}, bf16[160,128]{1,0:T(8,128)(2,1)S(1)}, u32[]{:S(2)}, u32[]{:S(2)}) collective-permute-start(bf16[160,128]{1,0:T(8,128)(2,1)} %get-tuple-element.107), channel_id=1, source_target_pairs={{0,24},{1,25},{2,26},{3,27},{4,28},{5,29},{6,30},{7,31},{8,16},{9,... | collective-permute-start | bytes 122888 | tf_op jit(solution)/shard_map/ppermute | solution.py:635
  8.1 3.8 %collective-permute-start.2 = (bf16[240,128]{1,0:T(8,128)(2,1)}, bf16[240,128]{1,0:T(8,128)(2,1)S(1)}, u32[]{:S(2)}, u32[]{:S(2)}) collective-permute-start(bf16[240,128]{1,0:T(8,128)(2,1)} %get-tuple-element.115), channel_id=1, source_target_pairs={{0,24},{1,25},{2,26},{3,27},{4,28},{5,29},{6,30},{7,31},{8,16},{9,... | collective-permute-start | bytes 184328 | tf_op jit(solution)/shard_map/ppermute | solution.py:635
  11.9 1.5 collective-permute-done.4
  13.4 0.8 pad_maximum_fusion.1.refs_0_
  14.2 2.5 %collective-permute-start.8 = (bf16[4,160,128]{2,1,0:T(8,128)(2,1)S(1)}, bf16[4,160,128]{2,1,0:T(8,128)(2,1)S(1)}, u32[]{:S(2)}, u32[]{:S(2)}) collective-permute-start(bf16[4,160,128]{2,1,0:T(8,128)(2,1)S(1)} %pad_maximum_fusion.1.refs_0_), channel_id=1, source_target_pairs={{0,6},{1,7},{2,4},{3,5},{4,2},{5,3},{6,0},{7,1},{8,14},{9,15},{10,... | collective-permute-start | bytes 491528 | tf_op jit(solution)/shard_map/ppermute | solution.py:635
  17.8 1.2 collective-permute-start.1
  19.8 3.3 %figures.1.cf_ref.refs_4_ = f32[16,8,256]{2,1,0:T(8,128)} custom-call(s32[1]{0:T(128)S(6)} %copy.37.cnt_ref.refs_0_, bf16[16,256,256]{2,1,0:T(8,128)(2,1)} %bitcast.178), custom_call_target="tpu_custom_call" | custom-call | flops 536870912 | bytes 8388608 | tf_op jit(solution)/shard_map/figures/pallas_call | solution.py:185
  25.6 2.5 %collective-permute-start.15 = (bf16[4,240,128]{2,1,0:T(8,128)(2,1)S(1)}, bf16[4,240,128]{2,1,0:T(8,128)(2,1)S(1)}, u32[]{:S(2)}, u32[]{:S(2)}) collective-permute-start(bf16[4,240,128]{2,1,0:T(8,128)(2,1)S(1)} %pad_maximum_fusion.refs_0_), channel_id=1, source_target_pairs={{0,6},{1,7},{2,4},{3,5},{4,2},{5,3},{6,0},{7,1},{8,14},{9,15},{10,... | collective-permute-start | bytes 737288 | tf_op jit(solution)/shard_map/ppermute | solution.py:635
  30.5 2.9 %unpack_first.1 = (bf16[2304,256]{1,0:T(8,128)(2,1)}, f32[16,256]{1,0:T(8,128)}) custom-call(s32[2]{0:T(128)} %pad_add_fusion.me.refs_6_.refs_3_, bf16[4,160,128]{2,1,0:T(8,128)(2,1)} %copy-done.2, bf16[4,160,128]{2,1,0:T(8,128)(2,1)} %copy-done.15, bf16[4,160,128]{2,1,0:T(8,128)(2,1)} %copy-done.14, bf16[4,160,128]{2,1,0:T(8,128)(2,1)} %copy-done.16, ...), custom_call_target="tpu_custom_call" | custom-call | tf_op jit(solution)/shard_map/unpack_first/pallas_call | solution.py:705
  33.4 8.0 %conv_one.1 = (f32[16,256,256]{2,1,0:T(8,128)}, bf16[16,288,768]{2,1,0:T(8,128)(2,1)}) custom-call(s32[1]{0:T(128)S(6)} %copy.37.cnt_ref.refs_0_, bf16[16,256,256]{2,1,0:T(8,128)(2,1)} %bitcast.179, f32[16,8,256]{2,1,0:T(8,128)} %figures.1.cf_ref.refs_4_, f32[16,256]{1,0:T(8,128)} %get-tuple-element.113.vec_ref.refs_5_, ...), custom_call_target="tpu_custom_call" | custom-call | flops 9663676416 | bytes 41943040 | tf_op jit(solution)/shard_map/conv_one/pallas_call | solution.py:185
  44.5 0.7 copy-done.11
  45.2 3.4 %unpack_second.1 = (bf16[256,512]{1,0:T(8,128)(2,1)}, bf16[2304,256]{1,0:T(8,128)(2,1)}, bf16[768,256]{1,0:T(8,128)(2,1)}, bf16[256,256]{1,0:T(8,128)(2,1)}) custom-call(s32[2]{0:T(128)} %pad_add_fusion.me.refs_6_.refs_3_, bf16[4,240,128]{2,1,0:T(8,128)(2,1)} %copy-done.1, bf16[4,240,128]{2,1,0:T(8,128)(2,1)} %copy-done.8, bf16[4,240,128]{2,1,0:T(8,128)(2,1)} %copy-done.7, ...), custom_call_target="tpu_custom_call" | custom-call | tf_op jit(solution)/shard_map/unpack_second/pallas_call | solution.py:705
  48.5 24.9 %middle.1 = (f32[16,256,256]{2,1,0:T(8,128)}, bf16[16,256,256]{2,1,0:T(8,128)(2,1)}, f32[16,256,256]{2,1,0:T(8,128)}, bf16[4,4,256,128]{3,2,1,0:T(8,128)(2,1)}, bf16[4,4,256,128]{3,2,1,0:T(8,128)(2,1)}) custom-call(s32[1]{0:T(128)S(6)} %copy.37.cnt_ref.refs_0_, bf16[16,256,256]{2,1,0:T(8,128)(2,1)} %bitcast.180, f32[16,256,256]{2,1,0:T(8,128)} %get-tuple-element.121.refs_2_, ...), custom_call_target="tpu_custom_call" | custom-call | flops 48318382080 | bytes 167772160 | tf_op jit(solution)/shard_map/middle/pallas_call | solution.py:185
  73.5 2.9 %collective-permute-done.20.got = bf16[4,4,256,128]{3,2,1,0:T(8,128)(2,1)S(1)} collective-permute-done((bf16[4,4,256,128]{3,2,1,0:T(8,128)(2,1)}, bf16[4,4,256,128]{3,2,1,0:T(8,128)(2,1)S(1)}, u32[]{:S(2)}, u32[]{:S(2)}) %collective-permute-start.20) | collective-permute-done | bytes 1048608 | tf_op jit(solution)/shard_map/ppermute | solution.py:635
  76.4 1.0 copy-done
  77.3 3.5 %core_sum.2 = (bf16[4,256,128]{2,1,0:T(8,128)(2,1)}, bf16[4,256,128]{2,1,0:T(8,128)(2,1)}, bf16[4,256,128]{2,1,0:T(8,128)(2,1)}, bf16[4,256,128]{2,1,0:T(8,128)(2,1)}) custom-call(bf16[4,4,256,128]{3,2,1,0:T(8,128)(2,1)} %get-tuple-element.132.keep, bf16[4,4,256,128]{3,2,1,0:T(8,128)(2,1)} %copy-done), custom_call_target="tpu_custom_call" | custom-call | tf_op jit(solution)/shard_map/core_sum/pallas_call | solution.py:789
  80.8 17.4 %collective-permute-start.21 = (bf16[4,256,128]{2,1,0:T(8,128)(2,1)}, bf16[4,256,128]{2,1,0:T(8,128)(2,1)S(1)}, u32[]{:S(2)}, u32[]{:S(2)}) collective-permute-start(bf16[4,256,128]{2,1,0:T(8,128)(2,1)} %get-tuple-element.143), channel_id=1, source_target_pairs={{0,2},{1,3},{2,0},{3,1},{4,6},{5,7},{6,4},{7,5},{8,10},{9,11},{10,... | collective-permute-start | bytes 786440 | tf_op jit(solution)/shard_map/ppermute | solution.py:635
  98.2 1.5 collective-permute-start.23
  99.8 6.3 %conv_one_grad.1 = (bf16[4,4,144,128]{3,2,1,0:T(8,128)(2,1)}, bf16[4,4,144,128]{3,2,1,0:T(8,128)(2,1)}) custom-call(s32[1]{0:T(128)S(6)} %copy.37.cnt_ref.refs_0_, bf16[16,256,256]{2,1,0:T(8,128)(2,1)} %get-tuple-element.138.refs_1_.refs_2_, bf16[16,288,768]{2,1,0:T(8,128)(2,1)} %get-tuple-element.140.refs_2_, s32[2]{0:T(128)} %pad_add_fusion.me.refs_6_.refs_3_), custom_call_target="tpu_custom_call" | custom-call | flops 9663676416 | bytes 41943040 | tf_op jit(solution)/shard_map/conv_one_grad/pallas_call | solution.py:185
  106.1 6.2 %collective-permute-done.22 = bf16[4,256,128]{2,1,0:T(8,128)(2,1)S(1)} collective-permute-done((bf16[4,256,128]{2,1,0:T(8,128)(2,1)}, bf16[4,256,128]{2,1,0:T(8,128)(2,1)S(1)}, u32[]{:S(2)}, u32[]{:S(2)}) %collective-permute-start.22) | collective-permute-done | bytes 262176 | tf_op jit(solution)/shard_map/ppermute | solution.py:635
  112.4 0.8 add_bitcast_fusion
  113.2 1.4 collective-permute-done.24.got
  114.6 0.8 copy-done.3
  115.4 3.3 %core_sum.3 = (bf16[4,144,128]{2,1,0:T(8,128)(2,1)}, bf16[4,144,128]{2,1,0:T(8,128)(2,1)}, bf16[4,144,128]{2,1,0:T(8,128)(2,1)}, bf16[4,144,128]{2,1,0:T(8,128)(2,1)}) custom-call(bf16[4,4,144,128]{3,2,1,0:T(8,128)(2,1)} %get-tuple-element.146.keep, bf16[4,4,144,128]{3,2,1,0:T(8,128)(2,1)} %copy-done.3), custom_call_target="tpu_custom_call" | custom-call | tf_op jit(solution)/shard_map/core_sum/pallas_call | solution.py:789
  119.0 4.2 %collective-permute-start.29 = (bf16[256,128]{1,0:T(8,128)(2,1)S(1)}, bf16[256,128]{1,0:T(8,128)(2,1)S(1)}, u32[]{:S(2)}, u32[]{:S(2)}) collective-permute-start(bf16[256,128]{1,0:T(8,128)(2,1)S(1)} %get-tuple-element.164), channel_id=1, source_target_pairs={{0,16},{1,17},{2,18},{3,19},{4,20},{5,21},{6,22},{7,23},{8,24},{9,... | collective-permute-start | bytes 196616 | tf_op jit(solution)/shard_map/ppermute | solution.py:635
  123.2 1.5 collective-permute-start.25
  125.3 1.4 collective-permute-start.27
  126.7 8.9 %input_grad.1 = (f32[16,256,256]{2,1,0:T(8,128)}, f32[4,4,128]{2,1,0:T(4,128)}, f32[4,4,128]{2,1,0:T(4,128)}) custom-call(s32[1]{0:T(128)S(6)} %copy.37.cnt_ref.refs_0_, bf16[16,256,256]{2,1,0:T(8,128)(2,1)} %bitcast.181, bf16[16,256,256]{2,1,0:T(8,128)(2,1)} %get-tuple-element.138.refs_1_.refs_2_, f32[16,256,256]{2,1,0:T(8,128)} %get-tuple-element.156.refs_3_, ...), custom_call_target="tpu_custom_call" | custom-call | flops 12884901888 | bytes 58720256 | tf_op jit(solution)/shard_map/input_grad/pallas_call | solution.py:185
  135.8 1.4 collective-permute-done.34
  137.2 0.7 add.201
  137.9 3.3 %collective-permute-start.35 = (f32[4,128]{1,0:T(4,128)S(1)}, f32[4,128]{1,0:T(4,128)S(1)}, u32[]{:S(2)}, u32[]{:S(2)}) collective-permute-start(f32[4,128]{1,0:T(4,128)S(1)} %get-tuple-element.205), channel_id=1, source_target_pairs={{0,2},{1,3},{2,0},{3,1},{4,6},{5,7},{6,4},{7,5},{8,10},{9,11},{10,... | collective-permute-start | bytes 6152 | tf_op jit(solution)/shard_map/ppermute | solution.py:635
  141.2 1.3 collective-permute-start.37
  142.8 2.9 %collective-permute-done.37 = f32[4,128]{1,0:T(4,128)S(1)} collective-permute-done((f32[4,128]{1,0:T(4,128)S(1)}, f32[4,128]{1,0:T(4,128)S(1)}, u32[]{:S(2)}, u32[]{:S(2)}) %collective-permute-start.37) | collective-permute-done | bytes 2080 | tf_op jit(solution)/shard_map/ppermute | solution.py:635
  146.1 4.4 %collective-permute-start.40 = (f32[128]{0:T(128)S(1)}, f32[128]{0:T(128)S(1)}, u32[]{:S(2)}, u32[]{:S(2)}) collective-permute-start(f32[128]{0:T(128)S(1)} %get-tuple-element.202), channel_id=1, source_target_pairs={{0,24},{1,25},{2,26},{3,27},{4,28},{5,29},{6,30},{7,31},{8,16},{9,... | collective-permute-start | bytes 1544 | tf_op jit(solution)/shard_map/ppermute | solution.py:635
  150.4 0.7 fusion.5
  151.2 4.4 %collective-permute-start.31 = (bf16[144,128]{1,0:T(8,128)(2,1)S(1)}, bf16[144,128]{1,0:T(8,128)(2,1)S(1)}, u32[]{:S(2)}, u32[]{:S(2)}) collective-permute-start(bf16[144,128]{1,0:T(8,128)(2,1)S(1)} %get-tuple-element.200), channel_id=1, source_target_pairs={{0,8},{1,9},{2,10},{3,11},{4,12},{5,13},{6,14},{7,15},{8,0},{9,1},... | collective-permute-start | bytes 110600 | tf_op jit(solution)/shard_map/ppermute | solution.py:635
  156.7 3.3 %collective-permute-done.39 = f32[128]{0:T(128)S(1)} collective-permute-done((f32[128]{0:T(128)S(1)}, f32[128]{0:T(128)S(1)}, u32[]{:S(2)}, u32[]{:S(2)}) %collective-permute-start.39) | collective-permute-done | bytes 544 | tf_op jit(solution)/shard_map/ppermute | solution.py:635
  160.7 1.9 %shares.1 = (f32[256,128]{1,0:T(8,128)}, f32[144,128]{1,0:T(8,128)}, f32[8,128]{1,0:T(8,128)}) custom-call(f32[256,128]{1,0:T(8,128)} %get-tuple-element.194.refs_0_, bf16[256,128]{1,0:T(8,128)(2,1)} %copy-done.20, bf16[256,128]{1,0:T(8,128)(2,1)} %copy-done.21, bf16[256,128]{1,0:T(8,128)(2,1)} %copy-done.22, f32[144,128]{1,0:T(8,128)} %get-tuple-element.201.refs_4_, ...), custom_call_target="tpu_custom_call" | custom-call | tf_op jit(solution)/shard_map/shares/pallas_call | solution.py:834
  162.5 1.4 collective-permute-done.41
  164.6 1.4 collective-permute-start.44
  166.0 2.0 %collective-permute-start.43 = (f32[8,128]{1,0:T(8,128)S(1)}, f32[8,128]{1,0:T(8,128)S(1)}, u32[]{:S(2)}, u32[]{:S(2)}) collective-permute-start(f32[8,128]{1,0:T(8,128)S(1)} %add.214), channel_id=1, source_target_pairs={{0,4},{1,5},{2,6},{3,7},{4,0},{5,1},{6,2},{7,3},{8,12},{9,13},{10,... | collective-permute-start | bytes 12296 | tf_op jit(solution)/shard_map/ppermute | solution.py:635
  168.1 1.0 collective-permute-done.44
  169.6 2.0 %collective-permute-done.42 = f32[8,128]{1,0:T(8,128)S(1)} collective-permute-done((f32[8,128]{1,0:T(8,128)S(1)}, f32[8,128]{1,0:T(8,128)S(1)}, u32[]{:S(2)}, u32[]{:S(2)}) %collective-permute-start.42) | collective-permute-done | bytes 4128 | tf_op jit(solution)/shard_map/ppermute | solution.py:635
  171.6 1.5 collective-permute-start.47
  173.7 2.3 %collective-permute-start.45 = (f32[8,128]{1,0:T(8,128)S(1)}, f32[8,128]{1,0:T(8,128)S(1)}, u32[]{:S(2)}, u32[]{:S(2)}) collective-permute-start(f32[8,128]{1,0:T(8,128)S(1)} %add_add_fusion.refs_0_), channel_id=1, source_target_pairs={{0,8},{1,9},{2,10},{3,11},{4,12},{5,13},{6,14},{7,15},{8,0},{9,1},... | collective-permute-start | bytes 12296 | tf_op jit(solution)/shard_map/ppermute | solution.py:635
  176.0 1.0 collective-permute-done.47.refs_3_
  178.2 2.6 %clipped_adamw.1 = (f32[18,32,64]{2,1,0:T(8,128)}, f32[18,32,64]{2,1,0:T(8,128)}, f32[18,32,64]{2,1,0:T(8,128)}, f32[32,128]{1,0:T(8,128)}, f32[32,128]{1,0:T(8,...) custom-call(f32[8,128]{1,0:T(8,128)} %copy-done.27, ...), custom_call_target="tpu_custom_call" | custom-call | tf_op jit(solution)/shard_map/clipped_adamw/pallas_call | solution.py:885
  (145 shorter events, 16.1 us)
Async XLA Ops:
  2.5 9.4 %collective-permute-start.5 = (bf16[160,128]{1,0:T(8,128)(2,1)}, bf16[160,128]{1,0:T(8,128)(2,1)S(1)}, u32[]{:S(2)}, u32[]{:S(2)}) collective-permute-start(bf16[160,128]{1,0:T(8,128)(2,1)} %get-tuple-element.107), channel_id=1, source_target_pairs={{0,24},{1,25},{2,26},{3,27},{4,28},{5,29},{6,30},{7,31},{8,16},{9,... | collective-permute-start | bytes 122888 | tf_op jit(solution)/shard_map/ppermute | solution.py:635
  7.5 5.9 %collective-permute-start.4 = (bf16[160,128]{1,0:T(8,128)(2,1)}, bf16[160,128]{1,0:T(8,128)(2,1)S(1)}, u32[]{:S(2)}, u32[]{:S(2)}) collective-permute-start(bf16[160,128]{1,0:T(8,128)(2,1)} %get-tuple-element.107), channel_id=1, source_target_pairs={{0,16},{1,17},{2,18},{3,19},{4,20},{5,21},{6,22},{7,23},{8,24},{9,... | collective-permute-start | bytes 122888 | tf_op jit(solution)/shard_map/ppermute | solution.py:635
  7.5 5.9 %collective-permute-start.3 = (bf16[160,128]{1,0:T(8,128)(2,1)}, bf16[160,128]{1,0:T(8,128)(2,1)S(1)}, u32[]{:S(2)}, u32[]{:S(2)}) collective-permute-start(bf16[160,128]{1,0:T(8,128)(2,1)} %get-tuple-element.107), channel_id=1, source_target_pairs={{0,8},{1,9},{2,10},{3,11},{4,12},{5,13},{6,14},{7,15},{8,0},{9,1},... | collective-permute-start | bytes 122888 | tf_op jit(solution)/shard_map/ppermute | solution.py:635
  8.1 10.9 %collective-permute-start.2 = (bf16[240,128]{1,0:T(8,128)(2,1)}, bf16[240,128]{1,0:T(8,128)(2,1)S(1)}, u32[]{:S(2)}, u32[]{:S(2)}) collective-permute-start(bf16[240,128]{1,0:T(8,128)(2,1)} %get-tuple-element.115), channel_id=1, source_target_pairs={{0,24},{1,25},{2,26},{3,27},{4,28},{5,29},{6,30},{7,31},{8,16},{9,... | collective-permute-start | bytes 184328 | tf_op jit(solution)/shard_map/ppermute | solution.py:635
  14.2 9.5 %collective-permute-start.8 = (bf16[4,160,128]{2,1,0:T(8,128)(2,1)S(1)}, bf16[4,160,128]{2,1,0:T(8,128)(2,1)S(1)}, u32[]{:S(2)}, u32[]{:S(2)}) collective-permute-start(bf16[4,160,128]{2,1,0:T(8,128)(2,1)S(1)} %pad_maximum_fusion.1.refs_0_), channel_id=1, source_target_pairs={{0,6},{1,7},{2,4},{3,5},{4,2},{5,3},{6,0},{7,1},{8,14},{9,15},{10,... | collective-permute-start | bytes 491528 | tf_op jit(solution)/shard_map/ppermute | solution.py:635
  16.8 7.0 %collective-permute-start.7 = (bf16[4,160,128]{2,1,0:T(8,128)(2,1)S(1)}, bf16[4,160,128]{2,1,0:T(8,128)(2,1)S(1)}, u32[]{:S(2)}, u32[]{:S(2)}) collective-permute-start(bf16[4,160,128]{2,1,0:T(8,128)(2,1)S(1)} %pad_maximum_fusion.1.refs_0_), channel_id=1, source_target_pairs={{0,4},{1,5},{2,6},{3,7},{4,0},{5,1},{6,2},{7,3},{8,12},{9,13},{10,... | collective-permute-start | bytes 491528 | tf_op jit(solution)/shard_map/ppermute | solution.py:635
  17.3 6.5 %collective-permute-start.6 = (bf16[4,160,128]{2,1,0:T(8,128)(2,1)S(1)}, bf16[4,160,128]{2,1,0:T(8,128)(2,1)S(1)}, u32[]{:S(2)}, u32[]{:S(2)}) collective-permute-start(bf16[4,160,128]{2,1,0:T(8,128)(2,1)S(1)} %pad_maximum_fusion.1.refs_0_), channel_id=1, source_target_pairs={{0,2},{1,3},{2,0},{3,1},{4,6},{5,7},{6,4},{7,5},{8,10},{9,11},{10,... | collective-permute-start | bytes 491528 | tf_op jit(solution)/shard_map/ppermute | solution.py:635
  17.8 5.4 %collective-permute-start.1 = (bf16[240,128]{1,0:T(8,128)(2,1)}, bf16[240,128]{1,0:T(8,128)(2,1)S(1)}, u32[]{:S(2)}, u32[]{:S(2)}) collective-permute-start(bf16[240,128]{1,0:T(8,128)(2,1)} %get-tuple-element.115), channel_id=1, source_target_pairs={{0,16},{1,17},{2,18},{3,19},{4,20},{5,21},{6,22},{7,23},{8,24},{9,... | collective-permute-start | bytes 184328 | tf_op jit(solution)/shard_map/ppermute | solution.py:635
  19.0 4.7 %collective-permute-start = (bf16[240,128]{1,0:T(8,128)(2,1)}, bf16[240,128]{1,0:T(8,128)(2,1)S(1)}, u32[]{:S(2)}, u32[]{:S(2)}) collective-permute-start(bf16[240,128]{1,0:T(8,128)(2,1)} %get-tuple-element.115), channel_id=1, source_target_pairs={{0,8},{1,9},{2,10},{3,11},{4,12},{5,13},{6,14},{7,15},{8,0},{9,1},... | collective-permute-start | bytes 184328 | tf_op jit(solution)/shard_map/ppermute | solution.py:635
  23.8 4.2 %collective-permute-start.9 = (bf16[4,160,128]{2,1,0:T(8,128)(2,1)S(1)}, bf16[4,160,128]{2,1,0:T(8,128)(2,1)S(1)}, u32[]{:S(2)}, u32[]{:S(2)}) collective-permute-start(bf16[4,160,128]{2,1,0:T(8,128)(2,1)S(1)} %pad_maximum_fusion.1.refs_0_), channel_id=1, source_target_pairs={{0,1},{1,0},{2,3},{3,2},{4,5},{5,4},{6,7},{7,6},{8,9},{9,8},{10,11... | collective-permute-start | bytes 491528 | tf_op jit(solution)/shard_map/ppermute | solution.py:635
  23.9 4.7 %collective-permute-start.10 = (bf16[4,160,128]{2,1,0:T(8,128)(2,1)S(1)}, bf16[4,160,128]{2,1,0:T(8,128)(2,1)S(1)}, u32[]{:S(2)}, u32[]{:S(2)}) collective-permute-start(bf16[4,160,128]{2,1,0:T(8,128)(2,1)S(1)} %collective-permute-done.6.refs_2_), channel_id=1, source_target_pairs={{0,1},{1,0},{2,3},{3,2},{4,5},{5,4},{6,7},{7,6},{8,9},{9,8},{10,11... | collective-permute-start | bytes 491528 | tf_op jit(solution)/shard_map/ppermute | solution.py:635
  24.4 4.7 %collective-permute-start.11 = (bf16[4,160,128]{2,1,0:T(8,128)(2,1)S(1)}, bf16[4,160,128]{2,1,0:T(8,128)(2,1)S(1)}, u32[]{:S(2)}, u32[]{:S(2)}) collective-permute-start(bf16[4,160,128]{2,1,0:T(8,128)(2,1)S(1)} %collective-permute-done.7.refs_4_), channel_id=1, source_target_pairs={{0,1},{1,0},{2,3},{3,2},{4,5},{5,4},{6,7},{7,6},{8,9},{9,8},{10,11... | collective-permute-start | bytes 491528 | tf_op jit(solution)/shard_map/ppermute | solution.py:635
  24.5 4.6 %collective-permute-start.12 = (bf16[4,160,128]{2,1,0:T(8,128)(2,1)S(1)}, bf16[4,160,128]{2,1,0:T(8,128)(2,1)S(1)}, u32[]{:S(2)}, u32[]{:S(2)}) collective-permute-start(bf16[4,160,128]{2,1,0:T(8,128)(2,1)S(1)} %collective-permute-done.8.refs_6_), channel_id=1, source_target_pairs={{0,1},{1,0},{2,3},{3,2},{4,5},{5,4},{6,7},{7,6},{8,9},{9,8},{10,11... | collective-permute-start | bytes 491528 | tf_op jit(solution)/shard_map/ppermute | solution.py:635
  25.6 15.8 %collective-permute-start.15 = (bf16[4,240,128]{2,1,0:T(8,128)(2,1)S(1)}, bf16[4,240,128]{2,1,0:T(8,128)(2,1)S(1)}, u32[]{:S(2)}, u32[]{:S(2)}) collective-permute-start(bf16[4,240,128]{2,1,0:T(8,128)(2,1)S(1)} %pad_maximum_fusion.refs_0_), channel_id=1, source_target_pairs={{0,6},{1,7},{2,4},{3,5},{4,2},{5,3},{6,0},{7,1},{8,14},{9,15},{10,... | collective-permute-start | bytes 737288 | tf_op jit(solution)/shard_map/ppermute | solution.py:635
  28.1 13.3 %collective-permute-start.14 = (bf16[4,240,128]{2,1,0:T(8,128)(2,1)S(1)}, bf16[4,240,128]{2,1,0:T(8,128)(2,1)S(1)}, u32[]{:S(2)}, u32[]{:S(2)}) collective-permute-start(bf16[4,240,128]{2,1,0:T(8,128)(2,1)S(1)} %pad_maximum_fusion.refs_0_), channel_id=1, source_target_pairs={{0,4},{1,5},{2,6},{3,7},{4,0},{5,1},{6,2},{7,3},{8,12},{9,13},{10,... | collective-permute-start | bytes 737288 | tf_op jit(solution)/shard_map/ppermute | solution.py:635
  28.6 12.8 %collective-permute-start.13 = (bf16[4,240,128]{2,1,0:T(8,128)(2,1)S(1)}, bf16[4,240,128]{2,1,0:T(8,128)(2,1)S(1)}, u32[]{:S(2)}, u32[]{:S(2)}) collective-permute-start(bf16[4,240,128]{2,1,0:T(8,128)(2,1)S(1)} %pad_maximum_fusion.refs_0_), channel_id=1, source_target_pairs={{0,2},{1,3},{2,0},{3,1},{4,6},{5,7},{6,4},{7,5},{8,10},{9,11},{10,... | collective-permute-start | bytes 737288 | tf_op jit(solution)/shard_map/ppermute | solution.py:635
  41.5 1.9 %collective-permute-start.16 = (bf16[4,240,128]{2,1,0:T(8,128)(2,1)S(1)}, bf16[4,240,128]{2,1,0:T(8,128)(2,1)S(1)}, u32[]{:S(2)}, u32[]{:S(2)}) collective-permute-start(bf16[4,240,128]{2,1,0:T(8,128)(2,1)S(1)} %pad_maximum_fusion.refs_0_), channel_id=1, source_target_pairs={{0,1},{1,0},{2,3},{3,2},{4,5},{5,4},{6,7},{7,6},{8,9},{9,8},{10,11... | collective-permute-start | bytes 737288 | tf_op jit(solution)/shard_map/ppermute | solution.py:635
  41.5 1.9 %collective-permute-start.17 = (bf16[4,240,128]{2,1,0:T(8,128)(2,1)S(1)}, bf16[4,240,128]{2,1,0:T(8,128)(2,1)S(1)}, u32[]{:S(2)}, u32[]{:S(2)}) collective-permute-start(bf16[4,240,128]{2,1,0:T(8,128)(2,1)S(1)} %collective-permute-done.13.refs_2_), channel_id=1, source_target_pairs={{0,1},{1,0},{2,3},{3,2},{4,5},{5,4},{6,7},{7,6},{8,9},{9,8},{10,11... | collective-permute-start | bytes 737288 | tf_op jit(solution)/shard_map/ppermute | solution.py:635
  42.0 1.7 collective-permute-start.18
  42.1 2.0 %collective-permute-start.19 = (bf16[4,240,128]{2,1,0:T(8,128)(2,1)S(1)}, bf16[4,240,128]{2,1,0:T(8,128)(2,1)S(1)}, u32[]{:S(2)}, u32[]{:S(2)}) collective-permute-start(bf16[4,240,128]{2,1,0:T(8,128)(2,1)S(1)} %collective-permute-done.15.refs_6_), channel_id=1, source_target_pairs={{0,1},{1,0},{2,3},{3,2},{4,5},{5,4},{6,7},{7,6},{8,9},{9,8},{10,11... | collective-permute-start | bytes 737288 | tf_op jit(solution)/shard_map/ppermute | solution.py:635
  73.4 2.9 %collective-permute-start.20 = (bf16[4,4,256,128]{3,2,1,0:T(8,128)(2,1)}, bf16[4,4,256,128]{3,2,1,0:T(8,128)(2,1)S(1)}, u32[]{:S(2)}, u32[]{:S(2)}) collective-permute-start(bf16[4,4,256,128]{3,2,1,0:T(8,128)(2,1)} %get-tuple-element.133), channel_id=1, source_target_pairs={{0,1},{1,0},{2,3},{3,2},{4,5},{5,4},{6,7},{7,6},{8,9},{9,8},{10,11... | collective-permute-start | bytes 3145736 | tf_op jit(solution)/shard_map/ppermute | solution.py:635
  80.8 25.3 %collective-permute-start.21 = (bf16[4,256,128]{2,1,0:T(8,128)(2,1)}, bf16[4,256,128]{2,1,0:T(8,128)(2,1)S(1)}, u32[]{:S(2)}, u32[]{:S(2)}) collective-permute-start(bf16[4,256,128]{2,1,0:T(8,128)(2,1)} %get-tuple-element.143), channel_id=1, source_target_pairs={{0,2},{1,3},{2,0},{3,1},{4,6},{5,7},{6,4},{7,5},{8,10},{9,11},{10,... | collective-permute-start | bytes 786440 | tf_op jit(solution)/shard_map/ppermute | solution.py:635
  98.2 14.1 %collective-permute-start.22 = (bf16[4,256,128]{2,1,0:T(8,128)(2,1)}, bf16[4,256,128]{2,1,0:T(8,128)(2,1)S(1)}, u32[]{:S(2)}, u32[]{:S(2)}) collective-permute-start(bf16[4,256,128]{2,1,0:T(8,128)(2,1)} %get-tuple-element.144), channel_id=1, source_target_pairs={{0,4},{1,5},{2,6},{3,7},{4,0},{5,1},{6,2},{7,3},{8,12},{9,13},{10,... | collective-permute-start | bytes 786440 | tf_op jit(solution)/shard_map/ppermute | solution.py:635
  98.2 14.1 %collective-permute-start.23 = (bf16[4,256,128]{2,1,0:T(8,128)(2,1)}, bf16[4,256,128]{2,1,0:T(8,128)(2,1)S(1)}, u32[]{:S(2)}, u32[]{:S(2)}) collective-permute-start(bf16[4,256,128]{2,1,0:T(8,128)(2,1)} %get-tuple-element.145), channel_id=1, source_target_pairs={{0,6},{1,7},{2,4},{3,5},{4,2},{5,3},{6,0},{7,1},{8,14},{9,15},{10,... | collective-permute-start | bytes 786440 | tf_op jit(solution)/shard_map/ppermute | solution.py:635
  112.4 2.2 %collective-permute-start.24 = (bf16[4,4,144,128]{3,2,1,0:T(8,128)(2,1)}, bf16[4,4,144,128]{3,2,1,0:T(8,128)(2,1)S(1)}, u32[]{:S(2)}, u32[]{:S(2)}) collective-permute-start(bf16[4,4,144,128]{3,2,1,0:T(8,128)(2,1)} %get-tuple-element.147), channel_id=1, source_target_pairs={{0,1},{1,0},{2,3},{3,2},{4,5},{5,4},{6,7},{7,6},{8,9},{9,8},{10,11... | collective-permute-start | bytes 1769480 | tf_op jit(solution)/shard_map/ppermute | solution.py:635
  118.7 6.6 %collective-permute-start.28 = (bf16[256,128]{1,0:T(8,128)(2,1)S(1)}, bf16[256,128]{1,0:T(8,128)(2,1)S(1)}, u32[]{:S(2)}, u32[]{:S(2)}) collective-permute-start(bf16[256,128]{1,0:T(8,128)(2,1)S(1)} %get-tuple-element.163), channel_id=1, source_target_pairs={{0,8},{1,9},{2,10},{3,11},{4,12},{5,13},{6,14},{7,15},{8,0},{9,1},... | collective-permute-start | bytes 196616 | tf_op jit(solution)/shard_map/ppermute | solution.py:635
  119.0 16.7 %collective-permute-start.29 = (bf16[256,128]{1,0:T(8,128)(2,1)S(1)}, bf16[256,128]{1,0:T(8,128)(2,1)S(1)}, u32[]{:S(2)}, u32[]{:S(2)}) collective-permute-start(bf16[256,128]{1,0:T(8,128)(2,1)S(1)} %get-tuple-element.164), channel_id=1, source_target_pairs={{0,16},{1,17},{2,18},{3,19},{4,20},{5,21},{6,22},{7,23},{8,24},{9,... | collective-permute-start | bytes 196616 | tf_op jit(solution)/shard_map/ppermute | solution.py:635
  123.2 12.4 %collective-permute-start.30 = (bf16[256,128]{1,0:T(8,128)(2,1)S(1)}, bf16[256,128]{1,0:T(8,128)(2,1)S(1)}, u32[]{:S(2)}, u32[]{:S(2)}) collective-permute-start(bf16[256,128]{1,0:T(8,128)(2,1)S(1)} %get-tuple-element.165), channel_id=1, source_target_pairs={{0,24},{1,25},{2,26},{3,27},{4,28},{5,29},{6,30},{7,31},{8,16},{9,... | collective-permute-start | bytes 196616 | tf_op jit(solution)/shard_map/ppermute | solution.py:635
  123.2 12.5 %collective-permute-start.25 = (bf16[4,144,128]{2,1,0:T(8,128)(2,1)}, bf16[4,144,128]{2,1,0:T(8,128)(2,1)S(1)}, u32[]{:S(2)}, u32[]{:S(2)}) collective-permute-start(bf16[4,144,128]{2,1,0:T(8,128)(2,1)} %get-tuple-element.160), channel_id=1, source_target_pairs={{0,2},{1,3},{2,0},{3,1},{4,6},{5,7},{6,4},{7,5},{8,10},{9,11},{10,... | collective-permute-start | bytes 442376 | tf_op jit(solution)/shard_map/ppermute | solution.py:635
  124.7 11.0 %collective-permute-start.26 = (bf16[4,144,128]{2,1,0:T(8,128)(2,1)}, bf16[4,144,128]{2,1,0:T(8,128)(2,1)S(1)}, u32[]{:S(2)}, u32[]{:S(2)}) collective-permute-start(bf16[4,144,128]{2,1,0:T(8,128)(2,1)} %get-tuple-element.161), channel_id=1, source_target_pairs={{0,4},{1,5},{2,6},{3,7},{4,0},{5,1},{6,2},{7,3},{8,12},{9,13},{10,... | collective-permute-start | bytes 442376 | tf_op jit(solution)/shard_map/ppermute | solution.py:635
  125.3 10.4 %collective-permute-start.27 = (bf16[4,144,128]{2,1,0:T(8,128)(2,1)}, bf16[4,144,128]{2,1,0:T(8,128)(2,1)S(1)}, u32[]{:S(2)}, u32[]{:S(2)}) collective-permute-start(bf16[4,144,128]{2,1,0:T(8,128)(2,1)} %get-tuple-element.162), channel_id=1, source_target_pairs={{0,6},{1,7},{2,4},{3,5},{4,2},{5,3},{6,0},{7,1},{8,14},{9,15},{10,... | collective-permute-start | bytes 442376 | tf_op jit(solution)/shard_map/ppermute | solution.py:635
  135.7 1.4 collective-permute-start.34
  137.9 4.9 %collective-permute-start.35 = (f32[4,128]{1,0:T(4,128)S(1)}, f32[4,128]{1,0:T(4,128)S(1)}, u32[]{:S(2)}, u32[]{:S(2)}) collective-permute-start(f32[4,128]{1,0:T(4,128)S(1)} %get-tuple-element.205), channel_id=1, source_target_pairs={{0,2},{1,3},{2,0},{3,1},{4,6},{5,7},{6,4},{7,5},{8,10},{9,11},{10,... | collective-permute-start | bytes 6152 | tf_op jit(solution)/shard_map/ppermute | solution.py:635
  141.2 4.5 %collective-permute-start.37 = (f32[4,128]{1,0:T(4,128)S(1)}, f32[4,128]{1,0:T(4,128)S(1)}, u32[]{:S(2)}, u32[]{:S(2)}) collective-permute-start(f32[4,128]{1,0:T(4,128)S(1)} %get-tuple-element.206), channel_id=1, source_target_pairs={{0,6},{1,7},{2,4},{3,5},{4,2},{5,3},{6,0},{7,1},{8,14},{9,15},{10,... | collective-permute-start | bytes 6152 | tf_op jit(solution)/shard_map/ppermute | solution.py:635
  142.5 3.6 %collective-permute-start.36 = (f32[4,128]{1,0:T(4,128)S(1)}, f32[4,128]{1,0:T(4,128)S(1)}, u32[]{:S(2)}, u32[]{:S(2)}) collective-permute-start(f32[4,128]{1,0:T(4,128)S(1)} %get-tuple-element.207), channel_id=1, source_target_pairs={{0,4},{1,5},{2,6},{3,7},{4,0},{5,1},{6,2},{7,3},{8,12},{9,13},{10,... | collective-permute-start | bytes 6152 | tf_op jit(solution)/shard_map/ppermute | solution.py:635
  146.1 9.5 %collective-permute-start.40 = (f32[128]{0:T(128)S(1)}, f32[128]{0:T(128)S(1)}, u32[]{:S(2)}, u32[]{:S(2)}) collective-permute-start(f32[128]{0:T(128)S(1)} %get-tuple-element.202), channel_id=1, source_target_pairs={{0,24},{1,25},{2,26},{3,27},{4,28},{5,29},{6,30},{7,31},{8,16},{9,... | collective-permute-start | bytes 1544 | tf_op jit(solution)/shard_map/ppermute | solution.py:635
  151.2 8.8 %collective-permute-start.33 = (bf16[144,128]{1,0:T(8,128)(2,1)S(1)}, bf16[144,128]{1,0:T(8,128)(2,1)S(1)}, u32[]{:S(2)}, u32[]{:S(2)}) collective-permute-start(bf16[144,128]{1,0:T(8,128)(2,1)S(1)} %get-tuple-element.198), channel_id=1, source_target_pairs={{0,24},{1,25},{2,26},{3,27},{4,28},{5,29},{6,30},{7,31},{8,16},{9,... | collective-permute-start | bytes 110600 | tf_op jit(solution)/shard_map/ppermute | solution.py:635
  151.2 8.8 %collective-permute-start.32 = (bf16[144,128]{1,0:T(8,128)(2,1)S(1)}, bf16[144,128]{1,0:T(8,128)(2,1)S(1)}, u32[]{:S(2)}, u32[]{:S(2)}) collective-permute-start(bf16[144,128]{1,0:T(8,128)(2,1)S(1)} %get-tuple-element.199), channel_id=1, source_target_pairs={{0,16},{1,17},{2,18},{3,19},{4,20},{5,21},{6,22},{7,23},{8,24},{9,... | collective-permute-start | bytes 110600 | tf_op jit(solution)/shard_map/ppermute | solution.py:635
  151.2 8.9 %collective-permute-start.31 = (bf16[144,128]{1,0:T(8,128)(2,1)S(1)}, bf16[144,128]{1,0:T(8,128)(2,1)S(1)}, u32[]{:S(2)}, u32[]{:S(2)}) collective-permute-start(bf16[144,128]{1,0:T(8,128)(2,1)S(1)} %get-tuple-element.200), channel_id=1, source_target_pairs={{0,8},{1,9},{2,10},{3,11},{4,12},{5,13},{6,14},{7,15},{8,0},{9,1},... | collective-permute-start | bytes 110600 | tf_op jit(solution)/shard_map/ppermute | solution.py:635
  155.5 4.4 %collective-permute-start.39 = (f32[128]{0:T(128)S(1)}, f32[128]{0:T(128)S(1)}, u32[]{:S(2)}, u32[]{:S(2)}) collective-permute-start(f32[128]{0:T(128)S(1)} %get-tuple-element.203), channel_id=1, source_target_pairs={{0,16},{1,17},{2,18},{3,19},{4,20},{5,21},{6,22},{7,23},{8,24},{9,... | collective-permute-start | bytes 1544 | tf_op jit(solution)/shard_map/ppermute | solution.py:635
  155.6 4.4 %collective-permute-start.38 = (f32[128]{0:T(128)S(1)}, f32[128]{0:T(128)S(1)}, u32[]{:S(2)}, u32[]{:S(2)}) collective-permute-start(f32[128]{0:T(128)S(1)} %get-tuple-element.204), channel_id=1, source_target_pairs={{0,8},{1,9},{2,10},{3,11},{4,12},{5,13},{6,14},{7,15},{8,0},{9,1},... | collective-permute-start | bytes 1544 | tf_op jit(solution)/shard_map/ppermute | solution.py:635
  162.5 1.4 collective-permute-start.41
  164.6 4.5 %collective-permute-start.44 = (f32[8,128]{1,0:T(8,128)S(1)}, f32[8,128]{1,0:T(8,128)S(1)}, u32[]{:S(2)}, u32[]{:S(2)}) collective-permute-start(f32[8,128]{1,0:T(8,128)S(1)} %add.214), channel_id=1, source_target_pairs={{0,6},{1,7},{2,4},{3,5},{4,2},{5,3},{6,0},{7,1},{8,14},{9,15},{10,... | collective-permute-start | bytes 12296 | tf_op jit(solution)/shard_map/ppermute | solution.py:635
  166.0 3.6 %collective-permute-start.43 = (f32[8,128]{1,0:T(8,128)S(1)}, f32[8,128]{1,0:T(8,128)S(1)}, u32[]{:S(2)}, u32[]{:S(2)}) collective-permute-start(f32[8,128]{1,0:T(8,128)S(1)} %add.214), channel_id=1, source_target_pairs={{0,4},{1,5},{2,6},{3,7},{4,0},{5,1},{6,2},{7,3},{8,12},{9,13},{10,... | collective-permute-start | bytes 12296 | tf_op jit(solution)/shard_map/ppermute | solution.py:635
  168.0 3.6 %collective-permute-start.42 = (f32[8,128]{1,0:T(8,128)S(1)}, f32[8,128]{1,0:T(8,128)S(1)}, u32[]{:S(2)}, u32[]{:S(2)}) collective-permute-start(f32[8,128]{1,0:T(8,128)S(1)} %add.214), channel_id=1, source_target_pairs={{0,2},{1,3},{2,0},{3,1},{4,6},{5,7},{6,4},{7,5},{8,10},{9,11},{10,... | collective-permute-start | bytes 12296 | tf_op jit(solution)/shard_map/ppermute | solution.py:635
  171.6 5.4 %collective-permute-start.47 = (f32[8,128]{1,0:T(8,128)S(1)}, f32[8,128]{1,0:T(8,128)S(1)}, u32[]{:S(2)}, u32[]{:S(2)}) collective-permute-start(f32[8,128]{1,0:T(8,128)S(1)} %add_add_fusion.refs_0_), channel_id=1, source_target_pairs={{0,24},{1,25},{2,26},{3,27},{4,28},{5,29},{6,30},{7,31},{8,16},{9,... | collective-permute-start | bytes 12296 | tf_op jit(solution)/shard_map/ppermute | solution.py:635
  173.1 4.5 %collective-permute-start.46 = (f32[8,128]{1,0:T(8,128)S(1)}, f32[8,128]{1,0:T(8,128)S(1)}, u32[]{:S(2)}, u32[]{:S(2)}) collective-permute-start(f32[8,128]{1,0:T(8,128)S(1)} %add_add_fusion.refs_0_), channel_id=1, source_target_pairs={{0,16},{1,17},{2,18},{3,19},{4,20},{5,21},{6,22},{7,23},{8,24},{9,... | collective-permute-start | bytes 12296 | tf_op jit(solution)/shard_map/ppermute | solution.py:635
  173.7 3.9 %collective-permute-start.45 = (f32[8,128]{1,0:T(8,128)S(1)}, f32[8,128]{1,0:T(8,128)S(1)}, u32[]{:S(2)}, u32[]{:S(2)}) collective-permute-start(f32[8,128]{1,0:T(8,128)S(1)} %add_add_fusion.refs_0_), channel_id=1, source_target_pairs={{0,8},{1,9},{2,10},{3,11},{4,12},{5,13},{6,14},{7,15},{8,0},{9,1},... | collective-permute-start | bytes 12296 | tf_op jit(solution)/shard_map/ppermute | solution.py:635
  (35 other events, 229.2 us)
where the time goes:
time: 182 us; the launch traced here: 181 us
  Pallas kernels  70.9 us (39%)
  starting transfers between devices  69.1 us (38%)
  waiting for transfers between devices  28.1 us (15%)
  other arithmetic  5.62 us (3%)
  local copies, waits for them, and re-layouts  5.38 us (3%)
  between operations  1.9 us (1%)
    ppermute x48, starting transfers between devices, swap(): return lax.ppermute(x, AXES, [(i, i ^ bits) for i in range(32)])  69.1 us
    pallas_call x5, Pallas kernels, image_call(): pl.pallas_call(body, grid_spec=pltpu.PrefetchScalarGridSpec(num_scalar_pr...  51.4 us
    ppermute x48, waiting for transfers between devices, swap(): return lax.ppermute(x, AXES, [(i, i ^ bits) for i in range(32)])  28.1 us
    pallas_call x2, Pallas kernels, over_core(): pl.pallas_call(core_sum_body, grid=(4,), in_specs=[pl.BlockSpec((4, 1) +...  6.83 us
    pallas_call x2, Pallas kernels, unpack(): pl.pallas_call(body, in_specs=[pl.BlockSpec(memory_space=pltpu.SMEM)] + [...  6.29 us
    unnamed x70, local copies, waits for them, and re-layouts  5.37 us
  transfers between devices with their start and end apart: 48, of which 19 were waited for; matrix products, arithmetic and copies ran while one was open for 2% of the time, Pallas kernels for 16%

commit v1 on v0

--- a/solution.py
+++ b/solution.py
@@ -482,9 +482,14 @@
 
     @pl.when(i * NB < cnt_ref[0])
     def _():
-        for n in range(NB):
-            gt[:, n * 256 : n * 256 + 256] = ga_ref[n].T
-        add_taps(dwa, gt[...], pa_ref, range(NB))
+        def part(N):
+            for n in N:
+                gt[:, n * 256 : n * 256 + 256] = ga_ref[n].T
+            yield
+            add_taps(dwa, gt[:, N.start * 256 : N.stop * 256], pa_ref, N)
+            yield
+
+        interleave([part(N) for N in parts()])
 
     @pl.when(i == pl.num_programs(0) - 1)
     def _():
@@ -506,11 +511,9 @@
     )
 
 
-def input_grad_body(finish, n_out, *refs):
+def input_grad_body(base, *refs):
     cnt_ref, x_ref, ga_ref, dm_ref, cf_ref, vec_ref, me_ref, wat_ref = refs[:8]
-    ig_ref = refs[8]
-    ends = refs[9 : 9 + n_out]
-    pg, dz, dvec = refs[9 + n_out :]
+    ig_ref, dvec, pg, dz = refs[-4:]
     i = pl.program_id(0)
 
     @pl.when(i == 0)
@@ -518,7 +521,7 @@
         zero_pads(pg)
         dvec[...] = jnp.zeros_like(dvec)
 
-    live = i * NB < cnt_ref[0]
+    live = (i + base) * NB < cnt_ref[0]
 
     @pl.when(jnp.logical_not(live))
     def _():
@@ -573,27 +576,44 @@
             yield
 
         interleave([part(N) for N in parts()])
-        dvec[...] += jnp.concatenate([tot["g1"], tot["b1"], jnp.zeros((14, 256), F32)], axis=0)
-
-    @pl.when(i == pl.num_programs(0) - 1)
-    def _():
-        finish(ends, me_ref, dvec[...])
-
-
-def input_grad(cnt, x, ga, dm, cf, vec, me, wat, finish, ends):
+        g = tot["g1"]
+        b = tot["b1"]
+        z = jnp.zeros((4, 128), F32)
+        dvec[...] += jnp.concatenate([g[:, :128], g[:, 128:], b[:, :128], b[:, 128:], z], axis=0)
+
+
+def input_grad(cnt, x, ga, dm, cf, vec, me, wat, base, steps, got):
     n = x.shape[0]
-    return image_call(
-        lambda *refs: input_grad_body(finish, len(ends), *refs),
-        "input_grad",
-        n,
-        (24, 14),
-        [blocks(256, 256)] * 3
-        + [blocks(8, 256), whole((16, 256)), pl.BlockSpec(memory_space=pltpu.SMEM), whole(wat.shape)],
-        [out_blocks(256, 256)] + [whole(e.shape) for e in ends],
-        [sd((n, 256, 256), F32)] + list(ends),
-        [pltpu.VMEM((NB, 288, 768), BF), pltpu.VMEM((NB * 256, 256), F32), pltpu.VMEM((16, 256), F32)],
-        (cnt, x, ga, dm, cf, vec, me, wat),
-    )
+    at = lambda i, c: jnp.minimum(i + base, jnp.maximum((c[0] - 1) // NB, base))
+    block = lambda *tail: pl.BlockSpec((NB,) + tail, lambda i, c: (at(i, c),) + (0,) * len(tail))
+    args = (cnt, x, ga, dm, cf, vec, me, wat)
+    in_specs = [block(256, 256)] * 3 + [block(8, 256), whole((16, 256))]
+    in_specs += [pl.BlockSpec(memory_space=pltpu.SMEM), whole(wat.shape)]
+    alias = {}
+    if got is not None:
+        alias = {len(args): 0}
+        args += (got,)
+        in_specs += [pl.BlockSpec(memory_space=pl.ANY)]
+    return pl.pallas_call(
+        lambda *refs: input_grad_body(base, *refs),
+        grid_spec=pltpu.PrefetchScalarGridSpec(
+            num_scalar_prefetch=1,
+            grid=(steps,),
+            in_specs=in_specs,
+            out_specs=[
+                pl.BlockSpec((NB, 256, 256), lambda i, c: (i + base, 0, 0)),
+                pl.BlockSpec((8, 128), lambda i, c: (0, 0)),
+            ],
+            scratch_shapes=[pltpu.VMEM((NB, 288, 768), BF), pltpu.VMEM((NB * 256, 256), F32)],
+        ),
+        out_shape=[sd((n, 256, 256), F32), sd((8, 128), F32)],
+        input_output_aliases=alias,
+        cost_estimate=pl.CostEstimate(
+            flops=steps * NB * 24 * 2 * 256**3, transcendentals=0, bytes_accessed=steps * NB * 14 * 4 * 256**2
+        ),
+        compiler_params=VMEM,
+        name="input_grad",
+    )(*args)
 
 
 def sinus_embed(steps_in):
@@ -772,34 +792,9 @@
         place(outs, me, dwa, 256 * (k // 3), 256 * (k % 3), 16 * k, 16, 32)
 
 
-def finish_v(outs, me, rows):
-    acc = spread_rows(rows, me)
-    for rf in range(8):
-        outs[rf & 1][rf >> 1] = acc[4 * rf : 4 * rf + 4]
-
-
-def core_sum_body(keep, got, *outs):
-    for j in range(4):
-        outs[j][...] = (keep[j].astype(F32) + got[j].astype(F32)).astype(outs[j].dtype)
-
-
 def over_core(keep, send):
     got = swap(send, 1)
-    tail = keep.shape[2:]
-    return pl.pallas_call(
-        core_sum_body,
-        grid=(4,),
-        in_specs=[pl.BlockSpec((4, 1) + tail, lambda i: (0, i, 0, 0))] * 2,
-        out_specs=[pl.BlockSpec((1,) + tail, lambda i: (i, 0, 0))] * 4,
-        out_shape=[pltpu.HBM((4,) + tail, keep.dtype)] * 4,
-        compiler_params=VMEM,
-        name="core_sum",
-    )(keep, got)
-
-
-def over_core_small(keep, send):
-    s = keep + swap(send, 1)
-    return [s[j] for j in range(4)]
+    return [(keep[j].astype(F32) + got[j].astype(F32)).astype(keep.dtype) for j in range(4)]
 
 
 def to_plane(parts):
@@ -816,27 +811,27 @@
 
 
 def shares_body(*refs):
-    sb, sa, sv = (refs[4 * k][...] + sum(r[...].astype(F32) for r in refs[4 * k + 1 : 4 * k + 4]) for k in range(3))
-    gb, ga, out = refs[12:]
-    gb[0:240, :] = sb[0:240]
-    vec = sb[240:241] + sv[0:1]
-    gb[240:256, :] = jnp.broadcast_to(vec, (16, 128))
+    sb, sa = (refs[4 * k][...] + sum(r[...].astype(F32) for r in refs[4 * k + 1 : 4 * k + 4]) for k in range(2))
+    v0, v1, gb, ga, out = refs[8:]
+    gb[...] = sb
     ga[...] = sa
     fold = lambda v: jnp.sum((v * v).reshape(-1, 8, 128), axis=0)
-    t = fsum(fold(sb[0:240]) + fold(sa)) + vec * vec
-    out[...] = jnp.broadcast_to(jnp.sum(t, axis=1, keepdims=True), (8, 128))
-
-
-def shares(b, a, v):
+    t = fsum(fold(sb[0:240]) + fold(sa)) + sb[240:241] * sb[240:241]
+    t = jnp.broadcast_to(jnp.sum(t, axis=1, keepdims=True), (8, 128))
+    line = lax.broadcasted_iota(jnp.int32, (8, 128), 0)
+    out[...] = jnp.where(line < 4, v0[...] + v1[...], t)
+
+
+def shares(b, a, vs):
     args = []
-    for own, got in (b, a, v):
+    for own, got in (b, a):
         args += [own, *got]
     return pl.pallas_call(
         shares_body,
         out_shape=[sd((GB, 128), F32), sd((GA, 128), F32), sd((8, 128), F32)],
         compiler_params=VMEM,
         name="shares",
-    )(*args)
+    )(*args, *vs)
 
 
 def total_over(s):
@@ -846,10 +841,21 @@
 
 
 def adam_body(*refs):
-    t0, t1, t2, t3, gb, ga = refs[:6]
-    state = refs[6:21]
-    outs = refs[21:]
-    norm = jnp.sqrt((t0[...] + t1[...]) + (t2[...] + t3[...]))[0:1]
+    me, t0, t1, t2, t3, gb, ga = refs[:7]
+    state = refs[7:22]
+    outs = refs[22:-1]
+    first = refs[-1]
+    total = (t0[...] + t1[...]) + (t2[...] + t3[...])
+    first[...] = total
+    top = total[0:4]
+    norm = jnp.sqrt(jnp.broadcast_to(jnp.sum(fsum(top * top), axis=1, keepdims=True), (1, 128)) + total[4:5])
+    lane = lax.broadcasted_iota(jnp.int32, (1, 128), 1)
+    vec = gb[240:241, :]
+    for u in range(3):
+        unit = 3 * (8 * me[0] + me[1]) + u
+        line = first[pl.ds(jnp.minimum(unit >> 2, 4), 1), :]
+        line = pltpu.roll(line, (32 * u + 128 - 32 * (unit & 3)) & 127, 1)
+        vec = vec + jnp.where(jnp.logical_and((lane >> 5) == u, unit < 16), line, 0.0)
     factor = clip_norm / jnp.maximum(norm, clip_norm)
 
     def put(kind, at, grad):
@@ -877,18 +883,21 @@
     put(2, (Ellipsis,), g[:64, :96])
     g = gb[192:208, :]
     put(3, (Ellipsis,), jnp.concatenate([g[:, :64], g[:, 64:]], axis=0))
-    put(4, (Ellipsis,), gb[240:241, :96])
+    put(4, (Ellipsis,), vec[:, :96])
     outs[15][0] = norm[0, 0]
 
 
-def adam(totals, gb, ga, state):
+def adam(me, totals, gb, ga, state):
+    args = (*totals, gb, ga, *state)
     return pl.pallas_call(
         adam_body,
+        in_specs=[pl.BlockSpec(memory_space=pltpu.SMEM)] + [pl.BlockSpec(a.shape) for a in args],
         out_specs=[pl.BlockSpec(s.shape) for s in state] + [pl.BlockSpec(memory_space=pltpu.SMEM)],
         out_shape=[sd(s.shape, F32) for s in state] + [sd((1,), F32)],
+        scratch_shapes=[pltpu.VMEM((8, 128), F32)],
         compiler_params=VMEM,
         name="clipped_adamw",
-    )(*totals, gb, ga, *state)
+    )(me, *args)
 
 
 def turned_state(state):
@@ -964,18 +973,17 @@
     dm, parts_a, others = lax.optimization_barrier((dm, parts_a, others))
     plane_a = to_plane(parts_a)
     got_b = over_line(others)
-    ig, keep, send = input_grad(counts, x, ga, dm, cf, vec, me, wat, finish_v, [sd((4, 4, 128), F32)] * 2)
-    keep, send, plane_a, got_b = lax.optimization_barrier((keep, send, plane_a, got_b))
+    half = n_img // NB // 2
+    rest = n_img // NB - half
+    ig, v0 = input_grad(counts, x, ga, dm, cf, vec, me, wat, 0, half, None)
+    ig, plane_a, got_b = lax.optimization_barrier((ig, plane_a, got_b))
     own_a, others = plane_sum(parts_a[0], plane_a)
+    ig, others = lax.optimization_barrier((ig, others))
     got_a = over_line(others)
-    parts_v = over_core_small(keep, send)
-    own_v, others = plane_sum(parts_v[0], to_plane(parts_v))
-    got_v = over_line(others)
-    wide = lambda v: v[None]
-    gb, ga, squares = shares(
-        (own_b, got_b), (own_a, got_a), (wide(own_v), [wide(g) for g in got_v])
-    )
-    results = adam(total_over(squares), gb, ga, state)
+    ig, v1 = input_grad(counts, x, ga, dm, cf, vec, me, wat, half, rest, ig)
+    v1, got_a = lax.optimization_barrier((v1, got_a))
+    gb, ga, sums = shares((own_b, got_b), (own_a, got_a), (v0, v1))
+    results = adam(me, total_over(sums), gb, ga, state)
     return (out.reshape(images.shape), ig.reshape(images.shape), *turned_back(results[:15]), results[15].reshape(()))
 
 
@@ -1052,7 +1060,8 @@
         counts, x, h0, cot, emb, vec, me, wet, conv[1], wqt, wot, finish_whole, ends
     )
     (dwa,) = conv_one_grad(counts, ga, pa1, me, finish_one, [sd((768, 768), F32)])
-    ig, first = input_grad(counts, x, ga, dm, cf, vec, me, conv[0], finish_one, [sd((16, 256), F32)])
+    ig, first = input_grad(counts, x, ga, dm, cf, vec, me, conv[0], 0, n_img // NB, None)
+    first = jnp.pad(first[:4].reshape(2, 256), ((0, 14), (0, 0)))
     apart = lambda w: w.reshape(3, 256, 3, 256).transpose(0, 2, 1, 3).reshape(9, 256, 256)
     shares_here = reduce_flat(
         (jnp.stack([apart(dwa), apart(dwb)]), (de, dwq.T, dwo), (rows + first)[:12]), dp, fs

time: 182 us -> 163 us (0.90)
  starting transfers between devices: 69.1 us -> 43.9 us
  Pallas kernels: 70.9 us -> 91.1 us
  waiting for transfers between devices: 28.1 us -> 15.5 us
    ppermute x48 -> x41, starting transfers between devices: 69.1 us -> 43.9 us  [swap(): return lax.ppermute(x, AXES, [(i, i ^ bits) for i in range(32)])]
    ppermute x48 -> x41, waiting for transfers between devices: 28.1 us -> 15.5 us  [swap(): return lax.ppermute(x, AXES, [(i, i ^ bits) for i in range(32)])]
    pallas_call x5 -> x4, Pallas kernels: 51.4 us -> 63.2 us  [image_call(): pl.pallas_call(body, grid_spec=pltpu.PrefetchScalarGridSpec(num_scalar_pr...]
    pallas_call x3, Pallas kernels: 9.43 us -> 17.9 us  [the longest x2 15.1 us: input_grad(): pl.pallas_call(lambda *refs: input_grad_body(base, *refs), grid_spec=pltp...]
    convert_element_type x0 -> x2, other arithmetic: none -> 2.76 us  [over_core(): (keep[j].astype(F32) + got[j].astype(F32)).astype(keep.dtype)]
    unnamed x70 -> x56, local copies, waits for them, and re-layouts: 5.37 us -> 3.56 us
  transfers between devices with their start and end apart: 48 -> 41, of which waited for: 19 -> 12; matrix products, arithmetic and copies ran while one was open for 2% -> 2% of each run, Pallas kernels for 16% -> 25%
where the time goes in v1:
time: 163 us
  Pallas kernels  91.1 us (56%)
  starting transfers between devices  43.9 us (27%)
  waiting for transfers between devices  15.5 us (10%)
  other arithmetic  7.18 us (4%)
  local copies, waits for them, and re-layouts  3.56 us (2%)
  between operations  1.93 us (1%)
    pallas_call x4, Pallas kernels, image_call(): pl.pallas_call(body, grid_spec=pltpu.PrefetchScalarGridSpec(num_scalar_pr...  63.2 us
    ppermute x41, starting transfers between devices, swap(): return lax.ppermute(x, AXES, [(i, i ^ bits) for i in range(32)])  43.9 us
    ppermute x41, waiting for transfers between devices, swap(): return lax.ppermute(x, AXES, [(i, i ^ bits) for i in range(32)])  15.5 us
    pallas_call x2, Pallas kernels, input_grad(): pl.pallas_call(lambda *refs: input_grad_body(base, *refs), grid_spec=pltp...  15.1 us
    pallas_call x2, Pallas kernels, unpack(): pl.pallas_call(body, in_specs=[pl.BlockSpec(memory_space=pltpu.SMEM)] + [...  6.24 us
    unnamed x56, local copies, waits for them, and re-layouts  3.56 us
  transfers between devices with their start and end apart: 41, of which 12 were waited for; matrix products, arithmetic and copies ran while one was open for 2% of the time, Pallas kernels for 25%

profile of v1, /device:TPU:0, one launch (start us, length us, event | category | flops | bytes accessed | tf_op | source)
XLA Modules:
  0.0 163.1 jit_solution(1906656312199375346)
XLA Ops:
  0.7 1.8 %pack_shards.1 = (bf16[160,128]{1,0:T(8,128)(2,1)}, bf16[240,128]{1,0:T(8,128)(2,1)}) custom-call(f32[18,32,64]{2,1,0:T(8,128)} %bitcast.107, f32[32,128]{1,0:T(8,128)} %bitcast.113, f32[64,96]{1,0:T(8,128)} %bitcast.111, f32[32,64]{1,0:T(8,128)} %bitcast.115, f32[1,96]{1,0:T(1,128)} %refs_19_.1), custom_call_target="tpu_custom_call" | custom-call | tf_op jit(solution)/shard_map/pack_shards/pallas_call | solution.py:649
  2.5 5.0 %collective-permute-start.5 = (bf16[160,128]{1,0:T(8,128)(2,1)}, bf16[160,128]{1,0:T(8,128)(2,1)S(1)}, u32[]{:S(2)}, u32[]{:S(2)}) collective-permute-start(bf16[160,128]{1,0:T(8,128)(2,1)} %get-tuple-element.107), channel_id=1, source_target_pairs={{0,24},{1,25},{2,26},{3,27},{4,28},{5,29},{6,30},{7,31},{8,16},{9,... | collective-permute-start | bytes 122888 | tf_op jit(solution)/shard_map/ppermute | solution.py:655
  7.5 0.6 collective-permute-start.3
  8.1 3.8 %collective-permute-start.2 = (bf16[240,128]{1,0:T(8,128)(2,1)}, bf16[240,128]{1,0:T(8,128)(2,1)S(1)}, u32[]{:S(2)}, u32[]{:S(2)}) collective-permute-start(bf16[240,128]{1,0:T(8,128)(2,1)} %get-tuple-element.115), channel_id=1, source_target_pairs={{0,24},{1,25},{2,26},{3,27},{4,28},{5,29},{6,30},{7,31},{8,16},{9,... | collective-permute-start | bytes 184328 | tf_op jit(solution)/shard_map/ppermute | solution.py:655
  11.9 1.5 collective-permute-done.4
  13.4 0.8 pad_maximum_fusion.1.refs_0_
  14.2 2.5 %collective-permute-start.8 = (bf16[4,160,128]{2,1,0:T(8,128)(2,1)S(1)}, bf16[4,160,128]{2,1,0:T(8,128)(2,1)S(1)}, u32[]{:S(2)}, u32[]{:S(2)}) collective-permute-start(bf16[4,160,128]{2,1,0:T(8,128)(2,1)S(1)} %pad_maximum_fusion.1.refs_0_), channel_id=1, source_target_pairs={{0,6},{1,7},{2,4},{3,5},{4,2},{5,3},{6,0},{7,1},{8,14},{9,15},{10,... | collective-permute-start | bytes 491528 | tf_op jit(solution)/shard_map/ppermute | solution.py:655
  17.8 1.2 collective-permute-start.1
  19.8 4.4 %figures.1.cf_ref.refs_4_ = f32[16,8,256]{2,1,0:T(8,128)} custom-call(s32[1]{0:T(128)S(6)} %copy.39.cnt_ref.refs_0_, bf16[16,256,256]{2,1,0:T(8,128)(2,1)} %bitcast.132), custom_call_target="tpu_custom_call" | custom-call | flops 536870912 | bytes 8388608 | tf_op jit(solution)/shard_map/figures/pallas_call | solution.py:185
  25.3 0.6 pad_add_fusion.me.refs_6_.refs_3_.refs_0_
  26.0 2.5 %collective-permute-start.15 = (bf16[4,240,128]{2,1,0:T(8,128)(2,1)S(1)}, bf16[4,240,128]{2,1,0:T(8,128)(2,1)S(1)}, u32[]{:S(2)}, u32[]{:S(2)}) collective-permute-start(bf16[4,240,128]{2,1,0:T(8,128)(2,1)S(1)} %pad_maximum_fusion.refs_0_), channel_id=1, source_target_pairs={{0,6},{1,7},{2,4},{3,5},{4,2},{5,3},{6,0},{7,1},{8,14},{9,15},{10,... | collective-permute-start | bytes 737288 | tf_op jit(solution)/shard_map/ppermute | solution.py:655
  28.6 0.9 collective-permute-start.13
  29.6 0.6 copy-done.14
  30.2 0.7 copy-done.15
  30.9 2.9 %unpack_first.1 = (bf16[2304,256]{1,0:T(8,128)(2,1)}, f32[16,256]{1,0:T(8,128)}) custom-call(s32[2]{0:T(128)} %pad_add_fusion.me.refs_6_.refs_3_.refs_0_, bf16[4,160,128]{2,1,0:T(8,128)(2,1)} %copy-done.1, bf16[4,160,128]{2,1,0:T(8,128)(2,1)} %copy-done.12, bf16[4,160,128]{2,1,0:T(8,128)(2,1)} %copy-done.11, bf16[4,160,128]{2,1,0:T(8,128)(2,1)} %copy-done.13, ...), custom_call_target="tpu_custom_call" | custom-call | tf_op jit(solution)/shard_map/unpack_first/pallas_call | solution.py:725
  33.7 9.3 %conv_one.1 = (f32[16,256,256]{2,1,0:T(8,128)}, bf16[16,288,768]{2,1,0:T(8,128)(2,1)}) custom-call(s32[1]{0:T(128)S(6)} %copy.39.cnt_ref.refs_0_, bf16[16,256,256]{2,1,0:T(8,128)(2,1)} %bitcast.133, f32[16,8,256]{2,1,0:T(8,128)} %figures.1.cf_ref.refs_4_, f32[16,256]{1,0:T(8,128)} %get-tuple-element.113.vec_ref.refs_5_, ...), custom_call_target="tpu_custom_call" | custom-call | flops 9663676416 | bytes 41943040 | tf_op jit(solution)/shard_map/conv_one/pallas_call | solution.py:185
  44.3 0.6 multiply_convert_fusion.refs_4_
  46.1 0.7 copy-done.8
  46.8 3.4 %unpack_second.1 = (bf16[256,512]{1,0:T(8,128)(2,1)}, bf16[2304,256]{1,0:T(8,128)(2,1)}, bf16[768,256]{1,0:T(8,128)(2,1)}, bf16[256,256]{1,0:T(8,128)(2,1)}) custom-call(s32[2]{0:T(128)} %pad_add_fusion.me.refs_6_.refs_3_.refs_0_, bf16[4,240,128]{2,1,0:T(8,128)(2,1)} %copy-done, bf16[4,240,128]{2,1,0:T(8,128)(2,1)} %copy-done.5, ...), custom_call_target="tpu_custom_call" | custom-call | tf_op jit(solution)/shard_map/unpack_second/pallas_call | solution.py:725
  50.1 40.3 %middle.1 = (f32[16,256,256]{2,1,0:T(8,128)}, bf16[16,256,256]{2,1,0:T(8,128)(2,1)}, f32[16,256,256]{2,1,0:T(8,128)}, bf16[4,4,256,128]{3,2,1,0:T(8,128)(2,1)}, bf16[4,4,256,128]{3,2,1,0:T(8,128)(2,1)}) custom-call(s32[1]{0:T(128)S(6)} %copy.39.cnt_ref.refs_0_, bf16[16,256,256]{2,1,0:T(8,128)(2,1)} %bitcast.134, f32[16,256,256]{2,1,0:T(8,128)} %get-tuple-element.121.refs_2_, ...), custom_call_target="tpu_custom_call" | custom-call | flops 48318382080 | bytes 167772160 | tf_op jit(solution)/shard_map/middle/pallas_call | solution.py:185
  90.6 2.9 %collective-permute-done.20 = bf16[4,4,256,128]{3,2,1,0:T(8,128)(2,1)S(1)} collective-permute-done((bf16[4,4,256,128]{3,2,1,0:T(8,128)(2,1)}, bf16[4,4,256,128]{3,2,1,0:T(8,128)(2,1)S(1)}, u32[]{:S(2)}, u32[]{:S(2)}) %collective-permute-start.20) | collective-permute-done | bytes 1048608 | tf_op jit(solution)/shard_map/ppermute | solution.py:655
  93.4 1.5 fusion.3
  95.0 3.0 %collective-permute-start.22 = (bf16[4,256,128]{2,1,0:T(8,128)(2,1)S(1)}, bf16[4,256,128]{2,1,0:T(8,128)(2,1)S(1)}, u32[]{:S(2)}, u32[]{:S(2)}) collective-permute-start(bf16[4,256,128]{2,1,0:T(8,128)(2,1)S(1)} %get-tuple-element.140), channel_id=1, source_target_pairs={{0,4},{1,5},{2,6},{3,7},{4,0},{5,1},{6,2},{7,3},{8,12},{9,13},{10,... | collective-permute-start | bytes 786440 | tf_op jit(solution)/shard_map/ppermute | solution.py:655
  98.5 9.3 %conv_one_grad.1 = (bf16[4,4,144,128]{3,2,1,0:T(8,128)(2,1)}, bf16[4,4,144,128]{3,2,1,0:T(8,128)(2,1)}) custom-call(s32[1]{0:T(128)S(6)} %copy.39.cnt_ref.refs_0_, bf16[16,256,256]{2,1,0:T(8,128)(2,1)} %get-tuple-element.134.refs_1_.refs_2_, bf16[16,288,768]{2,1,0:T(8,128)(2,1)} %get-tuple-element.136.refs_2_, s32[2]{0:T(128)} %pad_add_fusion.me.refs_6_.refs_3_.refs_0_), custom_call_target="tpu_custom_call" | custom-call | flops 9663676416 | bytes 41943040 | tf_op jit(solution)/shard_map/conv_one_grad/pallas_call | solution.py:185
  107.7 2.2 %collective-permute-done.22 = bf16[4,256,128]{2,1,0:T(8,128)(2,1)S(1)} collective-permute-done((bf16[4,256,128]{2,1,0:T(8,128)(2,1)S(1)}, bf16[4,256,128]{2,1,0:T(8,128)(2,1)S(1)}, u32[]{:S(2)}, u32[]{:S(2)}) %collective-permute-start.22) | collective-permute-done | bytes 262176 | tf_op jit(solution)/shard_map/ppermute | solution.py:655
  110.0 0.8 add_bitcast_fusion
  110.8 1.4 collective-permute-done.24
  112.2 1.3 fusion.7
  113.5 3.8 %collective-permute-start.29 = (bf16[256,128]{1,0:T(8,128)(2,1)S(1)}, bf16[256,128]{1,0:T(8,128)(2,1)S(1)}, u32[]{:S(2)}, u32[]{:S(2)}) collective-permute-start(bf16[256,128]{1,0:T(8,128)(2,1)S(1)} %get-tuple-element.154), channel_id=1, source_target_pairs={{0,16},{1,17},{2,18},{3,19},{4,20},{5,21},{6,22},{7,23},{8,24},{9,... | collective-permute-start | bytes 196616 | tf_op jit(solution)/shard_map/ppermute | solution.py:655
  117.9 1.5 collective-permute-start.25
  119.4 0.6 collective-permute-start.26
  120.0 1.4 collective-permute-start.27
  121.4 7.6 %input_grad.2 = (f32[16,256,256]{2,1,0:T(8,128)}, f32[8,128]{1,0:T(8,128)}) custom-call(s32[1]{0:T(128)S(6)} %copy.39.cnt_ref.refs_0_, bf16[16,256,256]{2,1,0:T(8,128)(2,1)} %bitcast.135, bf16[16,256,256]{2,1,0:T(8,128)(2,1)} %get-tuple-element.134.refs_1_.refs_2_, f32[16,256,256]{2,1,0:T(8,128)} %get-tuple-element.148.refs_3_, ...), custom_call_target="tpu_custom_call" | custom-call | flops 6442450944 | bytes 29360128 | tf_op jit(solution)/shard_map/input_grad/pallas_call | solution.py:597
  129.0 0.7 add_bitcast_fusion.1
  129.8 3.8 %collective-permute-start.32 = (bf16[144,128]{1,0:T(8,128)(2,1)S(1)}, bf16[144,128]{1,0:T(8,128)(2,1)S(1)}, u32[]{:S(2)}, u32[]{:S(2)}) collective-permute-start(bf16[144,128]{1,0:T(8,128)(2,1)S(1)} %get-tuple-element.168), channel_id=1, source_target_pairs={{0,16},{1,17},{2,18},{3,19},{4,20},{5,21},{6,22},{7,23},{8,24},{9,... | collective-permute-start | bytes 110600 | tf_op jit(solution)/shard_map/ppermute | solution.py:655
  134.1 7.6 %input_grad.3 = (f32[16,256,256]{2,1,0:T(8,128)}, f32[8,128]{1,0:T(8,128)}) custom-call(s32[1]{0:T(128)S(6)} %copy.39.cnt_ref.refs_0_, bf16[16,256,256]{2,1,0:T(8,128)(2,1)} %bitcast.136, bf16[16,256,256]{2,1,0:T(8,128)(2,1)} %get-tuple-element.134.refs_1_.refs_2_, f32[16,256,256]{2,1,0:T(8,128)} %get-tuple-element.148.refs_3_, ...), custom_call_target="tpu_custom_call", output_to_operand_aliasing={{0}: (8, {})} | custom-call | flops 6442450944 | bytes 29360128 | tf_op jit(solution)/shard_map/input_grad/pallas_call | solution.py:597
  142.4 1.9 %shares.1 = (f32[256,128]{1,0:T(8,128)}, f32[144,128]{1,0:T(8,128)}, f32[8,128]{1,0:T(8,128)}) custom-call(f32[256,128]{1,0:T(8,128)} %get-tuple-element.202.refs_0_, bf16[256,128]{1,0:T(8,128)(2,1)} %copy-done.16, bf16[256,128]{1,0:T(8,128)(2,1)} %copy-done.17, bf16[256,128]{1,0:T(8,128)(2,1)} %copy-done.18, f32[144,128]{1,0:T(8,128)} %get-tuple-element.206.refs_4_, ...), custom_call_target="tpu_custom_call" | custom-call | tf_op jit(solution)/shard_map/shares/pallas_call | solution.py:829
  144.2 1.4 collective-permute-done.34
  145.6 0.7 add.199
  146.3 1.5 collective-permute-start.37
  147.8 1.9 %collective-permute-start.35 = (f32[8,128]{1,0:T(8,128)S(1)}, f32[8,128]{1,0:T(8,128)S(1)}, u32[]{:S(2)}, u32[]{:S(2)}) collective-permute-start(f32[8,128]{1,0:T(8,128)S(1)} %add.199), channel_id=1, source_target_pairs={{0,2},{1,3},{2,0},{3,1},{4,6},{5,7},{6,4},{7,5},{8,10},{9,11},{10,... | collective-permute-start | bytes 12296 | tf_op jit(solution)/shard_map/ppermute | solution.py:655
  149.8 1.0 collective-permute-done.37
  150.8 0.6 collective-permute-done.36
  151.5 3.5 %collective-permute-start.40 = (f32[8,128]{1,0:T(8,128)S(1)}, f32[8,128]{1,0:T(8,128)S(1)}, u32[]{:S(2)}, u32[]{:S(2)}) collective-permute-start(f32[8,128]{1,0:T(8,128)S(1)} %add_add_fusion.refs_1_), channel_id=1, source_target_pairs={{0,24},{1,25},{2,26},{3,27},{4,28},{5,29},{6,30},{7,31},{8,16},{9,... | collective-permute-start | bytes 12296 | tf_op jit(solution)/shard_map/ppermute | solution.py:655
  155.0 0.9 collective-permute-start.38
  155.9 1.0 collective-permute-done.40.refs_4_
  156.9 2.6 %collective-permute-done.39.refs_3_ = f32[8,128]{1,0:T(8,128)S(1)} collective-permute-done((f32[8,128]{1,0:T(8,128)S(1)}, f32[8,128]{1,0:T(8,128)S(1)}, u32[]{:S(2)}, u32[]{:S(2)}) %collective-permute-start.39) | collective-permute-done | bytes 4128 | tf_op jit(solution)/shard_map/ppermute | solution.py:655
  160.1 2.8 %clipped_adamw.1 = (f32[18,32,64]{2,1,0:T(8,128)}, f32[18,32,64]{2,1,0:T(8,128)}, f32[18,32,64]{2,1,0:T(8,128)}, f32[32,128]{1,0:T(8,128)}, f32[32,128]{1,0:T(8,...) custom-call(s32[2]{0:T(128)} %pad_add_fusion.me.refs_6_.refs_3_.refs, ...), custom_call_target="tpu_custom_call" | custom-call | tf_op jit(solution)/shard_map/clipped_adamw/pallas_call | solution.py:892
  (114 shorter events, 7.8 us)
Async XLA Ops:
  0.7 25.3 %copy-start.27 = (s32[16]{0:T(128)S(1)}, s32[16]{0:T(128)}, u32[]{:S(2)}) copy-start(s32[16]{0:T(128)} %param.20) | copy-start | bytes 196
  2.5 23.4 %copy-start.19 = (bf16[240,128]{1,0:T(8,128)(2,1)S(1)}, bf16[240,128]{1,0:T(8,128)(2,1)}, u32[]{:S(2)}) copy-start(bf16[240,128]{1,0:T(8,128)(2,1)} %get-tuple-element.115) | copy-start | bytes 184324
  2.5 9.4 %collective-permute-start.5 = (bf16[160,128]{1,0:T(8,128)(2,1)}, bf16[160,128]{1,0:T(8,128)(2,1)S(1)}, u32[]{:S(2)}, u32[]{:S(2)}) collective-permute-start(bf16[160,128]{1,0:T(8,128)(2,1)} %get-tuple-element.107), channel_id=1, source_target_pairs={{0,24},{1,25},{2,26},{3,27},{4,28},{5,29},{6,30},{7,31},{8,16},{9,... | collective-permute-start | bytes 122888 | tf_op jit(solution)/shard_map/ppermute | solution.py:655
  7.5 5.9 %collective-permute-start.4 = (bf16[160,128]{1,0:T(8,128)(2,1)}, bf16[160,128]{1,0:T(8,128)(2,1)S(1)}, u32[]{:S(2)}, u32[]{:S(2)}) collective-permute-start(bf16[160,128]{1,0:T(8,128)(2,1)} %get-tuple-element.107), channel_id=1, source_target_pairs={{0,16},{1,17},{2,18},{3,19},{4,20},{5,21},{6,22},{7,23},{8,24},{9,... | collective-permute-start | bytes 122888 | tf_op jit(solution)/shard_map/ppermute | solution.py:655
  7.5 5.9 %collective-permute-start.3 = (bf16[160,128]{1,0:T(8,128)(2,1)}, bf16[160,128]{1,0:T(8,128)(2,1)S(1)}, u32[]{:S(2)}, u32[]{:S(2)}) collective-permute-start(bf16[160,128]{1,0:T(8,128)(2,1)} %get-tuple-element.107), channel_id=1, source_target_pairs={{0,8},{1,9},{2,10},{3,11},{4,12},{5,13},{6,14},{7,15},{8,0},{9,1},... | collective-permute-start | bytes 122888 | tf_op jit(solution)/shard_map/ppermute | solution.py:655
  8.1 10.9 %collective-permute-start.2 = (bf16[240,128]{1,0:T(8,128)(2,1)}, bf16[240,128]{1,0:T(8,128)(2,1)S(1)}, u32[]{:S(2)}, u32[]{:S(2)}) collective-permute-start(bf16[240,128]{1,0:T(8,128)(2,1)} %get-tuple-element.115), channel_id=1, source_target_pairs={{0,24},{1,25},{2,26},{3,27},{4,28},{5,29},{6,30},{7,31},{8,16},{9,... | collective-permute-start | bytes 184328 | tf_op jit(solution)/shard_map/ppermute | solution.py:655
  14.2 15.3 %copy-start.1 = (bf16[4,160,128]{2,1,0:T(8,128)(2,1)}, bf16[4,160,128]{2,1,0:T(8,128)(2,1)S(1)}, u32[]{:S(2)}) copy-start(bf16[4,160,128]{2,1,0:T(8,128)(2,1)S(1)} %pad_maximum_fusion.1.refs_0_) | copy-start | bytes 491524
  14.2 9.9 %collective-permute-start.8 = (bf16[4,160,128]{2,1,0:T(8,128)(2,1)S(1)}, bf16[4,160,128]{2,1,0:T(8,128)(2,1)S(1)}, u32[]{:S(2)}, u32[]{:S(2)}) collective-permute-start(bf16[4,160,128]{2,1,0:T(8,128)(2,1)S(1)} %pad_maximum_fusion.1.refs_0_), channel_id=1, source_target_pairs={{0,6},{1,7},{2,4},{3,5},{4,2},{5,3},{6,0},{7,1},{8,14},{9,15},{10,... | collective-permute-start | bytes 491528 | tf_op jit(solution)/shard_map/ppermute | solution.py:655
  16.8 7.4 %collective-permute-start.7 = (bf16[4,160,128]{2,1,0:T(8,128)(2,1)S(1)}, bf16[4,160,128]{2,1,0:T(8,128)(2,1)S(1)}, u32[]{:S(2)}, u32[]{:S(2)}) collective-permute-start(bf16[4,160,128]{2,1,0:T(8,128)(2,1)S(1)} %pad_maximum_fusion.1.refs_0_), channel_id=1, source_target_pairs={{0,4},{1,5},{2,6},{3,7},{4,0},{5,1},{6,2},{7,3},{8,12},{9,13},{10,... | collective-permute-start | bytes 491528 | tf_op jit(solution)/shard_map/ppermute | solution.py:655
  17.3 6.9 %collective-permute-start.6 = (bf16[4,160,128]{2,1,0:T(8,128)(2,1)S(1)}, bf16[4,160,128]{2,1,0:T(8,128)(2,1)S(1)}, u32[]{:S(2)}, u32[]{:S(2)}) collective-permute-start(bf16[4,160,128]{2,1,0:T(8,128)(2,1)S(1)} %pad_maximum_fusion.1.refs_0_), channel_id=1, source_target_pairs={{0,2},{1,3},{2,0},{3,1},{4,6},{5,7},{6,4},{7,5},{8,10},{9,11},{10,... | collective-permute-start | bytes 491528 | tf_op jit(solution)/shard_map/ppermute | solution.py:655
  17.8 6.4 %collective-permute-start.1 = (bf16[240,128]{1,0:T(8,128)(2,1)}, bf16[240,128]{1,0:T(8,128)(2,1)S(1)}, u32[]{:S(2)}, u32[]{:S(2)}) collective-permute-start(bf16[240,128]{1,0:T(8,128)(2,1)} %get-tuple-element.115), channel_id=1, source_target_pairs={{0,16},{1,17},{2,18},{3,19},{4,20},{5,21},{6,22},{7,23},{8,24},{9,... | collective-permute-start | bytes 184328 | tf_op jit(solution)/shard_map/ppermute | solution.py:655
  19.0 5.1 %collective-permute-start = (bf16[240,128]{1,0:T(8,128)(2,1)}, bf16[240,128]{1,0:T(8,128)(2,1)S(1)}, u32[]{:S(2)}, u32[]{:S(2)}) collective-permute-start(bf16[240,128]{1,0:T(8,128)(2,1)} %get-tuple-element.115), channel_id=1, source_target_pairs={{0,8},{1,9},{2,10},{3,11},{4,12},{5,13},{6,14},{7,15},{8,0},{9,1},... | collective-permute-start | bytes 184328 | tf_op jit(solution)/shard_map/ppermute | solution.py:655
  24.2 4.3 %collective-permute-start.9 = (bf16[4,160,128]{2,1,0:T(8,128)(2,1)S(1)}, bf16[4,160,128]{2,1,0:T(8,128)(2,1)S(1)}, u32[]{:S(2)}, u32[]{:S(2)}) collective-permute-start(bf16[4,160,128]{2,1,0:T(8,128)(2,1)S(1)} %pad_maximum_fusion.1.refs_0_), channel_id=1, source_target_pairs={{0,1},{1,0},{2,3},{3,2},{4,5},{5,4},{6,7},{7,6},{8,9},{9,8},{10,11... | collective-permute-start | bytes 491528 | tf_op jit(solution)/shard_map/ppermute | solution.py:655
  24.3 4.3 %collective-permute-start.10 = (bf16[4,160,128]{2,1,0:T(8,128)(2,1)S(1)}, bf16[4,160,128]{2,1,0:T(8,128)(2,1)S(1)}, u32[]{:S(2)}, u32[]{:S(2)}) collective-permute-start(bf16[4,160,128]{2,1,0:T(8,128)(2,1)S(1)} %collective-permute-done.6.refs_2_), channel_id=1, source_target_pairs={{0,1},{1,0},{2,3},{3,2},{4,5},{5,4},{6,7},{7,6},{8,9},{9,8},{10,11... | collective-permute-start | bytes 491528 | tf_op jit(solution)/shard_map/ppermute | solution.py:655
  24.8 4.7 %collective-permute-start.11 = (bf16[4,160,128]{2,1,0:T(8,128)(2,1)S(1)}, bf16[4,160,128]{2,1,0:T(8,128)(2,1)S(1)}, u32[]{:S(2)}, u32[]{:S(2)}) collective-permute-start(bf16[4,160,128]{2,1,0:T(8,128)(2,1)S(1)} %collective-permute-done.7.refs_4_), channel_id=1, source_target_pairs={{0,1},{1,0},{2,3},{3,2},{4,5},{5,4},{6,7},{7,6},{8,9},{9,8},{10,11... | collective-permute-start | bytes 491528 | tf_op jit(solution)/shard_map/ppermute | solution.py:655
  24.9 4.7 %collective-permute-start.12 = (bf16[4,160,128]{2,1,0:T(8,128)(2,1)S(1)}, bf16[4,160,128]{2,1,0:T(8,128)(2,1)S(1)}, u32[]{:S(2)}, u32[]{:S(2)}) collective-permute-start(bf16[4,160,128]{2,1,0:T(8,128)(2,1)S(1)} %collective-permute-done.8.refs_6_), channel_id=1, source_target_pairs={{0,1},{1,0},{2,3},{3,2},{4,5},{5,4},{6,7},{7,6},{8,9},{9,8},{10,11... | collective-permute-start | bytes 491528 | tf_op jit(solution)/shard_map/ppermute | solution.py:655
  26.0 17.1 %copy-start = (bf16[4,240,128]{2,1,0:T(8,128)(2,1)}, bf16[4,240,128]{2,1,0:T(8,128)(2,1)S(1)}, u32[]{:S(2)}) copy-start(bf16[4,240,128]{2,1,0:T(8,128)(2,1)S(1)} %pad_maximum_fusion.refs_0_) | copy-start | bytes 737284
  26.0 17.1 %collective-permute-start.15 = (bf16[4,240,128]{2,1,0:T(8,128)(2,1)S(1)}, bf16[4,240,128]{2,1,0:T(8,128)(2,1)S(1)}, u32[]{:S(2)}, u32[]{:S(2)}) collective-permute-start(bf16[4,240,128]{2,1,0:T(8,128)(2,1)S(1)} %pad_maximum_fusion.refs_0_), channel_id=1, source_target_pairs={{0,6},{1,7},{2,4},{3,5},{4,2},{5,3},{6,0},{7,1},{8,14},{9,15},{10,... | collective-permute-start | bytes 737288 | tf_op jit(solution)/shard_map/ppermute | solution.py:655
  28.5 14.5 %collective-permute-start.14 = (bf16[4,240,128]{2,1,0:T(8,128)(2,1)S(1)}, bf16[4,240,128]{2,1,0:T(8,128)(2,1)S(1)}, u32[]{:S(2)}, u32[]{:S(2)}) collective-permute-start(bf16[4,240,128]{2,1,0:T(8,128)(2,1)S(1)} %pad_maximum_fusion.refs_0_), channel_id=1, source_target_pairs={{0,4},{1,5},{2,6},{3,7},{4,0},{5,1},{6,2},{7,3},{8,12},{9,13},{10,... | collective-permute-start | bytes 737288 | tf_op jit(solution)/shard_map/ppermute | solution.py:655
  28.6 14.4 %collective-permute-start.13 = (bf16[4,240,128]{2,1,0:T(8,128)(2,1)S(1)}, bf16[4,240,128]{2,1,0:T(8,128)(2,1)S(1)}, u32[]{:S(2)}, u32[]{:S(2)}) collective-permute-start(bf16[4,240,128]{2,1,0:T(8,128)(2,1)S(1)} %pad_maximum_fusion.refs_0_), channel_id=1, source_target_pairs={{0,2},{1,3},{2,0},{3,1},{4,6},{5,7},{6,4},{7,5},{8,10},{9,11},{10,... | collective-permute-start | bytes 737288 | tf_op jit(solution)/shard_map/ppermute | solution.py:655
  43.1 1.9 %collective-permute-start.16 = (bf16[4,240,128]{2,1,0:T(8,128)(2,1)S(1)}, bf16[4,240,128]{2,1,0:T(8,128)(2,1)S(1)}, u32[]{:S(2)}, u32[]{:S(2)}) collective-permute-start(bf16[4,240,128]{2,1,0:T(8,128)(2,1)S(1)} %pad_maximum_fusion.refs_0_), channel_id=1, source_target_pairs={{0,1},{1,0},{2,3},{3,2},{4,5},{5,4},{6,7},{7,6},{8,9},{9,8},{10,11... | collective-permute-start | bytes 737288 | tf_op jit(solution)/shard_map/ppermute | solution.py:655
  43.2 1.9 %collective-permute-start.17 = (bf16[4,240,128]{2,1,0:T(8,128)(2,1)S(1)}, bf16[4,240,128]{2,1,0:T(8,128)(2,1)S(1)}, u32[]{:S(2)}, u32[]{:S(2)}) collective-permute-start(bf16[4,240,128]{2,1,0:T(8,128)(2,1)S(1)} %collective-permute-done.13.refs_2_), channel_id=1, source_target_pairs={{0,1},{1,0},{2,3},{3,2},{4,5},{5,4},{6,7},{7,6},{8,9},{9,8},{10,11... | collective-permute-start | bytes 737288 | tf_op jit(solution)/shard_map/ppermute | solution.py:655
  43.7 1.7 %collective-permute-start.18 = (bf16[4,240,128]{2,1,0:T(8,128)(2,1)S(1)}, bf16[4,240,128]{2,1,0:T(8,128)(2,1)S(1)}, u32[]{:S(2)}, u32[]{:S(2)}) collective-permute-start(bf16[4,240,128]{2,1,0:T(8,128)(2,1)S(1)} %collective-permute-done.14.refs_4_), channel_id=1, source_target_pairs={{0,1},{1,0},{2,3},{3,2},{4,5},{5,4},{6,7},{7,6},{8,9},{9,8},{10,11... | collective-permute-start | bytes 737288 | tf_op jit(solution)/shard_map/ppermute | solution.py:655
  43.7 2.0 %collective-permute-start.19 = (bf16[4,240,128]{2,1,0:T(8,128)(2,1)S(1)}, bf16[4,240,128]{2,1,0:T(8,128)(2,1)S(1)}, u32[]{:S(2)}, u32[]{:S(2)}) collective-permute-start(bf16[4,240,128]{2,1,0:T(8,128)(2,1)S(1)} %collective-permute-done.15.refs_6_), channel_id=1, source_target_pairs={{0,1},{1,0},{2,3},{3,2},{4,5},{5,4},{6,7},{7,6},{8,9},{9,8},{10,11... | collective-permute-start | bytes 737288 | tf_op jit(solution)/shard_map/ppermute | solution.py:655
  90.5 2.9 %collective-permute-start.20 = (bf16[4,4,256,128]{3,2,1,0:T(8,128)(2,1)}, bf16[4,4,256,128]{3,2,1,0:T(8,128)(2,1)S(1)}, u32[]{:S(2)}, u32[]{:S(2)}) collective-permute-start(bf16[4,4,256,128]{3,2,1,0:T(8,128)(2,1)} %get-tuple-element.133), channel_id=1, source_target_pairs={{0,1},{1,0},{2,3},{3,2},{4,5},{5,4},{6,7},{7,6},{8,9},{9,8},{10,11... | collective-permute-start | bytes 3145736 | tf_op jit(solution)/shard_map/ppermute | solution.py:655
  94.9 12.8 %collective-permute-start.21 = (bf16[4,256,128]{2,1,0:T(8,128)(2,1)S(1)}, bf16[4,256,128]{2,1,0:T(8,128)(2,1)S(1)}, u32[]{:S(2)}, u32[]{:S(2)}) collective-permute-start(bf16[4,256,128]{2,1,0:T(8,128)(2,1)S(1)} %get-tuple-element.139), channel_id=1, source_target_pairs={{0,2},{1,3},{2,0},{3,1},{4,6},{5,7},{6,4},{7,5},{8,10},{9,11},{10,... | collective-permute-start | bytes 786440 | tf_op jit(solution)/shard_map/ppermute | solution.py:655
  95.0 15.0 %collective-permute-start.22 = (bf16[4,256,128]{2,1,0:T(8,128)(2,1)S(1)}, bf16[4,256,128]{2,1,0:T(8,128)(2,1)S(1)}, u32[]{:S(2)}, u32[]{:S(2)}) collective-permute-start(bf16[4,256,128]{2,1,0:T(8,128)(2,1)S(1)} %get-tuple-element.140), channel_id=1, source_target_pairs={{0,4},{1,5},{2,6},{3,7},{4,0},{5,1},{6,2},{7,3},{8,12},{9,13},{10,... | collective-permute-start | bytes 786440 | tf_op jit(solution)/shard_map/ppermute | solution.py:655
  98.0 11.9 %collective-permute-start.23 = (bf16[4,256,128]{2,1,0:T(8,128)(2,1)S(1)}, bf16[4,256,128]{2,1,0:T(8,128)(2,1)S(1)}, u32[]{:S(2)}, u32[]{:S(2)}) collective-permute-start(bf16[4,256,128]{2,1,0:T(8,128)(2,1)S(1)} %get-tuple-element.141), channel_id=1, source_target_pairs={{0,6},{1,7},{2,4},{3,5},{4,2},{5,3},{6,0},{7,1},{8,14},{9,15},{10,... | collective-permute-start | bytes 786440 | tf_op jit(solution)/shard_map/ppermute | solution.py:655
  110.0 2.2 %collective-permute-start.24 = (bf16[4,4,144,128]{3,2,1,0:T(8,128)(2,1)}, bf16[4,4,144,128]{3,2,1,0:T(8,128)(2,1)S(1)}, u32[]{:S(2)}, u32[]{:S(2)}) collective-permute-start(bf16[4,4,144,128]{3,2,1,0:T(8,128)(2,1)} %get-tuple-element.143), channel_id=1, source_target_pairs={{0,1},{1,0},{2,3},{3,2},{4,5},{5,4},{6,7},{7,6},{8,9},{9,8},{10,11... | collective-permute-start | bytes 1769480 | tf_op jit(solution)/shard_map/ppermute | solution.py:655
  113.5 6.6 %collective-permute-start.28 = (bf16[256,128]{1,0:T(8,128)(2,1)S(1)}, bf16[256,128]{1,0:T(8,128)(2,1)S(1)}, u32[]{:S(2)}, u32[]{:S(2)}) collective-permute-start(bf16[256,128]{1,0:T(8,128)(2,1)S(1)} %get-tuple-element.153), channel_id=1, source_target_pairs={{0,8},{1,9},{2,10},{3,11},{4,12},{5,13},{6,14},{7,15},{8,0},{9,1},... | collective-permute-start | bytes 196616 | tf_op jit(solution)/shard_map/ppermute | solution.py:655
  113.5 15.4 %collective-permute-start.29 = (bf16[256,128]{1,0:T(8,128)(2,1)S(1)}, bf16[256,128]{1,0:T(8,128)(2,1)S(1)}, u32[]{:S(2)}, u32[]{:S(2)}) collective-permute-start(bf16[256,128]{1,0:T(8,128)(2,1)S(1)} %get-tuple-element.154), channel_id=1, source_target_pairs={{0,16},{1,17},{2,18},{3,19},{4,20},{5,21},{6,22},{7,23},{8,24},{9,... | collective-permute-start | bytes 196616 | tf_op jit(solution)/shard_map/ppermute | solution.py:655
  117.4 11.6 %collective-permute-start.30 = (bf16[256,128]{1,0:T(8,128)(2,1)S(1)}, bf16[256,128]{1,0:T(8,128)(2,1)S(1)}, u32[]{:S(2)}, u32[]{:S(2)}) collective-permute-start(bf16[256,128]{1,0:T(8,128)(2,1)S(1)} %get-tuple-element.155), channel_id=1, source_target_pairs={{0,24},{1,25},{2,26},{3,27},{4,28},{5,29},{6,30},{7,31},{8,16},{9,... | collective-permute-start | bytes 196616 | tf_op jit(solution)/shard_map/ppermute | solution.py:655
  117.9 11.1 %collective-permute-start.25 = (bf16[4,144,128]{2,1,0:T(8,128)(2,1)S(1)}, bf16[4,144,128]{2,1,0:T(8,128)(2,1)S(1)}, u32[]{:S(2)}, u32[]{:S(2)}) collective-permute-start(bf16[4,144,128]{2,1,0:T(8,128)(2,1)S(1)} %get-tuple-element.150), channel_id=1, source_target_pairs={{0,2},{1,3},{2,0},{3,1},{4,6},{5,7},{6,4},{7,5},{8,10},{9,11},{10,... | collective-permute-start | bytes 442376 | tf_op jit(solution)/shard_map/ppermute | solution.py:655
  119.4 9.7 %collective-permute-start.26 = (bf16[4,144,128]{2,1,0:T(8,128)(2,1)S(1)}, bf16[4,144,128]{2,1,0:T(8,128)(2,1)S(1)}, u32[]{:S(2)}, u32[]{:S(2)}) collective-permute-start(bf16[4,144,128]{2,1,0:T(8,128)(2,1)S(1)} %get-tuple-element.151), channel_id=1, source_target_pairs={{0,4},{1,5},{2,6},{3,7},{4,0},{5,1},{6,2},{7,3},{8,12},{9,13},{10,... | collective-permute-start | bytes 442376 | tf_op jit(solution)/shard_map/ppermute | solution.py:655
  120.0 8.9 %copy-start.16 = (bf16[256,128]{1,0:T(8,128)(2,1)}, bf16[256,128]{1,0:T(8,128)(2,1)S(1)}, u32[]{:S(2)}) copy-start(bf16[256,128]{1,0:T(8,128)(2,1)S(1)} %collective-permute-done.28.refs_1_) | copy-start | bytes 196612
  120.0 9.0 %collective-permute-start.27 = (bf16[4,144,128]{2,1,0:T(8,128)(2,1)S(1)}, bf16[4,144,128]{2,1,0:T(8,128)(2,1)S(1)}, u32[]{:S(2)}, u32[]{:S(2)}) collective-permute-start(bf16[4,144,128]{2,1,0:T(8,128)(2,1)S(1)} %get-tuple-element.152), channel_id=1, source_target_pairs={{0,6},{1,7},{2,4},{3,5},{4,2},{5,3},{6,0},{7,1},{8,14},{9,15},{10,... | collective-permute-start | bytes 442376 | tf_op jit(solution)/shard_map/ppermute | solution.py:655
  129.0 12.7 %copy-start.17 = (bf16[256,128]{1,0:T(8,128)(2,1)}, bf16[256,128]{1,0:T(8,128)(2,1)S(1)}, u32[]{:S(2)}) copy-start(bf16[256,128]{1,0:T(8,128)(2,1)S(1)} %collective-permute-done.29.refs_2_) | copy-start | bytes 196612
  129.0 12.7 %copy-start.18 = (bf16[256,128]{1,0:T(8,128)(2,1)}, bf16[256,128]{1,0:T(8,128)(2,1)S(1)}, u32[]{:S(2)}) copy-start(bf16[256,128]{1,0:T(8,128)(2,1)S(1)} %collective-permute-done.30.refs_3_) | copy-start | bytes 196612
  129.7 12.0 %collective-permute-start.31 = (bf16[144,128]{1,0:T(8,128)(2,1)S(1)}, bf16[144,128]{1,0:T(8,128)(2,1)S(1)}, u32[]{:S(2)}, u32[]{:S(2)}) collective-permute-start(bf16[144,128]{1,0:T(8,128)(2,1)S(1)} %get-tuple-element.167), channel_id=1, source_target_pairs={{0,8},{1,9},{2,10},{3,11},{4,12},{5,13},{6,14},{7,15},{8,0},{9,1},... | collective-permute-start | bytes 110600 | tf_op jit(solution)/shard_map/ppermute | solution.py:655
  129.8 12.0 %collective-permute-start.32 = (bf16[144,128]{1,0:T(8,128)(2,1)S(1)}, bf16[144,128]{1,0:T(8,128)(2,1)S(1)}, u32[]{:S(2)}, u32[]{:S(2)}) collective-permute-start(bf16[144,128]{1,0:T(8,128)(2,1)S(1)} %get-tuple-element.168), channel_id=1, source_target_pairs={{0,16},{1,17},{2,18},{3,19},{4,20},{5,21},{6,22},{7,23},{8,24},{9,... | collective-permute-start | bytes 110600 | tf_op jit(solution)/shard_map/ppermute | solution.py:655
  133.6 8.2 %collective-permute-start.33 = (bf16[144,128]{1,0:T(8,128)(2,1)S(1)}, bf16[144,128]{1,0:T(8,128)(2,1)S(1)}, u32[]{:S(2)}, u32[]{:S(2)}) collective-permute-start(bf16[144,128]{1,0:T(8,128)(2,1)S(1)} %get-tuple-element.169), channel_id=1, source_target_pairs={{0,24},{1,25},{2,26},{3,27},{4,28},{5,29},{6,30},{7,31},{8,16},{9,... | collective-permute-start | bytes 110600 | tf_op jit(solution)/shard_map/ppermute | solution.py:655
  144.2 1.4 collective-permute-start.34
  146.3 4.5 %collective-permute-start.37 = (f32[8,128]{1,0:T(8,128)S(1)}, f32[8,128]{1,0:T(8,128)S(1)}, u32[]{:S(2)}, u32[]{:S(2)}) collective-permute-start(f32[8,128]{1,0:T(8,128)S(1)} %add.199), channel_id=1, source_target_pairs={{0,6},{1,7},{2,4},{3,5},{4,2},{5,3},{6,0},{7,1},{8,14},{9,15},{10,... | collective-permute-start | bytes 12296 | tf_op jit(solution)/shard_map/ppermute | solution.py:655
  147.8 3.6 %collective-permute-start.36 = (f32[8,128]{1,0:T(8,128)S(1)}, f32[8,128]{1,0:T(8,128)S(1)}, u32[]{:S(2)}, u32[]{:S(2)}) collective-permute-start(f32[8,128]{1,0:T(8,128)S(1)} %add.199), channel_id=1, source_target_pairs={{0,4},{1,5},{2,6},{3,7},{4,0},{5,1},{6,2},{7,3},{8,12},{9,13},{10,... | collective-permute-start | bytes 12296 | tf_op jit(solution)/shard_map/ppermute | solution.py:655
  147.8 3.6 %collective-permute-start.35 = (f32[8,128]{1,0:T(8,128)S(1)}, f32[8,128]{1,0:T(8,128)S(1)}, u32[]{:S(2)}, u32[]{:S(2)}) collective-permute-start(f32[8,128]{1,0:T(8,128)S(1)} %add.199), channel_id=1, source_target_pairs={{0,2},{1,3},{2,0},{3,1},{4,6},{5,7},{6,4},{7,5},{8,10},{9,11},{10,... | collective-permute-start | bytes 12296 | tf_op jit(solution)/shard_map/ppermute | solution.py:655
  151.5 5.5 %collective-permute-start.40 = (f32[8,128]{1,0:T(8,128)S(1)}, f32[8,128]{1,0:T(8,128)S(1)}, u32[]{:S(2)}, u32[]{:S(2)}) collective-permute-start(f32[8,128]{1,0:T(8,128)S(1)} %add_add_fusion.refs_1_), channel_id=1, source_target_pairs={{0,24},{1,25},{2,26},{3,27},{4,28},{5,29},{6,30},{7,31},{8,16},{9,... | collective-permute-start | bytes 12296 | tf_op jit(solution)/shard_map/ppermute | solution.py:655
  155.0 4.5 %collective-permute-start.39 = (f32[8,128]{1,0:T(8,128)S(1)}, f32[8,128]{1,0:T(8,128)S(1)}, u32[]{:S(2)}, u32[]{:S(2)}) collective-permute-start(f32[8,128]{1,0:T(8,128)S(1)} %add_add_fusion.refs_1_), channel_id=1, source_target_pairs={{0,16},{1,17},{2,18},{3,19},{4,20},{5,21},{6,22},{7,23},{8,24},{9,... | collective-permute-start | bytes 12296 | tf_op jit(solution)/shard_map/ppermute | solution.py:655
  155.0 4.5 %collective-permute-start.38 = (f32[8,128]{1,0:T(8,128)S(1)}, f32[8,128]{1,0:T(8,128)S(1)}, u32[]{:S(2)}, u32[]{:S(2)}) collective-permute-start(f32[8,128]{1,0:T(8,128)S(1)} %add_add_fusion.refs_1_), channel_id=1, source_target_pairs={{0,8},{1,9},{2,10},{3,11},{4,12},{5,13},{6,14},{7,15},{8,0},{9,1},... | collective-permute-start | bytes 12296 | tf_op jit(solution)/shard_map/ppermute | solution.py:655
  (21 other events, 44.2 us)

commit v2 on v1

--- a/solution.py
+++ b/solution.py
@@ -26,8 +26,7 @@
 R = range(0, 256, CH)
 RA = 160
 RB = 240
-GB = 256
-GA = 144
+RG = 400
 
 sd = jax.ShapeDtypeStruct
 
@@ -103,9 +102,11 @@
     prev = jnp.where(col == 0, 0.0, pltpu.roll(a, 1, 0))
     post = jnp.where(col == 15, 0.0, pltpu.roll(a, rows - 1, 0))
     lo, hi = (post, prev) if rev else (prev, post)
+    low = a.astype(BF)
     pref[n, 16 + r : 16 + r + rows, 0:256] = lo.astype(BF)
-    pref[n, 16 + r : 16 + r + rows, 256:512] = a.astype(BF)
+    pref[n, 16 + r : 16 + r + rows, 256:512] = low
     pref[n, 16 + r : 16 + r + rows, 512:768] = hi.astype(BF)
+    return low
 
 
 def zero_pads(pref):
@@ -217,8 +218,10 @@
     )
 
 
-def conv_one_body(cnt_ref, x_ref, cf_ref, vec_ref, wat_ref, h0_ref, pa_ref):
-    zero_pads(pa_ref)
+def conv_one_body(cnt_ref, x_ref, cf_ref, vec_ref, wat_ref, h0_ref, a1_ref, pa):
+    @pl.when(pl.program_id(0) == 0)
+    def _():
+        zero_pads(pa)
 
     @pl.when(pl.program_id(0) * NB < cnt_ref[0])
     def _():
@@ -228,9 +231,9 @@
                 sh = 0.5 * row(vec_ref, 1) - cf_ref[n, 0:1, :] * sc
                 for r in R:
                     h = x_ref[n, r : r + CH, :].astype(F32) * sc + sh
-                    put3(pa_ref, n, r, h + h * jnp.tanh(h))
-            yield
-            h0_ref[N.start : N.stop] = conv_forward(pa_ref, wat_ref, N).reshape(len(N), 256, 256)
+                    a1_ref[n, r : r + CH, :] = put3(pa, n, r, h + h * jnp.tanh(h))
+            yield
+            h0_ref[N.start : N.stop] = conv_forward(pa, wat_ref, N).reshape(len(N), 256, 256)
             yield
 
         interleave([part(N) for N in parts()])
@@ -244,18 +247,18 @@
         n,
         (18, 10),
         [blocks(256, 256), blocks(8, 256), whole((16, 256)), whole((2304, 256))],
-        [out_blocks(256, 256), out_blocks(288, 768)],
-        [sd((n, 256, 256), F32), sd((n, 288, 768), BF)],
-        [],
+        [out_blocks(256, 256), out_blocks(256, 256)],
+        [sd((n, 256, 256), F32), sd((n, 256, 256), BF)],
+        [pltpu.VMEM((NB, 288, 768), BF)],
         (cnt, x, cf, vec, wat),
     )
 
 
 def middle_body(finish, n_out, *refs):
-    (cnt_ref, x_ref, h0_ref, cot_ref, emb_ref, vec_ref, me_ref, wet_ref, wbt_ref, wqt_ref, wot_ref) = refs[:11]
-    out_ref, ga_ref, dm_ref = refs[11:14]
-    ends = refs[14 : 14 + n_out]
-    (pa, pg, gt, mid, a3, mx, dmx, dz, she, dsr, dwb, dwq, dwo, dvec, turn) = refs[14 + n_out :]
+    (cnt_ref, x_ref, h0_ref, cot_ref, a1_ref, emb_ref, vec_ref, me_ref, wet_ref, wbt_ref, wqt_ref, wot_ref) = refs[:12]
+    out_ref, ga_ref, dm_ref = refs[12:15]
+    ends = refs[15 : 15 + n_out]
+    (pa, pg, pa1, gt, gt1, mid, a3, mx, dmx, dz, she, dsr, dwa, dwb, dwq, dwo, dvec, turn) = refs[15 + n_out :]
     i = pl.program_id(0)
     cnt = cnt_ref[0]
 
@@ -263,7 +266,8 @@
     def _():
         zero_pads(pa)
         zero_pads(pg)
-        for ref in (dwb, dwq, dwo, dvec, dsr):
+        zero_pads(pa1)
+        for ref in (dwa, dwb, dwq, dwo, dvec, dsr):
             ref[...] = jnp.zeros_like(ref)
         she[...] = dot_nt(emb_ref[...], wet_ref[...]) + (row(vec_ref, 2) + row(vec_ref, 3))
 
@@ -340,6 +344,9 @@
             dv = [dot(ptb[j], datt[L(j)]).astype(BF) for j in W]
             yield
             dst = []
+            for n in N:
+                for r in R:
+                    put3(pa1, n, r, a1_ref[n, r : r + CH, :].astype(F32))
             for j in W:
                 t = dpt[j] * pts[j]
                 dst.append((t - pts[j] * jnp.sum(t, axis=0, keepdims=True)).astype(BF))
@@ -420,6 +427,9 @@
                     ga_ref[n, r : r + CH, :] = dh.astype(BF)
                     ds = ds + csum(dh)
                 dsr[pl.ds(i * NB + n, 1), :] = fsum(ds)
+                gt1[:, n * 256 : n * 256 + 256] = ga_ref[n].T
+            yield
+            add_taps(dwa, gt1[:, lo:hi], pa1, N)
             yield
 
         interleave([part(N) for N in parts()])
@@ -433,18 +443,18 @@
         ds = dsr[...]
         total = fsum(ds)
         rows = jnp.concatenate([jnp.zeros((2, 256), F32), total, total, dvec[4:16, :]], axis=0)
-        finish(ends, me_ref, dwb, dwq, dwo, dot_tn(ds.astype(BF), emb_ref[...]), rows, turn)
-
-
-def middle(cnt, x, h0, cot, emb, vec, me, wet, wbt, wqt, wot, finish, ends):
+        finish(ends, me_ref, dwa, dwb, dwq, dwo, dot_tn(ds.astype(BF), emb_ref[...]), rows, turn)
+
+
+def middle(cnt, x, h0, cot, a1, emb, vec, me, wet, wbt, wqt, wot, finish, ends):
     n = x.shape[0]
     V = pltpu.VMEM
     return image_call(
         lambda *refs: middle_body(finish, len(ends), *refs),
         "middle",
         n,
-        (90, 40),
-        [blocks(256, 256)] * 3
+        (108, 44),
+        [blocks(256, 256)] * 4
         + [whole(emb.shape), whole((16, 256)), pl.BlockSpec(memory_space=pltpu.SMEM)]
         + [whole(w.shape) for w in (wet, wbt, wqt, wot)],
         [out_blocks(256, 256)] * 3 + [whole(e.shape) for e in ends],
@@ -452,6 +462,8 @@
         [
             V((NB, 288, 768), BF),
             V((NB, 288, 768), BF),
+            V((NB, 288, 768), BF),
+            V((256, NB * 256), BF),
             V((256, NB * 256), BF),
             V((NB, 256, 256), F32),
             V((NB * 256, 256), BF),
@@ -461,53 +473,13 @@
             V((n, 256), F32),
             V((n, 256), F32),
             V((768, 768), F32),
+            V((768, 768), F32),
             V((256, 768), F32),
             V((256, 256), F32),
             V((16, 256), F32),
             V((1280, 512), F32),
         ],
-        (cnt, x, h0, cot, emb, vec, me, wet, wbt, wqt, wot),
-    )
-
-
-def conv_one_grad_body(finish, n_out, *refs):
-    cnt_ref, ga_ref, pa_ref, me_ref = refs[:4]
-    ends = refs[4 : 4 + n_out]
-    gt, dwa = refs[4 + n_out :]
-    i = pl.program_id(0)
-
-    @pl.when(i == 0)
-    def _():
-        dwa[...] = jnp.zeros_like(dwa)
-
-    @pl.when(i * NB < cnt_ref[0])
-    def _():
-        def part(N):
-            for n in N:
-                gt[:, n * 256 : n * 256 + 256] = ga_ref[n].T
-            yield
-            add_taps(dwa, gt[:, N.start * 256 : N.stop * 256], pa_ref, N)
-            yield
-
-        interleave([part(N) for N in parts()])
-
-    @pl.when(i == pl.num_programs(0) - 1)
-    def _():
-        finish(ends, me_ref, dwa)
-
-
-def conv_one_grad(cnt, ga, pa, me, finish, ends):
-    n = ga.shape[0]
-    return image_call(
-        lambda *refs: conv_one_grad_body(finish, len(ends), *refs),
-        "conv_one_grad",
-        n,
-        (18, 10),
-        [blocks(256, 256), blocks(288, 768), pl.BlockSpec(memory_space=pltpu.SMEM)],
-        [whole(e.shape) for e in ends],
-        list(ends),
-        [pltpu.VMEM((256, NB * 256), BF), pltpu.VMEM((768, 768), F32)],
-        (cnt, ga, pa, me),
+        (cnt, x, h0, cot, a1, emb, vec, me, wet, wbt, wqt, wot),
     )
 
 
@@ -767,8 +739,9 @@
     return acc
 
 
-def finish_b(outs, me, dwb, dwq, dwo, de, rows, turn):
+def finish_all(outs, me, dwa, dwb, dwq, dwo, de, rows, turn):
     for k in range(9):
+        place(outs, me, dwa, 256 * (k // 3), 256 * (k % 3), 256 + 16 * k, 16, 32)
         place(outs, me, dwb, 256 * (k // 3), 256 * (k % 3), 16 * k, 16, 32)
     for k in range(3):
         turn[256 * k : 256 * k + 256, 0:256] = dwq[:, 256 * k : 256 * k + 256].T
@@ -787,11 +760,6 @@
             outs[rf & 1][rf >> 1, rz, 240:256, :] = jnp.broadcast_to(acc[r : r + 1], (16, 128)).astype(BF)
 
 
-def finish_a(outs, me, dwa):
-    for k in range(9):
-        place(outs, me, dwa, 256 * (k // 3), 256 * (k % 3), 16 * k, 16, 32)
-
-
 def over_core(keep, send):
     got = swap(send, 1)
     return [(keep[j].astype(F32) + got[j].astype(F32)).astype(keep.dtype) for j in range(4)]
@@ -810,28 +778,20 @@
     return [swap(v, 8 * (rz + 1)) for rz, v in enumerate(others)]
 
 
-def shares_body(*refs):
-    sb, sa = (refs[4 * k][...] + sum(r[...].astype(F32) for r in refs[4 * k + 1 : 4 * k + 4]) for k in range(2))
-    v0, v1, gb, ga, out = refs[8:]
-    gb[...] = sb
-    ga[...] = sa
-    fold = lambda v: jnp.sum((v * v).reshape(-1, 8, 128), axis=0)
-    t = fsum(fold(sb[0:240]) + fold(sa)) + sb[240:241] * sb[240:241]
+def shares_body(own, r1, r2, r3, v, g, out):
+    s = own[...] + sum(r[...].astype(F32) for r in (r1, r2, r3))
+    g[...] = s
+    fold = lambda a: jnp.sum((a * a).reshape(-1, 8, 128), axis=0)
+    t = fsum(fold(s[0:240]) + fold(s[256:400])) + s[240:241] * s[240:241]
     t = jnp.broadcast_to(jnp.sum(t, axis=1, keepdims=True), (8, 128))
     line = lax.broadcasted_iota(jnp.int32, (8, 128), 0)
-    out[...] = jnp.where(line < 4, v0[...] + v1[...], t)
-
-
-def shares(b, a, vs):
-    args = []
-    for own, got in (b, a):
-        args += [own, *got]
+    out[...] = jnp.where(line < 4, v[...], t)
+
+
+def shares(own, got, v):
     return pl.pallas_call(
-        shares_body,
-        out_shape=[sd((GB, 128), F32), sd((GA, 128), F32), sd((8, 128), F32)],
-        compiler_params=VMEM,
-        name="shares",
-    )(*args, *vs)
+        shares_body, out_shape=[sd((RG, 128), F32), sd((8, 128), F32)], compiler_params=VMEM, name="shares"
+    )(own, *got, v)
 
 
 def total_over(s):
@@ -841,16 +801,16 @@
 
 
 def adam_body(*refs):
-    me, t0, t1, t2, t3, gb, ga = refs[:7]
-    state = refs[7:22]
-    outs = refs[22:-1]
+    me, t0, t1, t2, t3, grads = refs[:6]
+    state = refs[6:21]
+    outs = refs[21:-1]
     first = refs[-1]
     total = (t0[...] + t1[...]) + (t2[...] + t3[...])
     first[...] = total
     top = total[0:4]
     norm = jnp.sqrt(jnp.broadcast_to(jnp.sum(fsum(top * top), axis=1, keepdims=True), (1, 128)) + total[4:5])
     lane = lax.broadcasted_iota(jnp.int32, (1, 128), 1)
-    vec = gb[240:241, :]
+    vec = grads[240:241, :]
     for u in range(3):
         unit = 3 * (8 * me[0] + me[1]) + u
         line = first[pl.ds(jnp.minimum(unit >> 2, 4), 1), :]
@@ -872,23 +832,23 @@
         outs[3 * kind + 1][at] = second_new
         outs[3 * kind + 2][at] = update
 
-    for side, ref in ((0, ga), (1, gb)):
+    for side, base in ((0, 256), (1, 0)):
         for k in range(9):
-            g = ref[16 * k : 16 * k + 16, :]
+            g = grads[base + 16 * k : base + 16 * k + 16, :]
             put(0, (9 * side + k,), jnp.concatenate([g[:, :64], g[:, 64:]], axis=0))
-    put(1, (Ellipsis,), gb[208:240, :])
-    g = gb[144:192, :]
+    put(1, (Ellipsis,), grads[208:240, :])
+    g = grads[144:192, :]
     g = jnp.concatenate([jnp.concatenate([g[:, :64], g[:, 64:]], axis=0), jnp.zeros((96, 64), F32)], axis=1)
     g = jnp.concatenate([g, jnp.zeros((32, 128), F32)], axis=0).T
     put(2, (Ellipsis,), g[:64, :96])
-    g = gb[192:208, :]
+    g = grads[192:208, :]
     put(3, (Ellipsis,), jnp.concatenate([g[:, :64], g[:, 64:]], axis=0))
     put(4, (Ellipsis,), vec[:, :96])
     outs[15][0] = norm[0, 0]
 
 
-def adam(me, totals, gb, ga, state):
-    args = (*totals, gb, ga, *state)
+def adam(me, totals, grads, state):
+    args = (*totals, grads, *state)
     return pl.pallas_call(
         adam_body,
         in_specs=[pl.BlockSpec(memory_space=pltpu.SMEM)] + [pl.BlockSpec(a.shape) for a in args],
@@ -949,7 +909,7 @@
         unpack_a_body, "unpack_first", me, all_a, [sd((2304, 256), BF), sd((16, 256), F32)], [pltpu.VMEM((32, 128), F32)]
     )
     wat, line_b = lax.optimization_barrier((wat, line_b))
-    h0, pa1 = conv_one(counts, x, cf, vec, wat)
+    h0, a1 = conv_one(counts, x, cf, vec, wat)
     h0, plane_b = lax.optimization_barrier((h0, plane_b))
     all_b = [p for line in plane_b for p in (line, swap(line, 1))]
     wet, wbt, wqt, wot = unpack(
@@ -961,29 +921,16 @@
         [],
     )
     out, ga, dm, keep, send = middle(
-        counts, x, h0, cot, emb, vec, me, wet, wbt, wqt, wot, finish_b, [sd((4, 4, GB, 128), BF)] * 2
+        counts, x, h0, cot, a1, emb, vec, me, wet, wbt, wqt, wot, finish_all, [sd((4, 4, RG, 128), BF)] * 2
     )
-    parts_b = over_core(keep, send)
-    ga, parts_b = lax.optimization_barrier((ga, parts_b))
-    plane_b = to_plane(parts_b)
-    keep, send = conv_one_grad(counts, ga, pa1, me, finish_a, [sd((4, 4, GA, 128), BF)] * 2)
-    keep, send, plane_b = lax.optimization_barrier((keep, send, plane_b))
-    parts_a = over_core(keep, send)
-    own_b, others = plane_sum(parts_b[0], plane_b)
-    dm, parts_a, others = lax.optimization_barrier((dm, parts_a, others))
-    plane_a = to_plane(parts_a)
-    got_b = over_line(others)
-    half = n_img // NB // 2
-    rest = n_img // NB - half
-    ig, v0 = input_grad(counts, x, ga, dm, cf, vec, me, wat, 0, half, None)
-    ig, plane_a, got_b = lax.optimization_barrier((ig, plane_a, got_b))
-    own_a, others = plane_sum(parts_a[0], plane_a)
-    ig, others = lax.optimization_barrier((ig, others))
-    got_a = over_line(others)
-    ig, v1 = input_grad(counts, x, ga, dm, cf, vec, me, wat, half, rest, ig)
-    v1, got_a = lax.optimization_barrier((v1, got_a))
-    gb, ga, sums = shares((own_b, got_b), (own_a, got_a), (v0, v1))
-    results = adam(me, total_over(sums), gb, ga, state)
+    parts = over_core(keep, send)
+    ga, parts = lax.optimization_barrier((ga, parts))
+    plane = to_plane(parts)
+    ig, v = input_grad(counts, x, ga, dm, cf, vec, me, wat, 0, n_img // NB, None)
+    v, plane = lax.optimization_barrier((v, plane))
+    own, others = plane_sum(parts[0], plane)
+    grads, sums = shares(own, over_line(others), v)
+    results = adam(me, total_over(sums), grads, state)
     return (out.reshape(images.shape), ig.reshape(images.shape), *turned_back(results[:15]), results[15].reshape(()))
 
 
@@ -1031,13 +978,9 @@
     return out
 
 
-def finish_whole(outs, me, dwb, dwq, dwo, de, rows, turn):
-    for out, got in zip(outs, (dwb[...], dwq[...], dwo[...], de, rows)):
+def finish_whole(outs, me, dwa, dwb, dwq, dwo, de, rows, turn):
+    for out, got in zip(outs, (dwa[...], dwb[...], dwq[...], dwo[...], de, rows)):
         out[...] = got
-
-
-def finish_one(outs, me, got):
-    outs[0][...] = got[...]
 
 
 def per_device_any(images, timesteps, counts, cotangent, *state):
@@ -1054,12 +997,11 @@
     conv, (wet, wqt, wot), vec = gather_flat(masters, dp, fs)
     vec = jnp.pad(vec, ((0, 4), (0, 0)))
     cf = figures(counts, x)
-    h0, pa1 = conv_one(counts, x, cf, vec, conv[0])
-    ends = [sd(s, F32) for s in ((768, 768), (256, 768), (256, 256), (256, 512), (16, 256))]
-    out, ga, dm, dwb, dwq, dwo, de, rows = middle(
-        counts, x, h0, cot, emb, vec, me, wet, conv[1], wqt, wot, finish_whole, ends
+    h0, a1 = conv_one(counts, x, cf, vec, conv[0])
+    ends = [sd(s, F32) for s in ((768, 768), (768, 768), (256, 768), (256, 256), (256, 512), (16, 256))]
+    out, ga, dm, dwa, dwb, dwq, dwo, de, rows = middle(
+        counts, x, h0, cot, a1, emb, vec, me, wet, conv[1], wqt, wot, finish_whole, ends
     )
-    (dwa,) = conv_one_grad(counts, ga, pa1, me, finish_one, [sd((768, 768), F32)])
     ig, first = input_grad(counts, x, ga, dm, cf, vec, me, conv[0], 0, n_img // NB, None)
     first = jnp.pad(first[:4].reshape(2, 256), ((0, 14), (0, 0)))
     apart = lambda w: w.reshape(3, 256, 3, 256).transpose(0, 2, 1, 3).reshape(9, 256, 256)

time: 163 us -> 157 us (0.963)
  Pallas kernels: 91.1 us -> 71.5 us
  waiting for transfers between devices: 15.5 us -> 27.8 us
  starting transfers between devices: 43.9 us -> 45.8 us
    pallas_call x4 -> x3, Pallas kernels: 63.2 us -> 48.5 us  [image_call(): pl.pallas_call(body, grid_spec=pltpu.PrefetchScalarGridSpec(num_scalar_pr...]
    ppermute x41 -> x34, waiting for transfers between devices: 15.5 us -> 27.8 us  [swap(): return lax.ppermute(x, AXES, [(i, i ^ bits) for i in range(32)])]
    pallas_call x2 -> x1, Pallas kernels: 15.1 us -> 10.2 us  [input_grad(): pl.pallas_call(lambda *refs: input_grad_body(base, *refs), grid_spec=pltp...]
    ppermute x41 -> x34, starting transfers between devices: 43.9 us -> 45.8 us  [swap(): return lax.ppermute(x, AXES, [(i, i ^ bits) for i in range(32)])]
    unnamed x56 -> x50, local copies, waits for them, and re-layouts: 3.56 us -> 3.64 us
  transfers between devices with their start and end apart: 41 -> 34, of which waited for: 12 -> 16; matrix products, arithmetic and copies ran while one was open for 2% -> 1% of each run, Pallas kernels for 25% -> 16%
where the time goes in v2:
time: 157 us; the launch traced here: 156 us
  Pallas kernels  71.5 us (46%)
  starting transfers between devices  45.8 us (29%)
  waiting for transfers between devices  27.8 us (18%)
  other arithmetic  5.66 us (4%)
  local copies, waits for them, and re-layouts  3.64 us (2%)
  between operations  1.75 us (1%)
    pallas_call x3, Pallas kernels, image_call(): pl.pallas_call(body, grid_spec=pltpu.PrefetchScalarGridSpec(num_scalar_pr...  48.5 us
    ppermute x34, starting transfers between devices, swap(): return lax.ppermute(x, AXES, [(i, i ^ bits) for i in range(32)])  45.8 us
    ppermute x34, waiting for transfers between devices, swap(): return lax.ppermute(x, AXES, [(i, i ^ bits) for i in range(32)])  27.8 us
    pallas_call x1, Pallas kernels, input_grad(): pl.pallas_call(lambda *refs: input_grad_body(base, *refs), grid_spec=pltp...  10.2 us
    pallas_call x2, Pallas kernels, unpack(): pl.pallas_call(body, in_specs=[pl.BlockSpec(memory_space=pltpu.SMEM)] + [...  6.32 us
    unnamed x50, local copies, waits for them, and re-layouts  3.64 us
  transfers between devices with their start and end apart: 34, of which 16 were waited for; matrix products, arithmetic and copies ran while one was open for 1% of the time, Pallas kernels for 16%

profile of v2, /device:TPU:0, one launch (start us, length us, event | category | flops | bytes accessed | tf_op | source)
XLA Modules:
  0.0 156.1 jit_solution(3328460448879918117)
XLA Ops:
  0.7 1.8 %pack_shards.1 = (bf16[160,128]{1,0:T(8,128)(2,1)}, bf16[240,128]{1,0:T(8,128)(2,1)}) custom-call(f32[18,32,64]{2,1,0:T(8,128)} %bitcast.91, f32[32,128]{1,0:T(8,128)} %bitcast.97, f32[64,96]{1,0:T(8,128)} %bitcast.95, f32[32,64]{1,0:T(8,128)} %bitcast.99, f32[1,96]{1,0:T(1,128)} %refs_18_.1), custom_call_target="tpu_custom_call" | custom-call | tf_op jit(solution)/shard_map/pack_shards/pallas_call | solution.py:621
  2.5 5.0 %collective-permute-start.5 = (bf16[160,128]{1,0:T(8,128)(2,1)}, bf16[160,128]{1,0:T(8,128)(2,1)S(1)}, u32[]{:S(2)}, u32[]{:S(2)}) collective-permute-start(bf16[160,128]{1,0:T(8,128)(2,1)} %get-tuple-element.78), channel_id=1, source_target_pairs={{0,24},{1,25},{2,26},{3,27},{4,28},{5,29},{6,30},{7,31},{8,16},{9,... | collective-permute-start | bytes 122888 | tf_op jit(solution)/shard_map/ppermute | solution.py:627
  7.5 0.6 collective-permute-start.3
  8.1 3.8 %collective-permute-start.2 = (bf16[240,128]{1,0:T(8,128)(2,1)}, bf16[240,128]{1,0:T(8,128)(2,1)S(1)}, u32[]{:S(2)}, u32[]{:S(2)}) collective-permute-start(bf16[240,128]{1,0:T(8,128)(2,1)} %get-tuple-element.86), channel_id=1, source_target_pairs={{0,24},{1,25},{2,26},{3,27},{4,28},{5,29},{6,30},{7,31},{8,16},{9,... | collective-permute-start | bytes 184328 | tf_op jit(solution)/shard_map/ppermute | solution.py:627
  11.9 1.5 collective-permute-done.4
  13.4 0.8 pad_maximum_fusion.1.refs_0_
  14.3 2.5 %collective-permute-start.8 = (bf16[4,160,128]{2,1,0:T(8,128)(2,1)S(1)}, bf16[4,160,128]{2,1,0:T(8,128)(2,1)S(1)}, u32[]{:S(2)}, u32[]{:S(2)}) collective-permute-start(bf16[4,160,128]{2,1,0:T(8,128)(2,1)S(1)} %pad_maximum_fusion.1.refs_0_), channel_id=1, source_target_pairs={{0,6},{1,7},{2,4},{3,5},{4,2},{5,3},{6,0},{7,1},{8,14},{9,15},{10,... | collective-permute-start | bytes 491528 | tf_op jit(solution)/shard_map/ppermute | solution.py:627
  17.3 0.5 collective-permute-start.6
  17.8 1.2 collective-permute-start.1
  19.8 3.7 %figures.1.cf_ref.refs_4_ = f32[16,8,256]{2,1,0:T(8,128)} custom-call(s32[1]{0:T(128)S(6)} %copy.37.cnt_ref.refs_0_, bf16[16,256,256]{2,1,0:T(8,128)(2,1)} %bitcast.116), custom_call_target="tpu_custom_call" | custom-call | flops 536870912 | bytes 8388608 | tf_op jit(solution)/shard_map/figures/pallas_call | solution.py:186
  24.9 0.6 pad_add_fusion.me.refs_7_.refs_6_.refs_0_
  25.6 2.5 %collective-permute-start.15 = (bf16[4,240,128]{2,1,0:T(8,128)(2,1)S(1)}, bf16[4,240,128]{2,1,0:T(8,128)(2,1)S(1)}, u32[]{:S(2)}, u32[]{:S(2)}) collective-permute-start(bf16[4,240,128]{2,1,0:T(8,128)(2,1)S(1)} %pad_maximum_fusion.refs_0_), channel_id=1, source_target_pairs={{0,6},{1,7},{2,4},{3,5},{4,2},{5,3},{6,0},{7,1},{8,14},{9,15},{10,... | collective-permute-start | bytes 737288 | tf_op jit(solution)/shard_map/ppermute | solution.py:627
  28.7 0.5 collective-permute-start.13
  29.3 0.5 copy-done.14
  29.9 0.7 copy-done.15
  30.5 2.9 %unpack_first.1 = (bf16[2304,256]{1,0:T(8,128)(2,1)}, f32[16,256]{1,0:T(8,128)}) custom-call(s32[2]{0:T(128)} %pad_add_fusion.me.refs_7_.refs_6_.refs_0_, bf16[4,160,128]{2,1,0:T(8,128)(2,1)} %copy-done.1, bf16[4,160,128]{2,1,0:T(8,128)(2,1)} %copy-done.12, bf16[4,160,128]{2,1,0:T(8,128)(2,1)} %copy-done.11, bf16[4,160,128]{2,1,0:T(8,128)(2,1)} %copy-done.13, ...), custom_call_target="tpu_custom_call" | custom-call | tf_op jit(solution)/shard_map/unpack_first/pallas_call | solution.py:697
  33.5 7.8 %conv_one.1 = (f32[16,256,256]{2,1,0:T(8,128)}, bf16[16,256,256]{2,1,0:T(8,128)(2,1)}) custom-call(s32[1]{0:T(128)S(6)} %copy.37.cnt_ref.refs_0_, bf16[16,256,256]{2,1,0:T(8,128)(2,1)} %bitcast.117, f32[16,8,256]{2,1,0:T(8,128)} %figures.1.cf_ref.refs_4_, f32[16,256]{1,0:T(8,128)} %get-tuple-element.84.vec_ref.refs_6_.refs_5_, ...), custom_call_target="tpu_custom_call" | custom-call | flops 9663676416 | bytes 41943040 | tf_op jit(solution)/shard_map/conv_one/pallas_call | solution.py:186
  42.6 0.6 multiply_convert_fusion.refs_5_
  44.3 0.7 copy-done.8
  45.1 3.4 %unpack_second.1 = (bf16[256,512]{1,0:T(8,128)(2,1)}, bf16[2304,256]{1,0:T(8,128)(2,1)}, bf16[768,256]{1,0:T(8,128)(2,1)}, bf16[256,256]{1,0:T(8,128)(2,1)}) custom-call(s32[2]{0:T(128)} %pad_add_fusion.me.refs_7_.refs_6_.refs_0_, bf16[4,240,128]{2,1,0:T(8,128)(2,1)} %copy-done, bf16[4,240,128]{2,1,0:T(8,128)(2,1)} %copy-done.5, ...), custom_call_target="tpu_custom_call" | custom-call | tf_op jit(solution)/shard_map/unpack_second/pallas_call | solution.py:697
  48.4 37.0 %middle.1 = (f32[16,256,256]{2,1,0:T(8,128)}, bf16[16,256,256]{2,1,0:T(8,128)(2,1)}, f32[16,256,256]{2,1,0:T(8,128)}, bf16[4,4,400,128]{3,2,1,0:T(8,128)(2,1)}, bf16[4,4,400,128]{3,2,1,0:T(8,128)(2,1)}) custom-call(s32[1]{0:T(128)S(6)} %copy.37.cnt_ref.refs_0_, bf16[16,256,256]{2,1,0:T(8,128)(2,1)} %bitcast.118, f32[16,256,256]{2,1,0:T(8,128)} %get-tuple-element.92.refs_2_, ...), custom_call_target="tpu_custom_call" | custom-call | flops 57982058496 | bytes 184549376 | tf_op jit(solution)/shard_map/middle/pallas_call | solution.py:186
  85.6 3.6 %collective-permute-done.20 = bf16[4,4,400,128]{3,2,1,0:T(8,128)(2,1)S(1)} collective-permute-done((bf16[4,4,400,128]{3,2,1,0:T(8,128)(2,1)}, bf16[4,4,400,128]{3,2,1,0:T(8,128)(2,1)S(1)}, u32[]{:S(2)}, u32[]{:S(2)}) %collective-permute-start.20) | collective-permute-done | bytes 1638432 | tf_op jit(solution)/shard_map/ppermute | solution.py:627
  89.2 1.8 %fusion.3 = (bf16[4,400,128]{2,1,0:T(8,128)(2,1)S(1)}, bf16[4,400,128]{2,1,0:T(8,128)(2,1)S(1)}, bf16[4,400,128]{2,1,0:T(8,128)(2,1)S(1)}, bf16[4,400,128]{2,1,0:T(8,128)(2,1)S(1)}) fusion(bf16[4,4,400,128]{3,2,1,0:T(8,128)(2,1)S(1)} %collective-permute-done.20, bf16[4,4,400,128]{3,2,1,0:T(8,128)(2,1)} %get-tuple-element.104), kind=kLoop, calls=%fused_computation.7 | loop fusion | flops 3276800 | bytes 4915200 | tf_op jit(solution)/shard_map/convert_element_type | solution.py:765
  91.4 10.7 %collective-permute-start.22 = (bf16[4,400,128]{2,1,0:T(8,128)(2,1)S(1)}, bf16[4,400,128]{2,1,0:T(8,128)(2,1)S(1)}, u32[]{:S(2)}, u32[]{:S(2)}) collective-permute-start(bf16[4,400,128]{2,1,0:T(8,128)(2,1)S(1)} %get-tuple-element.112), channel_id=1, source_target_pairs={{0,4},{1,5},{2,6},{3,7},{4,0},{5,1},{6,2},{7,3},{8,12},{9,13},{10,... | collective-permute-start | bytes 1228808 | tf_op jit(solution)/shard_map/ppermute | solution.py:627
  102.1 1.4 collective-permute-start.23
  103.5 10.2 %input_grad.1 = (f32[16,256,256]{2,1,0:T(8,128)}, f32[8,128]{1,0:T(8,128)}) custom-call(s32[1]{0:T(128)S(6)} %copy.37.cnt_ref.refs_0_, bf16[16,256,256]{2,1,0:T(8,128)(2,1)} %bitcast.119, bf16[16,256,256]{2,1,0:T(8,128)(2,1)} %get-tuple-element.106.refs_2_, f32[16,256,256]{2,1,0:T(8,128)} %get-tuple-element.107.refs_3_, ...), custom_call_target="tpu_custom_call" | custom-call | flops 12884901888 | bytes 58720256 | tf_op jit(solution)/shard_map/input_grad/pallas_call | solution.py:569
  113.7 6.5 %collective-permute-done.22 = bf16[4,400,128]{2,1,0:T(8,128)(2,1)S(1)} collective-permute-done((bf16[4,400,128]{2,1,0:T(8,128)(2,1)S(1)}, bf16[4,400,128]{2,1,0:T(8,128)(2,1)S(1)}, u32[]{:S(2)}, u32[]{:S(2)}) %collective-permute-start.22) | collective-permute-done | bytes 409632 | tf_op jit(solution)/shard_map/ppermute | solution.py:627
  120.2 1.8 %collective-permute-done.23 = bf16[4,400,128]{2,1,0:T(8,128)(2,1)S(1)} collective-permute-done((bf16[4,400,128]{2,1,0:T(8,128)(2,1)S(1)}, bf16[4,400,128]{2,1,0:T(8,128)(2,1)S(1)}, u32[]{:S(2)}, u32[]{:S(2)}) %collective-permute-start.23) | collective-permute-done | bytes 409632 | tf_op jit(solution)/shard_map/ppermute | solution.py:627
  122.0 0.9 fusion.6
  122.9 4.6 %collective-permute-start.26 = (bf16[400,128]{1,0:T(8,128)(2,1)S(1)}, bf16[400,128]{1,0:T(8,128)(2,1)S(1)}, u32[]{:S(2)}, u32[]{:S(2)}) collective-permute-start(bf16[400,128]{1,0:T(8,128)(2,1)S(1)} %get-tuple-element.140), channel_id=1, source_target_pairs={{0,24},{1,25},{2,26},{3,27},{4,28},{5,29},{6,30},{7,31},{8,16},{9,... | collective-permute-start | bytes 307208 | tf_op jit(solution)/shard_map/ppermute | solution.py:627
  128.1 2.9 %collective-permute-done.26.r3 = bf16[400,128]{1,0:T(8,128)(2,1)S(1)} collective-permute-done((bf16[400,128]{1,0:T(8,128)(2,1)S(1)}, bf16[400,128]{1,0:T(8,128)(2,1)S(1)}, u32[]{:S(2)}, u32[]{:S(2)}) %collective-permute-start.26) | collective-permute-done | bytes 102432 | tf_op jit(solution)/shard_map/ppermute | solution.py:627
  131.0 5.3 %collective-permute-done.25.r2 = bf16[400,128]{1,0:T(8,128)(2,1)S(1)} collective-permute-done((bf16[400,128]{1,0:T(8,128)(2,1)S(1)}, bf16[400,128]{1,0:T(8,128)(2,1)S(1)}, u32[]{:S(2)}, u32[]{:S(2)}) %collective-permute-start.25) | collective-permute-done | bytes 102432 | tf_op jit(solution)/shard_map/ppermute | solution.py:627
  136.2 0.6 copy-done.17
  136.9 1.9 %shares.1 = (f32[400,128]{1,0:T(8,128)}, f32[8,128]{1,0:T(8,128)}) custom-call(f32[400,128]{1,0:T(8,128)} %get-tuple-element.143.own, bf16[400,128]{1,0:T(8,128)(2,1)} %copy-done.18, bf16[400,128]{1,0:T(8,128)(2,1)} %copy-done.17, bf16[400,128]{1,0:T(8,128)(2,1)} %copy-done.16, f32[8,128]{1,0:T(8,128)} %get-tuple-element.117.v), custom_call_target="tpu_custom_call" | custom-call | tf_op jit(solution)/shard_map/shares/pallas_call | solution.py:792
  138.8 1.4 collective-permute-done.27
  140.1 0.7 add.108
  140.8 1.4 collective-permute-start.30
  142.3 0.6 collective-permute-start.29
  142.9 1.4 collective-permute-start.28
  144.3 1.0 collective-permute-done.30
  145.3 0.5 collective-permute-done.29
  145.9 0.6 collective-permute-done.28
  146.5 1.5 collective-permute-start.33
  148.1 2.8 %collective-permute-start.31 = (f32[8,128]{1,0:T(8,128)S(1)}, f32[8,128]{1,0:T(8,128)S(1)}, u32[]{:S(2)}, u32[]{:S(2)}) collective-permute-start(f32[8,128]{1,0:T(8,128)S(1)} %add_add_fusion.refs_1_), channel_id=1, source_target_pairs={{0,8},{1,9},{2,10},{3,11},{4,12},{5,13},{6,14},{7,15},{8,0},{9,1},... | collective-permute-start | bytes 12296 | tf_op jit(solution)/shard_map/ppermute | solution.py:627
  150.9 1.0 collective-permute-done.33.refs_4_
  151.9 0.6 collective-permute-done.32.refs_3_
  152.6 0.6 copy-done.22
  153.2 2.8 %clipped_adamw.1 = (f32[18,32,64]{2,1,0:T(8,128)}, f32[18,32,64]{2,1,0:T(8,128)}, f32[18,32,64]{2,1,0:T(8,128)}, f32[32,128]{1,0:T(8,128)}, f32[32,128]{1,0:T(8,...) custom-call(s32[2]{0:T(128)} %pad_add_fusion.me.refs_7_.refs_6_.refs, ...), custom_call_target="tpu_custom_call" | custom-call | tf_op jit(solution)/shard_map/clipped_adamw/pallas_call | solution.py:852
  (90 shorter events, 6.2 us)
Async XLA Ops:
  2.5 9.4 %collective-permute-start.5 = (bf16[160,128]{1,0:T(8,128)(2,1)}, bf16[160,128]{1,0:T(8,128)(2,1)S(1)}, u32[]{:S(2)}, u32[]{:S(2)}) collective-permute-start(bf16[160,128]{1,0:T(8,128)(2,1)} %get-tuple-element.78), channel_id=1, source_target_pairs={{0,24},{1,25},{2,26},{3,27},{4,28},{5,29},{6,30},{7,31},{8,16},{9,... | collective-permute-start | bytes 122888 | tf_op jit(solution)/shard_map/ppermute | solution.py:627
  7.5 5.9 %collective-permute-start.4 = (bf16[160,128]{1,0:T(8,128)(2,1)}, bf16[160,128]{1,0:T(8,128)(2,1)S(1)}, u32[]{:S(2)}, u32[]{:S(2)}) collective-permute-start(bf16[160,128]{1,0:T(8,128)(2,1)} %get-tuple-element.78), channel_id=1, source_target_pairs={{0,16},{1,17},{2,18},{3,19},{4,20},{5,21},{6,22},{7,23},{8,24},{9,... | collective-permute-start | bytes 122888 | tf_op jit(solution)/shard_map/ppermute | solution.py:627
  7.5 5.9 %collective-permute-start.3 = (bf16[160,128]{1,0:T(8,128)(2,1)}, bf16[160,128]{1,0:T(8,128)(2,1)S(1)}, u32[]{:S(2)}, u32[]{:S(2)}) collective-permute-start(bf16[160,128]{1,0:T(8,128)(2,1)} %get-tuple-element.78), channel_id=1, source_target_pairs={{0,8},{1,9},{2,10},{3,11},{4,12},{5,13},{6,14},{7,15},{8,0},{9,1},... | collective-permute-start | bytes 122888 | tf_op jit(solution)/shard_map/ppermute | solution.py:627
  8.1 11.0 %collective-permute-start.2 = (bf16[240,128]{1,0:T(8,128)(2,1)}, bf16[240,128]{1,0:T(8,128)(2,1)S(1)}, u32[]{:S(2)}, u32[]{:S(2)}) collective-permute-start(bf16[240,128]{1,0:T(8,128)(2,1)} %get-tuple-element.86), channel_id=1, source_target_pairs={{0,24},{1,25},{2,26},{3,27},{4,28},{5,29},{6,30},{7,31},{8,16},{9,... | collective-permute-start | bytes 184328 | tf_op jit(solution)/shard_map/ppermute | solution.py:627
  13.4 12.2 %copy-start.24 = (s32[16]{0:T(128)S(1)}, s32[16]{0:T(128)}, u32[]{:S(2)}) copy-start(s32[16]{0:T(128)} %param.20) | copy-start | bytes 196
  13.4 12.2 %copy-start.19 = (bf16[240,128]{1,0:T(8,128)(2,1)S(1)}, bf16[240,128]{1,0:T(8,128)(2,1)}, u32[]{:S(2)}) copy-start(bf16[240,128]{1,0:T(8,128)(2,1)} %get-tuple-element.86) | copy-start | bytes 184324
  14.2 11.4 %copy-start.1 = (bf16[4,160,128]{2,1,0:T(8,128)(2,1)}, bf16[4,160,128]{2,1,0:T(8,128)(2,1)S(1)}, u32[]{:S(2)}) copy-start(bf16[4,160,128]{2,1,0:T(8,128)(2,1)S(1)} %pad_maximum_fusion.1.refs_0_) | copy-start | bytes 491524
  14.3 9.5 %collective-permute-start.8 = (bf16[4,160,128]{2,1,0:T(8,128)(2,1)S(1)}, bf16[4,160,128]{2,1,0:T(8,128)(2,1)S(1)}, u32[]{:S(2)}, u32[]{:S(2)}) collective-permute-start(bf16[4,160,128]{2,1,0:T(8,128)(2,1)S(1)} %pad_maximum_fusion.1.refs_0_), channel_id=1, source_target_pairs={{0,6},{1,7},{2,4},{3,5},{4,2},{5,3},{6,0},{7,1},{8,14},{9,15},{10,... | collective-permute-start | bytes 491528 | tf_op jit(solution)/shard_map/ppermute | solution.py:627
  16.8 7.0 %collective-permute-start.7 = (bf16[4,160,128]{2,1,0:T(8,128)(2,1)S(1)}, bf16[4,160,128]{2,1,0:T(8,128)(2,1)S(1)}, u32[]{:S(2)}, u32[]{:S(2)}) collective-permute-start(bf16[4,160,128]{2,1,0:T(8,128)(2,1)S(1)} %pad_maximum_fusion.1.refs_0_), channel_id=1, source_target_pairs={{0,4},{1,5},{2,6},{3,7},{4,0},{5,1},{6,2},{7,3},{8,12},{9,13},{10,... | collective-permute-start | bytes 491528 | tf_op jit(solution)/shard_map/ppermute | solution.py:627
  17.3 6.5 %collective-permute-start.6 = (bf16[4,160,128]{2,1,0:T(8,128)(2,1)S(1)}, bf16[4,160,128]{2,1,0:T(8,128)(2,1)S(1)}, u32[]{:S(2)}, u32[]{:S(2)}) collective-permute-start(bf16[4,160,128]{2,1,0:T(8,128)(2,1)S(1)} %pad_maximum_fusion.1.refs_0_), channel_id=1, source_target_pairs={{0,2},{1,3},{2,0},{3,1},{4,6},{5,7},{6,4},{7,5},{8,10},{9,11},{10,... | collective-permute-start | bytes 491528 | tf_op jit(solution)/shard_map/ppermute | solution.py:627
  17.8 5.7 %collective-permute-start.1 = (bf16[240,128]{1,0:T(8,128)(2,1)}, bf16[240,128]{1,0:T(8,128)(2,1)S(1)}, u32[]{:S(2)}, u32[]{:S(2)}) collective-permute-start(bf16[240,128]{1,0:T(8,128)(2,1)} %get-tuple-element.86), channel_id=1, source_target_pairs={{0,16},{1,17},{2,18},{3,19},{4,20},{5,21},{6,22},{7,23},{8,24},{9,... | collective-permute-start | bytes 184328 | tf_op jit(solution)/shard_map/ppermute | solution.py:627
  19.1 4.7 %collective-permute-start = (bf16[240,128]{1,0:T(8,128)(2,1)}, bf16[240,128]{1,0:T(8,128)(2,1)S(1)}, u32[]{:S(2)}, u32[]{:S(2)}) collective-permute-start(bf16[240,128]{1,0:T(8,128)(2,1)} %get-tuple-element.86), channel_id=1, source_target_pairs={{0,8},{1,9},{2,10},{3,11},{4,12},{5,13},{6,14},{7,15},{8,0},{9,1},... | collective-permute-start | bytes 184328 | tf_op jit(solution)/shard_map/ppermute | solution.py:627
  23.8 5.4 %copy-start.9 = (bf16[4,160,128]{2,1,0:T(8,128)(2,1)}, bf16[4,160,128]{2,1,0:T(8,128)(2,1)S(1)}, u32[]{:S(2)}) copy-start(bf16[4,160,128]{2,1,0:T(8,128)(2,1)S(1)} %collective-permute-done.8.refs_6_) | copy-start | bytes 491524
  23.8 5.4 %copy-start.10 = (bf16[4,160,128]{2,1,0:T(8,128)(2,1)}, bf16[4,160,128]{2,1,0:T(8,128)(2,1)S(1)}, u32[]{:S(2)}) copy-start(bf16[4,160,128]{2,1,0:T(8,128)(2,1)S(1)} %collective-permute-done.7.refs_4_) | copy-start | bytes 491524
  23.8 5.4 %copy-start.11 = (bf16[4,160,128]{2,1,0:T(8,128)(2,1)}, bf16[4,160,128]{2,1,0:T(8,128)(2,1)S(1)}, u32[]{:S(2)}) copy-start(bf16[4,160,128]{2,1,0:T(8,128)(2,1)S(1)} %collective-permute-done.6.refs_2_) | copy-start | bytes 491524
  23.8 4.3 %collective-permute-start.9 = (bf16[4,160,128]{2,1,0:T(8,128)(2,1)S(1)}, bf16[4,160,128]{2,1,0:T(8,128)(2,1)S(1)}, u32[]{:S(2)}, u32[]{:S(2)}) collective-permute-start(bf16[4,160,128]{2,1,0:T(8,128)(2,1)S(1)} %pad_maximum_fusion.1.refs_0_), channel_id=1, source_target_pairs={{0,1},{1,0},{2,3},{3,2},{4,5},{5,4},{6,7},{7,6},{8,9},{9,8},{10,11... | collective-permute-start | bytes 491528 | tf_op jit(solution)/shard_map/ppermute | solution.py:627
  23.9 4.7 %collective-permute-start.10 = (bf16[4,160,128]{2,1,0:T(8,128)(2,1)S(1)}, bf16[4,160,128]{2,1,0:T(8,128)(2,1)S(1)}, u32[]{:S(2)}, u32[]{:S(2)}) collective-permute-start(bf16[4,160,128]{2,1,0:T(8,128)(2,1)S(1)} %collective-permute-done.6.refs_2_), channel_id=1, source_target_pairs={{0,1},{1,0},{2,3},{3,2},{4,5},{5,4},{6,7},{7,6},{8,9},{9,8},{10,11... | collective-permute-start | bytes 491528 | tf_op jit(solution)/shard_map/ppermute | solution.py:627
  24.4 4.8 %collective-permute-start.11 = (bf16[4,160,128]{2,1,0:T(8,128)(2,1)S(1)}, bf16[4,160,128]{2,1,0:T(8,128)(2,1)S(1)}, u32[]{:S(2)}, u32[]{:S(2)}) collective-permute-start(bf16[4,160,128]{2,1,0:T(8,128)(2,1)S(1)} %collective-permute-done.7.refs_4_), channel_id=1, source_target_pairs={{0,1},{1,0},{2,3},{3,2},{4,5},{5,4},{6,7},{7,6},{8,9},{9,8},{10,11... | collective-permute-start | bytes 491528 | tf_op jit(solution)/shard_map/ppermute | solution.py:627
  24.5 4.7 %collective-permute-start.12 = (bf16[4,160,128]{2,1,0:T(8,128)(2,1)S(1)}, bf16[4,160,128]{2,1,0:T(8,128)(2,1)S(1)}, u32[]{:S(2)}, u32[]{:S(2)}) collective-permute-start(bf16[4,160,128]{2,1,0:T(8,128)(2,1)S(1)} %collective-permute-done.8.refs_6_), channel_id=1, source_target_pairs={{0,1},{1,0},{2,3},{3,2},{4,5},{5,4},{6,7},{7,6},{8,9},{9,8},{10,11... | collective-permute-start | bytes 491528 | tf_op jit(solution)/shard_map/ppermute | solution.py:627
  25.6 15.7 %copy-start = (bf16[4,240,128]{2,1,0:T(8,128)(2,1)}, bf16[4,240,128]{2,1,0:T(8,128)(2,1)S(1)}, u32[]{:S(2)}) copy-start(bf16[4,240,128]{2,1,0:T(8,128)(2,1)S(1)} %pad_maximum_fusion.refs_0_) | copy-start | bytes 737284
  25.6 15.6 %collective-permute-start.15 = (bf16[4,240,128]{2,1,0:T(8,128)(2,1)S(1)}, bf16[4,240,128]{2,1,0:T(8,128)(2,1)S(1)}, u32[]{:S(2)}, u32[]{:S(2)}) collective-permute-start(bf16[4,240,128]{2,1,0:T(8,128)(2,1)S(1)} %pad_maximum_fusion.refs_0_), channel_id=1, source_target_pairs={{0,6},{1,7},{2,4},{3,5},{4,2},{5,3},{6,0},{7,1},{8,14},{9,15},{10,... | collective-permute-start | bytes 737288 | tf_op jit(solution)/shard_map/ppermute | solution.py:627
  28.2 1.1 copy-start.12
  28.2 13.1 %collective-permute-start.14 = (bf16[4,240,128]{2,1,0:T(8,128)(2,1)S(1)}, bf16[4,240,128]{2,1,0:T(8,128)(2,1)S(1)}, u32[]{:S(2)}, u32[]{:S(2)}) collective-permute-start(bf16[4,240,128]{2,1,0:T(8,128)(2,1)S(1)} %pad_maximum_fusion.refs_0_), channel_id=1, source_target_pairs={{0,4},{1,5},{2,6},{3,7},{4,0},{5,1},{6,2},{7,3},{8,12},{9,13},{10,... | collective-permute-start | bytes 737288 | tf_op jit(solution)/shard_map/ppermute | solution.py:627
  28.7 12.6 %collective-permute-start.13 = (bf16[4,240,128]{2,1,0:T(8,128)(2,1)S(1)}, bf16[4,240,128]{2,1,0:T(8,128)(2,1)S(1)}, u32[]{:S(2)}, u32[]{:S(2)}) collective-permute-start(bf16[4,240,128]{2,1,0:T(8,128)(2,1)S(1)} %pad_maximum_fusion.refs_0_), channel_id=1, source_target_pairs={{0,2},{1,3},{2,0},{3,1},{4,6},{5,7},{6,4},{7,5},{8,10},{9,11},{10,... | collective-permute-start | bytes 737288 | tf_op jit(solution)/shard_map/ppermute | solution.py:627
  41.3 2.7 %copy-start.2 = (bf16[4,240,128]{2,1,0:T(8,128)(2,1)}, bf16[4,240,128]{2,1,0:T(8,128)(2,1)S(1)}, u32[]{:S(2)}) copy-start(bf16[4,240,128]{2,1,0:T(8,128)(2,1)S(1)} %collective-permute-done.15.refs_6_) | copy-start | bytes 737284
  41.3 2.7 %copy-start.3 = (bf16[4,240,128]{2,1,0:T(8,128)(2,1)}, bf16[4,240,128]{2,1,0:T(8,128)(2,1)S(1)}, u32[]{:S(2)}) copy-start(bf16[4,240,128]{2,1,0:T(8,128)(2,1)S(1)} %collective-permute-done.14.refs_4_) | copy-start | bytes 737284
  41.3 2.7 %copy-start.4 = (bf16[4,240,128]{2,1,0:T(8,128)(2,1)}, bf16[4,240,128]{2,1,0:T(8,128)(2,1)S(1)}, u32[]{:S(2)}) copy-start(bf16[4,240,128]{2,1,0:T(8,128)(2,1)S(1)} %collective-permute-done.13.refs_2_) | copy-start | bytes 737284
  41.3 1.9 %collective-permute-start.16 = (bf16[4,240,128]{2,1,0:T(8,128)(2,1)S(1)}, bf16[4,240,128]{2,1,0:T(8,128)(2,1)S(1)}, u32[]{:S(2)}, u32[]{:S(2)}) collective-permute-start(bf16[4,240,128]{2,1,0:T(8,128)(2,1)S(1)} %pad_maximum_fusion.refs_0_), channel_id=1, source_target_pairs={{0,1},{1,0},{2,3},{3,2},{4,5},{5,4},{6,7},{7,6},{8,9},{9,8},{10,11... | collective-permute-start | bytes 737288 | tf_op jit(solution)/shard_map/ppermute | solution.py:627
  41.4 1.9 %collective-permute-start.17 = (bf16[4,240,128]{2,1,0:T(8,128)(2,1)S(1)}, bf16[4,240,128]{2,1,0:T(8,128)(2,1)S(1)}, u32[]{:S(2)}, u32[]{:S(2)}) collective-permute-start(bf16[4,240,128]{2,1,0:T(8,128)(2,1)S(1)} %collective-permute-done.13.refs_2_), channel_id=1, source_target_pairs={{0,1},{1,0},{2,3},{3,2},{4,5},{5,4},{6,7},{7,6},{8,9},{9,8},{10,11... | collective-permute-start | bytes 737288 | tf_op jit(solution)/shard_map/ppermute | solution.py:627
  41.9 1.7 %collective-permute-start.18 = (bf16[4,240,128]{2,1,0:T(8,128)(2,1)S(1)}, bf16[4,240,128]{2,1,0:T(8,128)(2,1)S(1)}, u32[]{:S(2)}, u32[]{:S(2)}) collective-permute-start(bf16[4,240,128]{2,1,0:T(8,128)(2,1)S(1)} %collective-permute-done.14.refs_4_), channel_id=1, source_target_pairs={{0,1},{1,0},{2,3},{3,2},{4,5},{5,4},{6,7},{7,6},{8,9},{9,8},{10,11... | collective-permute-start | bytes 737288 | tf_op jit(solution)/shard_map/ppermute | solution.py:627
  42.0 2.0 %collective-permute-start.19 = (bf16[4,240,128]{2,1,0:T(8,128)(2,1)S(1)}, bf16[4,240,128]{2,1,0:T(8,128)(2,1)S(1)}, u32[]{:S(2)}, u32[]{:S(2)}) collective-permute-start(bf16[4,240,128]{2,1,0:T(8,128)(2,1)S(1)} %collective-permute-done.15.refs_6_), channel_id=1, source_target_pairs={{0,1},{1,0},{2,3},{3,2},{4,5},{5,4},{6,7},{7,6},{8,9},{9,8},{10,11... | collective-permute-start | bytes 737288 | tf_op jit(solution)/shard_map/ppermute | solution.py:627
  43.2 0.8 copy-start.5
  85.4 3.8 %collective-permute-start.20 = (bf16[4,4,400,128]{3,2,1,0:T(8,128)(2,1)}, bf16[4,4,400,128]{3,2,1,0:T(8,128)(2,1)S(1)}, u32[]{:S(2)}, u32[]{:S(2)}) collective-permute-start(bf16[4,4,400,128]{3,2,1,0:T(8,128)(2,1)} %get-tuple-element.105), channel_id=1, source_target_pairs={{0,1},{1,0},{2,3},{3,2},{4,5},{5,4},{6,7},{7,6},{8,9},{9,8},{10,11... | collective-permute-start | bytes 4915208 | tf_op jit(solution)/shard_map/ppermute | solution.py:627
  91.0 22.7 %collective-permute-start.21 = (bf16[4,400,128]{2,1,0:T(8,128)(2,1)S(1)}, bf16[4,400,128]{2,1,0:T(8,128)(2,1)S(1)}, u32[]{:S(2)}, u32[]{:S(2)}) collective-permute-start(bf16[4,400,128]{2,1,0:T(8,128)(2,1)S(1)} %get-tuple-element.111), channel_id=1, source_target_pairs={{0,2},{1,3},{2,0},{3,1},{4,6},{5,7},{6,4},{7,5},{8,10},{9,11},{10,... | collective-permute-start | bytes 1228808 | tf_op jit(solution)/shard_map/ppermute | solution.py:627
  91.4 28.7 %collective-permute-start.22 = (bf16[4,400,128]{2,1,0:T(8,128)(2,1)S(1)}, bf16[4,400,128]{2,1,0:T(8,128)(2,1)S(1)}, u32[]{:S(2)}, u32[]{:S(2)}) collective-permute-start(bf16[4,400,128]{2,1,0:T(8,128)(2,1)S(1)} %get-tuple-element.112), channel_id=1, source_target_pairs={{0,4},{1,5},{2,6},{3,7},{4,0},{5,1},{6,2},{7,3},{8,12},{9,13},{10,... | collective-permute-start | bytes 1228808 | tf_op jit(solution)/shard_map/ppermute | solution.py:627
  102.1 19.9 %collective-permute-start.23 = (bf16[4,400,128]{2,1,0:T(8,128)(2,1)S(1)}, bf16[4,400,128]{2,1,0:T(8,128)(2,1)S(1)}, u32[]{:S(2)}, u32[]{:S(2)}) collective-permute-start(bf16[4,400,128]{2,1,0:T(8,128)(2,1)S(1)} %get-tuple-element.113), channel_id=1, source_target_pairs={{0,6},{1,7},{2,4},{3,5},{4,2},{5,3},{6,0},{7,1},{8,14},{9,15},{10,... | collective-permute-start | bytes 1228808 | tf_op jit(solution)/shard_map/ppermute | solution.py:627
  122.9 8.1 %collective-permute-start.26 = (bf16[400,128]{1,0:T(8,128)(2,1)S(1)}, bf16[400,128]{1,0:T(8,128)(2,1)S(1)}, u32[]{:S(2)}, u32[]{:S(2)}) collective-permute-start(bf16[400,128]{1,0:T(8,128)(2,1)S(1)} %get-tuple-element.140), channel_id=1, source_target_pairs={{0,24},{1,25},{2,26},{3,27},{4,28},{5,29},{6,30},{7,31},{8,16},{9,... | collective-permute-start | bytes 307208 | tf_op jit(solution)/shard_map/ppermute | solution.py:627
  127.5 8.7 %collective-permute-start.25 = (bf16[400,128]{1,0:T(8,128)(2,1)S(1)}, bf16[400,128]{1,0:T(8,128)(2,1)S(1)}, u32[]{:S(2)}, u32[]{:S(2)}) collective-permute-start(bf16[400,128]{1,0:T(8,128)(2,1)S(1)} %get-tuple-element.141), channel_id=1, source_target_pairs={{0,16},{1,17},{2,18},{3,19},{4,20},{5,21},{6,22},{7,23},{8,24},{9,... | collective-permute-start | bytes 307208 | tf_op jit(solution)/shard_map/ppermute | solution.py:627
  127.6 8.7 %collective-permute-start.24 = (bf16[400,128]{1,0:T(8,128)(2,1)S(1)}, bf16[400,128]{1,0:T(8,128)(2,1)S(1)}, u32[]{:S(2)}, u32[]{:S(2)}) collective-permute-start(bf16[400,128]{1,0:T(8,128)(2,1)S(1)} %get-tuple-element.142), channel_id=1, source_target_pairs={{0,8},{1,9},{2,10},{3,11},{4,12},{5,13},{6,14},{7,15},{8,0},{9,1},... | collective-permute-start | bytes 307208 | tf_op jit(solution)/shard_map/ppermute | solution.py:627
  131.0 5.3 %copy-start.16 = (bf16[400,128]{1,0:T(8,128)(2,1)}, bf16[400,128]{1,0:T(8,128)(2,1)S(1)}, u32[]{:S(2)}) copy-start(bf16[400,128]{1,0:T(8,128)(2,1)S(1)} %collective-permute-done.26.r3) | copy-start | bytes 307204
  138.8 1.4 collective-permute-start.27
  140.8 4.5 %collective-permute-start.30 = (f32[8,128]{1,0:T(8,128)S(1)}, f32[8,128]{1,0:T(8,128)S(1)}, u32[]{:S(2)}, u32[]{:S(2)}) collective-permute-start(f32[8,128]{1,0:T(8,128)S(1)} %add.108), channel_id=1, source_target_pairs={{0,6},{1,7},{2,4},{3,5},{4,2},{5,3},{6,0},{7,1},{8,14},{9,15},{10,... | collective-permute-start | bytes 12296 | tf_op jit(solution)/shard_map/ppermute | solution.py:627
  142.3 3.6 %collective-permute-start.29 = (f32[8,128]{1,0:T(8,128)S(1)}, f32[8,128]{1,0:T(8,128)S(1)}, u32[]{:S(2)}, u32[]{:S(2)}) collective-permute-start(f32[8,128]{1,0:T(8,128)S(1)} %add.108), channel_id=1, source_target_pairs={{0,4},{1,5},{2,6},{3,7},{4,0},{5,1},{6,2},{7,3},{8,12},{9,13},{10,... | collective-permute-start | bytes 12296 | tf_op jit(solution)/shard_map/ppermute | solution.py:627
  142.9 3.6 %collective-permute-start.28 = (f32[8,128]{1,0:T(8,128)S(1)}, f32[8,128]{1,0:T(8,128)S(1)}, u32[]{:S(2)}, u32[]{:S(2)}) collective-permute-start(f32[8,128]{1,0:T(8,128)S(1)} %add.108), channel_id=1, source_target_pairs={{0,2},{1,3},{2,0},{3,1},{4,6},{5,7},{6,4},{7,5},{8,10},{9,11},{10,... | collective-permute-start | bytes 12296 | tf_op jit(solution)/shard_map/ppermute | solution.py:627
  146.5 6.1 %copy-start.20 = (f32[8,128]{1,0:T(8,128)}, f32[8,128]{1,0:T(8,128)S(1)}, u32[]{:S(2)}) copy-start(f32[8,128]{1,0:T(8,128)S(1)} %add_add_fusion.refs_1_) | copy-start | bytes 12292
  146.5 5.4 %collective-permute-start.33 = (f32[8,128]{1,0:T(8,128)S(1)}, f32[8,128]{1,0:T(8,128)S(1)}, u32[]{:S(2)}, u32[]{:S(2)}) collective-permute-start(f32[8,128]{1,0:T(8,128)S(1)} %add_add_fusion.refs_1_), channel_id=1, source_target_pairs={{0,24},{1,25},{2,26},{3,27},{4,28},{5,29},{6,30},{7,31},{8,16},{9,... | collective-permute-start | bytes 12296 | tf_op jit(solution)/shard_map/ppermute | solution.py:627
  148.1 4.5 %collective-permute-start.32 = (f32[8,128]{1,0:T(8,128)S(1)}, f32[8,128]{1,0:T(8,128)S(1)}, u32[]{:S(2)}, u32[]{:S(2)}) collective-permute-start(f32[8,128]{1,0:T(8,128)S(1)} %add_add_fusion.refs_1_), channel_id=1, source_target_pairs={{0,16},{1,17},{2,18},{3,19},{4,20},{5,21},{6,22},{7,23},{8,24},{9,... | collective-permute-start | bytes 12296 | tf_op jit(solution)/shard_map/ppermute | solution.py:627
  148.1 4.5 %collective-permute-start.31 = (f32[8,128]{1,0:T(8,128)S(1)}, f32[8,128]{1,0:T(8,128)S(1)}, u32[]{:S(2)}, u32[]{:S(2)}) collective-permute-start(f32[8,128]{1,0:T(8,128)S(1)} %add_add_fusion.refs_1_), channel_id=1, source_target_pairs={{0,8},{1,9},{2,10},{3,11},{4,12},{5,13},{6,14},{7,15},{8,0},{9,1},... | collective-permute-start | bytes 12296 | tf_op jit(solution)/shard_map/ppermute | solution.py:627
  (11 other events, 7.3 us)

commit v3 on v2

--- a/solution.py
+++ b/solution.py
@@ -218,10 +218,15 @@
     )
 
 
-def conv_one_body(cnt_ref, x_ref, cf_ref, vec_ref, wat_ref, h0_ref, a1_ref, pa):
+def conv_one_body(fill, *refs):
+    cnt_ref, x_ref, cf_ref, me_ref = refs[:4]
+    given = refs[4:-6]
+    h0_ref, a1_ref, wat_ref, vec_ref, pa, vrows = refs[-6:]
+
     @pl.when(pl.program_id(0) == 0)
     def _():
         zero_pads(pa)
+        fill(me_ref, *given, wat_ref, vec_ref, vrows)
 
     @pl.when(pl.program_id(0) * NB < cnt_ref[0])
     def _():
@@ -239,26 +244,30 @@
         interleave([part(N) for N in parts()])
 
 
-def conv_one(cnt, x, cf, vec, wat):
+def conv_one(cnt, x, cf, me, given, fill):
     n = x.shape[0]
     return image_call(
-        conv_one_body,
+        lambda *refs: conv_one_body(fill, *refs),
         "conv_one",
         n,
         (18, 10),
-        [blocks(256, 256), blocks(8, 256), whole((16, 256)), whole((2304, 256))],
-        [out_blocks(256, 256), out_blocks(256, 256)],
-        [sd((n, 256, 256), F32), sd((n, 256, 256), BF)],
-        [pltpu.VMEM((NB, 288, 768), BF)],
-        (cnt, x, cf, vec, wat),
+        [blocks(256, 256), blocks(8, 256), pl.BlockSpec(memory_space=pltpu.SMEM)] + [whole(g.shape) for g in given],
+        [out_blocks(256, 256), out_blocks(256, 256), whole((2304, 256)), whole((16, 256))],
+        [sd((n, 256, 256), F32), sd((n, 256, 256), BF), sd((2304, 256), BF), sd((16, 256), F32)],
+        [pltpu.VMEM((NB, 288, 768), BF), pltpu.VMEM((32, 128), F32)],
+        (cnt, x, cf, me, *given),
     )
 
 
-def middle_body(finish, n_out, *refs):
-    (cnt_ref, x_ref, h0_ref, cot_ref, a1_ref, emb_ref, vec_ref, me_ref, wet_ref, wbt_ref, wqt_ref, wot_ref) = refs[:12]
-    out_ref, ga_ref, dm_ref = refs[12:15]
-    ends = refs[15 : 15 + n_out]
-    (pa, pg, pa1, gt, gt1, mid, a3, mx, dmx, dz, she, dsr, dwa, dwb, dwq, dwo, dvec, turn) = refs[15 + n_out :]
+def middle_body(fill, n_given, finish, n_out, *refs):
+    (cnt_ref, x_ref, h0_ref, cot_ref, a1_ref, emb_ref, vec_ref, me_ref) = refs[:8]
+    given = refs[8 : 8 + n_given]
+    refs = refs[8 + n_given :]
+    out_ref, ga_ref, dm_ref = refs[:3]
+    ends = refs[3 : 3 + n_out]
+    refs = refs[3 + n_out :]
+    (pa, pg, pa1, gt, gt1, mid, a3, mx, dmx, dz, she, dsr, dwa, dwb, dwq, dwo, dvec, turn) = refs[:18]
+    wet_ref, wbt_ref, wqt_ref, wot_ref = refs[18:]
     i = pl.program_id(0)
     cnt = cnt_ref[0]
 
@@ -269,6 +278,7 @@
         zero_pads(pa1)
         for ref in (dwa, dwb, dwq, dwo, dvec, dsr):
             ref[...] = jnp.zeros_like(ref)
+        fill(me_ref, *given, wet_ref, wbt_ref, wqt_ref, wot_ref)
         she[...] = dot_nt(emb_ref[...], wet_ref[...]) + (row(vec_ref, 2) + row(vec_ref, 3))
 
     live = i * NB < cnt
@@ -446,17 +456,17 @@
         finish(ends, me_ref, dwa, dwb, dwq, dwo, dot_tn(ds.astype(BF), emb_ref[...]), rows, turn)
 
 
-def middle(cnt, x, h0, cot, a1, emb, vec, me, wet, wbt, wqt, wot, finish, ends):
+def middle(cnt, x, h0, cot, a1, emb, vec, me, given, fill, finish, ends):
     n = x.shape[0]
     V = pltpu.VMEM
     return image_call(
-        lambda *refs: middle_body(finish, len(ends), *refs),
+        lambda *refs: middle_body(fill, len(given), finish, len(ends), *refs),
         "middle",
         n,
         (108, 44),
         [blocks(256, 256)] * 4
         + [whole(emb.shape), whole((16, 256)), pl.BlockSpec(memory_space=pltpu.SMEM)]
-        + [whole(w.shape) for w in (wet, wbt, wqt, wot)],
+        + [whole(w.shape) for w in given],
         [out_blocks(256, 256)] * 3 + [whole(e.shape) for e in ends],
         [sd((n, 256, 256), F32), sd((n, 256, 256), BF), sd((n, 256, 256), F32)] + list(ends),
         [
@@ -478,8 +488,12 @@
             V((256, 256), F32),
             V((16, 256), F32),
             V((1280, 512), F32),
+            V((256, 512), BF),
+            V((2304, 256), BF),
+            V((768, 256), BF),
+            V((256, 256), BF),
         ],
-        (cnt, x, h0, cot, a1, emb, vec, me, wet, wbt, wqt, wot),
+        (cnt, x, h0, cot, a1, emb, vec, me, *given),
     )
 
 
@@ -633,7 +647,7 @@
     return halves(s0, s1)
 
 
-def unpack_a_body(me, *refs):
+def unpack_a(me, *refs):
     gs = refs[:8]
     wat_ref, vec_ref, vrows = refs[8:]
     z = me[0]
@@ -665,7 +679,7 @@
         vec_ref[:, 128 * half : 128 * half + 128] = acc
 
 
-def unpack_b_body(me, *refs):
+def unpack_b(me, *refs):
     gs = refs[:8]
     wet_ref, wbt_ref, wqt_ref, wot_ref = refs[8:]
     z = me[0]
@@ -693,17 +707,6 @@
             wot_ref[pl.ds(at + 16, 16), lanes] = j1
 
 
-def unpack(body, name, me, gs, outs, scratch):
-    return pl.pallas_call(
-        body,
-        in_specs=[pl.BlockSpec(memory_space=pltpu.SMEM)] + [pl.BlockSpec(g.shape) for g in gs],
-        out_shape=outs,
-        scratch_shapes=scratch,
-        compiler_params=VMEM,
-        name=name,
-    )(me, *gs)
-
-
 def place(outs, me, src, base, lanes, lo, rows, step):
     z = me[0]
     f = me[1]
@@ -905,23 +908,12 @@
     all_a = [p for line in plane_a for p in (line, swap(line, 1))]
     line_b = jnp.stack(rows_b)
     plane_b = [line_b] + [swap(line_b, bits) for bits in (2, 4, 6)]
-    wat, vec = unpack(
-        unpack_a_body, "unpack_first", me, all_a, [sd((2304, 256), BF), sd((16, 256), F32)], [pltpu.VMEM((32, 128), F32)]
-    )
-    wat, line_b = lax.optimization_barrier((wat, line_b))
-    h0, a1 = conv_one(counts, x, cf, vec, wat)
+    all_a, line_b = lax.optimization_barrier((all_a, line_b))
+    h0, a1, wat, vec = conv_one(counts, x, cf, me, all_a, unpack_a)
     h0, plane_b = lax.optimization_barrier((h0, plane_b))
     all_b = [p for line in plane_b for p in (line, swap(line, 1))]
-    wet, wbt, wqt, wot = unpack(
-        unpack_b_body,
-        "unpack_second",
-        me,
-        all_b,
-        [sd((256, 512), BF), sd((2304, 256), BF), sd((768, 256), BF), sd((256, 256), BF)],
-        [],
-    )
     out, ga, dm, keep, send = middle(
-        counts, x, h0, cot, a1, emb, vec, me, wet, wbt, wqt, wot, finish_all, [sd((4, 4, RG, 128), BF)] * 2
+        counts, x, h0, cot, a1, emb, vec, me, all_b, unpack_b, finish_all, [sd((4, 4, RG, 128), BF)] * 2
     )
     parts = over_core(keep, send)
     ga, parts = lax.optimization_barrier((ga, parts))
@@ -983,6 +975,16 @@
         out[...] = got
 
 
+def fill_one(me, wat, vec, wat_ref, vec_ref, vrows):
+    wat_ref[...] = wat[...]
+    vec_ref[...] = vec[...]
+
+
+def fill_rest(me, *refs):
+    for k in range(4):
+        refs[4 + k][...] = refs[k][...]
+
+
 def per_device_any(images, timesteps, counts, cotangent, *state):
     masters = state[0::3]
     moments = state[1::3]
@@ -997,10 +999,10 @@
     conv, (wet, wqt, wot), vec = gather_flat(masters, dp, fs)
     vec = jnp.pad(vec, ((0, 4), (0, 0)))
     cf = figures(counts, x)
-    h0, a1 = conv_one(counts, x, cf, vec, conv[0])
+    h0, a1, wat, vec = conv_one(counts, x, cf, me, (conv[0], vec), fill_one)
     ends = [sd(s, F32) for s in ((768, 768), (768, 768), (256, 768), (256, 256), (256, 512), (16, 256))]
     out, ga, dm, dwa, dwb, dwq, dwo, de, rows = middle(
-        counts, x, h0, cot, a1, emb, vec, me, wet, conv[1], wqt, wot, finish_whole, ends
+        counts, x, h0, cot, a1, emb, vec, me, (wet, conv[1], wqt, wot), fill_rest, finish_whole, ends
     )
     ig, first = input_grad(counts, x, ga, dm, cf, vec, me, conv[0], 0, n_img // NB, None)
     first = jnp.pad(first[:4].reshape(2, 256), ((0, 14), (0, 0)))

time: 157 us -> 151 us (0.962)
  starting transfers between devices: 45.8 us -> 35.9 us
  Pallas kernels: 71.5 us -> 79.8 us
  waiting for transfers between devices: 27.8 us -> 24.6 us
    pallas_call x3, Pallas kernels: 48.5 us -> 61.3 us  [image_call(): pl.pallas_call(body, grid_spec=pltpu.PrefetchScalarGridSpec(num_scalar_pr...]
    ppermute x34, starting transfers between devices: 45.8 us -> 35.9 us  [swap(): return lax.ppermute(x, AXES, [(i, i ^ bits) for i in range(32)])]
    pallas_call x2 -> x0, Pallas kernels: 6.32 us -> none  [unpack(): pl.pallas_call(body, in_specs=[pl.BlockSpec(memory_space=pltpu.SMEM)] + [...]
    ppermute x34, waiting for transfers between devices: 27.8 us -> 24.6 us  [swap(): return lax.ppermute(x, AXES, [(i, i ^ bits) for i in range(32)])]
    pallas_call x1, Pallas kernels: 10.2 us -> 12.1 us  [input_grad(): pl.pallas_call(lambda *refs: input_grad_body(base, *refs), grid_spec=pltp...]
  transfers between devices with their start and end apart: 34 -> 34, of which waited for: 16 -> 15; matrix products, arithmetic and copies ran while one was open for 1% -> 2% of each run, Pallas kernels for 16% -> 17%
where the time goes in v3:
time: 151 us
  Pallas kernels  79.8 us (53%)
  starting transfers between devices  35.9 us (24%)
  waiting for transfers between devices  24.6 us (16%)
  other arithmetic  5.69 us (4%)
  local copies, waits for them, and re-layouts  3.26 us (2%)
  between operations  1.79 us (1%)
    pallas_call x3, Pallas kernels, image_call(): pl.pallas_call(body, grid_spec=pltpu.PrefetchScalarGridSpec(num_scalar_pr...  61.3 us
    ppermute x34, starting transfers between devices, swap(): return lax.ppermute(x, AXES, [(i, i ^ bits) for i in range(32)])  35.9 us
    ppermute x34, waiting for transfers between devices, swap(): return lax.ppermute(x, AXES, [(i, i ^ bits) for i in range(32)])  24.6 us
    pallas_call x1, Pallas kernels, input_grad(): pl.pallas_call(lambda *refs: input_grad_body(base, *refs), grid_spec=pltp...  12.1 us
    unnamed x50, local copies, waits for them, and re-layouts  3.26 us
  transfers between devices with their start and end apart: 34, of which 15 were waited for; matrix products, arithmetic and copies ran while one was open for 2% of the time, Pallas kernels for 17%

profile of v3, /device:TPU:0, one launch (start us, length us, event | category | flops | bytes accessed | tf_op | source)
XLA Modules:
  0.0 151.0 jit_solution(10860719294993357412)
XLA Ops:
  0.7 1.8 %pack_shards.1 = (bf16[160,128]{1,0:T(8,128)(2,1)}, bf16[240,128]{1,0:T(8,128)(2,1)}) custom-call(f32[18,32,64]{2,1,0:T(8,128)} %bitcast.91, f32[32,128]{1,0:T(8,128)} %bitcast.97, f32[64,96]{1,0:T(8,128)} %bitcast.95, f32[32,64]{1,0:T(8,128)} %bitcast.99, f32[1,96]{1,0:T(1,128)} %refs_18_.1), custom_call_target="tpu_custom_call" | custom-call | tf_op jit(solution)/shard_map/pack_shards/pallas_call | solution.py:635
  2.5 5.0 %collective-permute-start.5 = (bf16[160,128]{1,0:T(8,128)(2,1)}, bf16[160,128]{1,0:T(8,128)(2,1)S(1)}, u32[]{:S(2)}, u32[]{:S(2)}) collective-permute-start(bf16[160,128]{1,0:T(8,128)(2,1)} %get-tuple-element.81), channel_id=1, source_target_pairs={{0,24},{1,25},{2,26},{3,27},{4,28},{5,29},{6,30},{7,31},{8,16},{9,... | collective-permute-start | bytes 122888 | tf_op jit(solution)/shard_map/ppermute | solution.py:641
  7.5 0.6 collective-permute-start.3
  8.1 3.8 %collective-permute-start.2 = (bf16[240,128]{1,0:T(8,128)(2,1)}, bf16[240,128]{1,0:T(8,128)(2,1)S(1)}, u32[]{:S(2)}, u32[]{:S(2)}) collective-permute-start(bf16[240,128]{1,0:T(8,128)(2,1)} %get-tuple-element.87), channel_id=1, source_target_pairs={{0,24},{1,25},{2,26},{3,27},{4,28},{5,29},{6,30},{7,31},{8,16},{9,... | collective-permute-start | bytes 184328 | tf_op jit(solution)/shard_map/ppermute | solution.py:641
  11.9 1.5 collective-permute-done.4
  13.4 0.8 pad_maximum_fusion.1.refs_4_
  14.3 2.5 %collective-permute-start.8 = (bf16[4,160,128]{2,1,0:T(8,128)(2,1)S(1)}, bf16[4,160,128]{2,1,0:T(8,128)(2,1)S(1)}, u32[]{:S(2)}, u32[]{:S(2)}) collective-permute-start(bf16[4,160,128]{2,1,0:T(8,128)(2,1)S(1)} %pad_maximum_fusion.1.refs_4_), channel_id=1, source_target_pairs={{0,6},{1,7},{2,4},{3,5},{4,2},{5,3},{6,0},{7,1},{8,14},{9,15},{10,... | collective-permute-start | bytes 491528 | tf_op jit(solution)/shard_map/ppermute | solution.py:641
  16.8 0.5 collective-permute-start.7
  17.3 0.5 collective-permute-start.6
  17.8 1.2 collective-permute-start.1
  19.8 4.4 %figures.1.refs_2_.refs_4_ = f32[16,8,256]{2,1,0:T(8,128)} custom-call(s32[1]{0:T(128)S(6)} %copy.37.cnt_ref.refs_0_, bf16[16,256,256]{2,1,0:T(8,128)(2,1)} %bitcast.116), custom_call_target="tpu_custom_call" | custom-call | flops 536870912 | bytes 8388608 | tf_op jit(solution)/shard_map/figures/pallas_call | solution.py:186
  24.3 0.5 collective-permute-start.10
  25.3 0.7 pad_add_fusion.refs_3_.refs_7_.refs_6_.refs_0_
  26.0 2.1 %collective-permute-start.15 = (bf16[4,240,128]{2,1,0:T(8,128)(2,1)S(1)}, bf16[4,240,128]{2,1,0:T(8,128)(2,1)S(1)}, u32[]{:S(2)}, u32[]{:S(2)}) collective-permute-start(bf16[4,240,128]{2,1,0:T(8,128)(2,1)S(1)} %pad_maximum_fusion.refs_8_), channel_id=1, source_target_pairs={{0,6},{1,7},{2,4},{3,5},{4,2},{5,3},{6,0},{7,1},{8,14},{9,15},{10,... | collective-permute-start | bytes 737288 | tf_op jit(solution)/shard_map/ppermute | solution.py:641
  28.2 0.5 collective-permute-start.14
  28.7 0.9 collective-permute-start.13
  29.7 0.6 copy-done.22
  30.3 0.7 copy-done.23
  30.9 9.8 %conv_one.1 = (f32[16,256,256]{2,1,0:T(8,128)}, bf16[16,256,256]{2,1,0:T(8,128)(2,1)}, bf16[2304,256]{1,0:T(8,128)(2,1)}, f32[16,256]{1,0:T(8,128)}) custom-call(s32[1]{0:T(128)S(6)} %copy.37.cnt_ref.refs_0_, bf16[16,256,256]{2,1,0:T(8,128)(2,1)} %bitcast.117, f32[16,8,256]{2,1,0:T(8,128)} %figures.1.refs_2_.refs_4_, ...), custom_call_target="tpu_custom_call" | custom-call | flops 9663676416 | bytes 41943040 | tf_op jit(solution)/shard_map/conv_one/pallas_call | solution.py:186
  40.9 0.5 collective-permute-start.17
  42.1 0.6 multiply_convert_fusion.refs_5_
  44.2 47.1 %middle.1 = (f32[16,256,256]{2,1,0:T(8,128)}, bf16[16,256,256]{2,1,0:T(8,128)(2,1)}, f32[16,256,256]{2,1,0:T(8,128)}, bf16[4,4,400,128]{3,2,1,0:T(8,128)(2,1)}, bf16[4,4,400,128]{3,2,1,0:T(8,128)(2,1)}) custom-call(s32[1]{0:T(128)S(6)} %copy.37.cnt_ref.refs_0_, bf16[16,256,256]{2,1,0:T(8,128)(2,1)} %bitcast.118, f32[16,256,256]{2,1,0:T(8,128)} %get-tuple-element.100.refs_2_, ...), custom_call_target="tpu_custom_call" | custom-call | flops 57982058496 | bytes 184549376 | tf_op jit(solution)/shard_map/middle/pallas_call | solution.py:186
  91.4 3.7 %collective-permute-done.20 = bf16[4,4,400,128]{3,2,1,0:T(8,128)(2,1)S(1)} collective-permute-done((bf16[4,4,400,128]{3,2,1,0:T(8,128)(2,1)}, bf16[4,4,400,128]{3,2,1,0:T(8,128)(2,1)S(1)}, u32[]{:S(2)}, u32[]{:S(2)}) %collective-permute-start.20) | collective-permute-done | bytes 1638432 | tf_op jit(solution)/shard_map/ppermute | solution.py:641
  95.1 1.8 %fusion.3 = (bf16[4,400,128]{2,1,0:T(8,128)(2,1)S(1)}, bf16[4,400,128]{2,1,0:T(8,128)(2,1)S(1)}, bf16[4,400,128]{2,1,0:T(8,128)(2,1)S(1)}, bf16[4,400,128]{2,1,0:T(8,128)(2,1)S(1)}) fusion(bf16[4,4,400,128]{3,2,1,0:T(8,128)(2,1)S(1)} %collective-permute-done.20, bf16[4,4,400,128]{3,2,1,0:T(8,128)(2,1)} %get-tuple-element.109), kind=kLoop, calls=%fused_computation.7 | loop fusion | flops 3276800 | bytes 4915200 | tf_op jit(solution)/shard_map/convert_element_type | solution.py:768
  97.3 1.3 collective-permute-start.22
  98.5 1.9 %collective-permute-start.23 = (bf16[4,400,128]{2,1,0:T(8,128)(2,1)S(1)}, bf16[4,400,128]{2,1,0:T(8,128)(2,1)S(1)}, u32[]{:S(2)}, u32[]{:S(2)}) collective-permute-start(bf16[4,400,128]{2,1,0:T(8,128)(2,1)S(1)} %get-tuple-element.119), channel_id=1, source_target_pairs={{0,6},{1,7},{2,4},{3,5},{4,2},{5,3},{6,0},{7,1},{8,14},{9,15},{10,... | collective-permute-start | bytes 1228808 | tf_op jit(solution)/shard_map/ppermute | solution.py:641
  100.4 12.1 %input_grad.1 = (f32[16,256,256]{2,1,0:T(8,128)}, f32[8,128]{1,0:T(8,128)}) custom-call(s32[1]{0:T(128)S(6)} %copy.37.cnt_ref.refs_0_, bf16[16,256,256]{2,1,0:T(8,128)(2,1)} %bitcast.119, bf16[16,256,256]{2,1,0:T(8,128)(2,1)} %get-tuple-element.111.refs_2_, f32[16,256,256]{2,1,0:T(8,128)} %get-tuple-element.112.refs_3_, ...), custom_call_target="tpu_custom_call" | custom-call | flops 12884901888 | bytes 58720256 | tf_op jit(solution)/shard_map/input_grad/pallas_call | solution.py:583
  112.6 5.7 %collective-permute-done.23 = bf16[4,400,128]{2,1,0:T(8,128)(2,1)S(1)} collective-permute-done((bf16[4,400,128]{2,1,0:T(8,128)(2,1)S(1)}, bf16[4,400,128]{2,1,0:T(8,128)(2,1)S(1)}, u32[]{:S(2)}, u32[]{:S(2)}) %collective-permute-start.23) | collective-permute-done | bytes 409632 | tf_op jit(solution)/shard_map/ppermute | solution.py:641
  118.2 0.9 fusion.6
  119.1 2.1 %collective-permute-start.26 = (bf16[400,128]{1,0:T(8,128)(2,1)S(1)}, bf16[400,128]{1,0:T(8,128)(2,1)S(1)}, u32[]{:S(2)}, u32[]{:S(2)}) collective-permute-start(bf16[400,128]{1,0:T(8,128)(2,1)S(1)} %get-tuple-element.146), channel_id=1, source_target_pairs={{0,24},{1,25},{2,26},{3,27},{4,28},{5,29},{6,30},{7,31},{8,16},{9,... | collective-permute-start | bytes 307208 | tf_op jit(solution)/shard_map/ppermute | solution.py:641
  121.2 1.3 collective-permute-start.25
  122.5 1.0 collective-permute-start.24
  123.5 3.2 %collective-permute-done.26.r3 = bf16[400,128]{1,0:T(8,128)(2,1)S(1)} collective-permute-done((bf16[400,128]{1,0:T(8,128)(2,1)S(1)}, bf16[400,128]{1,0:T(8,128)(2,1)S(1)}, u32[]{:S(2)}, u32[]{:S(2)}) %collective-permute-start.26) | collective-permute-done | bytes 102432 | tf_op jit(solution)/shard_map/ppermute | solution.py:641
  126.7 4.5 %collective-permute-done.25.r2 = bf16[400,128]{1,0:T(8,128)(2,1)S(1)} collective-permute-done((bf16[400,128]{1,0:T(8,128)(2,1)S(1)}, bf16[400,128]{1,0:T(8,128)(2,1)S(1)}, u32[]{:S(2)}, u32[]{:S(2)}) %collective-permute-start.25) | collective-permute-done | bytes 102432 | tf_op jit(solution)/shard_map/ppermute | solution.py:641
  131.2 0.6 copy-done.3
  131.9 1.9 %shares.1 = (f32[400,128]{1,0:T(8,128)}, f32[8,128]{1,0:T(8,128)}) custom-call(f32[400,128]{1,0:T(8,128)} %get-tuple-element.149.own, bf16[400,128]{1,0:T(8,128)(2,1)} %copy-done.4, bf16[400,128]{1,0:T(8,128)(2,1)} %copy-done.3, bf16[400,128]{1,0:T(8,128)(2,1)} %copy-done.2, f32[8,128]{1,0:T(8,128)} %get-tuple-element.123.v), custom_call_target="tpu_custom_call" | custom-call | tf_op jit(solution)/shard_map/shares/pallas_call | solution.py:795
  133.7 1.4 collective-permute-done.27
  135.1 0.7 add.108
  135.8 1.4 collective-permute-start.30
  137.2 0.7 collective-permute-start.29
  137.9 1.4 collective-permute-start.28
  139.3 1.0 collective-permute-done.30
  140.3 0.5 collective-permute-done.29
  140.8 0.7 collective-permute-done.28
  141.5 1.4 collective-permute-start.33
  142.9 3.0 %collective-permute-start.31 = (f32[8,128]{1,0:T(8,128)S(1)}, f32[8,128]{1,0:T(8,128)S(1)}, u32[]{:S(2)}, u32[]{:S(2)}) collective-permute-start(f32[8,128]{1,0:T(8,128)S(1)} %add_add_fusion.refs_1_), channel_id=1, source_target_pairs={{0,8},{1,9},{2,10},{3,11},{4,12},{5,13},{6,14},{7,15},{8,0},{9,1},... | collective-permute-start | bytes 12296 | tf_op jit(solution)/shard_map/ppermute | solution.py:641
  145.9 1.0 collective-permute-done.33.refs_4_
  148.1 2.8 %clipped_adamw.1 = (f32[18,32,64]{2,1,0:T(8,128)}, f32[18,32,64]{2,1,0:T(8,128)}, f32[18,32,64]{2,1,0:T(8,128)}, f32[32,128]{1,0:T(8,128)}, f32[32,128]{1,0:T(8,...) custom-call(s32[2]{0:T(128)} %pad_add_fusion.refs_3_.refs_7_.refs_6_, ...), custom_call_target="tpu_custom_call" | custom-call | tf_op jit(solution)/shard_map/clipped_adamw/pallas_call | solution.py:855
  (88 shorter events, 4.6 us)
Async XLA Ops:
  2.5 9.4 %collective-permute-start.5 = (bf16[160,128]{1,0:T(8,128)(2,1)}, bf16[160,128]{1,0:T(8,128)(2,1)S(1)}, u32[]{:S(2)}, u32[]{:S(2)}) collective-permute-start(bf16[160,128]{1,0:T(8,128)(2,1)} %get-tuple-element.81), channel_id=1, source_target_pairs={{0,24},{1,25},{2,26},{3,27},{4,28},{5,29},{6,30},{7,31},{8,16},{9,... | collective-permute-start | bytes 122888 | tf_op jit(solution)/shard_map/ppermute | solution.py:641
  7.5 5.9 %collective-permute-start.4 = (bf16[160,128]{1,0:T(8,128)(2,1)}, bf16[160,128]{1,0:T(8,128)(2,1)S(1)}, u32[]{:S(2)}, u32[]{:S(2)}) collective-permute-start(bf16[160,128]{1,0:T(8,128)(2,1)} %get-tuple-element.81), channel_id=1, source_target_pairs={{0,16},{1,17},{2,18},{3,19},{4,20},{5,21},{6,22},{7,23},{8,24},{9,... | collective-permute-start | bytes 122888 | tf_op jit(solution)/shard_map/ppermute | solution.py:641
  7.5 5.9 %collective-permute-start.3 = (bf16[160,128]{1,0:T(8,128)(2,1)}, bf16[160,128]{1,0:T(8,128)(2,1)S(1)}, u32[]{:S(2)}, u32[]{:S(2)}) collective-permute-start(bf16[160,128]{1,0:T(8,128)(2,1)} %get-tuple-element.81), channel_id=1, source_target_pairs={{0,8},{1,9},{2,10},{3,11},{4,12},{5,13},{6,14},{7,15},{8,0},{9,1},... | collective-permute-start | bytes 122888 | tf_op jit(solution)/shard_map/ppermute | solution.py:641
  8.1 11.0 %collective-permute-start.2 = (bf16[240,128]{1,0:T(8,128)(2,1)}, bf16[240,128]{1,0:T(8,128)(2,1)S(1)}, u32[]{:S(2)}, u32[]{:S(2)}) collective-permute-start(bf16[240,128]{1,0:T(8,128)(2,1)} %get-tuple-element.87), channel_id=1, source_target_pairs={{0,24},{1,25},{2,26},{3,27},{4,28},{5,29},{6,30},{7,31},{8,16},{9,... | collective-permute-start | bytes 184328 | tf_op jit(solution)/shard_map/ppermute | solution.py:641
  13.4 12.6 %copy-start.24 = (s32[16]{0:T(128)S(1)}, s32[16]{0:T(128)}, u32[]{:S(2)}) copy-start(s32[16]{0:T(128)} %param.20) | copy-start | bytes 196
  13.4 12.6 %copy-start.5 = (bf16[240,128]{1,0:T(8,128)(2,1)S(1)}, bf16[240,128]{1,0:T(8,128)(2,1)}, u32[]{:S(2)}) copy-start(bf16[240,128]{1,0:T(8,128)(2,1)} %get-tuple-element.87) | copy-start | bytes 184324
  14.2 11.8 %copy-start.1 = (bf16[4,160,128]{2,1,0:T(8,128)(2,1)}, bf16[4,160,128]{2,1,0:T(8,128)(2,1)S(1)}, u32[]{:S(2)}) copy-start(bf16[4,160,128]{2,1,0:T(8,128)(2,1)S(1)} %pad_maximum_fusion.1.refs_4_) | copy-start | bytes 491524
  14.3 9.9 %collective-permute-start.8 = (bf16[4,160,128]{2,1,0:T(8,128)(2,1)S(1)}, bf16[4,160,128]{2,1,0:T(8,128)(2,1)S(1)}, u32[]{:S(2)}, u32[]{:S(2)}) collective-permute-start(bf16[4,160,128]{2,1,0:T(8,128)(2,1)S(1)} %pad_maximum_fusion.1.refs_4_), channel_id=1, source_target_pairs={{0,6},{1,7},{2,4},{3,5},{4,2},{5,3},{6,0},{7,1},{8,14},{9,15},{10,... | collective-permute-start | bytes 491528 | tf_op jit(solution)/shard_map/ppermute | solution.py:641
  16.8 7.4 %collective-permute-start.7 = (bf16[4,160,128]{2,1,0:T(8,128)(2,1)S(1)}, bf16[4,160,128]{2,1,0:T(8,128)(2,1)S(1)}, u32[]{:S(2)}, u32[]{:S(2)}) collective-permute-start(bf16[4,160,128]{2,1,0:T(8,128)(2,1)S(1)} %pad_maximum_fusion.1.refs_4_), channel_id=1, source_target_pairs={{0,4},{1,5},{2,6},{3,7},{4,0},{5,1},{6,2},{7,3},{8,12},{9,13},{10,... | collective-permute-start | bytes 491528 | tf_op jit(solution)/shard_map/ppermute | solution.py:641
  17.3 6.9 %collective-permute-start.6 = (bf16[4,160,128]{2,1,0:T(8,128)(2,1)S(1)}, bf16[4,160,128]{2,1,0:T(8,128)(2,1)S(1)}, u32[]{:S(2)}, u32[]{:S(2)}) collective-permute-start(bf16[4,160,128]{2,1,0:T(8,128)(2,1)S(1)} %pad_maximum_fusion.1.refs_4_), channel_id=1, source_target_pairs={{0,2},{1,3},{2,0},{3,1},{4,6},{5,7},{6,4},{7,5},{8,10},{9,11},{10,... | collective-permute-start | bytes 491528 | tf_op jit(solution)/shard_map/ppermute | solution.py:641
  17.8 6.4 %collective-permute-start.1 = (bf16[240,128]{1,0:T(8,128)(2,1)}, bf16[240,128]{1,0:T(8,128)(2,1)S(1)}, u32[]{:S(2)}, u32[]{:S(2)}) collective-permute-start(bf16[240,128]{1,0:T(8,128)(2,1)} %get-tuple-element.87), channel_id=1, source_target_pairs={{0,16},{1,17},{2,18},{3,19},{4,20},{5,21},{6,22},{7,23},{8,24},{9,... | collective-permute-start | bytes 184328 | tf_op jit(solution)/shard_map/ppermute | solution.py:641
  19.1 5.1 %collective-permute-start = (bf16[240,128]{1,0:T(8,128)(2,1)}, bf16[240,128]{1,0:T(8,128)(2,1)S(1)}, u32[]{:S(2)}, u32[]{:S(2)}) collective-permute-start(bf16[240,128]{1,0:T(8,128)(2,1)} %get-tuple-element.87), channel_id=1, source_target_pairs={{0,8},{1,9},{2,10},{3,11},{4,12},{5,13},{6,14},{7,15},{8,0},{9,1},... | collective-permute-start | bytes 184328 | tf_op jit(solution)/shard_map/ppermute | solution.py:641
  24.2 5.5 %copy-start.17 = (bf16[4,160,128]{2,1,0:T(8,128)(2,1)}, bf16[4,160,128]{2,1,0:T(8,128)(2,1)S(1)}, u32[]{:S(2)}) copy-start(bf16[4,160,128]{2,1,0:T(8,128)(2,1)S(1)} %collective-permute-done.8.refs_10_) | copy-start | bytes 491524
  24.2 5.4 %copy-start.18 = (bf16[4,160,128]{2,1,0:T(8,128)(2,1)}, bf16[4,160,128]{2,1,0:T(8,128)(2,1)S(1)}, u32[]{:S(2)}) copy-start(bf16[4,160,128]{2,1,0:T(8,128)(2,1)S(1)} %collective-permute-done.7.refs_8_) | copy-start | bytes 491524
  24.2 5.4 %copy-start.19 = (bf16[4,160,128]{2,1,0:T(8,128)(2,1)}, bf16[4,160,128]{2,1,0:T(8,128)(2,1)S(1)}, u32[]{:S(2)}) copy-start(bf16[4,160,128]{2,1,0:T(8,128)(2,1)S(1)} %collective-permute-done.6.refs_6_) | copy-start | bytes 491524
  24.2 4.0 %collective-permute-start.9 = (bf16[4,160,128]{2,1,0:T(8,128)(2,1)S(1)}, bf16[4,160,128]{2,1,0:T(8,128)(2,1)S(1)}, u32[]{:S(2)}, u32[]{:S(2)}) collective-permute-start(bf16[4,160,128]{2,1,0:T(8,128)(2,1)S(1)} %pad_maximum_fusion.1.refs_4_), channel_id=1, source_target_pairs={{0,1},{1,0},{2,3},{3,2},{4,5},{5,4},{6,7},{7,6},{8,9},{9,8},{10,11... | collective-permute-start | bytes 491528 | tf_op jit(solution)/shard_map/ppermute | solution.py:641
  24.3 4.4 %collective-permute-start.10 = (bf16[4,160,128]{2,1,0:T(8,128)(2,1)S(1)}, bf16[4,160,128]{2,1,0:T(8,128)(2,1)S(1)}, u32[]{:S(2)}, u32[]{:S(2)}) collective-permute-start(bf16[4,160,128]{2,1,0:T(8,128)(2,1)S(1)} %collective-permute-done.6.refs_6_), channel_id=1, source_target_pairs={{0,1},{1,0},{2,3},{3,2},{4,5},{5,4},{6,7},{7,6},{8,9},{9,8},{10,11... | collective-permute-start | bytes 491528 | tf_op jit(solution)/shard_map/ppermute | solution.py:641
  24.8 4.8 %collective-permute-start.11 = (bf16[4,160,128]{2,1,0:T(8,128)(2,1)S(1)}, bf16[4,160,128]{2,1,0:T(8,128)(2,1)S(1)}, u32[]{:S(2)}, u32[]{:S(2)}) collective-permute-start(bf16[4,160,128]{2,1,0:T(8,128)(2,1)S(1)} %collective-permute-done.7.refs_8_), channel_id=1, source_target_pairs={{0,1},{1,0},{2,3},{3,2},{4,5},{5,4},{6,7},{7,6},{8,9},{9,8},{10,11... | collective-permute-start | bytes 491528 | tf_op jit(solution)/shard_map/ppermute | solution.py:641
  24.9 4.7 %collective-permute-start.12 = (bf16[4,160,128]{2,1,0:T(8,128)(2,1)S(1)}, bf16[4,160,128]{2,1,0:T(8,128)(2,1)S(1)}, u32[]{:S(2)}, u32[]{:S(2)}) collective-permute-start(bf16[4,160,128]{2,1,0:T(8,128)(2,1)S(1)} %collective-permute-done.8.refs_10_), channel_id=1, source_target_pairs={{0,1},{1,0},{2,3},{3,2},{4,5},{5,4},{6,7},{7,6},{8,9},{9,8},{10,11... | collective-permute-start | bytes 491528 | tf_op jit(solution)/shard_map/ppermute | solution.py:641
  26.0 14.8 %copy-start = (bf16[4,240,128]{2,1,0:T(8,128)(2,1)}, bf16[4,240,128]{2,1,0:T(8,128)(2,1)S(1)}, u32[]{:S(2)}) copy-start(bf16[4,240,128]{2,1,0:T(8,128)(2,1)S(1)} %pad_maximum_fusion.refs_8_) | copy-start | bytes 737284
  26.0 14.7 %collective-permute-start.15 = (bf16[4,240,128]{2,1,0:T(8,128)(2,1)S(1)}, bf16[4,240,128]{2,1,0:T(8,128)(2,1)S(1)}, u32[]{:S(2)}, u32[]{:S(2)}) collective-permute-start(bf16[4,240,128]{2,1,0:T(8,128)(2,1)S(1)} %pad_maximum_fusion.refs_8_), channel_id=1, source_target_pairs={{0,6},{1,7},{2,4},{3,5},{4,2},{5,3},{6,0},{7,1},{8,14},{9,15},{10,... | collective-permute-start | bytes 737288 | tf_op jit(solution)/shard_map/ppermute | solution.py:641
  28.2 1.5 copy-start.20
  28.2 12.6 %collective-permute-start.14 = (bf16[4,240,128]{2,1,0:T(8,128)(2,1)S(1)}, bf16[4,240,128]{2,1,0:T(8,128)(2,1)S(1)}, u32[]{:S(2)}, u32[]{:S(2)}) collective-permute-start(bf16[4,240,128]{2,1,0:T(8,128)(2,1)S(1)} %pad_maximum_fusion.refs_8_), channel_id=1, source_target_pairs={{0,4},{1,5},{2,6},{3,7},{4,0},{5,1},{6,2},{7,3},{8,12},{9,13},{10,... | collective-permute-start | bytes 737288 | tf_op jit(solution)/shard_map/ppermute | solution.py:641
  28.7 1.0 copy-start.21
  28.7 12.1 %collective-permute-start.13 = (bf16[4,240,128]{2,1,0:T(8,128)(2,1)S(1)}, bf16[4,240,128]{2,1,0:T(8,128)(2,1)S(1)}, u32[]{:S(2)}, u32[]{:S(2)}) collective-permute-start(bf16[4,240,128]{2,1,0:T(8,128)(2,1)S(1)} %pad_maximum_fusion.refs_8_), channel_id=1, source_target_pairs={{0,2},{1,3},{2,0},{3,1},{4,6},{5,7},{6,4},{7,5},{8,10},{9,11},{10,... | collective-permute-start | bytes 737288 | tf_op jit(solution)/shard_map/ppermute | solution.py:641
  40.8 2.7 %copy-start.10 = (bf16[4,240,128]{2,1,0:T(8,128)(2,1)}, bf16[4,240,128]{2,1,0:T(8,128)(2,1)S(1)}, u32[]{:S(2)}) copy-start(bf16[4,240,128]{2,1,0:T(8,128)(2,1)S(1)} %collective-permute-done.15.refs_14_) | copy-start | bytes 737284
  40.8 2.7 %copy-start.11 = (bf16[4,240,128]{2,1,0:T(8,128)(2,1)}, bf16[4,240,128]{2,1,0:T(8,128)(2,1)S(1)}, u32[]{:S(2)}) copy-start(bf16[4,240,128]{2,1,0:T(8,128)(2,1)S(1)} %collective-permute-done.14.refs_12_) | copy-start | bytes 737284
  40.8 2.7 %copy-start.12 = (bf16[4,240,128]{2,1,0:T(8,128)(2,1)}, bf16[4,240,128]{2,1,0:T(8,128)(2,1)S(1)}, u32[]{:S(2)}) copy-start(bf16[4,240,128]{2,1,0:T(8,128)(2,1)S(1)} %collective-permute-done.13.refs_10_) | copy-start | bytes 737284
  40.9 1.9 %collective-permute-start.16 = (bf16[4,240,128]{2,1,0:T(8,128)(2,1)S(1)}, bf16[4,240,128]{2,1,0:T(8,128)(2,1)S(1)}, u32[]{:S(2)}, u32[]{:S(2)}) collective-permute-start(bf16[4,240,128]{2,1,0:T(8,128)(2,1)S(1)} %pad_maximum_fusion.refs_8_), channel_id=1, source_target_pairs={{0,1},{1,0},{2,3},{3,2},{4,5},{5,4},{6,7},{7,6},{8,9},{9,8},{10,11... | collective-permute-start | bytes 737288 | tf_op jit(solution)/shard_map/ppermute | solution.py:641
  40.9 1.9 %collective-permute-start.17 = (bf16[4,240,128]{2,1,0:T(8,128)(2,1)S(1)}, bf16[4,240,128]{2,1,0:T(8,128)(2,1)S(1)}, u32[]{:S(2)}, u32[]{:S(2)}) collective-permute-start(bf16[4,240,128]{2,1,0:T(8,128)(2,1)S(1)} %collective-permute-done.13.refs_10_), channel_id=1, source_target_pairs={{0,1},{1,0},{2,3},{3,2},{4,5},{5,4},{6,7},{7,6},{8,9},{9,8},{10,11... | collective-permute-start | bytes 737288 | tf_op jit(solution)/shard_map/ppermute | solution.py:641
  41.4 1.7 %collective-permute-start.18 = (bf16[4,240,128]{2,1,0:T(8,128)(2,1)S(1)}, bf16[4,240,128]{2,1,0:T(8,128)(2,1)S(1)}, u32[]{:S(2)}, u32[]{:S(2)}) collective-permute-start(bf16[4,240,128]{2,1,0:T(8,128)(2,1)S(1)} %collective-permute-done.14.refs_12_), channel_id=1, source_target_pairs={{0,1},{1,0},{2,3},{3,2},{4,5},{5,4},{6,7},{7,6},{8,9},{9,8},{10,11... | collective-permute-start | bytes 737288 | tf_op jit(solution)/shard_map/ppermute | solution.py:641
  41.5 2.0 %collective-permute-start.19 = (bf16[4,240,128]{2,1,0:T(8,128)(2,1)S(1)}, bf16[4,240,128]{2,1,0:T(8,128)(2,1)S(1)}, u32[]{:S(2)}, u32[]{:S(2)}) collective-permute-start(bf16[4,240,128]{2,1,0:T(8,128)(2,1)S(1)} %collective-permute-done.15.refs_14_), channel_id=1, source_target_pairs={{0,1},{1,0},{2,3},{3,2},{4,5},{5,4},{6,7},{7,6},{8,9},{9,8},{10,11... | collective-permute-start | bytes 737288 | tf_op jit(solution)/shard_map/ppermute | solution.py:641
  91.3 3.8 %collective-permute-start.20 = (bf16[4,4,400,128]{3,2,1,0:T(8,128)(2,1)}, bf16[4,4,400,128]{3,2,1,0:T(8,128)(2,1)S(1)}, u32[]{:S(2)}, u32[]{:S(2)}) collective-permute-start(bf16[4,4,400,128]{3,2,1,0:T(8,128)(2,1)} %get-tuple-element.110), channel_id=1, source_target_pairs={{0,1},{1,0},{2,3},{3,2},{4,5},{5,4},{6,7},{7,6},{8,9},{9,8},{10,11... | collective-permute-start | bytes 4915208 | tf_op jit(solution)/shard_map/ppermute | solution.py:641
  96.9 15.7 %collective-permute-start.21 = (bf16[4,400,128]{2,1,0:T(8,128)(2,1)S(1)}, bf16[4,400,128]{2,1,0:T(8,128)(2,1)S(1)}, u32[]{:S(2)}, u32[]{:S(2)}) collective-permute-start(bf16[4,400,128]{2,1,0:T(8,128)(2,1)S(1)} %get-tuple-element.117), channel_id=1, source_target_pairs={{0,2},{1,3},{2,0},{3,1},{4,6},{5,7},{6,4},{7,5},{8,10},{9,11},{10,... | collective-permute-start | bytes 1228808 | tf_op jit(solution)/shard_map/ppermute | solution.py:641
  97.3 15.3 %collective-permute-start.22 = (bf16[4,400,128]{2,1,0:T(8,128)(2,1)S(1)}, bf16[4,400,128]{2,1,0:T(8,128)(2,1)S(1)}, u32[]{:S(2)}, u32[]{:S(2)}) collective-permute-start(bf16[4,400,128]{2,1,0:T(8,128)(2,1)S(1)} %get-tuple-element.118), channel_id=1, source_target_pairs={{0,4},{1,5},{2,6},{3,7},{4,0},{5,1},{6,2},{7,3},{8,12},{9,13},{10,... | collective-permute-start | bytes 1228808 | tf_op jit(solution)/shard_map/ppermute | solution.py:641
  98.5 19.7 %collective-permute-start.23 = (bf16[4,400,128]{2,1,0:T(8,128)(2,1)S(1)}, bf16[4,400,128]{2,1,0:T(8,128)(2,1)S(1)}, u32[]{:S(2)}, u32[]{:S(2)}) collective-permute-start(bf16[4,400,128]{2,1,0:T(8,128)(2,1)S(1)} %get-tuple-element.119), channel_id=1, source_target_pairs={{0,6},{1,7},{2,4},{3,5},{4,2},{5,3},{6,0},{7,1},{8,14},{9,15},{10,... | collective-permute-start | bytes 1228808 | tf_op jit(solution)/shard_map/ppermute | solution.py:641
  119.1 7.6 %collective-permute-start.26 = (bf16[400,128]{1,0:T(8,128)(2,1)S(1)}, bf16[400,128]{1,0:T(8,128)(2,1)S(1)}, u32[]{:S(2)}, u32[]{:S(2)}) collective-permute-start(bf16[400,128]{1,0:T(8,128)(2,1)S(1)} %get-tuple-element.146), channel_id=1, source_target_pairs={{0,24},{1,25},{2,26},{3,27},{4,28},{5,29},{6,30},{7,31},{8,16},{9,... | collective-permute-start | bytes 307208 | tf_op jit(solution)/shard_map/ppermute | solution.py:641
  121.2 10.0 %collective-permute-start.25 = (bf16[400,128]{1,0:T(8,128)(2,1)S(1)}, bf16[400,128]{1,0:T(8,128)(2,1)S(1)}, u32[]{:S(2)}, u32[]{:S(2)}) collective-permute-start(bf16[400,128]{1,0:T(8,128)(2,1)S(1)} %get-tuple-element.147), channel_id=1, source_target_pairs={{0,16},{1,17},{2,18},{3,19},{4,20},{5,21},{6,22},{7,23},{8,24},{9,... | collective-permute-start | bytes 307208 | tf_op jit(solution)/shard_map/ppermute | solution.py:641
  122.5 8.7 %collective-permute-start.24 = (bf16[400,128]{1,0:T(8,128)(2,1)S(1)}, bf16[400,128]{1,0:T(8,128)(2,1)S(1)}, u32[]{:S(2)}, u32[]{:S(2)}) collective-permute-start(bf16[400,128]{1,0:T(8,128)(2,1)S(1)} %get-tuple-element.148), channel_id=1, source_target_pairs={{0,8},{1,9},{2,10},{3,11},{4,12},{5,13},{6,14},{7,15},{8,0},{9,1},... | collective-permute-start | bytes 307208 | tf_op jit(solution)/shard_map/ppermute | solution.py:641
  126.7 4.5 %copy-start.2 = (bf16[400,128]{1,0:T(8,128)(2,1)}, bf16[400,128]{1,0:T(8,128)(2,1)S(1)}, u32[]{:S(2)}) copy-start(bf16[400,128]{1,0:T(8,128)(2,1)S(1)} %collective-permute-done.26.r3) | copy-start | bytes 307204
  133.7 1.4 collective-permute-start.27
  135.8 4.5 %collective-permute-start.30 = (f32[8,128]{1,0:T(8,128)S(1)}, f32[8,128]{1,0:T(8,128)S(1)}, u32[]{:S(2)}, u32[]{:S(2)}) collective-permute-start(f32[8,128]{1,0:T(8,128)S(1)} %add.108), channel_id=1, source_target_pairs={{0,6},{1,7},{2,4},{3,5},{4,2},{5,3},{6,0},{7,1},{8,14},{9,15},{10,... | collective-permute-start | bytes 12296 | tf_op jit(solution)/shard_map/ppermute | solution.py:641
  137.2 3.6 %collective-permute-start.29 = (f32[8,128]{1,0:T(8,128)S(1)}, f32[8,128]{1,0:T(8,128)S(1)}, u32[]{:S(2)}, u32[]{:S(2)}) collective-permute-start(f32[8,128]{1,0:T(8,128)S(1)} %add.108), channel_id=1, source_target_pairs={{0,4},{1,5},{2,6},{3,7},{4,0},{5,1},{6,2},{7,3},{8,12},{9,13},{10,... | collective-permute-start | bytes 12296 | tf_op jit(solution)/shard_map/ppermute | solution.py:641
  137.9 3.6 %collective-permute-start.28 = (f32[8,128]{1,0:T(8,128)S(1)}, f32[8,128]{1,0:T(8,128)S(1)}, u32[]{:S(2)}, u32[]{:S(2)}) collective-permute-start(f32[8,128]{1,0:T(8,128)S(1)} %add.108), channel_id=1, source_target_pairs={{0,2},{1,3},{2,0},{3,1},{4,6},{5,7},{6,4},{7,5},{8,10},{9,11},{10,... | collective-permute-start | bytes 12296 | tf_op jit(solution)/shard_map/ppermute | solution.py:641
  141.5 6.0 %copy-start.6 = (f32[8,128]{1,0:T(8,128)}, f32[8,128]{1,0:T(8,128)S(1)}, u32[]{:S(2)}) copy-start(f32[8,128]{1,0:T(8,128)S(1)} %add_add_fusion.refs_1_) | copy-start | bytes 12292
  141.5 5.4 %collective-permute-start.33 = (f32[8,128]{1,0:T(8,128)S(1)}, f32[8,128]{1,0:T(8,128)S(1)}, u32[]{:S(2)}, u32[]{:S(2)}) collective-permute-start(f32[8,128]{1,0:T(8,128)S(1)} %add_add_fusion.refs_1_), channel_id=1, source_target_pairs={{0,24},{1,25},{2,26},{3,27},{4,28},{5,29},{6,30},{7,31},{8,16},{9,... | collective-permute-start | bytes 12296 | tf_op jit(solution)/shard_map/ppermute | solution.py:641
  142.9 4.5 %collective-permute-start.32 = (f32[8,128]{1,0:T(8,128)S(1)}, f32[8,128]{1,0:T(8,128)S(1)}, u32[]{:S(2)}, u32[]{:S(2)}) collective-permute-start(f32[8,128]{1,0:T(8,128)S(1)} %add_add_fusion.refs_1_), channel_id=1, source_target_pairs={{0,16},{1,17},{2,18},{3,19},{4,20},{5,21},{6,22},{7,23},{8,24},{9,... | collective-permute-start | bytes 12296 | tf_op jit(solution)/shard_map/ppermute | solution.py:641
  142.9 4.6 %collective-permute-start.31 = (f32[8,128]{1,0:T(8,128)S(1)}, f32[8,128]{1,0:T(8,128)S(1)}, u32[]{:S(2)}, u32[]{:S(2)}) collective-permute-start(f32[8,128]{1,0:T(8,128)S(1)} %add_add_fusion.refs_1_), channel_id=1, source_target_pairs={{0,8},{1,9},{2,10},{3,11},{4,12},{5,13},{6,14},{7,15},{8,0},{9,1},... | collective-permute-start | bytes 12296 | tf_op jit(solution)/shard_map/ppermute | solution.py:641
  (11 other events, 7.3 us)

commit v4 on v3

--- a/solution.py
+++ b/solution.py
@@ -26,7 +26,7 @@
 R = range(0, 256, CH)
 RA = 160
 RB = 240
-RG = 400
+RG = 384
 
 sd = jax.ShapeDtypeStruct
 
@@ -175,6 +175,9 @@
 
 def blocks(*tail):
     return pl.BlockSpec((NB,) + tail, lambda i, c: (clamped(i, c),) + (0,) * len(tail))
+
+
+ANY = pl.BlockSpec(memory_space=pl.ANY)
 
 
 def out_blocks(*tail):
@@ -712,39 +715,17 @@
     f = me[1]
     for rf in range(8):
         at = pl.multiple_of(base + (f ^ rf) * step, 16)
-        ref = outs[rf & 1]
+        ref = outs[4 * (rf & 1) + (rf >> 1)]
         for h in range(2):
             cut = slice(lanes + 128 * h, lanes + 128 * h + 128)
             e0, e1 = halves(src[pl.ds(at, rows), cut], src[pl.ds(at + rows, rows), cut])
-            ref[rf >> 1, z ^ (2 * h), lo : lo + rows, :] = e0.astype(BF)
-            ref[rf >> 1, z ^ (2 * h + 1), lo : lo + rows, :] = e1.astype(BF)
-
-
-def spread_rows(rows, me):
-    a8 = []
-    for s in range(8):
-        piece = rows[:, 128 * (s // 4) : 128 * (s // 4) + 128]
-        a8.append(pltpu.roll(piece, 128 - 32 * (s % 4), 1) if s % 4 else piece)
-    a8 = jnp.concatenate(a8, axis=0)
-    top = a8.astype(BF)
-    rest = (a8 - top.astype(F32)).astype(BF)
-    col = lax.broadcasted_iota(jnp.int32, (32, 128), 1)
-    line = lax.broadcasted_iota(jnp.int32, (32, 128), 0)
-    owner = ((line & 3) ^ me[0]) * 8 + ((line >> 2) ^ me[1])
-    acc = jnp.zeros((32, 128), F32)
-    unit = 8 * (col & 15) + (col >> 4)
-    for u in range(3):
-        sel = jnp.where(unit == 3 * owner + u, 1.0, 0.0).astype(BF)
-        piece = dot(sel, top) + dot(sel, rest)
-        if u:
-            piece = pltpu.roll(piece, 32 * u, 1)
-        acc = jnp.where((col >> 5) == u, piece, acc)
-    return acc
+            ref[z ^ (2 * h), lo : lo + rows, :] = e0.astype(BF)
+            ref[z ^ (2 * h + 1), lo : lo + rows, :] = e1.astype(BF)
 
 
 def finish_all(outs, me, dwa, dwb, dwq, dwo, de, rows, turn):
     for k in range(9):
-        place(outs, me, dwa, 256 * (k // 3), 256 * (k % 3), 256 + 16 * k, 16, 32)
+        place(outs, me, dwa, 256 * (k // 3), 256 * (k % 3), 240 + 16 * k, 16, 32)
         place(outs, me, dwb, 256 * (k // 3), 256 * (k % 3), 16 * k, 16, 32)
     for k in range(3):
         turn[256 * k : 256 * k + 256, 0:256] = dwq[:, 256 * k : 256 * k + 256].T
@@ -755,17 +736,13 @@
         for rf in range(8):
             at = pl.multiple_of(1024 + (me[1] ^ rf) * 32, 32)
             block = turn[pl.ds(at, 32), 128 * d : 128 * d + 128]
-            outs[rf & 1][rf >> 1, me[0] ^ d, 208:240, :] = block.astype(BF)
-    acc = spread_rows(rows, me)
-    for rf in range(8):
-        for rz in range(4):
-            r = 4 * rf + rz
-            outs[rf & 1][rf >> 1, rz, 240:256, :] = jnp.broadcast_to(acc[r : r + 1], (16, 128)).astype(BF)
-
-
-def over_core(keep, send):
-    got = swap(send, 1)
-    return [(keep[j].astype(F32) + got[j].astype(F32)).astype(keep.dtype) for j in range(4)]
+            outs[4 * (rf & 1) + (rf >> 1)][me[0] ^ d, 208:240, :] = block.astype(BF)
+    outs[8][...] = rows
+
+
+def over_core(ends):
+    got = [swap(v, 1) for v in ends[7:3:-1]][::-1]
+    return [(a.astype(F32) + b.astype(F32)).astype(a.dtype) for a, b in zip(ends[:4], got)]
 
 
 def to_plane(parts):
@@ -781,20 +758,21 @@
     return [swap(v, 8 * (rz + 1)) for rz, v in enumerate(others)]
 
 
-def shares_body(own, r1, r2, r3, v, g, out):
+def shares_body(own, r1, r2, r3, first, rows, g, out):
     s = own[...] + sum(r[...].astype(F32) for r in (r1, r2, r3))
     g[...] = s
-    fold = lambda a: jnp.sum((a * a).reshape(-1, 8, 128), axis=0)
-    t = fsum(fold(s[0:240]) + fold(s[256:400])) + s[240:241] * s[240:241]
-    t = jnp.broadcast_to(jnp.sum(t, axis=1, keepdims=True), (8, 128))
-    line = lax.broadcasted_iota(jnp.int32, (8, 128), 0)
-    out[...] = jnp.where(line < 4, v[...], t)
-
-
-def shares(own, got, v):
+    t = fsum(jnp.sum((s * s).reshape(-1, 8, 128), axis=0))
+    for k in range(2, 12):
+        out[2 * k : 2 * k + 1, :] = rows[k : k + 1, 0:128]
+        out[2 * k + 1 : 2 * k + 2, :] = rows[k : k + 1, 128:256]
+    out[0:4, :] = first[0:4, :]
+    out[24:32, :] = jnp.broadcast_to(jnp.sum(t, axis=1, keepdims=True), (8, 128))
+
+
+def shares(own, got, first, rows):
     return pl.pallas_call(
-        shares_body, out_shape=[sd((RG, 128), F32), sd((8, 128), F32)], compiler_params=VMEM, name="shares"
-    )(own, *got, v)
+        shares_body, out_shape=[sd((RG, 128), F32), sd((32, 128), F32)], compiler_params=VMEM, name="shares"
+    )(own, *got, first, rows)
 
 
 def total_over(s):
@@ -810,15 +788,14 @@
     first = refs[-1]
     total = (t0[...] + t1[...]) + (t2[...] + t3[...])
     first[...] = total
-    top = total[0:4]
-    norm = jnp.sqrt(jnp.broadcast_to(jnp.sum(fsum(top * top), axis=1, keepdims=True), (1, 128)) + total[4:5])
+    top = total[0:24]
+    norm = jnp.sqrt(jnp.broadcast_to(jnp.sum(fsum(top * top), axis=1, keepdims=True), (1, 128)) + total[24:25])
     lane = lax.broadcasted_iota(jnp.int32, (1, 128), 1)
-    vec = grads[240:241, :]
+    vec = jnp.zeros((1, 128), F32)
     for u in range(3):
         unit = 3 * (8 * me[0] + me[1]) + u
-        line = first[pl.ds(jnp.minimum(unit >> 2, 4), 1), :]
-        line = pltpu.roll(line, (32 * u + 128 - 32 * (unit & 3)) & 127, 1)
-        vec = vec + jnp.where(jnp.logical_and((lane >> 5) == u, unit < 16), line, 0.0)
+        line = pltpu.roll(first[pl.ds(unit >> 2, 1), :], (32 * u + 128 - 32 * (unit & 3)) & 127, 1)
+        vec = jnp.where((lane >> 5) == u, line, vec)
     factor = clip_norm / jnp.maximum(norm, clip_norm)
 
     def put(kind, at, grad):
@@ -835,7 +812,7 @@
         outs[3 * kind + 1][at] = second_new
         outs[3 * kind + 2][at] = update
 
-    for side, base in ((0, 256), (1, 0)):
+    for side, base in ((0, 240), (1, 0)):
         for k in range(9):
             g = grads[base + 16 * k : base + 16 * k + 16, :]
             put(0, (9 * side + k,), jnp.concatenate([g[:, :64], g[:, 64:]], axis=0))
@@ -857,7 +834,7 @@
         in_specs=[pl.BlockSpec(memory_space=pltpu.SMEM)] + [pl.BlockSpec(a.shape) for a in args],
         out_specs=[pl.BlockSpec(s.shape) for s in state] + [pl.BlockSpec(memory_space=pltpu.SMEM)],
         out_shape=[sd(s.shape, F32) for s in state] + [sd((1,), F32)],
-        scratch_shapes=[pltpu.VMEM((8, 128), F32)],
+        scratch_shapes=[pltpu.VMEM((32, 128), F32)],
         compiler_params=VMEM,
         name="clipped_adamw",
     )(me, *args)
@@ -904,7 +881,7 @@
     line_a = jnp.stack([sa] + [swap(sa, 8 * rz) for rz in range(1, 4)])
     rows_b = [sb] + [swap(sb, 8 * rz) for rz in range(1, 4)]
     plane_a = [line_a] + [swap(line_a, bits) for bits in (2, 4, 6)]
-    rows_b, plane_a, cf = lax.optimization_barrier((rows_b, plane_a, cf))
+    rows_b, plane_a, cf, me, emb = lax.optimization_barrier((rows_b, plane_a, cf, me, emb))
     all_a = [p for line in plane_a for p in (line, swap(line, 1))]
     line_b = jnp.stack(rows_b)
     plane_b = [line_b] + [swap(line_b, bits) for bits in (2, 4, 6)]
@@ -912,16 +889,16 @@
     h0, a1, wat, vec = conv_one(counts, x, cf, me, all_a, unpack_a)
     h0, plane_b = lax.optimization_barrier((h0, plane_b))
     all_b = [p for line in plane_b for p in (line, swap(line, 1))]
-    out, ga, dm, keep, send = middle(
-        counts, x, h0, cot, a1, emb, vec, me, all_b, unpack_b, finish_all, [sd((4, 4, RG, 128), BF)] * 2
+    out, ga, dm, *ends, rows = middle(
+        counts, x, h0, cot, a1, emb, vec, me, all_b, unpack_b, finish_all, [sd((4, RG, 128), BF)] * 8 + [sd((16, 256), F32)]
     )
-    parts = over_core(keep, send)
-    ga, parts = lax.optimization_barrier((ga, parts))
-    plane = to_plane(parts)
+    plane_parts = over_core(ends)
+    plane = to_plane(plane_parts)
+    ga, parts = lax.optimization_barrier((ga, plane_parts))
     ig, v = input_grad(counts, x, ga, dm, cf, vec, me, wat, 0, n_img // NB, None)
     v, plane = lax.optimization_barrier((v, plane))
     own, others = plane_sum(parts[0], plane)
-    grads, sums = shares(own, over_line(others), v)
+    grads, sums = shares(own, over_line(others), v, rows)
     results = adam(me, total_over(sums), grads, state)
     return (out.reshape(images.shape), ig.reshape(images.shape), *turned_back(results[:15]), results[15].reshape(()))
 

time: 151 us -> 149 us (0.987)
  Pallas kernels: 79.8 us -> 55.3 us
  starting transfers between devices: 35.9 us -> 53.4 us
  waiting for transfers between devices: 24.6 us -> 28.2 us
    pallas_call x3, Pallas kernels: 61.3 us -> 40.2 us  [image_call(): pl.pallas_call(body, grid_spec=pltpu.PrefetchScalarGridSpec(num_scalar_pr...]
    ppermute x34 -> x37, starting transfers between devices: 35.9 us -> 53.4 us  [swap(): return lax.ppermute(x, AXES, [(i, i ^ bits) for i in range(32)])]
    ppermute x34 -> x37, waiting for transfers between devices: 24.6 us -> 28.2 us  [swap(): return lax.ppermute(x, AXES, [(i, i ^ bits) for i in range(32)])]
    pallas_call x1, Pallas kernels: 12.1 us -> 8.65 us  [input_grad(): pl.pallas_call(lambda *refs: input_grad_body(base, *refs), grid_spec=pltp...]
    unnamed x50 -> x52, local copies, waits for them, and re-layouts: 3.26 us -> 3.27 us
  transfers between devices with their start and end apart: 34 -> 37, of which waited for: 15 -> 17; matrix products, arithmetic and copies ran while one was open for 2% -> 4% of each run, Pallas kernels for 17% -> 13%
where the time goes in v4:
time: 149 us
  Pallas kernels  55.3 us (37%)
  starting transfers between devices  53.4 us (36%)
  waiting for transfers between devices  28.2 us (19%)
  other arithmetic  6.91 us (5%)
  local copies, waits for them, and re-layouts  3.27 us (2%)
  between operations  1.78 us (1%)
    ppermute x37, starting transfers between devices, swap(): return lax.ppermute(x, AXES, [(i, i ^ bits) for i in range(32)])  53.4 us
    pallas_call x3, Pallas kernels, image_call(): pl.pallas_call(body, grid_spec=pltpu.PrefetchScalarGridSpec(num_scalar_pr...  40.2 us
    ppermute x37, waiting for transfers between devices, swap(): return lax.ppermute(x, AXES, [(i, i ^ bits) for i in range(32)])  28.2 us
    pallas_call x1, Pallas kernels, input_grad(): pl.pallas_call(lambda *refs: input_grad_body(base, *refs), grid_spec=pltp...  8.65 us
    unnamed x52, local copies, waits for them, and re-layouts  3.27 us
  transfers between devices with their start and end apart: 37, of which 17 were waited for; matrix products, arithmetic and copies ran while one was open for 4% of the time, Pallas kernels for 13%

profile of v4, /device:TPU:0, one launch (start us, length us, event | category | flops | bytes accessed | tf_op | source)
XLA Modules:
  0.0 148.9 jit_solution(10842660182158821244)
XLA Ops:
  0.7 1.8 %pack_shards.1 = (bf16[160,128]{1,0:T(8,128)(2,1)}, bf16[240,128]{1,0:T(8,128)(2,1)}) custom-call(f32[18,32,64]{2,1,0:T(8,128)} %bitcast.83, f32[32,128]{1,0:T(8,128)} %bitcast.89, f32[64,96]{1,0:T(8,128)} %bitcast.87, f32[32,64]{1,0:T(8,128)} %bitcast.91, f32[1,96]{1,0:T(1,128)} %refs_18_.1), custom_call_target="tpu_custom_call" | custom-call | tf_op jit(solution)/shard_map/pack_shards/pallas_call | solution.py:638
  2.5 5.0 %collective-permute-start.5 = (bf16[160,128]{1,0:T(8,128)(2,1)}, bf16[160,128]{1,0:T(8,128)(2,1)S(1)}, u32[]{:S(2)}, u32[]{:S(2)}) collective-permute-start(bf16[160,128]{1,0:T(8,128)(2,1)} %get-tuple-element.87), channel_id=1, source_target_pairs={{0,24},{1,25},{2,26},{3,27},{4,28},{5,29},{6,30},{7,31},{8,16},{9,... | collective-permute-start | bytes 122888 | tf_op jit(solution)/shard_map/ppermute | solution.py:644
  7.5 0.6 collective-permute-start.3
  8.1 3.8 %collective-permute-start.2 = (bf16[240,128]{1,0:T(8,128)(2,1)}, bf16[240,128]{1,0:T(8,128)(2,1)S(1)}, u32[]{:S(2)}, u32[]{:S(2)}) collective-permute-start(bf16[240,128]{1,0:T(8,128)(2,1)} %get-tuple-element.94), channel_id=1, source_target_pairs={{0,24},{1,25},{2,26},{3,27},{4,28},{5,29},{6,30},{7,31},{8,16},{9,... | collective-permute-start | bytes 184328 | tf_op jit(solution)/shard_map/ppermute | solution.py:644
  11.9 0.7 convert_element_type.109
  12.7 1.3 collective-permute-done.4
  14.1 0.8 pad_maximum_fusion.1.refs_4_
  14.9 2.5 %collective-permute-start.8 = (bf16[4,160,128]{2,1,0:T(8,128)(2,1)S(1)}, bf16[4,160,128]{2,1,0:T(8,128)(2,1)S(1)}, u32[]{:S(2)}, u32[]{:S(2)}) collective-permute-start(bf16[4,160,128]{2,1,0:T(8,128)(2,1)S(1)} %pad_maximum_fusion.1.refs_4_), channel_id=1, source_target_pairs={{0,6},{1,7},{2,4},{3,5},{4,2},{5,3},{6,0},{7,1},{8,14},{9,15},{10,... | collective-permute-start | bytes 491528 | tf_op jit(solution)/shard_map/ppermute | solution.py:644
  17.4 0.5 collective-permute-start.7
  17.9 0.5 collective-permute-start.6
  18.5 0.6 multiply_convert_fusion.refs_5_
  19.1 0.6 pad_add_fusion.refs_3_.refs_7_.refs_6_.refs_0_
  20.4 3.3 %figures.1.refs_2_.refs_4_ = f32[16,8,256]{2,1,0:T(8,128)} custom-call(s32[1]{0:T(128)S(6)} %copy.37.cnt_ref.refs_0_, bf16[16,256,256]{2,1,0:T(8,128)(2,1)} %bitcast.108), custom_call_target="tpu_custom_call" | custom-call | flops 536870912 | bytes 8388608 | tf_op jit(solution)/shard_map/figures/pallas_call | solution.py:189
  24.8 2.5 %collective-permute-start.15 = (bf16[4,240,128]{2,1,0:T(8,128)(2,1)S(1)}, bf16[4,240,128]{2,1,0:T(8,128)(2,1)S(1)}, u32[]{:S(2)}, u32[]{:S(2)}) collective-permute-start(bf16[4,240,128]{2,1,0:T(8,128)(2,1)S(1)} %pad_maximum_fusion.refs_8_), channel_id=1, source_target_pairs={{0,6},{1,7},{2,4},{3,5},{4,2},{5,3},{6,0},{7,1},{8,14},{9,15},{10,... | collective-permute-start | bytes 737288 | tf_op jit(solution)/shard_map/ppermute | solution.py:644
  27.4 1.0 collective-permute-start.14
  29.1 0.7 copy-done.25
  29.8 7.8 %conv_one.1 = (f32[16,256,256]{2,1,0:T(8,128)}, bf16[16,256,256]{2,1,0:T(8,128)(2,1)}, bf16[2304,256]{1,0:T(8,128)(2,1)}, f32[16,256]{1,0:T(8,128)}) custom-call(s32[1]{0:T(128)S(6)} %copy.37.cnt_ref.refs_0_, bf16[16,256,256]{2,1,0:T(8,128)(2,1)} %bitcast.109, f32[16,8,256]{2,1,0:T(8,128)} %figures.1.refs_2_.refs_4_, ...), custom_call_target="tpu_custom_call" | custom-call | flops 9663676416 | bytes 41943040 | tf_op jit(solution)/shard_map/conv_one/pallas_call | solution.py:189
  37.6 1.4 collective-permute-done.14.refs_12_
  39.0 0.6 collective-permute-done.13.refs_10_
  42.9 29.2 %middle.1 = (f32[16,256,256]{2,1,0:T(8,128)}, bf16[16,256,256]{2,1,0:T(8,128)(2,1)}, f32[16,256,256]{2,1,0:T(8,128)}, bf16[4,384,128]{2,1,0:T(8,128)(2,1)}, bf16...) custom-call(s32[1]{0:T(128)S(6)} %copy.37.cnt_ref.refs_0_, ...), custom_call_target="tpu_custom_call" | custom-call | flops 57982058496 | bytes 184549376 | tf_op jit(solution)/shard_map/middle/pallas_call | solution.py:189
  72.1 8.7 %collective-permute-start.21 = (bf16[4,384,128]{2,1,0:T(8,128)(2,1)}, bf16[4,384,128]{2,1,0:T(8,128)(2,1)S(1)}, u32[]{:S(2)}, u32[]{:S(2)}) collective-permute-start(bf16[4,384,128]{2,1,0:T(8,128)(2,1)} %get-tuple-element.120), channel_id=1, source_target_pairs={{0,1},{1,0},{2,3},{3,2},{4,5},{5,4},{6,7},{7,6},{8,9},{9,8},{10,11... | collective-permute-start | bytes 1179656 | tf_op jit(solution)/shard_map/ppermute | solution.py:644
  81.4 1.0 collective-permute-done.21
  82.4 1.1 add_convert_fusion.2
  83.5 11.1 %collective-permute-start.24 = (bf16[4,384,128]{2,1,0:T(8,128)(2,1)S(1)}, bf16[4,384,128]{2,1,0:T(8,128)(2,1)S(1)}, u32[]{:S(2)}, u32[]{:S(2)}) collective-permute-start(bf16[4,384,128]{2,1,0:T(8,128)(2,1)S(1)} %add_convert_fusion.2), channel_id=1, source_target_pairs={{0,2},{1,3},{2,0},{3,1},{4,6},{5,7},{6,4},{7,5},{8,10},{9,11},{10,... | collective-permute-start | bytes 1179656 | tf_op jit(solution)/shard_map/ppermute | solution.py:644
  94.5 1.1 add_convert_fusion.1
  95.7 0.8 collective-permute-start.25
  96.6 0.9 collective-permute-start.26
  97.6 8.7 %input_grad.1 = (f32[16,256,256]{2,1,0:T(8,128)}, f32[8,128]{1,0:T(8,128)}) custom-call(s32[1]{0:T(128)S(6)} %copy.37.cnt_ref.refs_0_, bf16[16,256,256]{2,1,0:T(8,128)(2,1)} %bitcast.111, bf16[16,256,256]{2,1,0:T(8,128)(2,1)} %get-tuple-element.125.refs_2_, f32[16,256,256]{2,1,0:T(8,128)} %get-tuple-element.126.refs_3_, ...), custom_call_target="tpu_custom_call" | custom-call | flops 12884901888 | bytes 58720256 | tf_op jit(solution)/shard_map/input_grad/pallas_call | solution.py:586
  106.2 9.0 %collective-permute-done.25 = bf16[4,384,128]{2,1,0:T(8,128)(2,1)S(1)} collective-permute-done((bf16[4,384,128]{2,1,0:T(8,128)(2,1)S(1)}, bf16[4,384,128]{2,1,0:T(8,128)(2,1)S(1)}, u32[]{:S(2)}, u32[]{:S(2)}) %collective-permute-start.25) | collective-permute-done | bytes 393248 | tf_op jit(solution)/shard_map/ppermute | solution.py:644
  115.3 0.9 fusion.2
  116.1 4.0 %collective-permute-start.29 = (bf16[384,128]{1,0:T(8,128)(2,1)S(1)}, bf16[384,128]{1,0:T(8,128)(2,1)S(1)}, u32[]{:S(2)}, u32[]{:S(2)}) collective-permute-start(bf16[384,128]{1,0:T(8,128)(2,1)S(1)} %get-tuple-element.154), channel_id=1, source_target_pairs={{0,24},{1,25},{2,26},{3,27},{4,28},{5,29},{6,30},{7,31},{8,16},{9,... | collective-permute-start | bytes 294920 | tf_op jit(solution)/shard_map/ppermute | solution.py:644
  120.2 0.6 collective-permute-start.28
  120.8 2.9 %collective-permute-done.29.r3 = bf16[384,128]{1,0:T(8,128)(2,1)S(1)} collective-permute-done((bf16[384,128]{1,0:T(8,128)(2,1)S(1)}, bf16[384,128]{1,0:T(8,128)(2,1)S(1)}, u32[]{:S(2)}, u32[]{:S(2)}) %collective-permute-start.29) | collective-permute-done | bytes 98336 | tf_op jit(solution)/shard_map/ppermute | solution.py:644
  123.7 5.1 %collective-permute-done.28.r2 = bf16[384,128]{1,0:T(8,128)(2,1)S(1)} collective-permute-done((bf16[384,128]{1,0:T(8,128)(2,1)S(1)}, bf16[384,128]{1,0:T(8,128)(2,1)S(1)}, u32[]{:S(2)}, u32[]{:S(2)}) %collective-permute-start.28) | collective-permute-done | bytes 98336 | tf_op jit(solution)/shard_map/ppermute | solution.py:644
  128.8 0.6 copy-done.5
  129.4 1.9 %shares.1 = (f32[384,128]{1,0:T(8,128)}, f32[32,128]{1,0:T(8,128)}) custom-call(f32[384,128]{1,0:T(8,128)} %get-tuple-element.157.own, bf16[384,128]{1,0:T(8,128)(2,1)} %copy-done.6, bf16[384,128]{1,0:T(8,128)(2,1)} %copy-done.5, bf16[384,128]{1,0:T(8,128)(2,1)} %copy-done.4, f32[8,128]{1,0:T(8,128)} %get-tuple-element.134.first, ...), custom_call_target="tpu_custom_call" | custom-call | tf_op jit(solution)/shard_map/shares/pallas_call | solution.py:773
  131.3 1.4 collective-permute-done.30
  132.7 0.7 add.104
  133.4 1.4 collective-permute-start.33
  135.2 1.7 %collective-permute-start.31 = (f32[32,128]{1,0:T(8,128)S(1)}, f32[32,128]{1,0:T(8,128)S(1)}, u32[]{:S(2)}, u32[]{:S(2)}) collective-permute-start(f32[32,128]{1,0:T(8,128)S(1)} %add.104), channel_id=1, source_target_pairs={{0,2},{1,3},{2,0},{3,1},{4,6},{5,7},{6,4},{7,5},{8,10},{9,11},{10,... | collective-permute-start | bytes 49160 | tf_op jit(solution)/shard_map/ppermute | solution.py:644
  136.9 1.1 collective-permute-done.33
  138.1 0.5 collective-permute-done.32
  139.0 1.7 %collective-permute-start.36 = (f32[32,128]{1,0:T(8,128)S(1)}, f32[32,128]{1,0:T(8,128)S(1)}, u32[]{:S(2)}, u32[]{:S(2)}) collective-permute-start(f32[32,128]{1,0:T(8,128)S(1)} %add_add_fusion.refs_1_), channel_id=1, source_target_pairs={{0,24},{1,25},{2,26},{3,27},{4,28},{5,29},{6,30},{7,31},{8,16},{9,... | collective-permute-start | bytes 49160 | tf_op jit(solution)/shard_map/ppermute | solution.py:644
  140.6 2.8 %collective-permute-start.34 = (f32[32,128]{1,0:T(8,128)S(1)}, f32[32,128]{1,0:T(8,128)S(1)}, u32[]{:S(2)}, u32[]{:S(2)}) collective-permute-start(f32[32,128]{1,0:T(8,128)S(1)} %add_add_fusion.refs_1_), channel_id=1, source_target_pairs={{0,8},{1,9},{2,10},{3,11},{4,12},{5,13},{6,14},{7,15},{8,0},{9,1},... | collective-permute-start | bytes 49160 | tf_op jit(solution)/shard_map/ppermute | solution.py:644
  143.4 1.1 collective-permute-done.36.refs_4_
  144.6 0.7 collective-permute-done.35.refs_3_
  145.3 0.6 copy-done.10
  145.9 2.8 %clipped_adamw.1 = (f32[18,32,64]{2,1,0:T(8,128)}, f32[18,32,64]{2,1,0:T(8,128)}, f32[18,32,64]{2,1,0:T(8,128)}, f32[32,128]{1,0:T(8,128)}, f32[32,128]{1,0:T(8,...) custom-call(s32[2]{0:T(128)} %pad_add_fusion.refs_3_.refs_7_.refs_6_, ...), custom_call_target="tpu_custom_call" | custom-call | tf_op jit(solution)/shard_map/clipped_adamw/pallas_call | solution.py:832
  (99 shorter events, 6.9 us)
Async XLA Ops:
  2.5 10.3 %collective-permute-start.5 = (bf16[160,128]{1,0:T(8,128)(2,1)}, bf16[160,128]{1,0:T(8,128)(2,1)S(1)}, u32[]{:S(2)}, u32[]{:S(2)}) collective-permute-start(bf16[160,128]{1,0:T(8,128)(2,1)} %get-tuple-element.87), channel_id=1, source_target_pairs={{0,24},{1,25},{2,26},{3,27},{4,28},{5,29},{6,30},{7,31},{8,16},{9,... | collective-permute-start | bytes 122888 | tf_op jit(solution)/shard_map/ppermute | solution.py:644
  7.5 6.5 %collective-permute-start.4 = (bf16[160,128]{1,0:T(8,128)(2,1)}, bf16[160,128]{1,0:T(8,128)(2,1)S(1)}, u32[]{:S(2)}, u32[]{:S(2)}) collective-permute-start(bf16[160,128]{1,0:T(8,128)(2,1)} %get-tuple-element.87), channel_id=1, source_target_pairs={{0,16},{1,17},{2,18},{3,19},{4,20},{5,21},{6,22},{7,23},{8,24},{9,... | collective-permute-start | bytes 122888 | tf_op jit(solution)/shard_map/ppermute | solution.py:644
  7.5 6.5 %collective-permute-start.3 = (bf16[160,128]{1,0:T(8,128)(2,1)}, bf16[160,128]{1,0:T(8,128)(2,1)S(1)}, u32[]{:S(2)}, u32[]{:S(2)}) collective-permute-start(bf16[160,128]{1,0:T(8,128)(2,1)} %get-tuple-element.87), channel_id=1, source_target_pairs={{0,8},{1,9},{2,10},{3,11},{4,12},{5,13},{6,14},{7,15},{8,0},{9,1},... | collective-permute-start | bytes 122888 | tf_op jit(solution)/shard_map/ppermute | solution.py:644
  8.1 11.0 %collective-permute-start.2 = (bf16[240,128]{1,0:T(8,128)(2,1)}, bf16[240,128]{1,0:T(8,128)(2,1)S(1)}, u32[]{:S(2)}, u32[]{:S(2)}) collective-permute-start(bf16[240,128]{1,0:T(8,128)(2,1)} %get-tuple-element.94), channel_id=1, source_target_pairs={{0,24},{1,25},{2,26},{3,27},{4,28},{5,29},{6,30},{7,31},{8,16},{9,... | collective-permute-start | bytes 184328 | tf_op jit(solution)/shard_map/ppermute | solution.py:644
  11.9 11.7 %collective-permute-start.1 = (bf16[240,128]{1,0:T(8,128)(2,1)}, bf16[240,128]{1,0:T(8,128)(2,1)S(1)}, u32[]{:S(2)}, u32[]{:S(2)}) collective-permute-start(bf16[240,128]{1,0:T(8,128)(2,1)} %get-tuple-element.94), channel_id=1, source_target_pairs={{0,16},{1,17},{2,18},{3,19},{4,20},{5,21},{6,22},{7,23},{8,24},{9,... | collective-permute-start | bytes 184328 | tf_op jit(solution)/shard_map/ppermute | solution.py:644
  14.9 9.9 %copy-start.3 = (bf16[4,160,128]{2,1,0:T(8,128)(2,1)}, bf16[4,160,128]{2,1,0:T(8,128)(2,1)S(1)}, u32[]{:S(2)}) copy-start(bf16[4,160,128]{2,1,0:T(8,128)(2,1)S(1)} %pad_maximum_fusion.1.refs_4_) | copy-start | bytes 491524
  14.9 9.9 %copy-start.8 = (bf16[240,128]{1,0:T(8,128)(2,1)S(1)}, bf16[240,128]{1,0:T(8,128)(2,1)}, u32[]{:S(2)}) copy-start(bf16[240,128]{1,0:T(8,128)(2,1)} %get-tuple-element.94) | copy-start | bytes 184324
  14.9 8.7 %collective-permute-start.8 = (bf16[4,160,128]{2,1,0:T(8,128)(2,1)S(1)}, bf16[4,160,128]{2,1,0:T(8,128)(2,1)S(1)}, u32[]{:S(2)}, u32[]{:S(2)}) collective-permute-start(bf16[4,160,128]{2,1,0:T(8,128)(2,1)S(1)} %pad_maximum_fusion.1.refs_4_), channel_id=1, source_target_pairs={{0,6},{1,7},{2,4},{3,5},{4,2},{5,3},{6,0},{7,1},{8,14},{9,15},{10,... | collective-permute-start | bytes 491528 | tf_op jit(solution)/shard_map/ppermute | solution.py:644
  17.4 6.2 %collective-permute-start.7 = (bf16[4,160,128]{2,1,0:T(8,128)(2,1)S(1)}, bf16[4,160,128]{2,1,0:T(8,128)(2,1)S(1)}, u32[]{:S(2)}, u32[]{:S(2)}) collective-permute-start(bf16[4,160,128]{2,1,0:T(8,128)(2,1)S(1)} %pad_maximum_fusion.1.refs_4_), channel_id=1, source_target_pairs={{0,4},{1,5},{2,6},{3,7},{4,0},{5,1},{6,2},{7,3},{8,12},{9,13},{10,... | collective-permute-start | bytes 491528 | tf_op jit(solution)/shard_map/ppermute | solution.py:644
  17.9 5.7 %collective-permute-start.6 = (bf16[4,160,128]{2,1,0:T(8,128)(2,1)S(1)}, bf16[4,160,128]{2,1,0:T(8,128)(2,1)S(1)}, u32[]{:S(2)}, u32[]{:S(2)}) collective-permute-start(bf16[4,160,128]{2,1,0:T(8,128)(2,1)S(1)} %pad_maximum_fusion.1.refs_4_), channel_id=1, source_target_pairs={{0,2},{1,3},{2,0},{3,1},{4,6},{5,7},{6,4},{7,5},{8,10},{9,11},{10,... | collective-permute-start | bytes 491528 | tf_op jit(solution)/shard_map/ppermute | solution.py:644
  19.1 4.5 %collective-permute-start = (bf16[240,128]{1,0:T(8,128)(2,1)}, bf16[240,128]{1,0:T(8,128)(2,1)S(1)}, u32[]{:S(2)}, u32[]{:S(2)}) collective-permute-start(bf16[240,128]{1,0:T(8,128)(2,1)} %get-tuple-element.94), channel_id=1, source_target_pairs={{0,8},{1,9},{2,10},{3,11},{4,12},{5,13},{6,14},{7,15},{8,0},{9,1},... | collective-permute-start | bytes 184328 | tf_op jit(solution)/shard_map/ppermute | solution.py:644
  23.6 4.8 %copy-start.19 = (bf16[4,160,128]{2,1,0:T(8,128)(2,1)}, bf16[4,160,128]{2,1,0:T(8,128)(2,1)S(1)}, u32[]{:S(2)}) copy-start(bf16[4,160,128]{2,1,0:T(8,128)(2,1)S(1)} %collective-permute-done.8.refs_10_) | copy-start | bytes 491524
  23.7 4.8 %copy-start.20 = (bf16[4,160,128]{2,1,0:T(8,128)(2,1)}, bf16[4,160,128]{2,1,0:T(8,128)(2,1)S(1)}, u32[]{:S(2)}) copy-start(bf16[4,160,128]{2,1,0:T(8,128)(2,1)S(1)} %collective-permute-done.7.refs_8_) | copy-start | bytes 491524
  23.7 4.8 %copy-start.21 = (bf16[4,160,128]{2,1,0:T(8,128)(2,1)}, bf16[4,160,128]{2,1,0:T(8,128)(2,1)S(1)}, u32[]{:S(2)}) copy-start(bf16[4,160,128]{2,1,0:T(8,128)(2,1)S(1)} %collective-permute-done.6.refs_6_) | copy-start | bytes 491524
  23.7 3.7 %collective-permute-start.9 = (bf16[4,160,128]{2,1,0:T(8,128)(2,1)S(1)}, bf16[4,160,128]{2,1,0:T(8,128)(2,1)S(1)}, u32[]{:S(2)}, u32[]{:S(2)}) collective-permute-start(bf16[4,160,128]{2,1,0:T(8,128)(2,1)S(1)} %pad_maximum_fusion.1.refs_4_), channel_id=1, source_target_pairs={{0,1},{1,0},{2,3},{3,2},{4,5},{5,4},{6,7},{7,6},{8,9},{9,8},{10,11... | collective-permute-start | bytes 491528 | tf_op jit(solution)/shard_map/ppermute | solution.py:644
  23.8 4.6 %collective-permute-start.10 = (bf16[4,160,128]{2,1,0:T(8,128)(2,1)S(1)}, bf16[4,160,128]{2,1,0:T(8,128)(2,1)S(1)}, u32[]{:S(2)}, u32[]{:S(2)}) collective-permute-start(bf16[4,160,128]{2,1,0:T(8,128)(2,1)S(1)} %collective-permute-done.6.refs_6_), channel_id=1, source_target_pairs={{0,1},{1,0},{2,3},{3,2},{4,5},{5,4},{6,7},{7,6},{8,9},{9,8},{10,11... | collective-permute-start | bytes 491528 | tf_op jit(solution)/shard_map/ppermute | solution.py:644
  24.3 4.2 %collective-permute-start.11 = (bf16[4,160,128]{2,1,0:T(8,128)(2,1)S(1)}, bf16[4,160,128]{2,1,0:T(8,128)(2,1)S(1)}, u32[]{:S(2)}, u32[]{:S(2)}) collective-permute-start(bf16[4,160,128]{2,1,0:T(8,128)(2,1)S(1)} %collective-permute-done.7.refs_8_), channel_id=1, source_target_pairs={{0,1},{1,0},{2,3},{3,2},{4,5},{5,4},{6,7},{7,6},{8,9},{9,8},{10,11... | collective-permute-start | bytes 491528 | tf_op jit(solution)/shard_map/ppermute | solution.py:644
  24.3 4.1 %collective-permute-start.12 = (bf16[4,160,128]{2,1,0:T(8,128)(2,1)S(1)}, bf16[4,160,128]{2,1,0:T(8,128)(2,1)S(1)}, u32[]{:S(2)}, u32[]{:S(2)}) collective-permute-start(bf16[4,160,128]{2,1,0:T(8,128)(2,1)S(1)} %collective-permute-done.8.refs_10_), channel_id=1, source_target_pairs={{0,1},{1,0},{2,3},{3,2},{4,5},{5,4},{6,7},{7,6},{8,9},{9,8},{10,11... | collective-permute-start | bytes 491528 | tf_op jit(solution)/shard_map/ppermute | solution.py:644
  24.8 14.8 %copy-start.2 = (bf16[4,240,128]{2,1,0:T(8,128)(2,1)}, bf16[4,240,128]{2,1,0:T(8,128)(2,1)S(1)}, u32[]{:S(2)}) copy-start(bf16[4,240,128]{2,1,0:T(8,128)(2,1)S(1)} %pad_maximum_fusion.refs_8_) | copy-start | bytes 737284
  24.8 12.7 %collective-permute-start.15 = (bf16[4,240,128]{2,1,0:T(8,128)(2,1)S(1)}, bf16[4,240,128]{2,1,0:T(8,128)(2,1)S(1)}, u32[]{:S(2)}, u32[]{:S(2)}) collective-permute-start(bf16[4,240,128]{2,1,0:T(8,128)(2,1)S(1)} %pad_maximum_fusion.refs_8_), channel_id=1, source_target_pairs={{0,6},{1,7},{2,4},{3,5},{4,2},{5,3},{6,0},{7,1},{8,14},{9,15},{10,... | collective-permute-start | bytes 737288 | tf_op jit(solution)/shard_map/ppermute | solution.py:644
  27.4 11.7 %collective-permute-start.14 = (bf16[4,240,128]{2,1,0:T(8,128)(2,1)S(1)}, bf16[4,240,128]{2,1,0:T(8,128)(2,1)S(1)}, u32[]{:S(2)}, u32[]{:S(2)}) collective-permute-start(bf16[4,240,128]{2,1,0:T(8,128)(2,1)S(1)} %pad_maximum_fusion.refs_8_), channel_id=1, source_target_pairs={{0,4},{1,5},{2,6},{3,7},{4,0},{5,1},{6,2},{7,3},{8,12},{9,13},{10,... | collective-permute-start | bytes 737288 | tf_op jit(solution)/shard_map/ppermute | solution.py:644
  28.3 11.2 %collective-permute-start.13 = (bf16[4,240,128]{2,1,0:T(8,128)(2,1)S(1)}, bf16[4,240,128]{2,1,0:T(8,128)(2,1)S(1)}, u32[]{:S(2)}, u32[]{:S(2)}) collective-permute-start(bf16[4,240,128]{2,1,0:T(8,128)(2,1)S(1)} %pad_maximum_fusion.refs_8_), channel_id=1, source_target_pairs={{0,2},{1,3},{2,0},{3,1},{4,6},{5,7},{6,4},{7,5},{8,10},{9,11},{10,... | collective-permute-start | bytes 737288 | tf_op jit(solution)/shard_map/ppermute | solution.py:644
  37.6 4.6 %copy-start.12 = (bf16[4,240,128]{2,1,0:T(8,128)(2,1)}, bf16[4,240,128]{2,1,0:T(8,128)(2,1)S(1)}, u32[]{:S(2)}) copy-start(bf16[4,240,128]{2,1,0:T(8,128)(2,1)S(1)} %collective-permute-done.15.refs_14_) | copy-start | bytes 737284
  39.6 1.5 %collective-permute-start.16 = (bf16[4,240,128]{2,1,0:T(8,128)(2,1)S(1)}, bf16[4,240,128]{2,1,0:T(8,128)(2,1)S(1)}, u32[]{:S(2)}, u32[]{:S(2)}) collective-permute-start(bf16[4,240,128]{2,1,0:T(8,128)(2,1)S(1)} %pad_maximum_fusion.refs_8_), channel_id=1, source_target_pairs={{0,1},{1,0},{2,3},{3,2},{4,5},{5,4},{6,7},{7,6},{8,9},{9,8},{10,11... | collective-permute-start | bytes 737288 | tf_op jit(solution)/shard_map/ppermute | solution.py:644
  39.6 1.9 %collective-permute-start.17 = (bf16[4,240,128]{2,1,0:T(8,128)(2,1)S(1)}, bf16[4,240,128]{2,1,0:T(8,128)(2,1)S(1)}, u32[]{:S(2)}, u32[]{:S(2)}) collective-permute-start(bf16[4,240,128]{2,1,0:T(8,128)(2,1)S(1)} %collective-permute-done.13.refs_10_), channel_id=1, source_target_pairs={{0,1},{1,0},{2,3},{3,2},{4,5},{5,4},{6,7},{7,6},{8,9},{9,8},{10,11... | collective-permute-start | bytes 737288 | tf_op jit(solution)/shard_map/ppermute | solution.py:644
  40.1 1.7 %collective-permute-start.18 = (bf16[4,240,128]{2,1,0:T(8,128)(2,1)S(1)}, bf16[4,240,128]{2,1,0:T(8,128)(2,1)S(1)}, u32[]{:S(2)}, u32[]{:S(2)}) collective-permute-start(bf16[4,240,128]{2,1,0:T(8,128)(2,1)S(1)} %collective-permute-done.14.refs_12_), channel_id=1, source_target_pairs={{0,1},{1,0},{2,3},{3,2},{4,5},{5,4},{6,7},{7,6},{8,9},{9,8},{10,11... | collective-permute-start | bytes 737288 | tf_op jit(solution)/shard_map/ppermute | solution.py:644
  40.2 2.0 %collective-permute-start.19 = (bf16[4,240,128]{2,1,0:T(8,128)(2,1)S(1)}, bf16[4,240,128]{2,1,0:T(8,128)(2,1)S(1)}, u32[]{:S(2)}, u32[]{:S(2)}) collective-permute-start(bf16[4,240,128]{2,1,0:T(8,128)(2,1)S(1)} %collective-permute-done.15.refs_14_), channel_id=1, source_target_pairs={{0,1},{1,0},{2,3},{3,2},{4,5},{5,4},{6,7},{7,6},{8,9},{9,8},{10,11... | collective-permute-start | bytes 737288 | tf_op jit(solution)/shard_map/ppermute | solution.py:644
  72.0 24.4 %copy-start.1 = (bf16[4,384,128]{2,1,0:T(8,128)(2,1)S(1)}, bf16[4,384,128]{2,1,0:T(8,128)(2,1)}, u32[]{:S(2)}) copy-start(bf16[4,384,128]{2,1,0:T(8,128)(2,1)} %get-tuple-element.123) | copy-start | bytes 1179652
  72.1 25.4 %copy-start = (bf16[4,384,128]{2,1,0:T(8,128)(2,1)S(1)}, bf16[4,384,128]{2,1,0:T(8,128)(2,1)}, u32[]{:S(2)}) copy-start(bf16[4,384,128]{2,1,0:T(8,128)(2,1)} %get-tuple-element.117) | copy-start | bytes 1179652
  72.1 10.3 %collective-permute-start.21 = (bf16[4,384,128]{2,1,0:T(8,128)(2,1)}, bf16[4,384,128]{2,1,0:T(8,128)(2,1)S(1)}, u32[]{:S(2)}, u32[]{:S(2)}) collective-permute-start(bf16[4,384,128]{2,1,0:T(8,128)(2,1)} %get-tuple-element.120), channel_id=1, source_target_pairs={{0,1},{1,0},{2,3},{3,2},{4,5},{5,4},{6,7},{7,6},{8,9},{9,8},{10,11... | collective-permute-start | bytes 1179656 | tf_op jit(solution)/shard_map/ppermute | solution.py:644
  80.8 13.8 %collective-permute-start.22 = (bf16[4,384,128]{2,1,0:T(8,128)(2,1)}, bf16[4,384,128]{2,1,0:T(8,128)(2,1)S(1)}, u32[]{:S(2)}, u32[]{:S(2)}) collective-permute-start(bf16[4,384,128]{2,1,0:T(8,128)(2,1)} %get-tuple-element.122), channel_id=1, source_target_pairs={{0,1},{1,0},{2,3},{3,2},{4,5},{5,4},{6,7},{7,6},{8,9},{9,8},{10,11... | collective-permute-start | bytes 1179656 | tf_op jit(solution)/shard_map/ppermute | solution.py:644
  80.9 16.6 %collective-permute-start.20 = (bf16[4,384,128]{2,1,0:T(8,128)(2,1)}, bf16[4,384,128]{2,1,0:T(8,128)(2,1)S(1)}, u32[]{:S(2)}, u32[]{:S(2)}) collective-permute-start(bf16[4,384,128]{2,1,0:T(8,128)(2,1)} %get-tuple-element.118), channel_id=1, source_target_pairs={{0,1},{1,0},{2,3},{3,2},{4,5},{5,4},{6,7},{7,6},{8,9},{9,8},{10,11... | collective-permute-start | bytes 1179656 | tf_op jit(solution)/shard_map/ppermute | solution.py:644
  81.3 15.1 %collective-permute-start.23 = (bf16[4,384,128]{2,1,0:T(8,128)(2,1)}, bf16[4,384,128]{2,1,0:T(8,128)(2,1)S(1)}, u32[]{:S(2)}, u32[]{:S(2)}) collective-permute-start(bf16[4,384,128]{2,1,0:T(8,128)(2,1)} %get-tuple-element.124), channel_id=1, source_target_pairs={{0,1},{1,0},{2,3},{3,2},{4,5},{5,4},{6,7},{7,6},{8,9},{9,8},{10,11... | collective-permute-start | bytes 1179656 | tf_op jit(solution)/shard_map/ppermute | solution.py:644
  83.5 22.8 %collective-permute-start.24 = (bf16[4,384,128]{2,1,0:T(8,128)(2,1)S(1)}, bf16[4,384,128]{2,1,0:T(8,128)(2,1)S(1)}, u32[]{:S(2)}, u32[]{:S(2)}) collective-permute-start(bf16[4,384,128]{2,1,0:T(8,128)(2,1)S(1)} %add_convert_fusion.2), channel_id=1, source_target_pairs={{0,2},{1,3},{2,0},{3,1},{4,6},{5,7},{6,4},{7,5},{8,10},{9,11},{10,... | collective-permute-start | bytes 1179656 | tf_op jit(solution)/shard_map/ppermute | solution.py:644
  95.7 19.6 %collective-permute-start.25 = (bf16[4,384,128]{2,1,0:T(8,128)(2,1)S(1)}, bf16[4,384,128]{2,1,0:T(8,128)(2,1)S(1)}, u32[]{:S(2)}, u32[]{:S(2)}) collective-permute-start(bf16[4,384,128]{2,1,0:T(8,128)(2,1)S(1)} %add_convert_fusion.1), channel_id=1, source_target_pairs={{0,4},{1,5},{2,6},{3,7},{4,0},{5,1},{6,2},{7,3},{8,12},{9,13},{10,... | collective-permute-start | bytes 1179656 | tf_op jit(solution)/shard_map/ppermute | solution.py:644
  96.6 18.7 %collective-permute-start.26 = (bf16[4,384,128]{2,1,0:T(8,128)(2,1)S(1)}, bf16[4,384,128]{2,1,0:T(8,128)(2,1)S(1)}, u32[]{:S(2)}, u32[]{:S(2)}) collective-permute-start(bf16[4,384,128]{2,1,0:T(8,128)(2,1)S(1)} %add_convert_fusion), channel_id=1, source_target_pairs={{0,6},{1,7},{2,4},{3,5},{4,2},{5,3},{6,0},{7,1},{8,14},{9,15},{10,... | collective-permute-start | bytes 1179656 | tf_op jit(solution)/shard_map/ppermute | solution.py:644
  116.1 7.6 %collective-permute-start.29 = (bf16[384,128]{1,0:T(8,128)(2,1)S(1)}, bf16[384,128]{1,0:T(8,128)(2,1)S(1)}, u32[]{:S(2)}, u32[]{:S(2)}) collective-permute-start(bf16[384,128]{1,0:T(8,128)(2,1)S(1)} %get-tuple-element.154), channel_id=1, source_target_pairs={{0,24},{1,25},{2,26},{3,27},{4,28},{5,29},{6,30},{7,31},{8,16},{9,... | collective-permute-start | bytes 294920 | tf_op jit(solution)/shard_map/ppermute | solution.py:644
  120.2 8.6 %collective-permute-start.28 = (bf16[384,128]{1,0:T(8,128)(2,1)S(1)}, bf16[384,128]{1,0:T(8,128)(2,1)S(1)}, u32[]{:S(2)}, u32[]{:S(2)}) collective-permute-start(bf16[384,128]{1,0:T(8,128)(2,1)S(1)} %get-tuple-element.155), channel_id=1, source_target_pairs={{0,16},{1,17},{2,18},{3,19},{4,20},{5,21},{6,22},{7,23},{8,24},{9,... | collective-permute-start | bytes 294920 | tf_op jit(solution)/shard_map/ppermute | solution.py:644
  120.8 7.9 %collective-permute-start.27 = (bf16[384,128]{1,0:T(8,128)(2,1)S(1)}, bf16[384,128]{1,0:T(8,128)(2,1)S(1)}, u32[]{:S(2)}, u32[]{:S(2)}) collective-permute-start(bf16[384,128]{1,0:T(8,128)(2,1)S(1)} %get-tuple-element.156), channel_id=1, source_target_pairs={{0,8},{1,9},{2,10},{3,11},{4,12},{5,13},{6,14},{7,15},{8,0},{9,1},... | collective-permute-start | bytes 294920 | tf_op jit(solution)/shard_map/ppermute | solution.py:644
  123.7 5.1 %copy-start.4 = (bf16[384,128]{1,0:T(8,128)(2,1)}, bf16[384,128]{1,0:T(8,128)(2,1)S(1)}, u32[]{:S(2)}) copy-start(bf16[384,128]{1,0:T(8,128)(2,1)S(1)} %collective-permute-done.29.r3) | copy-start | bytes 294916
  131.3 1.4 collective-permute-start.30
  133.4 4.6 %collective-permute-start.33 = (f32[32,128]{1,0:T(8,128)S(1)}, f32[32,128]{1,0:T(8,128)S(1)}, u32[]{:S(2)}, u32[]{:S(2)}) collective-permute-start(f32[32,128]{1,0:T(8,128)S(1)} %add.104), channel_id=1, source_target_pairs={{0,6},{1,7},{2,4},{3,5},{4,2},{5,3},{6,0},{7,1},{8,14},{9,15},{10,... | collective-permute-start | bytes 49160 | tf_op jit(solution)/shard_map/ppermute | solution.py:644
  134.9 3.7 %collective-permute-start.32 = (f32[32,128]{1,0:T(8,128)S(1)}, f32[32,128]{1,0:T(8,128)S(1)}, u32[]{:S(2)}, u32[]{:S(2)}) collective-permute-start(f32[32,128]{1,0:T(8,128)S(1)} %add.104), channel_id=1, source_target_pairs={{0,4},{1,5},{2,6},{3,7},{4,0},{5,1},{6,2},{7,3},{8,12},{9,13},{10,... | collective-permute-start | bytes 49160 | tf_op jit(solution)/shard_map/ppermute | solution.py:644
  135.2 3.7 %collective-permute-start.31 = (f32[32,128]{1,0:T(8,128)S(1)}, f32[32,128]{1,0:T(8,128)S(1)}, u32[]{:S(2)}, u32[]{:S(2)}) collective-permute-start(f32[32,128]{1,0:T(8,128)S(1)} %add.104), channel_id=1, source_target_pairs={{0,2},{1,3},{2,0},{3,1},{4,6},{5,7},{6,4},{7,5},{8,10},{9,11},{10,... | collective-permute-start | bytes 49160 | tf_op jit(solution)/shard_map/ppermute | solution.py:644
  139.0 6.4 %copy-start.7 = (f32[32,128]{1,0:T(8,128)}, f32[32,128]{1,0:T(8,128)S(1)}, u32[]{:S(2)}) copy-start(f32[32,128]{1,0:T(8,128)S(1)} %add_add_fusion.refs_1_) | copy-start | bytes 49156
  139.0 5.6 %collective-permute-start.36 = (f32[32,128]{1,0:T(8,128)S(1)}, f32[32,128]{1,0:T(8,128)S(1)}, u32[]{:S(2)}, u32[]{:S(2)}) collective-permute-start(f32[32,128]{1,0:T(8,128)S(1)} %add_add_fusion.refs_1_), channel_id=1, source_target_pairs={{0,24},{1,25},{2,26},{3,27},{4,28},{5,29},{6,30},{7,31},{8,16},{9,... | collective-permute-start | bytes 49160 | tf_op jit(solution)/shard_map/ppermute | solution.py:644
  140.6 4.7 %collective-permute-start.35 = (f32[32,128]{1,0:T(8,128)S(1)}, f32[32,128]{1,0:T(8,128)S(1)}, u32[]{:S(2)}, u32[]{:S(2)}) collective-permute-start(f32[32,128]{1,0:T(8,128)S(1)} %add_add_fusion.refs_1_), channel_id=1, source_target_pairs={{0,16},{1,17},{2,18},{3,19},{4,20},{5,21},{6,22},{7,23},{8,24},{9,... | collective-permute-start | bytes 49160 | tf_op jit(solution)/shard_map/ppermute | solution.py:644
  140.6 4.7 %collective-permute-start.34 = (f32[32,128]{1,0:T(8,128)S(1)}, f32[32,128]{1,0:T(8,128)S(1)}, u32[]{:S(2)}, u32[]{:S(2)}) collective-permute-start(f32[32,128]{1,0:T(8,128)S(1)} %add_add_fusion.refs_1_), channel_id=1, source_target_pairs={{0,8},{1,9},{2,10},{3,11},{4,12},{5,13},{6,14},{7,15},{8,0},{9,1},... | collective-permute-start | bytes 49160 | tf_op jit(solution)/shard_map/ppermute | solution.py:644
  (15 other events, 15.3 us)

commit v5 on v4

--- a/solution.py
+++ b/solution.py
@@ -20,8 +20,8 @@
 decays_kind = (0.1, 0.1, 0.1, 0.1, 0.0)
 AXES = ("dp", "fsdp")
 VMEM = pltpu.CompilerParams(vmem_limit_bytes=60 * 2**20)
-NB = 4
-HB = 2
+NB = 8
+HB = 4
 CH = 32
 R = range(0, 256, CH)
 RA = 160

time: 149 us -> 149 us (level)
  starting transfers between devices: 53.4 us -> 54.9 us
    pallas_call x3, Pallas kernels: 40.2 us -> 38.7 us  [image_call(): pl.pallas_call(body, grid_spec=pltpu.PrefetchScalarGridSpec(num_scalar_pr...]
    ppermute x37, starting transfers between devices: 53.4 us -> 54.9 us  [swap(): return lax.ppermute(x, AXES, [(i, i ^ bits) for i in range(32)])]
  transfers between devices with their start and end apart: 37 -> 37, of which waited for: 17 -> 19; matrix products, arithmetic and copies ran while one was open for 4% -> 4% of each run, Pallas kernels for 13% -> 13%
where the time goes in v5:
time: 149 us; the launch traced here: 148 us
  starting transfers between devices  54.9 us (37%)
  Pallas kernels  54 us (36%)
  waiting for transfers between devices  27.5 us (18%)
  other arithmetic  6.91 us (5%)
  local copies, waits for them, and re-layouts  3.27 us (2%)
  between operations  1.74 us (1%)
    ppermute x37, starting transfers between devices, swap(): return lax.ppermute(x, AXES, [(i, i ^ bits) for i in range(32)])  54.9 us
    pallas_call x3, Pallas kernels, image_call(): pl.pallas_call(body, grid_spec=pltpu.PrefetchScalarGridSpec(num_scalar_pr...  38.7 us
    ppermute x37, waiting for transfers between devices, swap(): return lax.ppermute(x, AXES, [(i, i ^ bits) for i in range(32)])  27.5 us
    pallas_call x1, Pallas kernels, input_grad(): pl.pallas_call(lambda *refs: input_grad_body(base, *refs), grid_spec=pltp...  8.81 us
    unnamed x52, local copies, waits for them, and re-layouts  3.27 us
  transfers between devices with their start and end apart: 37, of which 19 were waited for; matrix products, arithmetic and copies ran while one was open for 4% of the time, Pallas kernels for 13%

profile of v5, /device:TPU:0, one launch (start us, length us, event | category | flops | bytes accessed | tf_op | source)
XLA Modules:
  0.0 148.3 jit_solution(15209651094249427817)
XLA Ops:
  0.7 1.8 %pack_shards.1 = (bf16[160,128]{1,0:T(8,128)(2,1)}, bf16[240,128]{1,0:T(8,128)(2,1)}) custom-call(f32[18,32,64]{2,1,0:T(8,128)} %bitcast.83, f32[32,128]{1,0:T(8,128)} %bitcast.89, f32[64,96]{1,0:T(8,128)} %bitcast.87, f32[32,64]{1,0:T(8,128)} %bitcast.91, f32[1,96]{1,0:T(1,128)} %refs_18_.1), custom_call_target="tpu_custom_call" | custom-call | tf_op jit(solution)/shard_map/pack_shards/pallas_call | solution.py:638
  2.5 5.0 %collective-permute-start.5 = (bf16[160,128]{1,0:T(8,128)(2,1)}, bf16[160,128]{1,0:T(8,128)(2,1)S(1)}, u32[]{:S(2)}, u32[]{:S(2)}) collective-permute-start(bf16[160,128]{1,0:T(8,128)(2,1)} %get-tuple-element.87), channel_id=1, source_target_pairs={{0,24},{1,25},{2,26},{3,27},{4,28},{5,29},{6,30},{7,31},{8,16},{9,... | collective-permute-start | bytes 122888 | tf_op jit(solution)/shard_map/ppermute | solution.py:644
  7.5 0.6 collective-permute-start.3
  8.1 3.8 %collective-permute-start.2 = (bf16[240,128]{1,0:T(8,128)(2,1)}, bf16[240,128]{1,0:T(8,128)(2,1)S(1)}, u32[]{:S(2)}, u32[]{:S(2)}) collective-permute-start(bf16[240,128]{1,0:T(8,128)(2,1)} %get-tuple-element.94), channel_id=1, source_target_pairs={{0,24},{1,25},{2,26},{3,27},{4,28},{5,29},{6,30},{7,31},{8,16},{9,... | collective-permute-start | bytes 184328 | tf_op jit(solution)/shard_map/ppermute | solution.py:644
  11.9 0.7 convert_element_type.109
  12.7 1.3 collective-permute-done.4
  14.1 0.8 pad_maximum_fusion.1.refs_4_
  14.9 2.5 %collective-permute-start.8 = (bf16[4,160,128]{2,1,0:T(8,128)(2,1)S(1)}, bf16[4,160,128]{2,1,0:T(8,128)(2,1)S(1)}, u32[]{:S(2)}, u32[]{:S(2)}) collective-permute-start(bf16[4,160,128]{2,1,0:T(8,128)(2,1)S(1)} %pad_maximum_fusion.1.refs_4_), channel_id=1, source_target_pairs={{0,6},{1,7},{2,4},{3,5},{4,2},{5,3},{6,0},{7,1},{8,14},{9,15},{10,... | collective-permute-start | bytes 491528 | tf_op jit(solution)/shard_map/ppermute | solution.py:644
  17.4 0.5 collective-permute-start.7
  17.9 0.5 collective-permute-start.6
  18.5 0.6 multiply_convert_fusion.refs_5_
  19.1 0.6 pad_add_fusion.refs_3_.refs_7_.refs_6_.refs_0_
  20.4 2.6 %figures.1.refs_2_.refs_4_ = f32[16,8,256]{2,1,0:T(8,128)} custom-call(s32[1]{0:T(128)S(6)} %copy.37.cnt_ref.refs_0_, bf16[16,256,256]{2,1,0:T(8,128)(2,1)} %bitcast.108), custom_call_target="tpu_custom_call" | custom-call | flops 536870912 | bytes 8388608 | tf_op jit(solution)/shard_map/figures/pallas_call | solution.py:189
  23.0 0.6 collective-permute-done
  23.7 0.5 collective-permute-start.10
  24.7 2.5 %collective-permute-start.15 = (bf16[4,240,128]{2,1,0:T(8,128)(2,1)S(1)}, bf16[4,240,128]{2,1,0:T(8,128)(2,1)S(1)}, u32[]{:S(2)}, u32[]{:S(2)}) collective-permute-start(bf16[4,240,128]{2,1,0:T(8,128)(2,1)S(1)} %pad_maximum_fusion.refs_8_), channel_id=1, source_target_pairs={{0,6},{1,7},{2,4},{3,5},{4,2},{5,3},{6,0},{7,1},{8,14},{9,15},{10,... | collective-permute-start | bytes 737288 | tf_op jit(solution)/shard_map/ppermute | solution.py:644
  27.2 0.7 collective-permute-start.14
  29.0 0.7 copy-done.25
  29.6 8.0 %conv_one.1 = (f32[16,256,256]{2,1,0:T(8,128)}, bf16[16,256,256]{2,1,0:T(8,128)(2,1)}, bf16[2304,256]{1,0:T(8,128)(2,1)}, f32[16,256]{1,0:T(8,128)}) custom-call(s32[1]{0:T(128)S(6)} %copy.37.cnt_ref.refs_0_, bf16[16,256,256]{2,1,0:T(8,128)(2,1)} %bitcast.109, f32[16,8,256]{2,1,0:T(8,128)} %figures.1.refs_2_.refs_4_, ...), custom_call_target="tpu_custom_call" | custom-call | flops 9663676416 | bytes 41943040 | tf_op jit(solution)/shard_map/conv_one/pallas_call | solution.py:189
  37.7 1.2 collective-permute-done.14.refs_12_
  39.1 0.5 collective-permute-start.17
  42.4 28.0 %middle.1 = (f32[16,256,256]{2,1,0:T(8,128)}, bf16[16,256,256]{2,1,0:T(8,128)(2,1)}, f32[16,256,256]{2,1,0:T(8,128)}, bf16[4,384,128]{2,1,0:T(8,128)(2,1)}, bf16...) custom-call(s32[1]{0:T(128)S(6)} %copy.37.cnt_ref.refs_0_, ...), custom_call_target="tpu_custom_call" | custom-call | flops 57982058496 | bytes 184549376 | tf_op jit(solution)/shard_map/middle/pallas_call | solution.py:189
  71.6 0.9 collective-permute-done.21
  72.5 1.1 add_convert_fusion.2
  73.6 21.2 %collective-permute-start.24 = (bf16[4,384,128]{2,1,0:T(8,128)(2,1)S(1)}, bf16[4,384,128]{2,1,0:T(8,128)(2,1)S(1)}, u32[]{:S(2)}, u32[]{:S(2)}) collective-permute-start(bf16[4,384,128]{2,1,0:T(8,128)(2,1)S(1)} %add_convert_fusion.2), channel_id=1, source_target_pairs={{0,2},{1,3},{2,0},{3,1},{4,6},{5,7},{6,4},{7,5},{8,10},{9,11},{10,... | collective-permute-start | bytes 1179656 | tf_op jit(solution)/shard_map/ppermute | solution.py:644
  94.8 1.1 add_convert_fusion.1
  96.1 1.5 %collective-permute-start.26 = (bf16[4,384,128]{2,1,0:T(8,128)(2,1)S(1)}, bf16[4,384,128]{2,1,0:T(8,128)(2,1)S(1)}, u32[]{:S(2)}, u32[]{:S(2)}) collective-permute-start(bf16[4,384,128]{2,1,0:T(8,128)(2,1)S(1)} %add_convert_fusion), channel_id=1, source_target_pairs={{0,6},{1,7},{2,4},{3,5},{4,2},{5,3},{6,0},{7,1},{8,14},{9,15},{10,... | collective-permute-start | bytes 1179656 | tf_op jit(solution)/shard_map/ppermute | solution.py:644
  97.8 8.8 %input_grad.1 = (f32[16,256,256]{2,1,0:T(8,128)}, f32[8,128]{1,0:T(8,128)}) custom-call(s32[1]{0:T(128)S(6)} %copy.37.cnt_ref.refs_0_, bf16[16,256,256]{2,1,0:T(8,128)(2,1)} %bitcast.111, bf16[16,256,256]{2,1,0:T(8,128)(2,1)} %get-tuple-element.125.refs_2_, f32[16,256,256]{2,1,0:T(8,128)} %get-tuple-element.126.refs_3_, ...), custom_call_target="tpu_custom_call" | custom-call | flops 12884901888 | bytes 58720256 | tf_op jit(solution)/shard_map/input_grad/pallas_call | solution.py:586
  106.6 8.7 %collective-permute-done.25 = bf16[4,384,128]{2,1,0:T(8,128)(2,1)S(1)} collective-permute-done((bf16[4,384,128]{2,1,0:T(8,128)(2,1)S(1)}, bf16[4,384,128]{2,1,0:T(8,128)(2,1)S(1)}, u32[]{:S(2)}, u32[]{:S(2)}) %collective-permute-start.25) | collective-permute-done | bytes 393248 | tf_op jit(solution)/shard_map/ppermute | solution.py:644
  115.2 0.9 fusion.2
  116.1 2.9 %collective-permute-start.29 = (bf16[384,128]{1,0:T(8,128)(2,1)S(1)}, bf16[384,128]{1,0:T(8,128)(2,1)S(1)}, u32[]{:S(2)}, u32[]{:S(2)}) collective-permute-start(bf16[384,128]{1,0:T(8,128)(2,1)S(1)} %get-tuple-element.154), channel_id=1, source_target_pairs={{0,24},{1,25},{2,26},{3,27},{4,28},{5,29},{6,30},{7,31},{8,16},{9,... | collective-permute-start | bytes 294920 | tf_op jit(solution)/shard_map/ppermute | solution.py:644
  119.4 1.1 collective-permute-start.27
  120.5 2.4 %collective-permute-done.29.r3 = bf16[384,128]{1,0:T(8,128)(2,1)S(1)} collective-permute-done((bf16[384,128]{1,0:T(8,128)(2,1)S(1)}, bf16[384,128]{1,0:T(8,128)(2,1)S(1)}, u32[]{:S(2)}, u32[]{:S(2)}) %collective-permute-start.29) | collective-permute-done | bytes 98336 | tf_op jit(solution)/shard_map/ppermute | solution.py:644
  122.9 4.9 %collective-permute-done.28.r2 = bf16[384,128]{1,0:T(8,128)(2,1)S(1)} collective-permute-done((bf16[384,128]{1,0:T(8,128)(2,1)S(1)}, bf16[384,128]{1,0:T(8,128)(2,1)S(1)}, u32[]{:S(2)}, u32[]{:S(2)}) %collective-permute-start.28) | collective-permute-done | bytes 98336 | tf_op jit(solution)/shard_map/ppermute | solution.py:644
  127.8 0.6 copy-done.5
  128.4 1.9 %shares.1 = (f32[384,128]{1,0:T(8,128)}, f32[32,128]{1,0:T(8,128)}) custom-call(f32[384,128]{1,0:T(8,128)} %get-tuple-element.157.own, bf16[384,128]{1,0:T(8,128)(2,1)} %copy-done.6, bf16[384,128]{1,0:T(8,128)(2,1)} %copy-done.5, bf16[384,128]{1,0:T(8,128)(2,1)} %copy-done.4, f32[8,128]{1,0:T(8,128)} %get-tuple-element.134.first, ...), custom_call_target="tpu_custom_call" | custom-call | tf_op jit(solution)/shard_map/shares/pallas_call | solution.py:773
  130.3 1.4 collective-permute-done.30
  131.7 0.7 add.104
  132.4 1.5 collective-permute-start.33
  134.2 1.8 %collective-permute-start.31 = (f32[32,128]{1,0:T(8,128)S(1)}, f32[32,128]{1,0:T(8,128)S(1)}, u32[]{:S(2)}, u32[]{:S(2)}) collective-permute-start(f32[32,128]{1,0:T(8,128)S(1)} %add.104), channel_id=1, source_target_pairs={{0,2},{1,3},{2,0},{3,1},{4,6},{5,7},{6,4},{7,5},{8,10},{9,11},{10,... | collective-permute-start | bytes 49160 | tf_op jit(solution)/shard_map/ppermute | solution.py:644
  135.9 1.1 collective-permute-done.33
  137.0 0.6 collective-permute-done.32
  137.9 2.2 %collective-permute-start.36 = (f32[32,128]{1,0:T(8,128)S(1)}, f32[32,128]{1,0:T(8,128)S(1)}, u32[]{:S(2)}, u32[]{:S(2)}) collective-permute-start(f32[32,128]{1,0:T(8,128)S(1)} %add_add_fusion.refs_1_), channel_id=1, source_target_pairs={{0,24},{1,25},{2,26},{3,27},{4,28},{5,29},{6,30},{7,31},{8,16},{9,... | collective-permute-start | bytes 49160 | tf_op jit(solution)/shard_map/ppermute | solution.py:644
  140.1 2.2 %collective-permute-start.34 = (f32[32,128]{1,0:T(8,128)S(1)}, f32[32,128]{1,0:T(8,128)S(1)}, u32[]{:S(2)}, u32[]{:S(2)}) collective-permute-start(f32[32,128]{1,0:T(8,128)S(1)} %add_add_fusion.refs_1_), channel_id=1, source_target_pairs={{0,8},{1,9},{2,10},{3,11},{4,12},{5,13},{6,14},{7,15},{8,0},{9,1},... | collective-permute-start | bytes 49160 | tf_op jit(solution)/shard_map/ppermute | solution.py:644
  142.4 1.3 collective-permute-done.36.refs_4_
  143.6 1.1 collective-permute-done.35.refs_3_
  144.8 0.6 copy-done.10
  145.4 2.8 %clipped_adamw.1 = (f32[18,32,64]{2,1,0:T(8,128)}, f32[18,32,64]{2,1,0:T(8,128)}, f32[18,32,64]{2,1,0:T(8,128)}, f32[32,128]{1,0:T(8,128)}, f32[32,128]{1,0:T(8,...) custom-call(s32[2]{0:T(128)} %pad_add_fusion.refs_3_.refs_7_.refs_6_, ...), custom_call_target="tpu_custom_call" | custom-call | tf_op jit(solution)/shard_map/clipped_adamw/pallas_call | solution.py:832
  (99 shorter events, 7.3 us)
Async XLA Ops:
  2.5 10.3 %collective-permute-start.5 = (bf16[160,128]{1,0:T(8,128)(2,1)}, bf16[160,128]{1,0:T(8,128)(2,1)S(1)}, u32[]{:S(2)}, u32[]{:S(2)}) collective-permute-start(bf16[160,128]{1,0:T(8,128)(2,1)} %get-tuple-element.87), channel_id=1, source_target_pairs={{0,24},{1,25},{2,26},{3,27},{4,28},{5,29},{6,30},{7,31},{8,16},{9,... | collective-permute-start | bytes 122888 | tf_op jit(solution)/shard_map/ppermute | solution.py:644
  7.5 6.5 %collective-permute-start.4 = (bf16[160,128]{1,0:T(8,128)(2,1)}, bf16[160,128]{1,0:T(8,128)(2,1)S(1)}, u32[]{:S(2)}, u32[]{:S(2)}) collective-permute-start(bf16[160,128]{1,0:T(8,128)(2,1)} %get-tuple-element.87), channel_id=1, source_target_pairs={{0,16},{1,17},{2,18},{3,19},{4,20},{5,21},{6,22},{7,23},{8,24},{9,... | collective-permute-start | bytes 122888 | tf_op jit(solution)/shard_map/ppermute | solution.py:644
  7.5 6.5 %collective-permute-start.3 = (bf16[160,128]{1,0:T(8,128)(2,1)}, bf16[160,128]{1,0:T(8,128)(2,1)S(1)}, u32[]{:S(2)}, u32[]{:S(2)}) collective-permute-start(bf16[160,128]{1,0:T(8,128)(2,1)} %get-tuple-element.87), channel_id=1, source_target_pairs={{0,8},{1,9},{2,10},{3,11},{4,12},{5,13},{6,14},{7,15},{8,0},{9,1},... | collective-permute-start | bytes 122888 | tf_op jit(solution)/shard_map/ppermute | solution.py:644
  8.1 11.0 %collective-permute-start.2 = (bf16[240,128]{1,0:T(8,128)(2,1)}, bf16[240,128]{1,0:T(8,128)(2,1)S(1)}, u32[]{:S(2)}, u32[]{:S(2)}) collective-permute-start(bf16[240,128]{1,0:T(8,128)(2,1)} %get-tuple-element.94), channel_id=1, source_target_pairs={{0,24},{1,25},{2,26},{3,27},{4,28},{5,29},{6,30},{7,31},{8,16},{9,... | collective-permute-start | bytes 184328 | tf_op jit(solution)/shard_map/ppermute | solution.py:644
  11.9 11.1 %collective-permute-start.1 = (bf16[240,128]{1,0:T(8,128)(2,1)}, bf16[240,128]{1,0:T(8,128)(2,1)S(1)}, u32[]{:S(2)}, u32[]{:S(2)}) collective-permute-start(bf16[240,128]{1,0:T(8,128)(2,1)} %get-tuple-element.94), channel_id=1, source_target_pairs={{0,16},{1,17},{2,18},{3,19},{4,20},{5,21},{6,22},{7,23},{8,24},{9,... | collective-permute-start | bytes 184328 | tf_op jit(solution)/shard_map/ppermute | solution.py:644
  14.9 9.8 %copy-start.3 = (bf16[4,160,128]{2,1,0:T(8,128)(2,1)}, bf16[4,160,128]{2,1,0:T(8,128)(2,1)S(1)}, u32[]{:S(2)}) copy-start(bf16[4,160,128]{2,1,0:T(8,128)(2,1)S(1)} %pad_maximum_fusion.1.refs_4_) | copy-start | bytes 491524
  14.9 9.8 %copy-start.8 = (bf16[240,128]{1,0:T(8,128)(2,1)S(1)}, bf16[240,128]{1,0:T(8,128)(2,1)}, u32[]{:S(2)}) copy-start(bf16[240,128]{1,0:T(8,128)(2,1)} %get-tuple-element.94) | copy-start | bytes 184324
  14.9 8.6 %collective-permute-start.8 = (bf16[4,160,128]{2,1,0:T(8,128)(2,1)S(1)}, bf16[4,160,128]{2,1,0:T(8,128)(2,1)S(1)}, u32[]{:S(2)}, u32[]{:S(2)}) collective-permute-start(bf16[4,160,128]{2,1,0:T(8,128)(2,1)S(1)} %pad_maximum_fusion.1.refs_4_), channel_id=1, source_target_pairs={{0,6},{1,7},{2,4},{3,5},{4,2},{5,3},{6,0},{7,1},{8,14},{9,15},{10,... | collective-permute-start | bytes 491528 | tf_op jit(solution)/shard_map/ppermute | solution.py:644
  17.4 6.2 %collective-permute-start.7 = (bf16[4,160,128]{2,1,0:T(8,128)(2,1)S(1)}, bf16[4,160,128]{2,1,0:T(8,128)(2,1)S(1)}, u32[]{:S(2)}, u32[]{:S(2)}) collective-permute-start(bf16[4,160,128]{2,1,0:T(8,128)(2,1)S(1)} %pad_maximum_fusion.1.refs_4_), channel_id=1, source_target_pairs={{0,4},{1,5},{2,6},{3,7},{4,0},{5,1},{6,2},{7,3},{8,12},{9,13},{10,... | collective-permute-start | bytes 491528 | tf_op jit(solution)/shard_map/ppermute | solution.py:644
  17.9 5.7 %collective-permute-start.6 = (bf16[4,160,128]{2,1,0:T(8,128)(2,1)S(1)}, bf16[4,160,128]{2,1,0:T(8,128)(2,1)S(1)}, u32[]{:S(2)}, u32[]{:S(2)}) collective-permute-start(bf16[4,160,128]{2,1,0:T(8,128)(2,1)S(1)} %pad_maximum_fusion.1.refs_4_), channel_id=1, source_target_pairs={{0,2},{1,3},{2,0},{3,1},{4,6},{5,7},{6,4},{7,5},{8,10},{9,11},{10,... | collective-permute-start | bytes 491528 | tf_op jit(solution)/shard_map/ppermute | solution.py:644
  19.1 4.4 %collective-permute-start = (bf16[240,128]{1,0:T(8,128)(2,1)}, bf16[240,128]{1,0:T(8,128)(2,1)S(1)}, u32[]{:S(2)}, u32[]{:S(2)}) collective-permute-start(bf16[240,128]{1,0:T(8,128)(2,1)} %get-tuple-element.94), channel_id=1, source_target_pairs={{0,8},{1,9},{2,10},{3,11},{4,12},{5,13},{6,14},{7,15},{8,0},{9,1},... | collective-permute-start | bytes 184328 | tf_op jit(solution)/shard_map/ppermute | solution.py:644
  23.5 4.8 %copy-start.19 = (bf16[4,160,128]{2,1,0:T(8,128)(2,1)}, bf16[4,160,128]{2,1,0:T(8,128)(2,1)S(1)}, u32[]{:S(2)}) copy-start(bf16[4,160,128]{2,1,0:T(8,128)(2,1)S(1)} %collective-permute-done.8.refs_10_) | copy-start | bytes 491524
  23.6 4.7 %copy-start.20 = (bf16[4,160,128]{2,1,0:T(8,128)(2,1)}, bf16[4,160,128]{2,1,0:T(8,128)(2,1)S(1)}, u32[]{:S(2)}) copy-start(bf16[4,160,128]{2,1,0:T(8,128)(2,1)S(1)} %collective-permute-done.7.refs_8_) | copy-start | bytes 491524
  23.6 4.7 %copy-start.21 = (bf16[4,160,128]{2,1,0:T(8,128)(2,1)}, bf16[4,160,128]{2,1,0:T(8,128)(2,1)S(1)}, u32[]{:S(2)}) copy-start(bf16[4,160,128]{2,1,0:T(8,128)(2,1)S(1)} %collective-permute-done.6.refs_6_) | copy-start | bytes 491524
  23.6 3.6 %collective-permute-start.9 = (bf16[4,160,128]{2,1,0:T(8,128)(2,1)S(1)}, bf16[4,160,128]{2,1,0:T(8,128)(2,1)S(1)}, u32[]{:S(2)}, u32[]{:S(2)}) collective-permute-start(bf16[4,160,128]{2,1,0:T(8,128)(2,1)S(1)} %pad_maximum_fusion.1.refs_4_), channel_id=1, source_target_pairs={{0,1},{1,0},{2,3},{3,2},{4,5},{5,4},{6,7},{7,6},{8,9},{9,8},{10,11... | collective-permute-start | bytes 491528 | tf_op jit(solution)/shard_map/ppermute | solution.py:644
  23.7 4.2 %collective-permute-start.10 = (bf16[4,160,128]{2,1,0:T(8,128)(2,1)S(1)}, bf16[4,160,128]{2,1,0:T(8,128)(2,1)S(1)}, u32[]{:S(2)}, u32[]{:S(2)}) collective-permute-start(bf16[4,160,128]{2,1,0:T(8,128)(2,1)S(1)} %collective-permute-done.6.refs_6_), channel_id=1, source_target_pairs={{0,1},{1,0},{2,3},{3,2},{4,5},{5,4},{6,7},{7,6},{8,9},{9,8},{10,11... | collective-permute-start | bytes 491528 | tf_op jit(solution)/shard_map/ppermute | solution.py:644
  24.2 4.1 %collective-permute-start.11 = (bf16[4,160,128]{2,1,0:T(8,128)(2,1)S(1)}, bf16[4,160,128]{2,1,0:T(8,128)(2,1)S(1)}, u32[]{:S(2)}, u32[]{:S(2)}) collective-permute-start(bf16[4,160,128]{2,1,0:T(8,128)(2,1)S(1)} %collective-permute-done.7.refs_8_), channel_id=1, source_target_pairs={{0,1},{1,0},{2,3},{3,2},{4,5},{5,4},{6,7},{7,6},{8,9},{9,8},{10,11... | collective-permute-start | bytes 491528 | tf_op jit(solution)/shard_map/ppermute | solution.py:644
  24.2 4.1 %collective-permute-start.12 = (bf16[4,160,128]{2,1,0:T(8,128)(2,1)S(1)}, bf16[4,160,128]{2,1,0:T(8,128)(2,1)S(1)}, u32[]{:S(2)}, u32[]{:S(2)}) collective-permute-start(bf16[4,160,128]{2,1,0:T(8,128)(2,1)S(1)} %collective-permute-done.8.refs_10_), channel_id=1, source_target_pairs={{0,1},{1,0},{2,3},{3,2},{4,5},{5,4},{6,7},{7,6},{8,9},{9,8},{10,11... | collective-permute-start | bytes 491528 | tf_op jit(solution)/shard_map/ppermute | solution.py:644
  24.7 14.4 %copy-start.2 = (bf16[4,240,128]{2,1,0:T(8,128)(2,1)}, bf16[4,240,128]{2,1,0:T(8,128)(2,1)S(1)}, u32[]{:S(2)}) copy-start(bf16[4,240,128]{2,1,0:T(8,128)(2,1)S(1)} %pad_maximum_fusion.refs_8_) | copy-start | bytes 737284
  24.7 12.9 %collective-permute-start.15 = (bf16[4,240,128]{2,1,0:T(8,128)(2,1)S(1)}, bf16[4,240,128]{2,1,0:T(8,128)(2,1)S(1)}, u32[]{:S(2)}, u32[]{:S(2)}) collective-permute-start(bf16[4,240,128]{2,1,0:T(8,128)(2,1)S(1)} %pad_maximum_fusion.refs_8_), channel_id=1, source_target_pairs={{0,6},{1,7},{2,4},{3,5},{4,2},{5,3},{6,0},{7,1},{8,14},{9,15},{10,... | collective-permute-start | bytes 737288 | tf_op jit(solution)/shard_map/ppermute | solution.py:644
  27.2 11.7 %collective-permute-start.14 = (bf16[4,240,128]{2,1,0:T(8,128)(2,1)S(1)}, bf16[4,240,128]{2,1,0:T(8,128)(2,1)S(1)}, u32[]{:S(2)}, u32[]{:S(2)}) collective-permute-start(bf16[4,240,128]{2,1,0:T(8,128)(2,1)S(1)} %pad_maximum_fusion.refs_8_), channel_id=1, source_target_pairs={{0,4},{1,5},{2,6},{3,7},{4,0},{5,1},{6,2},{7,3},{8,12},{9,13},{10,... | collective-permute-start | bytes 737288 | tf_op jit(solution)/shard_map/ppermute | solution.py:644
  27.9 11.2 %collective-permute-start.13 = (bf16[4,240,128]{2,1,0:T(8,128)(2,1)S(1)}, bf16[4,240,128]{2,1,0:T(8,128)(2,1)S(1)}, u32[]{:S(2)}, u32[]{:S(2)}) collective-permute-start(bf16[4,240,128]{2,1,0:T(8,128)(2,1)S(1)} %pad_maximum_fusion.refs_8_), channel_id=1, source_target_pairs={{0,2},{1,3},{2,0},{3,1},{4,6},{5,7},{6,4},{7,5},{8,10},{9,11},{10,... | collective-permute-start | bytes 737288 | tf_op jit(solution)/shard_map/ppermute | solution.py:644
  37.7 4.0 %copy-start.12 = (bf16[4,240,128]{2,1,0:T(8,128)(2,1)}, bf16[4,240,128]{2,1,0:T(8,128)(2,1)S(1)}, u32[]{:S(2)}) copy-start(bf16[4,240,128]{2,1,0:T(8,128)(2,1)S(1)} %collective-permute-done.15.refs_14_) | copy-start | bytes 737284
  39.1 1.5 %collective-permute-start.16 = (bf16[4,240,128]{2,1,0:T(8,128)(2,1)S(1)}, bf16[4,240,128]{2,1,0:T(8,128)(2,1)S(1)}, u32[]{:S(2)}, u32[]{:S(2)}) collective-permute-start(bf16[4,240,128]{2,1,0:T(8,128)(2,1)S(1)} %pad_maximum_fusion.refs_8_), channel_id=1, source_target_pairs={{0,1},{1,0},{2,3},{3,2},{4,5},{5,4},{6,7},{7,6},{8,9},{9,8},{10,11... | collective-permute-start | bytes 737288 | tf_op jit(solution)/shard_map/ppermute | solution.py:644
  39.1 1.9 %collective-permute-start.17 = (bf16[4,240,128]{2,1,0:T(8,128)(2,1)S(1)}, bf16[4,240,128]{2,1,0:T(8,128)(2,1)S(1)}, u32[]{:S(2)}, u32[]{:S(2)}) collective-permute-start(bf16[4,240,128]{2,1,0:T(8,128)(2,1)S(1)} %collective-permute-done.13.refs_10_), channel_id=1, source_target_pairs={{0,1},{1,0},{2,3},{3,2},{4,5},{5,4},{6,7},{7,6},{8,9},{9,8},{10,11... | collective-permute-start | bytes 737288 | tf_op jit(solution)/shard_map/ppermute | solution.py:644
  39.6 1.7 %collective-permute-start.18 = (bf16[4,240,128]{2,1,0:T(8,128)(2,1)S(1)}, bf16[4,240,128]{2,1,0:T(8,128)(2,1)S(1)}, u32[]{:S(2)}, u32[]{:S(2)}) collective-permute-start(bf16[4,240,128]{2,1,0:T(8,128)(2,1)S(1)} %collective-permute-done.14.refs_12_), channel_id=1, source_target_pairs={{0,1},{1,0},{2,3},{3,2},{4,5},{5,4},{6,7},{7,6},{8,9},{9,8},{10,11... | collective-permute-start | bytes 737288 | tf_op jit(solution)/shard_map/ppermute | solution.py:644
  39.7 2.0 %collective-permute-start.19 = (bf16[4,240,128]{2,1,0:T(8,128)(2,1)S(1)}, bf16[4,240,128]{2,1,0:T(8,128)(2,1)S(1)}, u32[]{:S(2)}, u32[]{:S(2)}) collective-permute-start(bf16[4,240,128]{2,1,0:T(8,128)(2,1)S(1)} %collective-permute-done.15.refs_14_), channel_id=1, source_target_pairs={{0,1},{1,0},{2,3},{3,2},{4,5},{5,4},{6,7},{7,6},{8,9},{9,8},{10,11... | collective-permute-start | bytes 737288 | tf_op jit(solution)/shard_map/ppermute | solution.py:644
  70.4 25.5 %copy-start.1 = (bf16[4,384,128]{2,1,0:T(8,128)(2,1)S(1)}, bf16[4,384,128]{2,1,0:T(8,128)(2,1)}, u32[]{:S(2)}) copy-start(bf16[4,384,128]{2,1,0:T(8,128)(2,1)} %get-tuple-element.123) | copy-start | bytes 1179652
  70.5 27.2 %copy-start = (bf16[4,384,128]{2,1,0:T(8,128)(2,1)S(1)}, bf16[4,384,128]{2,1,0:T(8,128)(2,1)}, u32[]{:S(2)}) copy-start(bf16[4,384,128]{2,1,0:T(8,128)(2,1)} %get-tuple-element.117) | copy-start | bytes 1179652
  70.5 2.0 %collective-permute-start.21 = (bf16[4,384,128]{2,1,0:T(8,128)(2,1)}, bf16[4,384,128]{2,1,0:T(8,128)(2,1)S(1)}, u32[]{:S(2)}, u32[]{:S(2)}) collective-permute-start(bf16[4,384,128]{2,1,0:T(8,128)(2,1)} %get-tuple-element.120), channel_id=1, source_target_pairs={{0,1},{1,0},{2,3},{3,2},{4,5},{5,4},{6,7},{7,6},{8,9},{9,8},{10,11... | collective-permute-start | bytes 1179656 | tf_op jit(solution)/shard_map/ppermute | solution.py:644
  70.7 24.1 %collective-permute-start.22 = (bf16[4,384,128]{2,1,0:T(8,128)(2,1)}, bf16[4,384,128]{2,1,0:T(8,128)(2,1)S(1)}, u32[]{:S(2)}, u32[]{:S(2)}) collective-permute-start(bf16[4,384,128]{2,1,0:T(8,128)(2,1)} %get-tuple-element.122), channel_id=1, source_target_pairs={{0,1},{1,0},{2,3},{3,2},{4,5},{5,4},{6,7},{7,6},{8,9},{9,8},{10,11... | collective-permute-start | bytes 1179656 | tf_op jit(solution)/shard_map/ppermute | solution.py:644
  71.0 26.6 %collective-permute-start.20 = (bf16[4,384,128]{2,1,0:T(8,128)(2,1)}, bf16[4,384,128]{2,1,0:T(8,128)(2,1)S(1)}, u32[]{:S(2)}, u32[]{:S(2)}) collective-permute-start(bf16[4,384,128]{2,1,0:T(8,128)(2,1)} %get-tuple-element.118), channel_id=1, source_target_pairs={{0,1},{1,0},{2,3},{3,2},{4,5},{5,4},{6,7},{7,6},{8,9},{9,8},{10,11... | collective-permute-start | bytes 1179656 | tf_op jit(solution)/shard_map/ppermute | solution.py:644
  71.2 24.8 %collective-permute-start.23 = (bf16[4,384,128]{2,1,0:T(8,128)(2,1)}, bf16[4,384,128]{2,1,0:T(8,128)(2,1)S(1)}, u32[]{:S(2)}, u32[]{:S(2)}) collective-permute-start(bf16[4,384,128]{2,1,0:T(8,128)(2,1)} %get-tuple-element.124), channel_id=1, source_target_pairs={{0,1},{1,0},{2,3},{3,2},{4,5},{5,4},{6,7},{7,6},{8,9},{9,8},{10,11... | collective-permute-start | bytes 1179656 | tf_op jit(solution)/shard_map/ppermute | solution.py:644
  73.6 33.0 %collective-permute-start.24 = (bf16[4,384,128]{2,1,0:T(8,128)(2,1)S(1)}, bf16[4,384,128]{2,1,0:T(8,128)(2,1)S(1)}, u32[]{:S(2)}, u32[]{:S(2)}) collective-permute-start(bf16[4,384,128]{2,1,0:T(8,128)(2,1)S(1)} %add_convert_fusion.2), channel_id=1, source_target_pairs={{0,2},{1,3},{2,0},{3,1},{4,6},{5,7},{6,4},{7,5},{8,10},{9,11},{10,... | collective-permute-start | bytes 1179656 | tf_op jit(solution)/shard_map/ppermute | solution.py:644
  95.9 19.4 %collective-permute-start.25 = (bf16[4,384,128]{2,1,0:T(8,128)(2,1)S(1)}, bf16[4,384,128]{2,1,0:T(8,128)(2,1)S(1)}, u32[]{:S(2)}, u32[]{:S(2)}) collective-permute-start(bf16[4,384,128]{2,1,0:T(8,128)(2,1)S(1)} %add_convert_fusion.1), channel_id=1, source_target_pairs={{0,4},{1,5},{2,6},{3,7},{4,0},{5,1},{6,2},{7,3},{8,12},{9,13},{10,... | collective-permute-start | bytes 1179656 | tf_op jit(solution)/shard_map/ppermute | solution.py:644
  96.1 19.1 %collective-permute-start.26 = (bf16[4,384,128]{2,1,0:T(8,128)(2,1)S(1)}, bf16[4,384,128]{2,1,0:T(8,128)(2,1)S(1)}, u32[]{:S(2)}, u32[]{:S(2)}) collective-permute-start(bf16[4,384,128]{2,1,0:T(8,128)(2,1)S(1)} %add_convert_fusion), channel_id=1, source_target_pairs={{0,6},{1,7},{2,4},{3,5},{4,2},{5,3},{6,0},{7,1},{8,14},{9,15},{10,... | collective-permute-start | bytes 1179656 | tf_op jit(solution)/shard_map/ppermute | solution.py:644
  116.1 6.7 %collective-permute-start.29 = (bf16[384,128]{1,0:T(8,128)(2,1)S(1)}, bf16[384,128]{1,0:T(8,128)(2,1)S(1)}, u32[]{:S(2)}, u32[]{:S(2)}) collective-permute-start(bf16[384,128]{1,0:T(8,128)(2,1)S(1)} %get-tuple-element.154), channel_id=1, source_target_pairs={{0,24},{1,25},{2,26},{3,27},{4,28},{5,29},{6,30},{7,31},{8,16},{9,... | collective-permute-start | bytes 294920 | tf_op jit(solution)/shard_map/ppermute | solution.py:644
  119.0 8.7 %collective-permute-start.28 = (bf16[384,128]{1,0:T(8,128)(2,1)S(1)}, bf16[384,128]{1,0:T(8,128)(2,1)S(1)}, u32[]{:S(2)}, u32[]{:S(2)}) collective-permute-start(bf16[384,128]{1,0:T(8,128)(2,1)S(1)} %get-tuple-element.155), channel_id=1, source_target_pairs={{0,16},{1,17},{2,18},{3,19},{4,20},{5,21},{6,22},{7,23},{8,24},{9,... | collective-permute-start | bytes 294920 | tf_op jit(solution)/shard_map/ppermute | solution.py:644
  119.4 8.3 %collective-permute-start.27 = (bf16[384,128]{1,0:T(8,128)(2,1)S(1)}, bf16[384,128]{1,0:T(8,128)(2,1)S(1)}, u32[]{:S(2)}, u32[]{:S(2)}) collective-permute-start(bf16[384,128]{1,0:T(8,128)(2,1)S(1)} %get-tuple-element.156), channel_id=1, source_target_pairs={{0,8},{1,9},{2,10},{3,11},{4,12},{5,13},{6,14},{7,15},{8,0},{9,1},... | collective-permute-start | bytes 294920 | tf_op jit(solution)/shard_map/ppermute | solution.py:644
  122.9 4.9 %copy-start.4 = (bf16[384,128]{1,0:T(8,128)(2,1)}, bf16[384,128]{1,0:T(8,128)(2,1)S(1)}, u32[]{:S(2)}) copy-start(bf16[384,128]{1,0:T(8,128)(2,1)S(1)} %collective-permute-done.29.r3) | copy-start | bytes 294916
  130.3 1.4 collective-permute-start.30
  132.4 4.6 %collective-permute-start.33 = (f32[32,128]{1,0:T(8,128)S(1)}, f32[32,128]{1,0:T(8,128)S(1)}, u32[]{:S(2)}, u32[]{:S(2)}) collective-permute-start(f32[32,128]{1,0:T(8,128)S(1)} %add.104), channel_id=1, source_target_pairs={{0,6},{1,7},{2,4},{3,5},{4,2},{5,3},{6,0},{7,1},{8,14},{9,15},{10,... | collective-permute-start | bytes 49160 | tf_op jit(solution)/shard_map/ppermute | solution.py:644
  133.9 3.7 %collective-permute-start.32 = (f32[32,128]{1,0:T(8,128)S(1)}, f32[32,128]{1,0:T(8,128)S(1)}, u32[]{:S(2)}, u32[]{:S(2)}) collective-permute-start(f32[32,128]{1,0:T(8,128)S(1)} %add.104), channel_id=1, source_target_pairs={{0,4},{1,5},{2,6},{3,7},{4,0},{5,1},{6,2},{7,3},{8,12},{9,13},{10,... | collective-permute-start | bytes 49160 | tf_op jit(solution)/shard_map/ppermute | solution.py:644
  134.2 3.7 %collective-permute-start.31 = (f32[32,128]{1,0:T(8,128)S(1)}, f32[32,128]{1,0:T(8,128)S(1)}, u32[]{:S(2)}, u32[]{:S(2)}) collective-permute-start(f32[32,128]{1,0:T(8,128)S(1)} %add.104), channel_id=1, source_target_pairs={{0,2},{1,3},{2,0},{3,1},{4,6},{5,7},{6,4},{7,5},{8,10},{9,11},{10,... | collective-permute-start | bytes 49160 | tf_op jit(solution)/shard_map/ppermute | solution.py:644
  137.9 6.9 %copy-start.7 = (f32[32,128]{1,0:T(8,128)}, f32[32,128]{1,0:T(8,128)S(1)}, u32[]{:S(2)}) copy-start(f32[32,128]{1,0:T(8,128)S(1)} %add_add_fusion.refs_1_) | copy-start | bytes 49156
  137.9 5.7 %collective-permute-start.36 = (f32[32,128]{1,0:T(8,128)S(1)}, f32[32,128]{1,0:T(8,128)S(1)}, u32[]{:S(2)}, u32[]{:S(2)}) collective-permute-start(f32[32,128]{1,0:T(8,128)S(1)} %add_add_fusion.refs_1_), channel_id=1, source_target_pairs={{0,24},{1,25},{2,26},{3,27},{4,28},{5,29},{6,30},{7,31},{8,16},{9,... | collective-permute-start | bytes 49160 | tf_op jit(solution)/shard_map/ppermute | solution.py:644
  140.1 4.6 %collective-permute-start.35 = (f32[32,128]{1,0:T(8,128)S(1)}, f32[32,128]{1,0:T(8,128)S(1)}, u32[]{:S(2)}, u32[]{:S(2)}) collective-permute-start(f32[32,128]{1,0:T(8,128)S(1)} %add_add_fusion.refs_1_), channel_id=1, source_target_pairs={{0,16},{1,17},{2,18},{3,19},{4,20},{5,21},{6,22},{7,23},{8,24},{9,... | collective-permute-start | bytes 49160 | tf_op jit(solution)/shard_map/ppermute | solution.py:644
  140.1 4.6 %collective-permute-start.34 = (f32[32,128]{1,0:T(8,128)S(1)}, f32[32,128]{1,0:T(8,128)S(1)}, u32[]{:S(2)}, u32[]{:S(2)}) collective-permute-start(f32[32,128]{1,0:T(8,128)S(1)} %add_add_fusion.refs_1_), channel_id=1, source_target_pairs={{0,8},{1,9},{2,10},{3,11},{4,12},{5,13},{6,14},{7,15},{8,0},{9,1},... | collective-permute-start | bytes 49160 | tf_op jit(solution)/shard_map/ppermute | solution.py:644
  (15 other events, 15.3 us)

commit v6 on v5

--- a/solution.py
+++ b/solution.py
@@ -22,7 +22,7 @@
 VMEM = pltpu.CompilerParams(vmem_limit_bytes=60 * 2**20)
 NB = 8
 HB = 4
-CH = 32
+CH = 64
 R = range(0, 256, CH)
 RA = 160
 RB = 240

time: 149 us -> 149 us (level)
  Pallas kernels: 54 us -> 80.1 us
  starting transfers between devices: 54.9 us -> 35.8 us
  waiting for transfers between devices: 27.5 us -> 21.1 us
    pallas_call x3, Pallas kernels: 38.7 us -> 60.9 us  [image_call(): pl.pallas_call(body, grid_spec=pltpu.PrefetchScalarGridSpec(num_scalar_pr...]
    ppermute x37, starting transfers between devices: 54.9 us -> 35.8 us  [swap(): return lax.ppermute(x, AXES, [(i, i ^ bits) for i in range(32)])]
    ppermute x37, waiting for transfers between devices: 27.5 us -> 21.1 us  [swap(): return lax.ppermute(x, AXES, [(i, i ^ bits) for i in range(32)])]
    pallas_call x1, Pallas kernels: 8.81 us -> 12.7 us  [input_grad(): pl.pallas_call(lambda *refs: input_grad_body(base, *refs), grid_spec=pltp...]
  transfers between devices with their start and end apart: 37 -> 37, of which waited for: 19 -> 14; matrix products, arithmetic and copies ran while one was open for 4% -> 4% of each run, Pallas kernels for 13% -> 17%
where the time goes in v6:
time: 149 us
  Pallas kernels  80.1 us (54%)
  starting transfers between devices  35.8 us (24%)
  waiting for transfers between devices  21.1 us (14%)
  other arithmetic  6.91 us (5%)
  local copies, waits for them, and re-layouts  3.28 us (2%)
  between operations  1.82 us (1%)
    pallas_call x3, Pallas kernels, image_call(): pl.pallas_call(body, grid_spec=pltpu.PrefetchScalarGridSpec(num_scalar_pr...  60.9 us
    ppermute x37, starting transfers between devices, swap(): return lax.ppermute(x, AXES, [(i, i ^ bits) for i in range(32)])  35.8 us
    ppermute x37, waiting for transfers between devices, swap(): return lax.ppermute(x, AXES, [(i, i ^ bits) for i in range(32)])  21.1 us
    pallas_call x1, Pallas kernels, input_grad(): pl.pallas_call(lambda *refs: input_grad_body(base, *refs), grid_spec=pltp...  12.7 us
    unnamed x52, local copies, waits for them, and re-layouts  3.28 us
  transfers between devices with their start and end apart: 37, of which 14 were waited for; matrix products, arithmetic and copies ran while one was open for 4% of the time, Pallas kernels for 17%

profile of v6, /device:TPU:0, one launch (start us, length us, event | category | flops | bytes accessed | tf_op | source)
XLA Modules:
  0.0 149.0 jit_solution(18213645070161528334)
XLA Ops:
  0.7 1.8 %pack_shards.1 = (bf16[160,128]{1,0:T(8,128)(2,1)}, bf16[240,128]{1,0:T(8,128)(2,1)}) custom-call(f32[18,32,64]{2,1,0:T(8,128)} %bitcast.83, f32[32,128]{1,0:T(8,128)} %bitcast.89, f32[64,96]{1,0:T(8,128)} %bitcast.87, f32[32,64]{1,0:T(8,128)} %bitcast.91, f32[1,96]{1,0:T(1,128)} %refs_18_.1), custom_call_target="tpu_custom_call" | custom-call | tf_op jit(solution)/shard_map/pack_shards/pallas_call | solution.py:638
  2.5 5.0 %collective-permute-start.5 = (bf16[160,128]{1,0:T(8,128)(2,1)}, bf16[160,128]{1,0:T(8,128)(2,1)S(1)}, u32[]{:S(2)}, u32[]{:S(2)}) collective-permute-start(bf16[160,128]{1,0:T(8,128)(2,1)} %get-tuple-element.87), channel_id=1, source_target_pairs={{0,24},{1,25},{2,26},{3,27},{4,28},{5,29},{6,30},{7,31},{8,16},{9,... | collective-permute-start | bytes 122888 | tf_op jit(solution)/shard_map/ppermute | solution.py:644
  7.5 0.6 collective-permute-start.3
  8.1 3.8 %collective-permute-start.2 = (bf16[240,128]{1,0:T(8,128)(2,1)}, bf16[240,128]{1,0:T(8,128)(2,1)S(1)}, u32[]{:S(2)}, u32[]{:S(2)}) collective-permute-start(bf16[240,128]{1,0:T(8,128)(2,1)} %get-tuple-element.94), channel_id=1, source_target_pairs={{0,24},{1,25},{2,26},{3,27},{4,28},{5,29},{6,30},{7,31},{8,16},{9,... | collective-permute-start | bytes 184328 | tf_op jit(solution)/shard_map/ppermute | solution.py:644
  11.9 0.7 convert_element_type.109
  12.7 1.3 collective-permute-done.4
  14.1 0.8 pad_maximum_fusion.1.refs_4_
  14.9 2.5 %collective-permute-start.8 = (bf16[4,160,128]{2,1,0:T(8,128)(2,1)S(1)}, bf16[4,160,128]{2,1,0:T(8,128)(2,1)S(1)}, u32[]{:S(2)}, u32[]{:S(2)}) collective-permute-start(bf16[4,160,128]{2,1,0:T(8,128)(2,1)S(1)} %pad_maximum_fusion.1.refs_4_), channel_id=1, source_target_pairs={{0,6},{1,7},{2,4},{3,5},{4,2},{5,3},{6,0},{7,1},{8,14},{9,15},{10,... | collective-permute-start | bytes 491528 | tf_op jit(solution)/shard_map/ppermute | solution.py:644
  17.4 0.5 collective-permute-start.7
  17.9 0.5 collective-permute-start.6
  18.5 0.6 multiply_convert_fusion.refs_5_
  19.1 0.6 pad_add_fusion.refs_3_.refs_7_.refs_6_.refs_0_
  20.4 3.3 %figures.1.refs_2_.refs_4_ = f32[16,8,256]{2,1,0:T(8,128)} custom-call(s32[1]{0:T(128)S(6)} %copy.37.cnt_ref.refs_0_, bf16[16,256,256]{2,1,0:T(8,128)(2,1)} %bitcast.108), custom_call_target="tpu_custom_call" | custom-call | flops 536870912 | bytes 8388608 | tf_op jit(solution)/shard_map/figures/pallas_call | solution.py:189
  24.8 2.4 %collective-permute-start.15 = (bf16[4,240,128]{2,1,0:T(8,128)(2,1)S(1)}, bf16[4,240,128]{2,1,0:T(8,128)(2,1)S(1)}, u32[]{:S(2)}, u32[]{:S(2)}) collective-permute-start(bf16[4,240,128]{2,1,0:T(8,128)(2,1)S(1)} %pad_maximum_fusion.refs_8_), channel_id=1, source_target_pairs={{0,6},{1,7},{2,4},{3,5},{4,2},{5,3},{6,0},{7,1},{8,14},{9,15},{10,... | collective-permute-start | bytes 737288 | tf_op jit(solution)/shard_map/ppermute | solution.py:644
  27.2 0.6 collective-permute-start.14
  27.9 0.5 collective-permute-start.13
  28.5 0.5 copy-done.24
  29.1 0.7 copy-done.25
  29.7 10.0 %conv_one.1 = (f32[16,256,256]{2,1,0:T(8,128)}, bf16[16,256,256]{2,1,0:T(8,128)(2,1)}, bf16[2304,256]{1,0:T(8,128)(2,1)}, f32[16,256]{1,0:T(8,128)}) custom-call(s32[1]{0:T(128)S(6)} %copy.37.cnt_ref.refs_0_, bf16[16,256,256]{2,1,0:T(8,128)(2,1)} %bitcast.109, f32[16,8,256]{2,1,0:T(8,128)} %figures.1.refs_2_.refs_4_, ...), custom_call_target="tpu_custom_call" | custom-call | flops 9663676416 | bytes 41943040 | tf_op jit(solution)/shard_map/conv_one/pallas_call | solution.py:189
  43.1 47.7 %middle.1 = (f32[16,256,256]{2,1,0:T(8,128)}, bf16[16,256,256]{2,1,0:T(8,128)(2,1)}, f32[16,256,256]{2,1,0:T(8,128)}, bf16[4,384,128]{2,1,0:T(8,128)(2,1)}, bf16...) custom-call(s32[1]{0:T(128)S(6)} %copy.37.cnt_ref.refs_0_, ...), custom_call_target="tpu_custom_call" | custom-call | flops 57982058496 | bytes 184549376 | tf_op jit(solution)/shard_map/middle/pallas_call | solution.py:189
  91.9 0.9 collective-permute-done.21
  92.8 1.1 add_convert_fusion.2
  94.0 1.6 %collective-permute-start.24 = (bf16[4,384,128]{2,1,0:T(8,128)(2,1)S(1)}, bf16[4,384,128]{2,1,0:T(8,128)(2,1)S(1)}, u32[]{:S(2)}, u32[]{:S(2)}) collective-permute-start(bf16[4,384,128]{2,1,0:T(8,128)(2,1)S(1)} %add_convert_fusion.2), channel_id=1, source_target_pairs={{0,2},{1,3},{2,0},{3,1},{4,6},{5,7},{6,4},{7,5},{8,10},{9,11},{10,... | collective-permute-start | bytes 1179656 | tf_op jit(solution)/shard_map/ppermute | solution.py:644
  95.5 1.1 add_convert_fusion.1
  96.9 2.0 %collective-permute-start.26 = (bf16[4,384,128]{2,1,0:T(8,128)(2,1)S(1)}, bf16[4,384,128]{2,1,0:T(8,128)(2,1)S(1)}, u32[]{:S(2)}, u32[]{:S(2)}) collective-permute-start(bf16[4,384,128]{2,1,0:T(8,128)(2,1)S(1)} %add_convert_fusion), channel_id=1, source_target_pairs={{0,6},{1,7},{2,4},{3,5},{4,2},{5,3},{6,0},{7,1},{8,14},{9,15},{10,... | collective-permute-start | bytes 1179656 | tf_op jit(solution)/shard_map/ppermute | solution.py:644
  99.0 12.7 %input_grad.1 = (f32[16,256,256]{2,1,0:T(8,128)}, f32[8,128]{1,0:T(8,128)}) custom-call(s32[1]{0:T(128)S(6)} %copy.37.cnt_ref.refs_0_, bf16[16,256,256]{2,1,0:T(8,128)(2,1)} %bitcast.111, bf16[16,256,256]{2,1,0:T(8,128)(2,1)} %get-tuple-element.125.refs_2_, f32[16,256,256]{2,1,0:T(8,128)} %get-tuple-element.126.refs_3_, ...), custom_call_target="tpu_custom_call" | custom-call | flops 12884901888 | bytes 58720256 | tf_op jit(solution)/shard_map/input_grad/pallas_call | solution.py:586
  111.7 4.3 %collective-permute-done.25 = bf16[4,384,128]{2,1,0:T(8,128)(2,1)S(1)} collective-permute-done((bf16[4,384,128]{2,1,0:T(8,128)(2,1)S(1)}, bf16[4,384,128]{2,1,0:T(8,128)(2,1)S(1)}, u32[]{:S(2)}, u32[]{:S(2)}) %collective-permute-start.25) | collective-permute-done | bytes 393248 | tf_op jit(solution)/shard_map/ppermute | solution.py:644
  116.0 0.9 fusion.2
  116.9 1.9 %collective-permute-start.29 = (bf16[384,128]{1,0:T(8,128)(2,1)S(1)}, bf16[384,128]{1,0:T(8,128)(2,1)S(1)}, u32[]{:S(2)}, u32[]{:S(2)}) collective-permute-start(bf16[384,128]{1,0:T(8,128)(2,1)S(1)} %get-tuple-element.154), channel_id=1, source_target_pairs={{0,24},{1,25},{2,26},{3,27},{4,28},{5,29},{6,30},{7,31},{8,16},{9,... | collective-permute-start | bytes 294920 | tf_op jit(solution)/shard_map/ppermute | solution.py:644
  118.8 1.6 %collective-permute-start.28 = (bf16[384,128]{1,0:T(8,128)(2,1)S(1)}, bf16[384,128]{1,0:T(8,128)(2,1)S(1)}, u32[]{:S(2)}, u32[]{:S(2)}) collective-permute-start(bf16[384,128]{1,0:T(8,128)(2,1)S(1)} %get-tuple-element.155), channel_id=1, source_target_pairs={{0,16},{1,17},{2,18},{3,19},{4,20},{5,21},{6,22},{7,23},{8,24},{9,... | collective-permute-start | bytes 294920 | tf_op jit(solution)/shard_map/ppermute | solution.py:644
  120.4 0.9 collective-permute-start.27
  121.3 3.1 %collective-permute-done.29.r3 = bf16[384,128]{1,0:T(8,128)(2,1)S(1)} collective-permute-done((bf16[384,128]{1,0:T(8,128)(2,1)S(1)}, bf16[384,128]{1,0:T(8,128)(2,1)S(1)}, u32[]{:S(2)}, u32[]{:S(2)}) %collective-permute-start.29) | collective-permute-done | bytes 98336 | tf_op jit(solution)/shard_map/ppermute | solution.py:644
  124.4 3.9 %collective-permute-done.28.r2 = bf16[384,128]{1,0:T(8,128)(2,1)S(1)} collective-permute-done((bf16[384,128]{1,0:T(8,128)(2,1)S(1)}, bf16[384,128]{1,0:T(8,128)(2,1)S(1)}, u32[]{:S(2)}, u32[]{:S(2)}) %collective-permute-start.28) | collective-permute-done | bytes 98336 | tf_op jit(solution)/shard_map/ppermute | solution.py:644
  128.4 0.6 copy-done.5
  129.0 1.9 %shares.1 = (f32[384,128]{1,0:T(8,128)}, f32[32,128]{1,0:T(8,128)}) custom-call(f32[384,128]{1,0:T(8,128)} %get-tuple-element.157.own, bf16[384,128]{1,0:T(8,128)(2,1)} %copy-done.6, bf16[384,128]{1,0:T(8,128)(2,1)} %copy-done.5, bf16[384,128]{1,0:T(8,128)(2,1)} %copy-done.4, f32[8,128]{1,0:T(8,128)} %get-tuple-element.134.first, ...), custom_call_target="tpu_custom_call" | custom-call | tf_op jit(solution)/shard_map/shares/pallas_call | solution.py:773
  130.9 1.4 collective-permute-done.30
  132.3 0.7 add.104
  133.0 0.8 collective-permute-start.33
  133.8 1.3 collective-permute-start.32
  135.1 1.4 collective-permute-start.31
  136.5 1.3 collective-permute-done.33
  137.8 1.0 collective-permute-done.31
  138.8 2.0 %collective-permute-start.36 = (f32[32,128]{1,0:T(8,128)S(1)}, f32[32,128]{1,0:T(8,128)S(1)}, u32[]{:S(2)}, u32[]{:S(2)}) collective-permute-start(f32[32,128]{1,0:T(8,128)S(1)} %add_add_fusion.refs_1_), channel_id=1, source_target_pairs={{0,24},{1,25},{2,26},{3,27},{4,28},{5,29},{6,30},{7,31},{8,16},{9,... | collective-permute-start | bytes 49160 | tf_op jit(solution)/shard_map/ppermute | solution.py:644
  140.8 2.4 %collective-permute-start.34 = (f32[32,128]{1,0:T(8,128)S(1)}, f32[32,128]{1,0:T(8,128)S(1)}, u32[]{:S(2)}, u32[]{:S(2)}) collective-permute-start(f32[32,128]{1,0:T(8,128)S(1)} %add_add_fusion.refs_1_), channel_id=1, source_target_pairs={{0,8},{1,9},{2,10},{3,11},{4,12},{5,13},{6,14},{7,15},{8,0},{9,1},... | collective-permute-start | bytes 49160 | tf_op jit(solution)/shard_map/ppermute | solution.py:644
  143.3 1.1 collective-permute-done.36.refs_4_
  144.4 1.0 collective-permute-done.35.refs_3_
  145.5 0.6 copy-done.10
  146.1 2.8 %clipped_adamw.1 = (f32[18,32,64]{2,1,0:T(8,128)}, f32[18,32,64]{2,1,0:T(8,128)}, f32[18,32,64]{2,1,0:T(8,128)}, f32[32,128]{1,0:T(8,128)}, f32[32,128]{1,0:T(8,...) custom-call(s32[2]{0:T(128)} %pad_add_fusion.refs_3_.refs_7_.refs_6_, ...), custom_call_target="tpu_custom_call" | custom-call | tf_op jit(solution)/shard_map/clipped_adamw/pallas_call | solution.py:832
  (99 shorter events, 6.3 us)
Async XLA Ops:
  2.5 10.3 %collective-permute-start.5 = (bf16[160,128]{1,0:T(8,128)(2,1)}, bf16[160,128]{1,0:T(8,128)(2,1)S(1)}, u32[]{:S(2)}, u32[]{:S(2)}) collective-permute-start(bf16[160,128]{1,0:T(8,128)(2,1)} %get-tuple-element.87), channel_id=1, source_target_pairs={{0,24},{1,25},{2,26},{3,27},{4,28},{5,29},{6,30},{7,31},{8,16},{9,... | collective-permute-start | bytes 122888 | tf_op jit(solution)/shard_map/ppermute | solution.py:644
  7.5 6.5 %collective-permute-start.4 = (bf16[160,128]{1,0:T(8,128)(2,1)}, bf16[160,128]{1,0:T(8,128)(2,1)S(1)}, u32[]{:S(2)}, u32[]{:S(2)}) collective-permute-start(bf16[160,128]{1,0:T(8,128)(2,1)} %get-tuple-element.87), channel_id=1, source_target_pairs={{0,16},{1,17},{2,18},{3,19},{4,20},{5,21},{6,22},{7,23},{8,24},{9,... | collective-permute-start | bytes 122888 | tf_op jit(solution)/shard_map/ppermute | solution.py:644
  7.5 6.5 %collective-permute-start.3 = (bf16[160,128]{1,0:T(8,128)(2,1)}, bf16[160,128]{1,0:T(8,128)(2,1)S(1)}, u32[]{:S(2)}, u32[]{:S(2)}) collective-permute-start(bf16[160,128]{1,0:T(8,128)(2,1)} %get-tuple-element.87), channel_id=1, source_target_pairs={{0,8},{1,9},{2,10},{3,11},{4,12},{5,13},{6,14},{7,15},{8,0},{9,1},... | collective-permute-start | bytes 122888 | tf_op jit(solution)/shard_map/ppermute | solution.py:644
  8.1 11.0 %collective-permute-start.2 = (bf16[240,128]{1,0:T(8,128)(2,1)}, bf16[240,128]{1,0:T(8,128)(2,1)S(1)}, u32[]{:S(2)}, u32[]{:S(2)}) collective-permute-start(bf16[240,128]{1,0:T(8,128)(2,1)} %get-tuple-element.94), channel_id=1, source_target_pairs={{0,24},{1,25},{2,26},{3,27},{4,28},{5,29},{6,30},{7,31},{8,16},{9,... | collective-permute-start | bytes 184328 | tf_op jit(solution)/shard_map/ppermute | solution.py:644
  11.9 11.7 %collective-permute-start.1 = (bf16[240,128]{1,0:T(8,128)(2,1)}, bf16[240,128]{1,0:T(8,128)(2,1)S(1)}, u32[]{:S(2)}, u32[]{:S(2)}) collective-permute-start(bf16[240,128]{1,0:T(8,128)(2,1)} %get-tuple-element.94), channel_id=1, source_target_pairs={{0,16},{1,17},{2,18},{3,19},{4,20},{5,21},{6,22},{7,23},{8,24},{9,... | collective-permute-start | bytes 184328 | tf_op jit(solution)/shard_map/ppermute | solution.py:644
  14.9 9.9 %copy-start.3 = (bf16[4,160,128]{2,1,0:T(8,128)(2,1)}, bf16[4,160,128]{2,1,0:T(8,128)(2,1)S(1)}, u32[]{:S(2)}) copy-start(bf16[4,160,128]{2,1,0:T(8,128)(2,1)S(1)} %pad_maximum_fusion.1.refs_4_) | copy-start | bytes 491524
  14.9 9.9 %copy-start.8 = (bf16[240,128]{1,0:T(8,128)(2,1)S(1)}, bf16[240,128]{1,0:T(8,128)(2,1)}, u32[]{:S(2)}) copy-start(bf16[240,128]{1,0:T(8,128)(2,1)} %get-tuple-element.94) | copy-start | bytes 184324
  14.9 8.7 %collective-permute-start.8 = (bf16[4,160,128]{2,1,0:T(8,128)(2,1)S(1)}, bf16[4,160,128]{2,1,0:T(8,128)(2,1)S(1)}, u32[]{:S(2)}, u32[]{:S(2)}) collective-permute-start(bf16[4,160,128]{2,1,0:T(8,128)(2,1)S(1)} %pad_maximum_fusion.1.refs_4_), channel_id=1, source_target_pairs={{0,6},{1,7},{2,4},{3,5},{4,2},{5,3},{6,0},{7,1},{8,14},{9,15},{10,... | collective-permute-start | bytes 491528 | tf_op jit(solution)/shard_map/ppermute | solution.py:644
  17.4 6.2 %collective-permute-start.7 = (bf16[4,160,128]{2,1,0:T(8,128)(2,1)S(1)}, bf16[4,160,128]{2,1,0:T(8,128)(2,1)S(1)}, u32[]{:S(2)}, u32[]{:S(2)}) collective-permute-start(bf16[4,160,128]{2,1,0:T(8,128)(2,1)S(1)} %pad_maximum_fusion.1.refs_4_), channel_id=1, source_target_pairs={{0,4},{1,5},{2,6},{3,7},{4,0},{5,1},{6,2},{7,3},{8,12},{9,13},{10,... | collective-permute-start | bytes 491528 | tf_op jit(solution)/shard_map/ppermute | solution.py:644
  17.9 5.8 %collective-permute-start.6 = (bf16[4,160,128]{2,1,0:T(8,128)(2,1)S(1)}, bf16[4,160,128]{2,1,0:T(8,128)(2,1)S(1)}, u32[]{:S(2)}, u32[]{:S(2)}) collective-permute-start(bf16[4,160,128]{2,1,0:T(8,128)(2,1)S(1)} %pad_maximum_fusion.1.refs_4_), channel_id=1, source_target_pairs={{0,2},{1,3},{2,0},{3,1},{4,6},{5,7},{6,4},{7,5},{8,10},{9,11},{10,... | collective-permute-start | bytes 491528 | tf_op jit(solution)/shard_map/ppermute | solution.py:644
  19.1 4.5 %collective-permute-start = (bf16[240,128]{1,0:T(8,128)(2,1)}, bf16[240,128]{1,0:T(8,128)(2,1)S(1)}, u32[]{:S(2)}, u32[]{:S(2)}) collective-permute-start(bf16[240,128]{1,0:T(8,128)(2,1)} %get-tuple-element.94), channel_id=1, source_target_pairs={{0,8},{1,9},{2,10},{3,11},{4,12},{5,13},{6,14},{7,15},{8,0},{9,1},... | collective-permute-start | bytes 184328 | tf_op jit(solution)/shard_map/ppermute | solution.py:644
  23.6 4.8 %copy-start.19 = (bf16[4,160,128]{2,1,0:T(8,128)(2,1)}, bf16[4,160,128]{2,1,0:T(8,128)(2,1)S(1)}, u32[]{:S(2)}) copy-start(bf16[4,160,128]{2,1,0:T(8,128)(2,1)S(1)} %collective-permute-done.8.refs_10_) | copy-start | bytes 491524
  23.7 4.8 %copy-start.20 = (bf16[4,160,128]{2,1,0:T(8,128)(2,1)}, bf16[4,160,128]{2,1,0:T(8,128)(2,1)S(1)}, u32[]{:S(2)}) copy-start(bf16[4,160,128]{2,1,0:T(8,128)(2,1)S(1)} %collective-permute-done.7.refs_8_) | copy-start | bytes 491524
  23.7 4.8 %copy-start.21 = (bf16[4,160,128]{2,1,0:T(8,128)(2,1)}, bf16[4,160,128]{2,1,0:T(8,128)(2,1)S(1)}, u32[]{:S(2)}) copy-start(bf16[4,160,128]{2,1,0:T(8,128)(2,1)S(1)} %collective-permute-done.6.refs_6_) | copy-start | bytes 491524
  23.7 3.5 %collective-permute-start.9 = (bf16[4,160,128]{2,1,0:T(8,128)(2,1)S(1)}, bf16[4,160,128]{2,1,0:T(8,128)(2,1)S(1)}, u32[]{:S(2)}, u32[]{:S(2)}) collective-permute-start(bf16[4,160,128]{2,1,0:T(8,128)(2,1)S(1)} %pad_maximum_fusion.1.refs_4_), channel_id=1, source_target_pairs={{0,1},{1,0},{2,3},{3,2},{4,5},{5,4},{6,7},{7,6},{8,9},{9,8},{10,11... | collective-permute-start | bytes 491528 | tf_op jit(solution)/shard_map/ppermute | solution.py:644
  23.8 4.1 %collective-permute-start.10 = (bf16[4,160,128]{2,1,0:T(8,128)(2,1)S(1)}, bf16[4,160,128]{2,1,0:T(8,128)(2,1)S(1)}, u32[]{:S(2)}, u32[]{:S(2)}) collective-permute-start(bf16[4,160,128]{2,1,0:T(8,128)(2,1)S(1)} %collective-permute-done.6.refs_6_), channel_id=1, source_target_pairs={{0,1},{1,0},{2,3},{3,2},{4,5},{5,4},{6,7},{7,6},{8,9},{9,8},{10,11... | collective-permute-start | bytes 491528 | tf_op jit(solution)/shard_map/ppermute | solution.py:644
  24.3 4.1 %collective-permute-start.11 = (bf16[4,160,128]{2,1,0:T(8,128)(2,1)S(1)}, bf16[4,160,128]{2,1,0:T(8,128)(2,1)S(1)}, u32[]{:S(2)}, u32[]{:S(2)}) collective-permute-start(bf16[4,160,128]{2,1,0:T(8,128)(2,1)S(1)} %collective-permute-done.7.refs_8_), channel_id=1, source_target_pairs={{0,1},{1,0},{2,3},{3,2},{4,5},{5,4},{6,7},{7,6},{8,9},{9,8},{10,11... | collective-permute-start | bytes 491528 | tf_op jit(solution)/shard_map/ppermute | solution.py:644
  24.4 4.1 %collective-permute-start.12 = (bf16[4,160,128]{2,1,0:T(8,128)(2,1)S(1)}, bf16[4,160,128]{2,1,0:T(8,128)(2,1)S(1)}, u32[]{:S(2)}, u32[]{:S(2)}) collective-permute-start(bf16[4,160,128]{2,1,0:T(8,128)(2,1)S(1)} %collective-permute-done.8.refs_10_), channel_id=1, source_target_pairs={{0,1},{1,0},{2,3},{3,2},{4,5},{5,4},{6,7},{7,6},{8,9},{9,8},{10,11... | collective-permute-start | bytes 491528 | tf_op jit(solution)/shard_map/ppermute | solution.py:644
  24.8 14.9 %copy-start.2 = (bf16[4,240,128]{2,1,0:T(8,128)(2,1)}, bf16[4,240,128]{2,1,0:T(8,128)(2,1)S(1)}, u32[]{:S(2)}) copy-start(bf16[4,240,128]{2,1,0:T(8,128)(2,1)S(1)} %pad_maximum_fusion.refs_8_) | copy-start | bytes 737284
  24.8 14.9 %collective-permute-start.15 = (bf16[4,240,128]{2,1,0:T(8,128)(2,1)S(1)}, bf16[4,240,128]{2,1,0:T(8,128)(2,1)S(1)}, u32[]{:S(2)}, u32[]{:S(2)}) collective-permute-start(bf16[4,240,128]{2,1,0:T(8,128)(2,1)S(1)} %pad_maximum_fusion.refs_8_), channel_id=1, source_target_pairs={{0,6},{1,7},{2,4},{3,5},{4,2},{5,3},{6,0},{7,1},{8,14},{9,15},{10,... | collective-permute-start | bytes 737288 | tf_op jit(solution)/shard_map/ppermute | solution.py:644
  27.2 12.5 %collective-permute-start.14 = (bf16[4,240,128]{2,1,0:T(8,128)(2,1)S(1)}, bf16[4,240,128]{2,1,0:T(8,128)(2,1)S(1)}, u32[]{:S(2)}, u32[]{:S(2)}) collective-permute-start(bf16[4,240,128]{2,1,0:T(8,128)(2,1)S(1)} %pad_maximum_fusion.refs_8_), channel_id=1, source_target_pairs={{0,4},{1,5},{2,6},{3,7},{4,0},{5,1},{6,2},{7,3},{8,12},{9,13},{10,... | collective-permute-start | bytes 737288 | tf_op jit(solution)/shard_map/ppermute | solution.py:644
  27.9 11.9 %collective-permute-start.13 = (bf16[4,240,128]{2,1,0:T(8,128)(2,1)S(1)}, bf16[4,240,128]{2,1,0:T(8,128)(2,1)S(1)}, u32[]{:S(2)}, u32[]{:S(2)}) collective-permute-start(bf16[4,240,128]{2,1,0:T(8,128)(2,1)S(1)} %pad_maximum_fusion.refs_8_), channel_id=1, source_target_pairs={{0,2},{1,3},{2,0},{3,1},{4,6},{5,7},{6,4},{7,5},{8,10},{9,11},{10,... | collective-permute-start | bytes 737288 | tf_op jit(solution)/shard_map/ppermute | solution.py:644
  39.7 2.7 %copy-start.12 = (bf16[4,240,128]{2,1,0:T(8,128)(2,1)}, bf16[4,240,128]{2,1,0:T(8,128)(2,1)S(1)}, u32[]{:S(2)}) copy-start(bf16[4,240,128]{2,1,0:T(8,128)(2,1)S(1)} %collective-permute-done.15.refs_14_) | copy-start | bytes 737284
  39.8 1.6 %collective-permute-start.16 = (bf16[4,240,128]{2,1,0:T(8,128)(2,1)S(1)}, bf16[4,240,128]{2,1,0:T(8,128)(2,1)S(1)}, u32[]{:S(2)}, u32[]{:S(2)}) collective-permute-start(bf16[4,240,128]{2,1,0:T(8,128)(2,1)S(1)} %pad_maximum_fusion.refs_8_), channel_id=1, source_target_pairs={{0,1},{1,0},{2,3},{3,2},{4,5},{5,4},{6,7},{7,6},{8,9},{9,8},{10,11... | collective-permute-start | bytes 737288 | tf_op jit(solution)/shard_map/ppermute | solution.py:644
  39.9 1.9 %collective-permute-start.17 = (bf16[4,240,128]{2,1,0:T(8,128)(2,1)S(1)}, bf16[4,240,128]{2,1,0:T(8,128)(2,1)S(1)}, u32[]{:S(2)}, u32[]{:S(2)}) collective-permute-start(bf16[4,240,128]{2,1,0:T(8,128)(2,1)S(1)} %collective-permute-done.13.refs_10_), channel_id=1, source_target_pairs={{0,1},{1,0},{2,3},{3,2},{4,5},{5,4},{6,7},{7,6},{8,9},{9,8},{10,11... | collective-permute-start | bytes 737288 | tf_op jit(solution)/shard_map/ppermute | solution.py:644
  40.4 1.7 %collective-permute-start.18 = (bf16[4,240,128]{2,1,0:T(8,128)(2,1)S(1)}, bf16[4,240,128]{2,1,0:T(8,128)(2,1)S(1)}, u32[]{:S(2)}, u32[]{:S(2)}) collective-permute-start(bf16[4,240,128]{2,1,0:T(8,128)(2,1)S(1)} %collective-permute-done.14.refs_12_), channel_id=1, source_target_pairs={{0,1},{1,0},{2,3},{3,2},{4,5},{5,4},{6,7},{7,6},{8,9},{9,8},{10,11... | collective-permute-start | bytes 737288 | tf_op jit(solution)/shard_map/ppermute | solution.py:644
  40.4 2.0 %collective-permute-start.19 = (bf16[4,240,128]{2,1,0:T(8,128)(2,1)S(1)}, bf16[4,240,128]{2,1,0:T(8,128)(2,1)S(1)}, u32[]{:S(2)}, u32[]{:S(2)}) collective-permute-start(bf16[4,240,128]{2,1,0:T(8,128)(2,1)S(1)} %collective-permute-done.15.refs_14_), channel_id=1, source_target_pairs={{0,1},{1,0},{2,3},{3,2},{4,5},{5,4},{6,7},{7,6},{8,9},{9,8},{10,11... | collective-permute-start | bytes 737288 | tf_op jit(solution)/shard_map/ppermute | solution.py:644
  90.8 5.9 %copy-start.1 = (bf16[4,384,128]{2,1,0:T(8,128)(2,1)S(1)}, bf16[4,384,128]{2,1,0:T(8,128)(2,1)}, u32[]{:S(2)}) copy-start(bf16[4,384,128]{2,1,0:T(8,128)(2,1)} %get-tuple-element.123) | copy-start | bytes 1179652
  90.8 8.0 %copy-start = (bf16[4,384,128]{2,1,0:T(8,128)(2,1)S(1)}, bf16[4,384,128]{2,1,0:T(8,128)(2,1)}, u32[]{:S(2)}) copy-start(bf16[4,384,128]{2,1,0:T(8,128)(2,1)} %get-tuple-element.117) | copy-start | bytes 1179652
  90.8 2.0 %collective-permute-start.21 = (bf16[4,384,128]{2,1,0:T(8,128)(2,1)}, bf16[4,384,128]{2,1,0:T(8,128)(2,1)S(1)}, u32[]{:S(2)}, u32[]{:S(2)}) collective-permute-start(bf16[4,384,128]{2,1,0:T(8,128)(2,1)} %get-tuple-element.120), channel_id=1, source_target_pairs={{0,1},{1,0},{2,3},{3,2},{4,5},{5,4},{6,7},{7,6},{8,9},{9,8},{10,11... | collective-permute-start | bytes 1179656 | tf_op jit(solution)/shard_map/ppermute | solution.py:644
  91.1 4.4 %collective-permute-start.22 = (bf16[4,384,128]{2,1,0:T(8,128)(2,1)}, bf16[4,384,128]{2,1,0:T(8,128)(2,1)S(1)}, u32[]{:S(2)}, u32[]{:S(2)}) collective-permute-start(bf16[4,384,128]{2,1,0:T(8,128)(2,1)} %get-tuple-element.122), channel_id=1, source_target_pairs={{0,1},{1,0},{2,3},{3,2},{4,5},{5,4},{6,7},{7,6},{8,9},{9,8},{10,11... | collective-permute-start | bytes 1179656 | tf_op jit(solution)/shard_map/ppermute | solution.py:644
  91.4 7.4 %collective-permute-start.20 = (bf16[4,384,128]{2,1,0:T(8,128)(2,1)}, bf16[4,384,128]{2,1,0:T(8,128)(2,1)S(1)}, u32[]{:S(2)}, u32[]{:S(2)}) collective-permute-start(bf16[4,384,128]{2,1,0:T(8,128)(2,1)} %get-tuple-element.118), channel_id=1, source_target_pairs={{0,1},{1,0},{2,3},{3,2},{4,5},{5,4},{6,7},{7,6},{8,9},{9,8},{10,11... | collective-permute-start | bytes 1179656 | tf_op jit(solution)/shard_map/ppermute | solution.py:644
  91.6 5.2 %collective-permute-start.23 = (bf16[4,384,128]{2,1,0:T(8,128)(2,1)}, bf16[4,384,128]{2,1,0:T(8,128)(2,1)S(1)}, u32[]{:S(2)}, u32[]{:S(2)}) collective-permute-start(bf16[4,384,128]{2,1,0:T(8,128)(2,1)} %get-tuple-element.124), channel_id=1, source_target_pairs={{0,1},{1,0},{2,3},{3,2},{4,5},{5,4},{6,7},{7,6},{8,9},{9,8},{10,11... | collective-permute-start | bytes 1179656 | tf_op jit(solution)/shard_map/ppermute | solution.py:644
  94.0 17.7 %collective-permute-start.24 = (bf16[4,384,128]{2,1,0:T(8,128)(2,1)S(1)}, bf16[4,384,128]{2,1,0:T(8,128)(2,1)S(1)}, u32[]{:S(2)}, u32[]{:S(2)}) collective-permute-start(bf16[4,384,128]{2,1,0:T(8,128)(2,1)S(1)} %add_convert_fusion.2), channel_id=1, source_target_pairs={{0,2},{1,3},{2,0},{3,1},{4,6},{5,7},{6,4},{7,5},{8,10},{9,11},{10,... | collective-permute-start | bytes 1179656 | tf_op jit(solution)/shard_map/ppermute | solution.py:644
  96.6 19.4 %collective-permute-start.25 = (bf16[4,384,128]{2,1,0:T(8,128)(2,1)S(1)}, bf16[4,384,128]{2,1,0:T(8,128)(2,1)S(1)}, u32[]{:S(2)}, u32[]{:S(2)}) collective-permute-start(bf16[4,384,128]{2,1,0:T(8,128)(2,1)S(1)} %add_convert_fusion.1), channel_id=1, source_target_pairs={{0,4},{1,5},{2,6},{3,7},{4,0},{5,1},{6,2},{7,3},{8,12},{9,13},{10,... | collective-permute-start | bytes 1179656 | tf_op jit(solution)/shard_map/ppermute | solution.py:644
  96.9 19.2 %collective-permute-start.26 = (bf16[4,384,128]{2,1,0:T(8,128)(2,1)S(1)}, bf16[4,384,128]{2,1,0:T(8,128)(2,1)S(1)}, u32[]{:S(2)}, u32[]{:S(2)}) collective-permute-start(bf16[4,384,128]{2,1,0:T(8,128)(2,1)S(1)} %add_convert_fusion), channel_id=1, source_target_pairs={{0,6},{1,7},{2,4},{3,5},{4,2},{5,3},{6,0},{7,1},{8,14},{9,15},{10,... | collective-permute-start | bytes 1179656 | tf_op jit(solution)/shard_map/ppermute | solution.py:644
  116.9 7.5 %collective-permute-start.29 = (bf16[384,128]{1,0:T(8,128)(2,1)S(1)}, bf16[384,128]{1,0:T(8,128)(2,1)S(1)}, u32[]{:S(2)}, u32[]{:S(2)}) collective-permute-start(bf16[384,128]{1,0:T(8,128)(2,1)S(1)} %get-tuple-element.154), channel_id=1, source_target_pairs={{0,24},{1,25},{2,26},{3,27},{4,28},{5,29},{6,30},{7,31},{8,16},{9,... | collective-permute-start | bytes 294920 | tf_op jit(solution)/shard_map/ppermute | solution.py:644
  118.8 9.6 %collective-permute-start.28 = (bf16[384,128]{1,0:T(8,128)(2,1)S(1)}, bf16[384,128]{1,0:T(8,128)(2,1)S(1)}, u32[]{:S(2)}, u32[]{:S(2)}) collective-permute-start(bf16[384,128]{1,0:T(8,128)(2,1)S(1)} %get-tuple-element.155), channel_id=1, source_target_pairs={{0,16},{1,17},{2,18},{3,19},{4,20},{5,21},{6,22},{7,23},{8,24},{9,... | collective-permute-start | bytes 294920 | tf_op jit(solution)/shard_map/ppermute | solution.py:644
  120.4 8.0 %collective-permute-start.27 = (bf16[384,128]{1,0:T(8,128)(2,1)S(1)}, bf16[384,128]{1,0:T(8,128)(2,1)S(1)}, u32[]{:S(2)}, u32[]{:S(2)}) collective-permute-start(bf16[384,128]{1,0:T(8,128)(2,1)S(1)} %get-tuple-element.156), channel_id=1, source_target_pairs={{0,8},{1,9},{2,10},{3,11},{4,12},{5,13},{6,14},{7,15},{8,0},{9,1},... | collective-permute-start | bytes 294920 | tf_op jit(solution)/shard_map/ppermute | solution.py:644
  124.4 3.9 %copy-start.4 = (bf16[384,128]{1,0:T(8,128)(2,1)}, bf16[384,128]{1,0:T(8,128)(2,1)S(1)}, u32[]{:S(2)}) copy-start(bf16[384,128]{1,0:T(8,128)(2,1)S(1)} %collective-permute-done.29.r3) | copy-start | bytes 294916
  130.9 1.4 collective-permute-start.30
  133.0 4.8 %collective-permute-start.33 = (f32[32,128]{1,0:T(8,128)S(1)}, f32[32,128]{1,0:T(8,128)S(1)}, u32[]{:S(2)}, u32[]{:S(2)}) collective-permute-start(f32[32,128]{1,0:T(8,128)S(1)} %add.104), channel_id=1, source_target_pairs={{0,6},{1,7},{2,4},{3,5},{4,2},{5,3},{6,0},{7,1},{8,14},{9,15},{10,... | collective-permute-start | bytes 49160 | tf_op jit(solution)/shard_map/ppermute | solution.py:644
  133.8 4.0 %collective-permute-start.32 = (f32[32,128]{1,0:T(8,128)S(1)}, f32[32,128]{1,0:T(8,128)S(1)}, u32[]{:S(2)}, u32[]{:S(2)}) collective-permute-start(f32[32,128]{1,0:T(8,128)S(1)} %add.104), channel_id=1, source_target_pairs={{0,4},{1,5},{2,6},{3,7},{4,0},{5,1},{6,2},{7,3},{8,12},{9,13},{10,... | collective-permute-start | bytes 49160 | tf_op jit(solution)/shard_map/ppermute | solution.py:644
  135.1 3.7 %collective-permute-start.31 = (f32[32,128]{1,0:T(8,128)S(1)}, f32[32,128]{1,0:T(8,128)S(1)}, u32[]{:S(2)}, u32[]{:S(2)}) collective-permute-start(f32[32,128]{1,0:T(8,128)S(1)} %add.104), channel_id=1, source_target_pairs={{0,2},{1,3},{2,0},{3,1},{4,6},{5,7},{6,4},{7,5},{8,10},{9,11},{10,... | collective-permute-start | bytes 49160 | tf_op jit(solution)/shard_map/ppermute | solution.py:644
  138.8 6.7 %copy-start.7 = (f32[32,128]{1,0:T(8,128)}, f32[32,128]{1,0:T(8,128)S(1)}, u32[]{:S(2)}) copy-start(f32[32,128]{1,0:T(8,128)S(1)} %add_add_fusion.refs_1_) | copy-start | bytes 49156
  138.8 5.6 %collective-permute-start.36 = (f32[32,128]{1,0:T(8,128)S(1)}, f32[32,128]{1,0:T(8,128)S(1)}, u32[]{:S(2)}, u32[]{:S(2)}) collective-permute-start(f32[32,128]{1,0:T(8,128)S(1)} %add_add_fusion.refs_1_), channel_id=1, source_target_pairs={{0,24},{1,25},{2,26},{3,27},{4,28},{5,29},{6,30},{7,31},{8,16},{9,... | collective-permute-start | bytes 49160 | tf_op jit(solution)/shard_map/ppermute | solution.py:644
  140.8 4.6 %collective-permute-start.35 = (f32[32,128]{1,0:T(8,128)S(1)}, f32[32,128]{1,0:T(8,128)S(1)}, u32[]{:S(2)}, u32[]{:S(2)}) collective-permute-start(f32[32,128]{1,0:T(8,128)S(1)} %add_add_fusion.refs_1_), channel_id=1, source_target_pairs={{0,16},{1,17},{2,18},{3,19},{4,20},{5,21},{6,22},{7,23},{8,24},{9,... | collective-permute-start | bytes 49160 | tf_op jit(solution)/shard_map/ppermute | solution.py:644
  140.8 4.6 %collective-permute-start.34 = (f32[32,128]{1,0:T(8,128)S(1)}, f32[32,128]{1,0:T(8,128)S(1)}, u32[]{:S(2)}, u32[]{:S(2)}) collective-permute-start(f32[32,128]{1,0:T(8,128)S(1)} %add_add_fusion.refs_1_), channel_id=1, source_target_pairs={{0,8},{1,9},{2,10},{3,11},{4,12},{5,13},{6,14},{7,15},{8,0},{9,1},... | collective-permute-start | bytes 49160 | tf_op jit(solution)/shard_map/ppermute | solution.py:644
  (15 other events, 15.3 us)
